TPU v7x, 32 devices: a whole 2x2x4 slice. The times are simulated.
32 devices in a mesh: clips: 2 (over y), space: 4 (over z), tm: 2 (over x), chan: 2 (over core).
Axes of the slice: x: 2, y: 2, z: 4, core: 2. Of those that a mesh axis runs over, the one named last changes fastest.
Arguments:
- frames_in: bfloat16 [4, 16, 160, 384], P(('clips', 'tm'), 'space', None, 'chan'), parts along dimension 0, may hold values from -6 to 6
- cache: bfloat16 [4, 16, 160, 384], P('clips', 'space'), parts along dimension 0, may hold values from -6 to 6
- gain_one: bfloat16 [384], replicated, may hold values from 0.099609375 to 1.8984375
- gain_two: bfloat16 [384], replicated, may hold values from 0.099609375 to 1.8984375
- w_query: bfloat16 [384, 384], replicated, may hold values from -10 to 10
- w_key: bfloat16 [384, 384], replicated, may hold values from -10 to 10
- w_value: bfloat16 [384, 384], replicated, may hold values from -0.3125 to 0.3125
- w_out: bfloat16 [384, 384], replicated, may hold values from -0.3125 to 0.3125
- conv_weight: bfloat16 [3, 3, 3, 384, 384], P(None, None, None, None, 'chan'), may hold values from -0.0625 to 0.0625
Outputs:
- decoded: bfloat16 [4, 16, 160, 384], P(('clips', 'tm'), 'space', None, 'chan'), parts along dimension 0
There are 2 independent parts, one for each index of `clips`. A program takes and returns all parts, laid end to end along the dimension named above; an argument that names none is the same for every part. Nothing has to cross between parts.
All inputs are finite; a program needn't handle non-finite values.
Results may differ from a plain program's by a relative error of at most 0.0062.
Values may be sent and summed in bfloat16 or wider, within the bound.
No kernel may reach another device: no remote copies, remote signals or barrier semaphores. Data moves between devices by JAX's collectives and lax.ppermute only.
A program may use at most 128 MiB of HBM per device.

v0:
```python
import jax
import jax.numpy as jnp
from jax import lax
from jax.sharding import PartitionSpec as P


def from_behind(array, axis, by):
    devices = lax.axis_size(axis)
    pairs = [(i, i + by) for i in range(devices) if 0 <= i + by < devices]
    return lax.ppermute(array, axis, pairs)


def padded_2(cells, sides, width):
    for axis, dim in sides:
        count = lax.axis_size(axis)
        ends = count - 1
        head = lax.slice_in_dim(cells, 0, width, axis=dim)
        tail = lax.slice_in_dim(cells, cells.shape[dim] - width, cells.shape[dim], axis=dim)
        cells = jnp.concatenate(
            [
                lax.ppermute(tail, axis, [(i, (i + 1) % count) for i in range(ends)]),
                cells,
                lax.ppermute(head, axis, [((i + 1) % count, i) for i in range(ends)]),
            ],
            axis=dim,
        )
    return cells


def rms_scaled(values, gain):
    wide = values.astype(jnp.float32)
    factor = lax.rsqrt(jnp.mean(wide * wide, axis=-1, keepdims=True) + 1e-06)
    return wide * factor * gain.astype(jnp.float32)


def body(frames_in, cache, gain_one, gain_two, w_query, w_key, w_value, w_out, conv_weight):
    mine = lax.axis_index("chan")
    own = lax.all_to_all(frames_in, "chan", split_axis=1, concat_axis=3, tiled=True)
    half_rows, cells, width = (own.shape[1], own.shape[2], own.shape[3])
    tokens = own.reshape(half_rows * cells, width)
    normed = rms_scaled(tokens, gain_one).astype(jnp.bfloat16)
    query = jnp.dot(normed, w_query, preferred_element_type=jnp.float32).astype(jnp.bfloat16)
    scale = width ** (-0.5)
    count = tokens.shape[0]
    piece = lax.all_gather(normed, ("space", "chan"), axis=0, tiled=True)
    keys = jnp.dot(piece, w_key, preferred_element_type=jnp.float32).astype(jnp.bfloat16)
    values = jnp.dot(piece, w_value, preferred_element_type=jnp.float32).astype(jnp.bfloat16)
    top = jnp.full((count, 1), -1e30, jnp.float32)
    scores = jnp.einsum("qc,kc->qk", query, keys, preferred_element_type=jnp.float32) * scale
    new_top = jnp.maximum(top, jnp.max(scores, axis=-1, keepdims=True))
    weights = jnp.exp(scores - new_top)
    total = jnp.sum(weights, axis=-1, keepdims=True)
    accum = jnp.dot(weights.astype(jnp.bfloat16), values, preferred_element_type=jnp.float32)
    top, total, accum = (new_top, total, accum)
    attended = (accum / total).astype(jnp.bfloat16)
    joined = tokens.astype(jnp.float32) + jnp.dot(
        attended, w_out, preferred_element_type=jnp.float32
    )
    joined = joined.astype(jnp.bfloat16).reshape(1, half_rows, cells, width)
    whole = lax.all_gather(joined, "chan", axis=1, tiled=True)
    act = jax.nn.silu(rms_scaled(whole, gain_two)).astype(jnp.bfloat16)
    moment = lax.axis_index("tm")
    first = from_behind(act, "tm", 1)
    second = from_behind(act, "tm", 2)
    prev_one = jnp.where(moment == 0, cache[1:2], first)
    prev_two = jnp.where(moment == 0, cache[0:1], jnp.where(moment == 1, cache[1:2], second))
    stacked = jnp.concatenate([prev_two, prev_one, act], axis=0)
    rimmed = padded_2(stacked, (("space", 1),), 1)
    padded = jnp.pad(rimmed, ((0, 0), (0, 0), (1, 1), (0, 0)))
    conv = lax.conv_general_dilated(
        padded[None],
        conv_weight,
        (1, 1, 1),
        "VALID",
        dimension_numbers=("NDHWC", "DHWIO", "NDHWC"),
        preferred_element_type=jnp.float32,
    )[0]
    share = conv_weight.shape[4]
    own_joined = lax.dynamic_slice_in_dim(whole, mine * share, share, 3)
    return (own_joined.astype(jnp.float32) + conv).astype(jnp.bfloat16)


def solution(mesh):
    return jax.shard_map(
        body,
        mesh=mesh,
        in_specs=(
            P(("clips", "tm"), "space", None, "chan"),
            P("clips", "space", None, None),
            P(),
            P(),
            P(),
            P(),
            P(),
            P(),
            P(None, None, None, None, "chan"),
        ),
        out_specs=P(("clips", "tm"), "space", None, "chan"),
        check_vma=False,
    )
```

profile of v0, /device:TPU:0, one launch (start us, length us, event | category | flops | bytes accessed | tf_op | source)
XLA Modules:
  0.0 116.3 jit_solution(1926624197613109839)
XLA Ops:
  6.5 0.0 copy-start
  6.5 0.0 all-gather.2.cloned.1.call-start
  6.6 5.2 %all_to_all.4 = bf16[1,4,160,192]{3,2,0,1:T(8,128)(2,1)S(1)} all-to-all(bf16[1,4,160,192]{3,2,0,1:T(8,128)(2,1)} %bitcast.55), channel_id=1, replica_groups=mesh['clips'=2,'space'=4,'tm'=2,'chan'=2] {'chan'}, dimensions={1} | all-to-all | bytes 491520 | tf_op jit(solution)/shard_map/all_to_all | solution.py:38
  11.8 0.3 copy.58
  12.1 0.5 reshape.60
  12.6 0.2 multiply_reduce_fusion
  12.9 0.1 rsqrt.20
  13.0 0.0 copy-done.4
  13.0 0.8 multiply_convert_fusion
  13.8 0.0 all-gather.2.cloned.1.call-update
  13.8 0.0 copy-done.5
  13.8 0.0 copy-done.2
  13.8 1.3 %convolution_convert_fusion.2 = bf16[320,384]{1,0:T(8,128)(2,1)S(1)} fusion(bf16[320,384]{1,0:T(8,128)(2,1)} %multiply_convert_fusion, bf16[384,384]{1,0:T(8,128)(2,1)S(1)} %copy-done.2), kind=kOutput, calls=%fused_computation.32 | convolution fusion | flops 94494720 | bytes 786432 | tf_op jit(solution)/shard_map/dot_general | solution.py:42
  15.1 29.6 %all-gather.2.cloned.1.call-done = bf16[2560,384]{1,0:T(8,128)(2,1)} async-done(((bf16[320,384]{1,0:T(8,128)(2,1)}), bf16[2560,384]{1,0:T(8,128)(2,1)}) %all-gather.2.cloned.1.call-update) | async-done | bytes 1966096 | tf_op jit(solution)/shard_map/all_gather | solution.py:45
  44.7 5.4 %fusion.46 = (f32[320]{0:T(512)S(1)}, f32[320,2560]{1,0:T(8,128)}) fusion(bf16[320,384]{1,0:T(8,128)(2,1)S(1)} %convolution_convert_fusion.2, bf16[2560,384]{1,0:T(8,128)(2,1)} %all-gather.2.cloned.1.call-done, bf16[384,384]{1,0:T(8,128)(2,1)S(1)} %copy-done), kind=kOutput, calls=%fused_computation.64 | convolution fusion | flops 1386741504 | bytes 5784832 | tf_op jit(solution)/shard_map/qc,kc->qk/dot_general | solution.py:49
  50.1 2.6 %fusion.2 = f32[320]{0:T(512)S(1)} fusion(f32[320,2560]{1,0:T(8,128)} %get-tuple-element.10, f32[320]{0:T(512)S(1)} %broadcast_maximum_fusion), kind=kLoop, calls=%fused_computation.9 | loop fusion | flops 1638080 | bytes 3279360 | tf_op jit(solution)/shard_map/reduce_sum | solution.py:52
  52.7 0.0 copy-start.3
  52.7 4.8 %fusion.28 = bf16[320,384]{1,0:T(8,128)(2,1)S(1)} fusion(f32[320,2560]{1,0:T(8,128)} %get-tuple-element.10, f32[320]{0:T(512)S(1)} %broadcast_maximum_fusion, bf16[2560,384]{1,0:T(8,128)(2,1)} %all-gather.2.cloned.1.call-done, bf16[384,384]{1,0:T(8,128)(2,1)S(1)} %copy-done.7, f32[320]{0:T(512)S(1)} %fusion.2), kind=kOutput, calls=%fused_computation.35 | convolution fusion | flops 1386987520 | bytes 5786112 | tf_op jit(solution)/shard_map/dot_general | solution.py:53
  57.5 0.0 copy-done.3
  57.5 0.0 copy-start.1
  57.5 0.3 fusion.24
  57.9 2.2 %all_gather.7 = bf16[1,4,160,384]{3,2,0,1:T(8,128)(2,1)S(1)} all-gather(bf16[1,2,160,384]{3,2,0,1:T(8,128)(2,1)S(1)} %bitcast.53), channel_id=1, replica_groups=mesh['clips'=2,'space'=4,'tm'=2,'chan'=2] {'chan'}, dimensions={1}, use_global_device_ids=true | all-gather | bytes 737280 | tf_op jit(solution)/shard_map/all_gather | solution.py:60
  60.0 0.2 fusion.31
  60.3 0.4 fusion.38
  60.6 1.4 %collective-permute-start = (bf16[1,4,160,384]{3,2,0,1:T(8,128)(2,1)S(1)}, bf16[1,4,160,384]{3,2,0,1:T(8,128)(2,1)}, u32[]{:S(2)}, u32[]{:S(2)}) collective-permute-start(bf16[1,4,160,384]{3,2,0,1:T(8,128)(2,1)S(1)} %fusion.38), channel_id=1, source_target_pairs={} | collective-permute-start | bytes 1474568 | tf_op jit(solution)/shard_map/ppermute | solution.py:10
  62.1 4.2 %collective-permute-start.1 = (bf16[1,4,160,384]{3,2,0,1:T(8,128)(2,1)S(1)}, bf16[1,4,160,384]{3,2,0,1:T(8,128)(2,1)}, u32[]{:S(2)}, u32[]{:S(2)}) collective-permute-start(bf16[1,4,160,384]{3,2,0,1:T(8,128)(2,1)S(1)} %fusion.38), channel_id=1, source_target_pairs={{0,2},{1,3},{4,6},{5,7},{8,10},{9,11},{12,14},{13,15},{16,18},{17,... | collective-permute-start | bytes 1474568 | tf_op jit(solution)/shard_map/ppermute | solution.py:10
  66.2 0.0 collective-permute-done
  66.2 10.1 %collective-permute-done.1 = bf16[1,4,160,384]{3,2,0,1:T(8,128)(2,1)} collective-permute-done((bf16[1,4,160,384]{3,2,0,1:T(8,128)(2,1)S(1)}, bf16[1,4,160,384]{3,2,0,1:T(8,128)(2,1)}, u32[]{:S(2)}, u32[]{:S(2)}) %collective-permute-start.1) | collective-permute-done | bytes 491552 | tf_op jit(solution)/shard_map/ppermute | solution.py:10
  76.3 1.1 fusion.41
  77.5 1.0 maximum_bitcast_fusion
  78.4 3.5 %collective-permute-start.2 = (bf16[3,1,160,384]{3,2,1,0:T(8,128)(2,1)}, bf16[3,1,160,384]{3,2,1,0:T(8,128)(2,1)S(1)}, u32[]{:S(2)}, u32[]{:S(2)}) collective-permute-start(bf16[3,1,160,384]{3,2,1,0:T(8,128)(2,1)} %get-tuple-element.5), channel_id=1, source_target_pairs={{0,4},{4,8},{8,12},{1,5},{5,9},{9,13},{2,6},{6,10},{10,14},{3,7},{... | collective-permute-start | bytes 1105928 | tf_op jit(solution)/shard_map/ppermute | solution.py:21
  81.9 1.5 %collective-permute-start.3 = (bf16[3,1,160,384]{3,2,1,0:T(8,128)(2,1)}, bf16[3,1,160,384]{3,2,1,0:T(8,128)(2,1)}, u32[]{:S(2)}, u32[]{:S(2)}) collective-permute-start(bf16[3,1,160,384]{3,2,1,0:T(8,128)(2,1)} %get-tuple-element.6), channel_id=1, source_target_pairs={{4,0},{8,4},{12,8},{5,1},{9,5},{13,9},{6,2},{10,6},{14,10},{7,3},{... | collective-permute-start | bytes 1105928 | tf_op jit(solution)/shard_map/ppermute | solution.py:23
  83.4 0.2 constant_dynamic-slice_fusion
  83.6 6.1 %collective-permute-done.2 = bf16[3,1,160,384]{3,2,1,0:T(8,128)(2,1)S(1)} collective-permute-done((bf16[3,1,160,384]{3,2,1,0:T(8,128)(2,1)}, bf16[3,1,160,384]{3,2,1,0:T(8,128)(2,1)S(1)}, u32[]{:S(2)}, u32[]{:S(2)}) %collective-permute-start.2) | collective-permute-done | bytes 368672 | tf_op jit(solution)/shard_map/ppermute | solution.py:21
  89.7 4.1 %collective-permute-done.3 = bf16[3,1,160,384]{3,2,1,0:T(8,128)(2,1)} collective-permute-done((bf16[3,1,160,384]{3,2,1,0:T(8,128)(2,1)}, bf16[3,1,160,384]{3,2,1,0:T(8,128)(2,1)}, u32[]{:S(2)}, u32[]{:S(2)}) %collective-permute-start.3) | collective-permute-done | bytes 368672 | tf_op jit(solution)/shard_map/ppermute | solution.py:23
  93.8 3.1 %fusion.11 = bf16[3,6,1,162,384]{4,3,0,1,2:T(8,128)(2,1)S(1)} fusion(bf16[3,1,160,384]{3,2,0,1:T(8,128)(2,1)} %bitcast.8, bf16[3,1,160,384]{3,2,0,1:T(8,128)(2,1)S(1)} %bitcast.54, bf16[1,4,160,384]{3,2,0,1:T(8,128)(2,1)S(1)} %fusion.38, bf16[1,4,160,384]{3,2,0,1:T(8,128)(2,1)S(1)} %get-tuple-element.8, bf16[1,4,160,384]{3,2,0,1:T(8,128)(2,1)S(1)} %get-tuple-element.7), kind=kLoop, calls=%fused_computation.18 | loop fusion | flops 20155392 | bytes 4451328 | tf_op jit(solution)/shard_map/broadcast_in_dim | solution.py:71
  96.9 1.6 %pad.5 = bf16[3,6,1,168,384]{4,3,0,1,2:T(8,128)(2,1)} pad(bf16[3,6,1,162,384]{4,3,0,1,2:T(8,128)(2,1)S(1)} %fusion.11, bf16[]{:T(256)} %constant.34.clone.1), padding=0_0x0_0x0_0x0_6x0_0 | pad | bytes 4561922 | tf_op jit(solution)/shard_map/broadcast_in_dim | solution.py:71
  98.5 3.5 %reshape.69 = bf16[3,6,1,8,21,384]{5,4,3,0,1,2:T(8,128)(2,1)S(1)} reshape(bf16[3,6,1,168,384]{4,3,0,1,2:T(8,128)(2,1)} %pad.5) | data formatting | bytes 4644864 | tf_op jit(solution)/shard_map/conv_general_dilated | solution.py:70
  102.0 0.0 copy-start.6
  102.0 0.0 copy-start.8
  102.1 0.3 copy.47
  102.4 0.1 slice.19
  102.4 1.7 %copy-done.6 = bf16[3,3,3,384,192]{3,4,2,1,0:T(8,128)(2,1)S(1)} copy-done((bf16[3,3,3,384,192]{3,4,2,1,0:T(8,128)(2,1)S(1)}, bf16[3,3,3,384,192]{3,4,2,1,0:T(8,128)(2,1)}, u32[]{:S(2)}) %copy-start.6) | copy-done | bytes 3981336
  104.2 0.0 copy-done.8
  104.2 3.9 %fusion.21 = f32[1,4,8,21,192]{4,2,3,1,0:T(8,128)S(1)} fusion(bf16[3,3,3,384,192]{3,4,2,1,0:T(8,128)(2,1)S(1)} %copy-done.6, bf16[3,6,1,7,2,384]{5,3,4,1,0,2:T(8,128)(2,1)S(1)} %slice.19, bf16[3,6,1,8,21,384]{5,3,4,1,0,2:T(8,128)(2,1)S(1)} %copy.47, pred[8,21]{0,1:T(8,128)(4,1)S(1)} %copy-done.8), kind=kOutput, calls=%fused_computation.28 | convolution fusion | flops 2683201536 | bytes 7013544 | tf_op jit(solution)/shard_map/conv_general_dilated | solution.py:70
  108.1 0.3 copy.48
  108.4 0.3 fusion.40
  108.7 0.8 copy.49
  (14 shorter events, 0.1 us)
Async XLA Ops:
  6.5 38.2 %copy-start = (bf16[384,384]{1,0:T(8,128)(2,1)S(1)}, bf16[384,384]{1,0:T(8,128)(2,1)}, u32[]{:S(2)}) copy-start(bf16[384,384]{1,0:T(8,128)(2,1)} %param.14) | copy-start | bytes 884740
  6.5 6.4 %copy-start.4 = (bf16[384]{0:T(512)(128)(2,1)S(1)}, bf16[384]{0:T(512)(128)(2,1)}, u32[]{:S(2)}) copy-start(bf16[384]{0:T(512)(128)(2,1)} %param.11) | copy-start | bytes 2308
  6.5 7.3 %copy-start.5 = (bf16[384]{0:T(512)(128)(2,1)S(1)}, bf16[384]{0:T(512)(128)(2,1)}, u32[]{:S(2)}) copy-start(bf16[384]{0:T(512)(128)(2,1)} %param.12) | copy-start | bytes 2308
  6.5 7.3 %copy-start.2 = (bf16[384,384]{1,0:T(8,128)(2,1)S(1)}, bf16[384,384]{1,0:T(8,128)(2,1)}, u32[]{:S(2)}) copy-start(bf16[384,384]{1,0:T(8,128)(2,1)} %param.13) | copy-start | bytes 884740
  6.5 38.1 %all-gather.2.cloned.1.call-start = ((), (), s32[]{:S(2)}) async-start(), calls=%async_computation.1 | async-start | bytes 2211840 | tf_op jit(solution)/shard_map/all_gather | solution.py:45
  50.1 2.6 %copy-start.7 = (bf16[384,384]{1,0:T(8,128)(2,1)S(1)}, bf16[384,384]{1,0:T(8,128)(2,1)}, u32[]{:S(2)}) copy-start(bf16[384,384]{1,0:T(8,128)(2,1)} %param.15) | copy-start | bytes 884740
  52.7 4.8 %copy-start.3 = (bf16[384,384]{1,0:T(8,128)(2,1)S(1)}, bf16[384,384]{1,0:T(8,128)(2,1)}, u32[]{:S(2)}) copy-start(bf16[384,384]{1,0:T(8,128)(2,1)} %param.16) | copy-start | bytes 884740
  57.5 18.8 %copy-start.1 = (bf16[2,4,160,384]{3,2,1,0:T(8,128)(2,1)S(1)}, bf16[2,4,160,384]{3,2,1,0:T(8,128)(2,1)}, u32[]{:S(2)}) copy-start(bf16[2,4,160,384]{3,2,1,0:T(8,128)(2,1)} %param.10) | copy-start | bytes 2949124
  60.6 5.6 %collective-permute-start = (bf16[1,4,160,384]{3,2,0,1:T(8,128)(2,1)S(1)}, bf16[1,4,160,384]{3,2,0,1:T(8,128)(2,1)}, u32[]{:S(2)}, u32[]{:S(2)}) collective-permute-start(bf16[1,4,160,384]{3,2,0,1:T(8,128)(2,1)S(1)} %fusion.38), channel_id=1, source_target_pairs={} | collective-permute-start | bytes 1474568 | tf_op jit(solution)/shard_map/ppermute | solution.py:10
  62.1 14.2 %collective-permute-start.1 = (bf16[1,4,160,384]{3,2,0,1:T(8,128)(2,1)S(1)}, bf16[1,4,160,384]{3,2,0,1:T(8,128)(2,1)}, u32[]{:S(2)}, u32[]{:S(2)}) collective-permute-start(bf16[1,4,160,384]{3,2,0,1:T(8,128)(2,1)S(1)} %fusion.38), channel_id=1, source_target_pairs={{0,2},{1,3},{4,6},{5,7},{8,10},{9,11},{12,14},{13,15},{16,18},{17,... | collective-permute-start | bytes 1474568 | tf_op jit(solution)/shard_map/ppermute | solution.py:10
  78.4 11.2 %collective-permute-start.2 = (bf16[3,1,160,384]{3,2,1,0:T(8,128)(2,1)}, bf16[3,1,160,384]{3,2,1,0:T(8,128)(2,1)S(1)}, u32[]{:S(2)}, u32[]{:S(2)}) collective-permute-start(bf16[3,1,160,384]{3,2,1,0:T(8,128)(2,1)} %get-tuple-element.5), channel_id=1, source_target_pairs={{0,4},{4,8},{8,12},{1,5},{5,9},{9,13},{2,6},{6,10},{10,14},{3,7},{... | collective-permute-start | bytes 1105928 | tf_op jit(solution)/shard_map/ppermute | solution.py:21
  81.9 11.9 %collective-permute-start.3 = (bf16[3,1,160,384]{3,2,1,0:T(8,128)(2,1)}, bf16[3,1,160,384]{3,2,1,0:T(8,128)(2,1)}, u32[]{:S(2)}, u32[]{:S(2)}) collective-permute-start(bf16[3,1,160,384]{3,2,1,0:T(8,128)(2,1)} %get-tuple-element.6), channel_id=1, source_target_pairs={{4,0},{8,4},{12,8},{5,1},{9,5},{13,9},{6,2},{10,6},{14,10},{7,3},{... | collective-permute-start | bytes 1105928 | tf_op jit(solution)/shard_map/ppermute | solution.py:23
  102.0 2.1 %copy-start.6 = (bf16[3,3,3,384,192]{3,4,2,1,0:T(8,128)(2,1)S(1)}, bf16[3,3,3,384,192]{3,4,2,1,0:T(8,128)(2,1)}, u32[]{:S(2)}) copy-start(bf16[3,3,3,384,192]{3,4,2,1,0:T(8,128)(2,1)} %param.17) | copy-start | bytes 11943940
  102.0 2.1 %copy-start.8 = (pred[8,21]{0,1:T(8,128)(4,1)S(1)}, pred[8,21]{0,1:T(8,128)(4,1)}, u32[]{:S(2)}) copy-start(pred[8,21]{0,1:T(8,128)(4,1)} %constant.42) | copy-start | bytes 508
Sparse Core Ops, SparseCore 0:
  13.9 30.7 all-gather.1
where the time goes:
time: 117 us; the launch traced here: 116 us
  waiting for transfers between devices  49.9 us (43%)
  matrix products  15.7 us (13%)
  between operations  13.6 us (12%)
  starting transfers between devices  10.6 us (9%)
  other arithmetic  9.76 us (8%)
  local copies, waits for them, and re-layouts  9.41 us (8%)
  blocking collectives  7.34 us (6%)
    all_gather x1, waiting for transfers between devices, body(): piece = lax.all_gather(normed, ('space', 'chan'), axis=0, tiled=True)  29.6 us
    ppermute x2, waiting for transfers between devices, from_behind(): return lax.ppermute(array, axis, pairs)  10.1 us
    ppermute x1, waiting for transfers between devices, padded_2(): lax.ppermute(tail, axis, [(i, (i + 1) % count) for i in range(ends)])  6.08 us
    ppermute x2, starting transfers between devices, from_behind(): return lax.ppermute(array, axis, pairs)  5.6 us
    dot_general x1, matrix products, body(): jnp.einsum('qc,kc->qk', query, keys, preferred_element_type=jnp.float32)  5.41 us
    all_to_all x1, blocking collectives, body(): lax.all_to_all(frames_in, 'chan', split_axis=1, concat_axis=3, tiled=True)  5.19 us
    dot_general x1, matrix products, body(): jnp.dot(weights.astype(jnp.bfloat16), values, preferred_element_type=jnp....  4.79 us
    ppermute x1, waiting for transfers between devices, padded_2(): lax.ppermute(head, axis, [((i + 1) % count, i) for i in range(ends)])  4.14 us
  transfers between devices with their start and end apart: 5, of which 4 were waited for; matrix products, arithmetic and copies ran while one was open for 1% of the time, Pallas kernels for 0%

commit v1 on v0

v1 whole, which is shorter than its diff:
```python
import functools
import math
import jax
import jax.numpy as jnp
from jax import lax
from jax.experimental import pallas as pl
from jax.experimental.pallas import tpu as pltpu
from jax.sharding import PartitionSpec as P

EPS = 1e-06
LANES = 128
BF = jnp.bfloat16
F32 = jnp.float32


def cycle(array, axis, by):
    count = lax.axis_size(axis)
    return lax.ppermute(array, axis, [(i, (i + by) % count) for i in range(count)])


def call(kernel, outs, args, scratch=(), flops=0, exps=0):
    vmem = pl.BlockSpec(memory_space=pltpu.VMEM)
    moved = sum(math.prod(a.shape) * a.dtype.itemsize for a in list(args) + list(outs))
    return pl.pallas_call(
        kernel,
        out_shape=outs,
        in_specs=[pl.BlockSpec(memory_space=pltpu.SMEM)] + [vmem] * (len(args) - 1),
        out_specs=[vmem] * len(outs),
        scratch_shapes=list(scratch),
        compiler_params=pltpu.CompilerParams(vmem_limit_bytes=36 * 2**20),
        cost_estimate=pl.CostEstimate(flops=flops, bytes_accessed=moved, transcendentals=exps),
    )(*args)


def shaped(shape, dtype):
    return jax.ShapeDtypeStruct(shape, dtype)


def dot(a, b):
    return jnp.dot(a, b, preferred_element_type=F32)


def dot_t(a, b):
    return lax.dot_general(a, b, (((1,), (1,)), ((), ())), preferred_element_type=F32)


def pack_kernel(where, x, out):
    tokens, width = x.shape
    rest = width - LANES
    out[:tokens, :] = x[:, :LANES]
    out[tokens:, :rest] = x[: tokens // 2, LANES:]
    out[tokens:, rest:] = x[tokens // 2 :, LANES:]


def joined_halves(core, mine, theirs):
    a, b = mine[...].astype(F32), theirs[...].astype(F32)
    first = jnp.where(core == 0, a, b)
    second = jnp.where(core == 0, b, a)
    tokens = a.shape[0] * 2 // 3
    low = lax.broadcasted_iota(jnp.int32, (tokens // 2, LANES), 1) < LANES // 2
    left, right = first[tokens:], second[tokens:]
    rest = jnp.concatenate(
        [
            jnp.where(low, left, pltpu.roll(right, LANES // 2, 1)),
            jnp.where(low, pltpu.roll(left, LANES // 2, 1), right),
        ],
        axis=0,
    )
    return jnp.concatenate([first[:tokens], second[:tokens], rest], axis=1)


def shuffled(array, axis):
    half = array.shape[axis] // 2
    take = lambda start, stop: lax.slice_in_dim(array, start, stop, axis=axis)
    return jnp.concatenate(
        [take(0, LANES), take(half, half + LANES), take(LANES, half), take(half + LANES, 2 * half)],
        axis=axis,
    )


def rms_scaled(wide, gain):
    factor = lax.rsqrt(jnp.mean(wide * wide, axis=-1, keepdims=True) + EPS)
    return wide * factor * gain.astype(F32)


def attend(query, keys, top, total, accum):
    scores = [dot_t(query, k) for k in keys]
    new_top = top
    for s in scores:
        most = jnp.max(s, axis=-1, keepdims=True)
        new_top = most if new_top is None else jnp.maximum(new_top, most)
    if top is not None:
        fade = jnp.exp2(top - new_top)
        total, accum = total * fade, accum * fade
    for s, k in zip(scores, keys):
        weights = jnp.exp2(s - new_top)
        part = jnp.sum(weights, axis=-1, keepdims=True)
        mixed = dot(weights.astype(BF), k)
        total = part if total is None else total + part
        accum = mixed if accum is None else accum + mixed
    return new_top, total, accum


def first_kernel(where, gain, w_query, w_key, *refs):
    core = where[0]
    tiles, (query_out, raw_out, top_out, total_out, accum_out), normed = refs[:6], refs[6:11], refs[11]
    tokens = normed.shape[1]
    edge = raw_out.shape[0] - tokens // 2
    raws = [joined_halves(core, tiles[2 * i], tiles[2 * i + 1]) for i in range(3)]
    for i in range(3):
        normed[i] = rms_scaled(raws[i], gain[...]).astype(BF)
    own, behind, ahead = raws
    half = tokens // 2
    raw_out[...] = jnp.where(
        core == 0,
        jnp.concatenate([behind[tokens - edge :], own[:half]], axis=0),
        jnp.concatenate([own[half:], ahead[:edge]], axis=0),
    ).astype(BF)
    rows = rms_scaled(raw_out[...].astype(F32), gain[...]).astype(BF)
    width = rows.shape[1]
    query = dot(rows, w_query[...]).astype(BF)
    scale = width ** (-0.5) * math.log2(math.e)
    query = (dot_t(query, w_key[...]) * scale).astype(BF)
    query_out[...] = query
    top, total, accum = attend(query, [normed[i] for i in range(3)], None, None, None)
    top_out[...] = jnp.broadcast_to(top, top_out.shape)
    total_out[...] = jnp.broadcast_to(total, total_out.shape)
    accum_out[...] = accum


def middle_kernel(count, where, gain, query, top, total, accum, *refs):
    core = where[0]
    tiles, (top_out, total_out, accum_out) = refs[: 2 * count], refs[2 * count :]
    keys = [
        rms_scaled(joined_halves(core, tiles[2 * i], tiles[2 * i + 1]), gain[...]).astype(BF)
        for i in range(count)
    ]
    new = attend(query[...], keys, top[:, :1], total[:, :1], accum[...])
    top_out[...] = jnp.broadcast_to(new[0], top_out.shape)
    total_out[...] = jnp.broadcast_to(new[1], total_out.shape)
    accum_out[...] = new[2]


def last_kernel(where, gain, gain_two, w_value, w_out, query, raw, top, total, accum, mine, theirs, act_out, joined_out):
    core, place, places = where[0], where[1], where[2]
    keys = [rms_scaled(joined_halves(core, mine, theirs), gain[...]).astype(BF)]
    _, total, accum = attend(query[...], keys, top[:, :1], total[:, :1], accum[...])
    mixed = (accum / total).astype(BF)
    attended = dot(mixed, w_value[...]).astype(BF)
    joined = (raw[...].astype(F32) + dot(attended, w_out[...])).astype(BF)
    joined_out[...] = joined
    act = rms_scaled(joined.astype(F32), gain_two[...])
    act = act / (1.0 + jnp.exp(-act))
    row = lax.broadcasted_iota(jnp.int32, (act.shape[0], 1), 0)
    edge = act.shape[0] // 3
    beyond = ((core == 0) & (place == 0) & (row < edge)) | (
        (core == 1) & (place == places - 1) & (row >= 2 * edge)
    )
    act_out[...] = jnp.where(beyond, 0.0, act).astype(BF)


def taps(padded, weights, cells):
    tokens = padded.shape[0] - 2 * cells
    wide = jnp.concatenate([padded[i * cells : i * cells + tokens] for i in range(3)], axis=1)
    return [dot(wide, weights[i]) for i in range(3)]


def gathered(parts, cells):
    left, middle, right = parts
    tokens = middle.shape[0]
    cell = lax.rem(lax.broadcasted_iota(jnp.int32, (tokens, 1), 0), cells)
    left = jnp.where(cell == 0, 0.0, pltpu.roll(left, 1, 0))
    right = jnp.where(cell == cells - 1, 0.0, pltpu.roll(right, tokens - 1, 0))
    return middle + left + right


def whole_tile(core, mine, theirs):
    a, b = mine[...], theirs[...]
    return jnp.concatenate([jnp.where(core == 0, a, b), jnp.where(core == 0, b, a)], axis=0)


def send_kernel(cells, where, act, other, weights, out):
    conv = gathered(taps(whole_tile(where[0], act, other), weights, cells), cells)
    tokens, width = conv.shape
    rest = width - LANES
    out[:tokens, :] = conv[:, :LANES].astype(BF)
    out[tokens:, :] = jnp.concatenate(
        [conv[: tokens // 2, LANES:], conv[tokens // 2 :, LANES:]], axis=1
    ).astype(BF)


def rest_kernel(cells, where, act, other, cache, halo, halo_other, w_act, w_cache, out, sums):
    core, place, places, moment = where[0], where[1], where[2], where[3]
    for i, part in enumerate(taps(whole_tile(core, act, other), w_act, cells)):
        sums[i] = part
    above = jnp.where(core == 0, halo[...], halo_other[...])
    below = jnp.where(core == 0, halo_other[...], halo[...])
    above = jnp.where(place == 0, jnp.zeros_like(above), above)
    below = jnp.where(place == places - 1, jnp.zeros_like(below), below)

    def add(frame, back):
        padded = jnp.concatenate([above[frame], cache[frame], below[frame]], axis=0)
        for i, part in enumerate(taps(padded, w_cache.at[back], cells)):
            sums[i] += part

    @pl.when(moment == 0)
    def _():
        add(0, 0)
        add(1, 1)

    @pl.when(moment == 1)
    def _():
        add(1, 0)

    out[...] = gathered([sums[i] for i in range(3)], cells)


def final_kernel(where, rest, mine, theirs, *refs):
    core, moment = where[0], where[3]
    received, out = refs[:-1], refs[-1]
    tokens, width = rest.shape
    more = width - LANES
    total = rest[...]
    for back, ref in enumerate(received):
        packed = jnp.where(moment > back, ref[...].astype(F32), 0.0)
        tail = packed[tokens:]
        tail = jnp.concatenate([tail[:, :more], tail[:, more:]], axis=0)
        total = total + jnp.concatenate([packed[:tokens], tail], axis=1)
    total = total + jnp.where(
        core == 0,
        jnp.concatenate([mine[...], theirs[...]], axis=0),
        jnp.concatenate([theirs[...], mine[...]], axis=0),
    ).astype(F32)
    out[...] = total.astype(BF)


def body(frames_in, cache, gain_one, gain_two, w_query, w_key, w_value, w_out, conv_weight):
    core, place, moment = lax.axis_index("chan"), lax.axis_index("space"), lax.axis_index("tm")
    places, moments = lax.axis_size("space"), lax.axis_size("tm")
    where = jnp.stack([core, place, jnp.int32(places), moment]).astype(jnp.int32)
    _, rows, cells, half = frames_in.shape
    tokens, width = rows * cells, 2 * half
    count = tokens // 2 + cells

    gain = shuffled(gain_one, 0).reshape(1, width)
    gain_act = shuffled(gain_two, 0).reshape(1, width)
    w_query, w_key, w_value = shuffled(w_query, 0), shuffled(w_key, 0), shuffled(w_value, 0)
    w_out = shuffled(w_out, 1)
    by_cell = conv_weight.transpose(0, 2, 1, 3, 4)
    w_cache = by_cell[:2].reshape(2, 3, 3 * width, half)
    w_act = shuffled(by_cell, 3).reshape(3, 3, 3 * width, half)

    (packed,) = call(
        pack_kernel, [shaped((tokens * 3 // 2, LANES), BF)], [where, frames_in.reshape(tokens, half)]
    )
    behind, ahead = cycle(packed, "space", 1), cycle(packed, "space", -1)
    tiles = []
    for tile in (packed, behind, ahead):
        tiles += [tile, cycle(tile, "chan", 1)]
    up, down = behind, ahead
    groups = []
    for step in range(2, places // 2 + 1):
        down = cycle(down, "space", -1)
        if 2 * step < places:
            up = cycle(up, "space", 1)
            groups.append([up, down])
        else:
            groups.append([down])

    edge = jnp.where(core == 0, cache[:, rows - 1], cache[:, 0])
    edge, down = lax.optimization_barrier((edge, down))
    groups[-1][-1] = down
    pairs = [
        (2 * i + c, 2 * ((i + 1 - 2 * c) % places) + c) for i in range(places) for c in range(2)
    ]
    halo = lax.ppermute(edge, ("space", "chan"), pairs)
    halo_other = cycle(halo, "chan", 1)

    state = [
        shaped((count, LANES), F32),
        shaped((count, LANES), F32),
        shaped((count, width), F32),
    ]
    pair_flops = 4 * count * width * tokens
    query, raw, top, total, accum = call(
        first_kernel,
        [shaped((count, width), BF), shaped((count, width), BF)] + state,
        [where, gain, w_query, w_key] + tiles,
        [pltpu.VMEM((3, tokens, width), BF)],
        flops=3 * pair_flops,
        exps=3 * count * tokens,
    )
    for group in groups[:-1]:
        tiles = []
        for tile in group:
            tiles += [tile, cycle(tile, "chan", 1)]
        top, total, accum = call(
            functools.partial(middle_kernel, len(group)),
            state,
            [where, gain, query, top, total, accum] + tiles,
            flops=len(group) * pair_flops,
            exps=len(group) * count * tokens,
        )
    tile = groups[-1][0]
    act, joined = call(
        last_kernel,
        [shaped((count, width), BF)] * 2,
        [where, gain, gain_act, w_value, w_out, query, raw, top, total, accum, tile, cycle(tile, "chan", 1)],
        flops=pair_flops + 4 * count * width * width,
        exps=count * tokens,
    )
    other = cycle(act, "chan", 1)
    kept = lax.dynamic_slice_in_dim(joined, (1 - core) * cells, tokens // 2, 0)
    lanes = lambda c: jnp.concatenate(
        [kept[:, c * LANES : (c + 1) * LANES], kept[:, 2 * LANES + c * (half - LANES) : 2 * LANES + (c + 1) * (half - LANES)]],
        axis=1,
    )
    low, high = lanes(0), lanes(1)
    mine = jnp.where(core == 0, low, high)
    theirs = cycle(jnp.where(core == 0, high, low), "chan", 1)

    conv_flops = 2 * tokens * 9 * width * half
    received = []
    for back in range(1, min(moments, 3)):
        (term,) = call(
            functools.partial(send_kernel, cells),
            [shaped((tokens * 3 // 2, LANES), BF)],
            [where, act, other, w_act[2 - back]],
            flops=conv_flops,
        )
        received.append(cycle(term, "tm", back))
    (rest,) = call(
        functools.partial(rest_kernel, cells),
        [shaped((tokens, half), F32)],
        [where, act, other, cache.reshape(2, tokens, width), halo, halo_other, w_act[2], w_cache],
        [pltpu.VMEM((3, tokens, half), F32)],
        flops=3 * conv_flops,
    )
    (out,) = call(
        final_kernel,
        [shaped((tokens, half), BF)],
        [where, rest, mine, theirs] + received,
    )
    return out.reshape(1, rows, cells, half)


def solution(mesh):
    return jax.shard_map(
        body,
        mesh=mesh,
        in_specs=(
            P(("clips", "tm"), "space", None, "chan"),
            P("clips", "space", None, None),
            P(),
            P(),
            P(),
            P(),
            P(),
            P(),
            P(None, None, None, None, "chan"),
        ),
        out_specs=P(("clips", "tm"), "space", None, "chan"),
        check_vma=False,
    )
```

time: 117 us -> 79.2 us (0.68)
  waiting for transfers between devices: 49.9 us -> 5.14 us
  local copies, waits for them, and re-layouts: 9.41 us -> 33.9 us
  Pallas kernels: 0 us -> 19 us
  matrix products: 15.7 us -> 0 us
  between operations: 13.6 us -> 0.26 us
  blocking collectives: 7.34 us -> 0 us
  other arithmetic: 9.76 us -> 3.98 us
  starting transfers between devices: 10.6 us -> 16.2 us
    slice x0 -> x20, local copies, waits for them, and re-layouts: none -> 31.4 us  [the longest x14 15.8 us: shuffled(): take = lambda start, stop: lax.slice_in_dim(array, start, stop, axis=axis)]
    all_gather x1 -> x0, waiting for transfers between devices: 29.6 us -> none  [body(): piece = lax.all_gather(normed, ('space', 'chan'), axis=0, tiled=True)]
    pallas_call x0 -> x6, Pallas kernels: none -> 19 us  [call(): pl.pallas_call(kernel, out_shape=outs, in_specs=[pl.BlockSpec(memory_spac...]
    ppermute x4 -> x12, waiting for transfers between devices: 20.3 us -> 5.14 us  [the longest x11 5.14 us: cycle(): lax.ppermute(array, axis, [(i, (i + by) % count) for i in range(count)])]
    dot_general x4 -> x0, matrix products: 11.8 us -> none  [the longest x1 5.41 us: body(): jnp.einsum('qc,kc->qk', query, keys, preferred_element_type=jnp.float32)]
    ppermute x4 -> x12, starting transfers between devices: 10.5 us -> 16.2 us  [the longest x11 16 us: cycle(): lax.ppermute(array, axis, [(i, (i + by) % count) for i in range(count)])]
    all_to_all x1 -> x0, blocking collectives: 5.19 us -> none  [body(): lax.all_to_all(frames_in, 'chan', split_axis=1, concat_axis=3, tiled=True)]
    conv_general_dilated x4 -> x0, local copies, waits for them, and re-layouts: 4.14 us -> none  [body(): lax.conv_general_dilated(padded[None], conv_weight, (1, 1, 1), 'VALID', d...]
  transfers between devices with their start and end apart: 5 -> 12, of which waited for: 4 -> 2; matrix products, arithmetic and copies ran while one was open for 1% -> 45% of each run, Pallas kernels for 0% -> 22%
where the time goes in v1:
time: 79.2 us; the launch traced here: 78.5 us
  local copies, waits for them, and re-layouts  33.9 us (43%)
  Pallas kernels  19 us (24%)
  starting transfers between devices  16.2 us (20%)
  waiting for transfers between devices  5.14 us (6%)
  other arithmetic  3.98 us (5%)
    pallas_call x6, Pallas kernels, call(): pl.pallas_call(kernel, out_shape=outs, in_specs=[pl.BlockSpec(memory_spac...  19 us
    ppermute x11, starting transfers between devices, cycle(): lax.ppermute(array, axis, [(i, (i + by) % count) for i in range(count)])  16 us
    slice x14, local copies, waits for them, and re-layouts, shuffled(): take = lambda start, stop: lax.slice_in_dim(array, start, stop, axis=axis)  15.8 us
    slice x2, local copies, waits for them, and re-layouts, body(): w_cache = by_cell[:2].reshape(2, 3, 3 * width, half)  7.69 us
    ppermute x11, waiting for transfers between devices, cycle(): lax.ppermute(array, axis, [(i, (i + by) % count) for i in range(count)])  5.14 us
    slice x1, local copies, waits for them, and re-layouts, body(): w_act[2 - back]  3.65 us
    concatenate x5, other arithmetic, shuffled(): jnp.concatenate([take(0, LANES), take(half, half + LANES), take(LANES, ha...  3.11 us
    unnamed x44, local copies, waits for them, and re-layouts  2.52 us
  transfers between devices with their start and end apart: 12, of which 2 were waited for; matrix products, arithmetic and copies ran while one was open for 45% of the time, Pallas kernels for 22%

profile of v1, /device:TPU:0, one launch (start us, length us, event | category | flops | bytes accessed | tf_op | source)
XLA Modules:
  0.0 78.5 jit_solution(14134051231547258020)
XLA Ops:
  0.0 0.1 pad_add_fusion.where
  0.1 1.0 %copy-done.2 = bf16[1,4,160,192]{3,2,1,0:T(8,128)(2,1)S(1)} copy-done((bf16[1,4,160,192]{3,2,1,0:T(8,128)(2,1)S(1)}, bf16[1,4,160,192]{3,2,1,0:T(8,128)(2,1)}, u32[]{:S(2)}) %copy-start.2) | copy-done | bytes 245784
  1.1 0.6 shard_map.91.refs_0_
  1.7 5.1 %collective-permute-start.3 = (bf16[960,128]{1,0:T(8,128)(2,1)S(1)}, bf16[960,128]{1,0:T(8,128)(2,1)S(1)}, u32[]{:S(2)}, u32[]{:S(2)}) collective-permute-start(bf16[960,128]{1,0:T(8,128)(2,1)S(1)} %shard_map.91.refs_0_), channel_id=1, source_target_pairs={{0,12},{4,0},{8,4},{12,8},{1,13},{5,1},{9,5},{13,9},{2,14},{6,2},{... | collective-permute-start | bytes 737288 | tf_op jit(solution)/shard_map/ppermute | solution.py:18
  6.8 1.6 %fusion.4 = (bf16[128,384]{1,0:T(8,128)(2,1)}, bf16[128,384]{1,0:T(8,128)(2,1)}) fusion(bf16[384,384]{1,0:T(8,128)(2,1)} %param.14), kind=kLoop, calls=%fused_computation.21 | loop fusion | bytes 393216 | tf_op jit(solution)/shard_map/slice | solution.py:74
  8.4 1.4 %fusion.5 = (bf16[64,384]{1,0:T(8,128)(2,1)S(1)}, bf16[64,384]{1,0:T(8,128)(2,1)}) fusion(bf16[384,384]{1,0:T(8,128)(2,1)} %param.14), kind=kLoop, calls=%fused_computation.22 | loop fusion | bytes 196608 | tf_op jit(solution)/shard_map/slice | solution.py:74
  9.9 1.6 %fusion.6 = (bf16[128,384]{1,0:T(8,128)(2,1)}, bf16[128,384]{1,0:T(8,128)(2,1)}) fusion(bf16[384,384]{1,0:T(8,128)(2,1)} %param.13), kind=kLoop, calls=%fused_computation.23 | loop fusion | bytes 393216 | tf_op jit(solution)/shard_map/slice | solution.py:74
  11.5 1.5 %fusion.7 = (bf16[64,384]{1,0:T(8,128)(2,1)}, bf16[64,384]{1,0:T(8,128)(2,1)}) fusion(bf16[384,384]{1,0:T(8,128)(2,1)} %param.13), kind=kLoop, calls=%fused_computation.24 | loop fusion | bytes 196608 | tf_op jit(solution)/shard_map/slice | solution.py:74
  13.0 0.1 fusion.14
  13.1 0.6 fusion.15
  13.7 0.1 fusion.8
  13.8 0.7 fusion.9
  14.5 4.0 %fusion.1 = (bf16[3,3,3,128,192]{3,4,1,2,0:T(8,128)(2,1)S(1)}, bf16[3,3,3,128,192]{3,4,1,2,0:T(8,128)(2,1)}) fusion(bf16[3,3,3,384,192]{3,4,1,2,0:T(8,128)(2,1)} %bitcast.23), kind=kLoop, calls=%fused_computation.18 | loop fusion | bytes 5308416 | tf_op jit(solution)/shard_map/slice | solution.py:74
  18.5 2.2 %fusion.2 = (bf16[3,3,3,64,192]{3,4,1,2,0:T(8,128)(2,1)}, bf16[3,3,3,64,192]{3,4,1,2,0:T(8,128)(2,1)}) fusion(bf16[3,3,3,384,192]{3,4,1,2,0:T(8,128)(2,1)S(1)} %bitcast.25), kind=kLoop, calls=%fused_computation.19 | loop fusion | bytes 2654208 | tf_op jit(solution)/shard_map/slice | solution.py:74
  20.7 1.0 %fusion.10 = (bf16[128,384]{1,0:T(8,128)(2,1)S(1)}, bf16[128,384]{1,0:T(8,128)(2,1)S(1)}) fusion(bf16[384,384]{1,0:T(8,128)(2,1)} %param.15), kind=kLoop, calls=%fused_computation.27 | loop fusion | bytes 393216 | tf_op jit(solution)/shard_map/slice | solution.py:74
  21.7 0.1 fusion.12
  21.8 0.7 fusion
  22.5 0.1 fusion.13
  22.6 0.7 pad_maximum_fusion.10
  23.3 0.1 pad_maximum_fusion.11
  23.4 3.6 %slice.154 = bf16[2,3,3,384,192]{3,4,1,2,0:T(8,128)(2,1)} slice(bf16[3,3,3,384,192]{3,4,1,2,0:T(8,128)(2,1)} %bitcast.24), slice={[0:2], [0:3], [0:3], [0:384], [0:192]} | slice | bytes 5308416 | tf_op jit(solution)/shard_map/slice | solution.py:250
  27.0 3.9 %collective-permute-start.5 = (bf16[960,128]{1,0:T(8,128)(2,1)S(1)}, bf16[960,128]{1,0:T(8,128)(2,1)S(1)}, u32[]{:S(2)}, u32[]{:S(2)}) collective-permute-start(bf16[960,128]{1,0:T(8,128)(2,1)S(1)} %collective-permute-done.3.refs_4_), channel_id=1, source_target_pairs={{0,12},{4,0},{8,4},{12,8},{1,13},{5,1},{9,5},{13,9},{2,14},{6,2},{... | collective-permute-start | bytes 737288 | tf_op jit(solution)/shard_map/ppermute | solution.py:18
  30.9 0.8 %fusion.11 = (bf16[64,384]{1,0:T(8,128)(2,1)S(1)}, bf16[64,384]{1,0:T(8,128)(2,1)S(1)}) fusion(bf16[384,384]{1,0:T(8,128)(2,1)} %param.15), kind=kLoop, calls=%fused_computation.28 | loop fusion | bytes 196608 | tf_op jit(solution)/shard_map/slice | solution.py:74
  31.7 0.3 collective-permute-start.4
  32.0 0.0 collective-permute-done.1.refs_2_
  32.0 0.3 collective-permute-start.2
  32.4 0.1 pad_maximum_fusion.6
  32.4 4.3 %collective-permute-done.5.mine = bf16[960,128]{1,0:T(8,128)(2,1)S(1)} collective-permute-done((bf16[960,128]{1,0:T(8,128)(2,1)S(1)}, bf16[960,128]{1,0:T(8,128)(2,1)S(1)}, u32[]{:S(2)}, u32[]{:S(2)}) %collective-permute-start.5) | collective-permute-done | bytes 245792 | tf_op jit(solution)/shard_map/ppermute | solution.py:18
  36.8 0.1 pad_maximum_fusion.4
  36.9 0.2 collective-permute-start.8
  37.2 4.5 %shard_map.92 = (bf16[480,384]{1,0:T(8,128)(2,1)S(1)}, bf16[480,384]{1,0:T(8,128)(2,1)S(1)}, f32[480,128]{1,0:T(8,128)S(1)}, f32[480,128]{1,0:T(8,128)S(1)}, f32[480,384]{1,0:T(8,128)S(1)}) custom-call(s32[4]{0:T(128)S(1)} %pad_add_fusion.where, bf16[1,384]{1,0:T(2,128)(2,1)S(1)} %reshape.25.gain, bf16[384,384]{1,0:T(8,128)(2,1)S(1)} %get-tuple-element.59.w_query, ...), custom_call_target="tpu_custom_call" | custom-call | flops 1415577600 | bytes 4031248 | tf_op jit(solution)/shard_map/pallas_call | solution.py:24
  41.8 3.9 %shard_map.93 = (bf16[480,384]{1,0:T(8,128)(2,1)}, bf16[480,384]{1,0:T(8,128)(2,1)S(1)}) custom-call(s32[4]{0:T(128)S(1)} %pad_add_fusion.where, bf16[1,384]{1,0:T(2,128)(2,1)S(1)} %reshape.25.gain, bf16[1,384]{1,0:T(2,128)(2,1)S(1)} %reshape.26.gain_two, bf16[384,384]{1,0:T(8,128)(2,1)S(1)} %get-tuple-element.61.w_value, ...), custom_call_target="tpu_custom_call" | custom-call | flops 754974720 | bytes 3786256 | tf_op jit(solution)/shard_map/pallas_call | solution.py:24
  45.7 4.5 %collective-permute-start.7 = (bf16[480,384]{1,0:T(8,128)(2,1)}, bf16[480,384]{1,0:T(8,128)(2,1)}, u32[]{:S(2)}, u32[]{:S(2)}) collective-permute-start(bf16[480,384]{1,0:T(8,128)(2,1)} %get-tuple-element.20.act), channel_id=1, source_target_pairs={{0,1},{1,0},{2,3},{3,2},{4,5},{5,4},{6,7},{7,6},{8,9},{9,8},{10,11... | collective-permute-start | bytes 1105928 | tf_op jit(solution)/shard_map/ppermute | solution.py:18
  50.2 2.1 %pad_maximum_fusion = (bf16[1,3,3,384,192]{3,4,1,2,0:T(8,128)(2,1)}, bf16[1,3,3,384,192]{3,4,1,2,0:T(8,128)(2,1)S(1)}) fusion(bf16[3,3,3,64,192]{3,4,1,2,0:T(8,128)(2,1)S(1)} %copy-done.9, bf16[3,3,3,64,192]{3,4,1,2,0:T(8,128)(2,1)S(1)} %copy-done.8, bf16[3,3,3,128,192]{3,4,1,2,0:T(8,128)(2,1)S(1)} %copy-done.7, ...), kind=kLoop, calls=%fused_computation | loop fusion | flops 10616832 | bytes 6635520 | tf_op jit(solution)/shard_map/concatenate | solution.py:75
  52.3 3.6 %copy.14 = bf16[1,3,3,384,192]{4,3,2,1,0:T(8,128)(2,1)} copy(bf16[1,3,3,384,192]{3,4,1,2,0:T(8,128)(2,1)} %get-tuple-element.23) | data formatting | bytes 2654208 | tf_op jit(solution)/shard_map/slice | solution.py:328
  56.0 2.2 %copy.12 = bf16[1,3,3,384,192]{4,3,2,1,0:T(8,128)(2,1)} copy(bf16[1,3,3,384,192]{3,4,1,2,0:T(8,128)(2,1)S(1)} %get-tuple-element.24) | data formatting | bytes 2654208 | tf_op jit(solution)/shard_map/slice | solution.py:335
  58.2 4.1 %copy.13 = bf16[2,3,3,384,192]{4,3,2,1,0:T(8,128)(2,1)S(1)} copy(bf16[2,3,3,384,192]{3,4,1,2,0:T(8,128)(2,1)} %slice.154) | data formatting | bytes 5308416 | tf_op jit(solution)/shard_map/slice | solution.py:250
  62.3 0.1 collective-permute-start.9
  62.4 0.9 %constant_dynamic-slice_fusion = (bf16[320,128]{1,0:T(8,128)(2,1)S(1)}, bf16[320,128]{1,0:T(8,128)(2,1)S(1)}) fusion(bf16[480,384]{1,0:T(8,128)(2,1)} %copy-done.3, s32[]{:T(128)S(6)} %select_n.30, s32[]{:T(128)S(6)} %add.8), kind=kLoop, calls=%fused_computation.17 | loop fusion | bytes 327688 | tf_op jit(solution)/shard_map/slice | solution.py:315
  63.4 1.1 %fusion.3 = (bf16[320,64]{1,0:T(8,128)(2,1)S(1)}, bf16[320,64]{1,0:T(8,128)(2,1)S(1)}) fusion(bf16[480,384]{1,0:T(8,128)(2,1)} %copy-done.3, s32[]{:T(128)S(6)} %select_n.30, s32[]{:T(128)S(6)} %add.7, s32[]{:T(128)S(6)} %add.9), kind=kLoop, calls=%fused_computation.20 | loop fusion | bytes 163852 | tf_op jit(solution)/shard_map/slice | solution.py:315
  64.5 1.5 %copy-done.1 = bf16[1,3,3,384,192]{4,3,2,1,0:T(8,128)(2,1)S(1)} copy-done((bf16[1,3,3,384,192]{4,3,2,1,0:T(8,128)(2,1)S(1)}, bf16[1,3,3,384,192]{4,3,2,1,0:T(8,128)(2,1)}, u32[]{:S(2)}) %copy-start.1) | copy-done | bytes 1327128
  65.9 2.8 %shard_map.95 = bf16[960,128]{1,0:T(8,128)(2,1)S(1)} custom-call(s32[4]{0:T(128)S(1)} %pad_add_fusion.where, bf16[480,384]{1,0:T(8,128)(2,1)} %get-tuple-element.20.act, bf16[480,384]{1,0:T(8,128)(2,1)} %collective-permute-done.7.other, bf16[3,1152,192]{2,1,0:T(8,128)(2,1)S(1)} %bitcast.20), custom_call_target="tpu_custom_call" | custom-call | flops 849346560 | bytes 2310160 | tf_op jit(solution)/shard_map/pallas_call | solution.py:24
  68.7 1.6 %collective-permute-start.11 = (bf16[960,128]{1,0:T(8,128)(2,1)S(1)}, bf16[960,128]{1,0:T(8,128)(2,1)S(1)}, u32[]{:S(2)}, u32[]{:S(2)}) collective-permute-start(bf16[960,128]{1,0:T(8,128)(2,1)S(1)} %shard_map.95), channel_id=1, source_target_pairs={{0,2},{2,0},{1,3},{3,1},{4,6},{6,4},{5,7},{7,5},{8,10},{10,8},{9,1... | collective-permute-start | bytes 737288 | tf_op jit(solution)/shard_map/ppermute | solution.py:18
  70.3 0.1 broadcast_select_fusion
  70.4 0.3 collective-permute-start.10
  70.7 5.7 %shard_map.94.rest = f32[640,192]{1,0:T(8,128)S(1)} custom-call(s32[4]{0:T(128)S(1)} %pad_add_fusion.where, bf16[480,384]{1,0:T(8,128)(2,1)} %get-tuple-element.20.act, bf16[480,384]{1,0:T(8,128)(2,1)} %collective-permute-done.7.other, bf16[2,640,384]{2,1,0:T(8,128)(2,1)S(1)} %bitcast.22, bf16[2,160,384]{2,1,0:T(8,128)(2,1)} %collective-permute-done.8.halo, ...), custom_call_target="tpu_custom_call" | custom-call | flops 2548039680 | bytes 6684688 | tf_op jit(solution)/shard_map/pallas_call | solution.py:24
  76.4 0.8 collective-permute-done.11.refs_0_
  77.1 1.4 %shard_map.96 = bf16[640,192]{1,0:T(8,128)(2,1)} custom-call(s32[4]{0:T(128)S(1)} %pad_add_fusion.where, f32[640,192]{1,0:T(8,128)S(1)} %shard_map.94.rest, bf16[320,192]{1,0:T(8,128)(2,1)S(1)} %get-tuple-element.34.mine, bf16[320,192]{1,0:T(8,128)(2,1)S(1)} %collective-permute-done.10.theirs, bf16[960,128]{1,0:T(8,128)(2,1)S(1)} %collective-permute-done.11.refs_0_), custom_call_target="tpu_custom_call" | custom-call | bytes 1228816 | tf_op jit(solution)/shard_map/pallas_call | solution.py:24
  (56 shorter events, 0.1 us)
Async XLA Ops:
  0.0 13.0 %copy-start.20 = (bf16[384]{0:T(512)(128)(2,1)S(1)}, bf16[384]{0:T(512)(128)(2,1)}, u32[]{:S(2)}) copy-start(bf16[384]{0:T(512)(128)(2,1)} %param.11) | copy-start | bytes 2308
  0.1 1.0 %copy-start.2 = (bf16[1,4,160,192]{3,2,1,0:T(8,128)(2,1)S(1)}, bf16[1,4,160,192]{3,2,1,0:T(8,128)(2,1)}, u32[]{:S(2)}) copy-start(bf16[1,4,160,192]{3,2,1,0:T(8,128)(2,1)} %param.9) | copy-start | bytes 737284
  1.1 12.6 %copy-start.10 = (bf16[384,384]{1,0:T(8,128)(2,1)S(1)}, bf16[384,384]{1,0:T(8,128)(2,1)}, u32[]{:S(2)}) copy-start(bf16[384,384]{1,0:T(8,128)(2,1)} %param.16) | copy-start | bytes 884740
  1.7 25.3 %collective-permute-start.3 = (bf16[960,128]{1,0:T(8,128)(2,1)S(1)}, bf16[960,128]{1,0:T(8,128)(2,1)S(1)}, u32[]{:S(2)}, u32[]{:S(2)}) collective-permute-start(bf16[960,128]{1,0:T(8,128)(2,1)S(1)} %shard_map.91.refs_0_), channel_id=1, source_target_pairs={{0,12},{4,0},{8,4},{12,8},{1,13},{5,1},{9,5},{13,9},{2,14},{6,2},{... | collective-permute-start | bytes 737288 | tf_op jit(solution)/shard_map/ppermute | solution.py:18
  6.8 25.2 %collective-permute-start.1 = (bf16[960,128]{1,0:T(8,128)(2,1)S(1)}, bf16[960,128]{1,0:T(8,128)(2,1)S(1)}, u32[]{:S(2)}, u32[]{:S(2)}) collective-permute-start(bf16[960,128]{1,0:T(8,128)(2,1)S(1)} %shard_map.91.refs_0_), channel_id=1, source_target_pairs={{0,4},{4,8},{8,12},{12,0},{1,5},{5,9},{9,13},{13,1},{2,6},{6,10},{... | collective-permute-start | bytes 737288 | tf_op jit(solution)/shard_map/ppermute | solution.py:18
  6.8 30.3 %collective-permute-start = (bf16[960,128]{1,0:T(8,128)(2,1)S(1)}, bf16[960,128]{1,0:T(8,128)(2,1)S(1)}, u32[]{:S(2)}, u32[]{:S(2)}) collective-permute-start(bf16[960,128]{1,0:T(8,128)(2,1)S(1)} %shard_map.91.refs_0_), channel_id=1, source_target_pairs={{0,1},{1,0},{2,3},{3,2},{4,5},{5,4},{6,7},{7,6},{8,9},{9,8},{10,11... | collective-permute-start | bytes 737288 | tf_op jit(solution)/shard_map/ppermute | solution.py:18
  14.5 4.0 %copy-start.6 = (bf16[3,3,3,384,192]{3,4,2,1,0:T(8,128)(2,1)S(1)}, bf16[3,3,3,384,192]{3,4,2,1,0:T(8,128)(2,1)}, u32[]{:S(2)}) copy-start(bf16[3,3,3,384,192]{3,4,2,1,0:T(8,128)(2,1)} %param.17) | copy-start | bytes 11943940
  18.5 3.2 %copy-start.21 = (bf16[384]{0:T(512)(128)(2,1)S(1)}, bf16[384]{0:T(512)(128)(2,1)}, u32[]{:S(2)}) copy-start(bf16[384]{0:T(512)(128)(2,1)} %param.12) | copy-start | bytes 2308
  18.5 3.2 %copy-start.4 = (bf16[2,4,160,384]{3,2,1,0:T(8,128)(2,1)S(1)}, bf16[2,4,160,384]{3,2,1,0:T(8,128)(2,1)}, u32[]{:S(2)}) copy-start(bf16[2,4,160,384]{3,2,1,0:T(8,128)(2,1)} %param.10) | copy-start | bytes 2949124
  23.4 8.9 %copy-start.13 = (bf16[128,384]{1,0:T(8,128)(2,1)S(1)}, bf16[128,384]{1,0:T(8,128)(2,1)}, u32[]{:S(2)}) copy-start(bf16[128,384]{1,0:T(8,128)(2,1)} %get-tuple-element.35) | copy-start | bytes 294916
  23.4 8.9 %copy-start.14 = (bf16[128,384]{1,0:T(8,128)(2,1)S(1)}, bf16[128,384]{1,0:T(8,128)(2,1)}, u32[]{:S(2)}) copy-start(bf16[128,384]{1,0:T(8,128)(2,1)} %get-tuple-element.36) | copy-start | bytes 294916
  23.4 8.9 %copy-start.15 = (bf16[128,384]{1,0:T(8,128)(2,1)S(1)}, bf16[128,384]{1,0:T(8,128)(2,1)}, u32[]{:S(2)}) copy-start(bf16[128,384]{1,0:T(8,128)(2,1)} %get-tuple-element.39) | copy-start | bytes 294916
  23.4 8.9 %copy-start.16 = (bf16[128,384]{1,0:T(8,128)(2,1)S(1)}, bf16[128,384]{1,0:T(8,128)(2,1)}, u32[]{:S(2)}) copy-start(bf16[128,384]{1,0:T(8,128)(2,1)} %get-tuple-element.40) | copy-start | bytes 294916
  23.4 8.9 %copy-start.17 = (bf16[64,384]{1,0:T(8,128)(2,1)S(1)}, bf16[64,384]{1,0:T(8,128)(2,1)}, u32[]{:S(2)}) copy-start(bf16[64,384]{1,0:T(8,128)(2,1)} %get-tuple-element.38) | copy-start | bytes 147460
  23.4 8.9 %copy-start.18 = (bf16[64,384]{1,0:T(8,128)(2,1)S(1)}, bf16[64,384]{1,0:T(8,128)(2,1)}, u32[]{:S(2)}) copy-start(bf16[64,384]{1,0:T(8,128)(2,1)} %get-tuple-element.41) | copy-start | bytes 147460
  23.4 8.9 %copy-start.19 = (bf16[64,384]{1,0:T(8,128)(2,1)S(1)}, bf16[64,384]{1,0:T(8,128)(2,1)}, u32[]{:S(2)}) copy-start(bf16[64,384]{1,0:T(8,128)(2,1)} %get-tuple-element.42) | copy-start | bytes 147460
  27.0 9.8 %copy-start.11 = (bf16[384,64]{1,0:T(8,128)(2,1)S(1)}, bf16[384,64]{1,0:T(8,128)(2,1)}, u32[]{:S(2)}) copy-start(bf16[384,64]{1,0:T(8,128)(2,1)} %get-tuple-element.45) | copy-start | bytes 147460
  27.0 9.8 %copy-start.12 = (bf16[384,64]{1,0:T(8,128)(2,1)S(1)}, bf16[384,64]{1,0:T(8,128)(2,1)}, u32[]{:S(2)}) copy-start(bf16[384,64]{1,0:T(8,128)(2,1)} %get-tuple-element.46) | copy-start | bytes 147460
  27.0 9.8 %collective-permute-start.5 = (bf16[960,128]{1,0:T(8,128)(2,1)S(1)}, bf16[960,128]{1,0:T(8,128)(2,1)S(1)}, u32[]{:S(2)}, u32[]{:S(2)}) collective-permute-start(bf16[960,128]{1,0:T(8,128)(2,1)S(1)} %collective-permute-done.3.refs_4_), channel_id=1, source_target_pairs={{0,12},{4,0},{8,4},{12,8},{1,13},{5,1},{9,5},{13,9},{2,14},{6,2},{... | collective-permute-start | bytes 737288 | tf_op jit(solution)/shard_map/ppermute | solution.py:18
  31.7 5.4 %collective-permute-start.4 = (bf16[960,128]{1,0:T(8,128)(2,1)S(1)}, bf16[960,128]{1,0:T(8,128)(2,1)S(1)}, u32[]{:S(2)}, u32[]{:S(2)}) collective-permute-start(bf16[960,128]{1,0:T(8,128)(2,1)S(1)} %collective-permute-done.3.refs_4_), channel_id=1, source_target_pairs={{0,1},{1,0},{2,3},{3,2},{4,5},{5,4},{6,7},{7,6},{8,9},{9,8},{10,11... | collective-permute-start | bytes 737288 | tf_op jit(solution)/shard_map/ppermute | solution.py:18
  32.0 5.1 %collective-permute-start.2 = (bf16[960,128]{1,0:T(8,128)(2,1)S(1)}, bf16[960,128]{1,0:T(8,128)(2,1)S(1)}, u32[]{:S(2)}, u32[]{:S(2)}) collective-permute-start(bf16[960,128]{1,0:T(8,128)(2,1)S(1)} %collective-permute-done.1.refs_2_), channel_id=1, source_target_pairs={{0,1},{1,0},{2,3},{3,2},{4,5},{5,4},{6,7},{7,6},{8,9},{9,8},{10,11... | collective-permute-start | bytes 737288 | tf_op jit(solution)/shard_map/ppermute | solution.py:18
  36.8 4.9 %collective-permute-start.6 = (bf16[960,128]{1,0:T(8,128)(2,1)S(1)}, bf16[960,128]{1,0:T(8,128)(2,1)S(1)}, u32[]{:S(2)}, u32[]{:S(2)}) collective-permute-start(bf16[960,128]{1,0:T(8,128)(2,1)S(1)} %collective-permute-done.5.mine), channel_id=1, source_target_pairs={{0,1},{1,0},{2,3},{3,2},{4,5},{5,4},{6,7},{7,6},{8,9},{9,8},{10,11... | collective-permute-start | bytes 737288 | tf_op jit(solution)/shard_map/ppermute | solution.py:18
  36.9 25.4 %collective-permute-start.8 = (bf16[2,160,384]{2,1,0:T(8,128)(2,1)}, bf16[2,160,384]{2,1,0:T(8,128)(2,1)}, u32[]{:S(2)}, u32[]{:S(2)}) collective-permute-start(bf16[2,160,384]{2,1,0:T(8,128)(2,1)} %fusion), channel_id=1, source_target_pairs={{0,4},{1,13},{4,8},{5,1},{8,12},{9,5},{12,0},{13,9},{2,6},{3,15},{... | collective-permute-start | bytes 737288 | tf_op jit(solution)/shard_map/ppermute | solution.py:276
  37.2 13.0 %copy-start.9 = (bf16[3,3,3,64,192]{3,4,1,2,0:T(8,128)(2,1)S(1)}, bf16[3,3,3,64,192]{3,4,1,2,0:T(8,128)(2,1)}, u32[]{:S(2)}) copy-start(bf16[3,3,3,64,192]{3,4,1,2,0:T(8,128)(2,1)} %get-tuple-element.28) | copy-start | bytes 1990660
  41.7 8.5 %copy-start.7 = (bf16[3,3,3,128,192]{3,4,1,2,0:T(8,128)(2,1)S(1)}, bf16[3,3,3,128,192]{3,4,1,2,0:T(8,128)(2,1)}, u32[]{:S(2)}) copy-start(bf16[3,3,3,128,192]{3,4,1,2,0:T(8,128)(2,1)} %get-tuple-element.26) | copy-start | bytes 3981316
  41.7 8.4 %copy-start.8 = (bf16[3,3,3,64,192]{3,4,1,2,0:T(8,128)(2,1)S(1)}, bf16[3,3,3,64,192]{3,4,1,2,0:T(8,128)(2,1)}, u32[]{:S(2)}) copy-start(bf16[3,3,3,64,192]{3,4,1,2,0:T(8,128)(2,1)} %get-tuple-element.27) | copy-start | bytes 1990660
  45.7 6.6 %copy-start.3 = (bf16[480,384]{1,0:T(8,128)(2,1)}, bf16[480,384]{1,0:T(8,128)(2,1)S(1)}, u32[]{:S(2)}) copy-start(bf16[480,384]{1,0:T(8,128)(2,1)S(1)} %get-tuple-element.22) | copy-start | bytes 1105924
  45.7 18.7 %collective-permute-start.7 = (bf16[480,384]{1,0:T(8,128)(2,1)}, bf16[480,384]{1,0:T(8,128)(2,1)}, u32[]{:S(2)}, u32[]{:S(2)}) collective-permute-start(bf16[480,384]{1,0:T(8,128)(2,1)} %get-tuple-element.20.act), channel_id=1, source_target_pairs={{0,1},{1,0},{2,3},{3,2},{4,5},{5,4},{6,7},{7,6},{8,9},{9,8},{10,11... | collective-permute-start | bytes 1105928 | tf_op jit(solution)/shard_map/ppermute | solution.py:18
  62.3 8.3 %collective-permute-start.9 = (bf16[2,160,384]{2,1,0:T(8,128)(2,1)}, bf16[2,160,384]{2,1,0:T(8,128)(2,1)S(1)}, u32[]{:S(2)}, u32[]{:S(2)}) collective-permute-start(bf16[2,160,384]{2,1,0:T(8,128)(2,1)} %collective-permute-done.8.halo), channel_id=1, source_target_pairs={{0,1},{1,0},{2,3},{3,2},{4,5},{5,4},{6,7},{7,6},{8,9},{9,8},{10,11... | collective-permute-start | bytes 737288 | tf_op jit(solution)/shard_map/ppermute | solution.py:18
  64.5 1.5 %copy-start.1 = (bf16[1,3,3,384,192]{4,3,2,1,0:T(8,128)(2,1)S(1)}, bf16[1,3,3,384,192]{4,3,2,1,0:T(8,128)(2,1)}, u32[]{:S(2)}) copy-start(bf16[1,3,3,384,192]{4,3,2,1,0:T(8,128)(2,1)} %copy.14) | copy-start | bytes 3981316
  65.9 4.7 %copy-start = (bf16[1,3,3,384,192]{4,3,2,1,0:T(8,128)(2,1)S(1)}, bf16[1,3,3,384,192]{4,3,2,1,0:T(8,128)(2,1)}, u32[]{:S(2)}) copy-start(bf16[1,3,3,384,192]{4,3,2,1,0:T(8,128)(2,1)} %copy.12) | copy-start | bytes 3981316
  65.9 4.7 %copy-start.5 = (bf16[2,4,160,384]{3,2,1,0:T(8,128)(2,1)S(1)}, bf16[2,4,160,384]{3,2,1,0:T(8,128)(2,1)}, u32[]{:S(2)}) copy-start(bf16[2,4,160,384]{3,2,1,0:T(8,128)(2,1)} %param.10) | copy-start | bytes 2949124
  68.7 8.4 %collective-permute-start.11 = (bf16[960,128]{1,0:T(8,128)(2,1)S(1)}, bf16[960,128]{1,0:T(8,128)(2,1)S(1)}, u32[]{:S(2)}, u32[]{:S(2)}) collective-permute-start(bf16[960,128]{1,0:T(8,128)(2,1)S(1)} %shard_map.95), channel_id=1, source_target_pairs={{0,2},{2,0},{1,3},{3,1},{4,6},{6,4},{5,7},{7,5},{8,10},{10,8},{9,1... | collective-permute-start | bytes 737288 | tf_op jit(solution)/shard_map/ppermute | solution.py:18
  70.4 6.0 %collective-permute-start.10 = (bf16[320,192]{1,0:T(8,128)(2,1)S(1)}, bf16[320,192]{1,0:T(8,128)(2,1)S(1)}, u32[]{:S(2)}, u32[]{:S(2)}) collective-permute-start(bf16[320,192]{1,0:T(8,128)(2,1)S(1)} %get-tuple-element.33), channel_id=1, source_target_pairs={{0,1},{1,0},{2,3},{3,2},{4,5},{5,4},{6,7},{7,6},{8,9},{9,8},{10,11... | collective-permute-start | bytes 368648 | tf_op jit(solution)/shard_map/ppermute | solution.py:18

commit v2 on v1

--- a/solution.py
+++ b/solution.py
@@ -57,24 +57,13 @@
     first = jnp.where(core == 0, a, b)
     second = jnp.where(core == 0, b, a)
     tokens = a.shape[0] * 2 // 3
-    low = lax.broadcasted_iota(jnp.int32, (tokens // 2, LANES), 1) < LANES // 2
-    left, right = first[tokens:], second[tokens:]
-    rest = jnp.concatenate(
-        [
-            jnp.where(low, left, pltpu.roll(right, LANES // 2, 1)),
-            jnp.where(low, pltpu.roll(left, LANES // 2, 1), right),
-        ],
-        axis=0,
-    )
-    return jnp.concatenate([first[:tokens], second[:tokens], rest], axis=1)
-
-
-def shuffled(array, axis):
-    half = array.shape[axis] // 2
-    take = lambda start, stop: lax.slice_in_dim(array, start, stop, axis=axis)
+    turn = lambda v: pltpu.roll(v, LANES // 2, 1)
+    low = lax.broadcasted_iota(jnp.int32, (tokens, LANES), 1) < LANES // 2
+    middle = turn(second[:tokens])
+    left = jnp.concatenate([first[tokens:], turn(first[tokens:])], axis=0)
+    right = jnp.concatenate([turn(second[tokens:]), second[tokens:]], axis=0)
     return jnp.concatenate(
-        [take(0, LANES), take(half, half + LANES), take(LANES, half), take(half + LANES, 2 * half)],
-        axis=axis,
+        [first[:tokens], jnp.where(low, left, middle), jnp.where(low, middle, right)], axis=1
     )
 
 
@@ -141,28 +130,35 @@
     accum_out[...] = new[2]
 
 
-def last_kernel(where, gain, gain_two, w_value, w_out, query, raw, top, total, accum, mine, theirs, act_out, joined_out):
+def last_kernel(where, gain, gain_two, w_value, w_out, query, raw, top, total, accum, mine, theirs, act_out, keep_out, give_out):
     core, place, places = where[0], where[1], where[2]
     keys = [rms_scaled(joined_halves(core, mine, theirs), gain[...]).astype(BF)]
     _, total, accum = attend(query[...], keys, top[:, :1], total[:, :1], accum[...])
     mixed = (accum / total).astype(BF)
     attended = dot(mixed, w_value[...]).astype(BF)
     joined = (raw[...].astype(F32) + dot(attended, w_out[...])).astype(BF)
-    joined_out[...] = joined
+    edge = joined.shape[0] // 3
+    own = jnp.where(core == 0, joined[edge:], joined[: 2 * edge]).astype(F32)
+    half = own.shape[1] // 2
+    low, high = own[:, :half], own[:, half:]
+    keep_out[...] = jnp.where(core == 0, low, high).astype(BF)
+    give_out[...] = jnp.where(core == 0, high, low).astype(BF)
     act = rms_scaled(joined.astype(F32), gain_two[...])
     act = act / (1.0 + jnp.exp(-act))
     row = lax.broadcasted_iota(jnp.int32, (act.shape[0], 1), 0)
-    edge = act.shape[0] // 3
     beyond = ((core == 0) & (place == 0) & (row < edge)) | (
         (core == 1) & (place == places - 1) & (row >= 2 * edge)
     )
     act_out[...] = jnp.where(beyond, 0.0, act).astype(BF)
 
 
-def taps(padded, weights, cells):
+def taps(padded, weights, back, cells):
     tokens = padded.shape[0] - 2 * cells
     wide = jnp.concatenate([padded[i * cells : i * cells + tokens] for i in range(3)], axis=1)
-    return [dot(wide, weights[i]) for i in range(3)]
+    return [
+        dot_t(wide, jnp.concatenate([weights[back, row, cell] for row in range(3)], axis=1))
+        for cell in range(3)
+    ]
 
 
 def gathered(parts, cells):
@@ -179,8 +175,8 @@
     return jnp.concatenate([jnp.where(core == 0, a, b), jnp.where(core == 0, b, a)], axis=0)
 
 
-def send_kernel(cells, where, act, other, weights, out):
-    conv = gathered(taps(whole_tile(where[0], act, other), weights, cells), cells)
+def send_kernel(cells, back, where, act, other, weights, out):
+    conv = gathered(taps(whole_tile(where[0], act, other), weights, back, cells), cells)
     tokens, width = conv.shape
     rest = width - LANES
     out[:tokens, :] = conv[:, :LANES].astype(BF)
@@ -189,9 +185,9 @@
     ).astype(BF)
 
 
-def rest_kernel(cells, where, act, other, cache, halo, halo_other, w_act, w_cache, out, sums):
+def rest_kernel(cells, where, act, other, cache, halo, halo_other, weights, out, sums):
     core, place, places, moment = where[0], where[1], where[2], where[3]
-    for i, part in enumerate(taps(whole_tile(core, act, other), w_act, cells)):
+    for i, part in enumerate(taps(whole_tile(core, act, other), weights, 2, cells)):
         sums[i] = part
     above = jnp.where(core == 0, halo[...], halo_other[...])
     below = jnp.where(core == 0, halo_other[...], halo[...])
@@ -200,7 +196,7 @@
 
     def add(frame, back):
         padded = jnp.concatenate([above[frame], cache[frame], below[frame]], axis=0)
-        for i, part in enumerate(taps(padded, w_cache.at[back], cells)):
+        for i, part in enumerate(taps(padded, weights, back, cells)):
             sums[i] += part
 
     @pl.when(moment == 0)
@@ -242,13 +238,9 @@
     tokens, width = rows * cells, 2 * half
     count = tokens // 2 + cells
 
-    gain = shuffled(gain_one, 0).reshape(1, width)
-    gain_act = shuffled(gain_two, 0).reshape(1, width)
-    w_query, w_key, w_value = shuffled(w_query, 0), shuffled(w_key, 0), shuffled(w_value, 0)
-    w_out = shuffled(w_out, 1)
-    by_cell = conv_weight.transpose(0, 2, 1, 3, 4)
-    w_cache = by_cell[:2].reshape(2, 3, 3 * width, half)
-    w_act = shuffled(by_cell, 3).reshape(3, 3, 3 * width, half)
+    gain = gain_one.reshape(1, width)
+    gain_act = gain_two.reshape(1, width)
+    weights = conv_weight.transpose(0, 1, 2, 4, 3)
 
     (packed,) = call(
         pack_kernel, [shaped((tokens * 3 // 2, LANES), BF)], [where, frames_in.reshape(tokens, half)]
@@ -301,45 +293,38 @@
             flops=len(group) * pair_flops,
             exps=len(group) * count * tokens,
         )
-    tile = groups[-1][0]
-    act, joined = call(
+    tile, accum = lax.optimization_barrier((groups[-1][0], accum))
+    act, keep, give = call(
         last_kernel,
-        [shaped((count, width), BF)] * 2,
+        [shaped((count, width), BF)] + [shaped((tokens // 2, half), BF)] * 2,
         [where, gain, gain_act, w_value, w_out, query, raw, top, total, accum, tile, cycle(tile, "chan", 1)],
         flops=pair_flops + 4 * count * width * width,
         exps=count * tokens,
     )
     other = cycle(act, "chan", 1)
-    kept = lax.dynamic_slice_in_dim(joined, (1 - core) * cells, tokens // 2, 0)
-    lanes = lambda c: jnp.concatenate(
-        [kept[:, c * LANES : (c + 1) * LANES], kept[:, 2 * LANES + c * (half - LANES) : 2 * LANES + (c + 1) * (half - LANES)]],
-        axis=1,
-    )
-    low, high = lanes(0), lanes(1)
-    mine = jnp.where(core == 0, low, high)
-    theirs = cycle(jnp.where(core == 0, high, low), "chan", 1)
+    theirs = cycle(give, "chan", 1)
 
     conv_flops = 2 * tokens * 9 * width * half
     received = []
     for back in range(1, min(moments, 3)):
         (term,) = call(
-            functools.partial(send_kernel, cells),
+            functools.partial(send_kernel, cells, 2 - back),
             [shaped((tokens * 3 // 2, LANES), BF)],
-            [where, act, other, w_act[2 - back]],
+            [where, act, other, weights],
             flops=conv_flops,
         )
         received.append(cycle(term, "tm", back))
     (rest,) = call(
         functools.partial(rest_kernel, cells),
         [shaped((tokens, half), F32)],
-        [where, act, other, cache.reshape(2, tokens, width), halo, halo_other, w_act[2], w_cache],
+        [where, act, other, cache.reshape(2, tokens, width), halo, halo_other, weights],
         [pltpu.VMEM((3, tokens, half), F32)],
         flops=3 * conv_flops,
     )
     (out,) = call(
         final_kernel,
         [shaped((tokens, half), BF)],
-        [where, rest, mine, theirs] + received,
+        [where, rest, keep, theirs] + received,
     )
     return out.reshape(1, rows, cells, half)
 

time: 79.2 us -> 52.5 us (0.66)
  local copies, waits for them, and re-layouts: 33.9 us -> 3.6 us
  waiting for transfers between devices: 5.14 us -> 15 us
  other arithmetic: 3.98 us -> 1.17 us
  Pallas kernels: 19 us -> 17.5 us
  starting transfers between devices: 16.2 us -> 14.9 us
    slice x20 -> x0, local copies, waits for them, and re-layouts: 31.4 us -> none  [the longest x14 15.8 us: shuffled(): take = lambda start, stop: lax.slice_in_dim(array, start, stop, axis=axis)]
    ppermute x11, waiting for transfers between devices: 5.14 us -> 12.2 us  [cycle(): lax.ppermute(array, axis, [(i, (i + by) % count) for i in range(count)])]
    concatenate x5 -> x0, other arithmetic: 3.11 us -> none  [shuffled(): jnp.concatenate([take(0, LANES), take(half, half + LANES), take(LANES, ha...]
    ppermute x1, waiting for transfers between devices: 0.01 us -> 2.79 us  [body(): halo = lax.ppermute(edge, ('space', 'chan'), pairs)]
    ppermute x11, starting transfers between devices: 16 us -> 14.2 us  [cycle(): lax.ppermute(array, axis, [(i, (i + by) % count) for i in range(count)])]
    pallas_call x6, Pallas kernels: 19 us -> 17.5 us  [call(): pl.pallas_call(kernel, out_shape=outs, in_specs=[pl.BlockSpec(memory_spac...]
    unnamed x44 -> x16, local copies, waits for them, and re-layouts: 2.52 us -> 2.91 us
  transfers between devices with their start and end apart: 12 -> 12, of which waited for: 2 -> 6; matrix products, arithmetic and copies ran while one was open for 45% -> 3% of each run, Pallas kernels for 22% -> 20%
where the time goes in v2:
time: 52.5 us; the launch traced here: 52.3 us
  Pallas kernels  17.5 us (33%)
  waiting for transfers between devices  15 us (29%)
  starting transfers between devices  14.9 us (28%)
  local copies, waits for them, and re-layouts  3.6 us (7%)
  other arithmetic  1.17 us (2%)
    pallas_call x6, Pallas kernels, call(): pl.pallas_call(kernel, out_shape=outs, in_specs=[pl.BlockSpec(memory_spac...  17.5 us
    ppermute x11, starting transfers between devices, cycle(): lax.ppermute(array, axis, [(i, (i + by) % count) for i in range(count)])  14.2 us
    ppermute x11, waiting for transfers between devices, cycle(): lax.ppermute(array, axis, [(i, (i + by) % count) for i in range(count)])  12.2 us
    unnamed x16, local copies, waits for them, and re-layouts  2.91 us
    ppermute x1, waiting for transfers between devices, body(): halo = lax.ppermute(edge, ('space', 'chan'), pairs)  2.79 us
    select_n x1, other arithmetic, body(): edge = jnp.where(core == 0, cache[:, rows - 1], cache[:, 0])  1.1 us
  transfers between devices with their start and end apart: 12, of which 6 were waited for; matrix products, arithmetic and copies ran while one was open for 3% of the time, Pallas kernels for 20%

profile of v2, /device:TPU:0, one launch (start us, length us, event | category | flops | bytes accessed | tf_op | source)
XLA Modules:
  0.0 52.3 jit_solution(4462668260512906237)
XLA Ops:
  0.0 0.0 copy-start.7
  0.0 0.1 pad_add_fusion.where
  0.1 0.0 copy-start.1
  0.1 1.0 %copy-done.1 = bf16[1,4,160,192]{3,2,1,0:T(8,128)(2,1)S(1)} copy-done((bf16[1,4,160,192]{3,2,1,0:T(8,128)(2,1)S(1)}, bf16[1,4,160,192]{3,2,1,0:T(8,128)(2,1)}, u32[]{:S(2)}) %copy-start.1) | copy-done | bytes 245784
  1.1 0.0 copy-start.2
  1.1 0.0 copy-start.3
  1.1 0.6 %shard_map.91.refs_0_ = bf16[960,128]{1,0:T(8,128)(2,1)S(1)} custom-call(s32[4]{0:T(128)S(1)} %pad_add_fusion.where, bf16[640,192]{1,0:T(8,128)(2,1)S(1)} %bitcast.17), custom_call_target="tpu_custom_call" | custom-call | bytes 491536 | tf_op jit(solution)/shard_map/pallas_call | solution.py:24
  1.7 5.1 %collective-permute-start.3 = (bf16[960,128]{1,0:T(8,128)(2,1)S(1)}, bf16[960,128]{1,0:T(8,128)(2,1)S(1)}, u32[]{:S(2)}, u32[]{:S(2)}) collective-permute-start(bf16[960,128]{1,0:T(8,128)(2,1)S(1)} %shard_map.91.refs_0_), channel_id=1, source_target_pairs={{0,12},{4,0},{8,4},{12,8},{1,13},{5,1},{9,5},{13,9},{2,14},{6,2},{... | collective-permute-start | bytes 737288 | tf_op jit(solution)/shard_map/ppermute | solution.py:18
  6.8 0.0 collective-permute-start.1
  6.8 6.4 %collective-permute-done.3.refs_4_ = bf16[960,128]{1,0:T(8,128)(2,1)S(1)} collective-permute-done((bf16[960,128]{1,0:T(8,128)(2,1)S(1)}, bf16[960,128]{1,0:T(8,128)(2,1)S(1)}, u32[]{:S(2)}, u32[]{:S(2)}) %collective-permute-start.3) | collective-permute-done | bytes 245792 | tf_op jit(solution)/shard_map/ppermute | solution.py:18
  13.2 4.3 %collective-permute-start.5 = (bf16[960,128]{1,0:T(8,128)(2,1)S(1)}, bf16[960,128]{1,0:T(8,128)(2,1)S(1)}, u32[]{:S(2)}, u32[]{:S(2)}) collective-permute-start(bf16[960,128]{1,0:T(8,128)(2,1)S(1)} %collective-permute-done.3.refs_4_), channel_id=1, source_target_pairs={{0,12},{4,0},{8,4},{12,8},{1,13},{5,1},{9,5},{13,9},{2,14},{6,2},{... | collective-permute-start | bytes 737288 | tf_op jit(solution)/shard_map/ppermute | solution.py:18
  17.5 0.0 collective-permute-start
  17.5 0.5 collective-permute-start.4
  18.0 1.4 %collective-permute-done.1.refs_2_ = bf16[960,128]{1,0:T(8,128)(2,1)S(1)} collective-permute-done((bf16[960,128]{1,0:T(8,128)(2,1)S(1)}, bf16[960,128]{1,0:T(8,128)(2,1)S(1)}, u32[]{:S(2)}, u32[]{:S(2)}) %collective-permute-start.1) | collective-permute-done | bytes 245792 | tf_op jit(solution)/shard_map/ppermute | solution.py:18
  19.4 0.0 collective-permute-start.2
  19.4 0.7 %reshape.17.gain = bf16[1,384]{1,0:T(2,128)(2,1)S(1)} reshape(bf16[384]{0:T(512)(128)(2,1)} %param.11) | data formatting | bytes 1536 | tf_op jit(solution)/shard_map/reshape | solution.py:241
  20.1 1.1 %fusion = bf16[2,160,384]{2,1,0:T(8,128)(2,1)S(1)} fusion(bf16[2,4,160,384]{3,2,1,0:T(8,128)(2,1)} %param.10, pred[]{:T(512)S(6)} %eq.3), kind=kLoop, calls=%fused_computation.1 | loop fusion | flops 122880 | bytes 737281 | tf_op jit(solution)/shard_map/jit(_where)/select_n | solution.py:262
  21.2 0.0 copy-start
  21.2 2.1 %collective-permute-done.5.mine = bf16[960,128]{1,0:T(8,128)(2,1)S(1)} collective-permute-done((bf16[960,128]{1,0:T(8,128)(2,1)S(1)}, bf16[960,128]{1,0:T(8,128)(2,1)S(1)}, u32[]{:S(2)}, u32[]{:S(2)}) %collective-permute-start.5) | collective-permute-done | bytes 245792 | tf_op jit(solution)/shard_map/ppermute | solution.py:18
  23.3 0.0 collective-permute-done.refs_1_
  23.3 0.0 collective-permute-done.4.refs_5_
  23.3 0.0 collective-permute-done.2.refs_3_
  23.3 0.0 copy-start.5
  23.3 1.0 %copy-done.5 = bf16[384,384]{1,0:T(8,128)(2,1)S(1)} copy-done((bf16[384,384]{1,0:T(8,128)(2,1)S(1)}, bf16[384,384]{1,0:T(8,128)(2,1)}, u32[]{:S(2)}) %copy-start.5) | copy-done | bytes 294936
  24.2 0.0 copy-start.6
  24.2 1.0 %copy-done.6 = bf16[384,384]{1,0:T(8,128)(2,1)S(1)} copy-done((bf16[384,384]{1,0:T(8,128)(2,1)S(1)}, bf16[384,384]{1,0:T(8,128)(2,1)}, u32[]{:S(2)}) %copy-start.6) | copy-done | bytes 294936
  25.2 4.8 %shard_map.92 = (bf16[480,384]{1,0:T(8,128)(2,1)S(1)}, bf16[480,384]{1,0:T(8,128)(2,1)S(1)}, f32[480,128]{1,0:T(8,128)S(1)}, f32[480,128]{1,0:T(8,128)S(1)}, f32[480,384]{1,0:T(8,128)S(1)}) custom-call(s32[4]{0:T(128)S(1)} %pad_add_fusion.where, bf16[1,384]{1,0:T(2,128)(2,1)S(1)} %reshape.17.gain, bf16[384,384]{1,0:T(8,128)(2,1)S(1)} %copy-done.5, ...), custom_call_target="tpu_custom_call" | custom-call | flops 1415577600 | bytes 4031248 | tf_op jit(solution)/shard_map/pallas_call | solution.py:24
  30.0 0.1 collective-permute-start.6
  30.0 0.0 copy-done.7
  30.1 0.7 %collective-permute-start.8 = (bf16[2,160,384]{2,1,0:T(8,128)(2,1)S(1)}, bf16[2,160,384]{2,1,0:T(8,128)(2,1)S(1)}, u32[]{:S(2)}, u32[]{:S(2)}) collective-permute-start(bf16[2,160,384]{2,1,0:T(8,128)(2,1)S(1)} %fusion), channel_id=1, source_target_pairs={{0,4},{1,13},{4,8},{5,1},{8,12},{9,5},{12,0},{13,9},{2,6},{3,15},{... | collective-permute-start | bytes 737288 | tf_op jit(solution)/shard_map/ppermute | solution.py:268
  30.7 0.8 %collective-permute-done.6.theirs = bf16[960,128]{1,0:T(8,128)(2,1)S(1)} collective-permute-done((bf16[960,128]{1,0:T(8,128)(2,1)S(1)}, bf16[960,128]{1,0:T(8,128)(2,1)S(1)}, u32[]{:S(2)}, u32[]{:S(2)}) %collective-permute-start.6) | collective-permute-done | bytes 245792 | tf_op jit(solution)/shard_map/ppermute | solution.py:18
  31.5 0.0 copy-done.2
  31.5 0.0 copy-done.3
  31.5 3.5 %shard_map.93 = (bf16[480,384]{1,0:T(8,128)(2,1)S(1)}, bf16[320,192]{1,0:T(8,128)(2,1)S(1)}, bf16[320,192]{1,0:T(8,128)(2,1)S(1)}) custom-call(s32[4]{0:T(128)S(1)} %pad_add_fusion.where, bf16[1,384]{1,0:T(2,128)(2,1)S(1)} %reshape.17.gain, bf16[1,384]{1,0:T(2,128)(2,1)S(1)} %reshape.18.gain_two, bf16[384,384]{1,0:T(8,128)(2,1)S(1)} %copy-done.2, ...), custom_call_target="tpu_custom_call" | custom-call | flops 754974720 | bytes 3663376 | tf_op jit(solution)/shard_map/pallas_call | solution.py:24
  35.1 2.4 %collective-permute-start.7 = (bf16[480,384]{1,0:T(8,128)(2,1)S(1)}, bf16[480,384]{1,0:T(8,128)(2,1)S(1)}, u32[]{:S(2)}, u32[]{:S(2)}) collective-permute-start(bf16[480,384]{1,0:T(8,128)(2,1)S(1)} %get-tuple-element.25.act), channel_id=1, source_target_pairs={{0,1},{1,0},{2,3},{3,2},{4,5},{5,4},{6,7},{7,6},{8,9},{9,8},{10,11... | collective-permute-start | bytes 1105928 | tf_op jit(solution)/shard_map/ppermute | solution.py:18
  37.5 2.8 %collective-permute-done.8.halo = bf16[2,160,384]{2,1,0:T(8,128)(2,1)S(1)} collective-permute-done((bf16[2,160,384]{2,1,0:T(8,128)(2,1)S(1)}, bf16[2,160,384]{2,1,0:T(8,128)(2,1)S(1)}, u32[]{:S(2)}, u32[]{:S(2)}) %collective-permute-start.8) | collective-permute-done | bytes 245792 | tf_op jit(solution)/shard_map/ppermute | solution.py:268
  40.3 0.0 collective-permute-start.9
  40.3 0.0 collective-permute-done.7.other
  40.3 0.0 copy-done
  40.3 2.1 %shard_map.95 = bf16[960,128]{1,0:T(8,128)(2,1)S(1)} custom-call(s32[4]{0:T(128)S(1)} %pad_add_fusion.where, bf16[480,384]{1,0:T(8,128)(2,1)S(1)} %get-tuple-element.25.act, bf16[480,384]{1,0:T(8,128)(2,1)S(1)} %collective-permute-done.7.other, bf16[3,3,3,192,384]{4,3,2,1,0:T(8,128)(2,1)S(1)} %bitcast.15), custom_call_target="tpu_custom_call" | custom-call | flops 849346560 | bytes 4964368 | tf_op jit(solution)/shard_map/pallas_call | solution.py:24
  42.4 1.6 %collective-permute-start.11 = (bf16[960,128]{1,0:T(8,128)(2,1)S(1)}, bf16[960,128]{1,0:T(8,128)(2,1)S(1)}, u32[]{:S(2)}, u32[]{:S(2)}) collective-permute-start(bf16[960,128]{1,0:T(8,128)(2,1)S(1)} %shard_map.95), channel_id=1, source_target_pairs={{0,2},{2,0},{1,3},{3,1},{4,6},{6,4},{5,7},{7,5},{8,10},{10,8},{9,1... | collective-permute-start | bytes 737288 | tf_op jit(solution)/shard_map/ppermute | solution.py:18
  44.0 0.2 collective-permute-start.10
  44.2 0.0 collective-permute-done.9.halo_other
  44.2 0.0 copy-done.4
  44.2 5.1 %shard_map.94.rest = f32[640,192]{1,0:T(8,128)S(1)} custom-call(s32[4]{0:T(128)S(1)} %pad_add_fusion.where, bf16[480,384]{1,0:T(8,128)(2,1)S(1)} %get-tuple-element.25.act, bf16[480,384]{1,0:T(8,128)(2,1)S(1)} %collective-permute-done.7.other, bf16[2,640,384]{2,1,0:T(8,128)(2,1)S(1)} %bitcast.18, bf16[2,160,384]{2,1,0:T(8,128)(2,1)S(1)} %collective-permute-done.8.halo, ...), custom_call_target="tpu_custom_call" | custom-call | flops 2548039680 | bytes 6684688 | tf_op jit(solution)/shard_map/pallas_call | solution.py:24
  49.3 0.0 collective-permute-done.10.theirs
  49.3 1.5 %collective-permute-done.11.refs_0_ = bf16[960,128]{1,0:T(8,128)(2,1)S(1)} collective-permute-done((bf16[960,128]{1,0:T(8,128)(2,1)S(1)}, bf16[960,128]{1,0:T(8,128)(2,1)S(1)}, u32[]{:S(2)}, u32[]{:S(2)}) %collective-permute-start.11) | collective-permute-done | bytes 245792 | tf_op jit(solution)/shard_map/ppermute | solution.py:18
  50.8 1.4 %shard_map.96 = bf16[640,192]{1,0:T(8,128)(2,1)} custom-call(s32[4]{0:T(128)S(1)} %pad_add_fusion.where, f32[640,192]{1,0:T(8,128)S(1)} %shard_map.94.rest, bf16[320,192]{1,0:T(8,128)(2,1)S(1)} %get-tuple-element.27.mine, bf16[320,192]{1,0:T(8,128)(2,1)S(1)} %collective-permute-done.10.theirs, bf16[960,128]{1,0:T(8,128)(2,1)S(1)} %collective-permute-done.11.refs_0_), custom_call_target="tpu_custom_call" | custom-call | bytes 1228816 | tf_op jit(solution)/shard_map/pallas_call | solution.py:24
  (2 shorter events, 0.0 us)
Async XLA Ops:
  0.0 30.0 %copy-start.7 = (bf16[384]{0:T(512)(128)(2,1)S(1)}, bf16[384]{0:T(512)(128)(2,1)}, u32[]{:S(2)}) copy-start(bf16[384]{0:T(512)(128)(2,1)} %param.12) | copy-start | bytes 2308
  0.1 1.0 %copy-start.1 = (bf16[1,4,160,192]{3,2,1,0:T(8,128)(2,1)S(1)}, bf16[1,4,160,192]{3,2,1,0:T(8,128)(2,1)}, u32[]{:S(2)}) copy-start(bf16[1,4,160,192]{3,2,1,0:T(8,128)(2,1)} %param.9) | copy-start | bytes 737284
  1.1 30.5 %copy-start.2 = (bf16[384,384]{1,0:T(8,128)(2,1)S(1)}, bf16[384,384]{1,0:T(8,128)(2,1)}, u32[]{:S(2)}) copy-start(bf16[384,384]{1,0:T(8,128)(2,1)} %w_value.1) | copy-start | bytes 884740
  1.1 30.5 %copy-start.3 = (bf16[384,384]{1,0:T(8,128)(2,1)S(1)}, bf16[384,384]{1,0:T(8,128)(2,1)}, u32[]{:S(2)}) copy-start(bf16[384,384]{1,0:T(8,128)(2,1)} %w_out.1) | copy-start | bytes 884740
  1.7 11.5 %collective-permute-start.3 = (bf16[960,128]{1,0:T(8,128)(2,1)S(1)}, bf16[960,128]{1,0:T(8,128)(2,1)S(1)}, u32[]{:S(2)}, u32[]{:S(2)}) collective-permute-start(bf16[960,128]{1,0:T(8,128)(2,1)S(1)} %shard_map.91.refs_0_), channel_id=1, source_target_pairs={{0,12},{4,0},{8,4},{12,8},{1,13},{5,1},{9,5},{13,9},{2,14},{6,2},{... | collective-permute-start | bytes 737288 | tf_op jit(solution)/shard_map/ppermute | solution.py:18
  6.8 12.6 %collective-permute-start.1 = (bf16[960,128]{1,0:T(8,128)(2,1)S(1)}, bf16[960,128]{1,0:T(8,128)(2,1)S(1)}, u32[]{:S(2)}, u32[]{:S(2)}) collective-permute-start(bf16[960,128]{1,0:T(8,128)(2,1)S(1)} %shard_map.91.refs_0_), channel_id=1, source_target_pairs={{0,4},{4,8},{8,12},{12,0},{1,5},{5,9},{9,13},{13,1},{2,6},{6,10},{... | collective-permute-start | bytes 737288 | tf_op jit(solution)/shard_map/ppermute | solution.py:18
  13.2 10.1 %collective-permute-start.5 = (bf16[960,128]{1,0:T(8,128)(2,1)S(1)}, bf16[960,128]{1,0:T(8,128)(2,1)S(1)}, u32[]{:S(2)}, u32[]{:S(2)}) collective-permute-start(bf16[960,128]{1,0:T(8,128)(2,1)S(1)} %collective-permute-done.3.refs_4_), channel_id=1, source_target_pairs={{0,12},{4,0},{8,4},{12,8},{1,13},{5,1},{9,5},{13,9},{2,14},{6,2},{... | collective-permute-start | bytes 737288 | tf_op jit(solution)/shard_map/ppermute | solution.py:18
  17.5 5.8 %collective-permute-start = (bf16[960,128]{1,0:T(8,128)(2,1)S(1)}, bf16[960,128]{1,0:T(8,128)(2,1)S(1)}, u32[]{:S(2)}, u32[]{:S(2)}) collective-permute-start(bf16[960,128]{1,0:T(8,128)(2,1)S(1)} %shard_map.91.refs_0_), channel_id=1, source_target_pairs={{0,1},{1,0},{2,3},{3,2},{4,5},{5,4},{6,7},{7,6},{8,9},{9,8},{10,11... | collective-permute-start | bytes 737288 | tf_op jit(solution)/shard_map/ppermute | solution.py:18
  17.5 5.8 %collective-permute-start.4 = (bf16[960,128]{1,0:T(8,128)(2,1)S(1)}, bf16[960,128]{1,0:T(8,128)(2,1)S(1)}, u32[]{:S(2)}, u32[]{:S(2)}) collective-permute-start(bf16[960,128]{1,0:T(8,128)(2,1)S(1)} %collective-permute-done.3.refs_4_), channel_id=1, source_target_pairs={{0,1},{1,0},{2,3},{3,2},{4,5},{5,4},{6,7},{7,6},{8,9},{9,8},{10,11... | collective-permute-start | bytes 737288 | tf_op jit(solution)/shard_map/ppermute | solution.py:18
  19.4 3.9 %collective-permute-start.2 = (bf16[960,128]{1,0:T(8,128)(2,1)S(1)}, bf16[960,128]{1,0:T(8,128)(2,1)S(1)}, u32[]{:S(2)}, u32[]{:S(2)}) collective-permute-start(bf16[960,128]{1,0:T(8,128)(2,1)S(1)} %collective-permute-done.1.refs_2_), channel_id=1, source_target_pairs={{0,1},{1,0},{2,3},{3,2},{4,5},{5,4},{6,7},{7,6},{8,9},{9,8},{10,11... | collective-permute-start | bytes 737288 | tf_op jit(solution)/shard_map/ppermute | solution.py:18
  21.2 19.1 %copy-start = (bf16[3,3,3,384,192]{3,4,2,1,0:T(8,128)(2,1)S(1)}, bf16[3,3,3,384,192]{3,4,2,1,0:T(8,128)(2,1)}, u32[]{:S(2)}) copy-start(bf16[3,3,3,384,192]{3,4,2,1,0:T(8,128)(2,1)} %param.17) | copy-start | bytes 11943940
  23.3 1.0 %copy-start.5 = (bf16[384,384]{1,0:T(8,128)(2,1)S(1)}, bf16[384,384]{1,0:T(8,128)(2,1)}, u32[]{:S(2)}) copy-start(bf16[384,384]{1,0:T(8,128)(2,1)} %w_query.1) | copy-start | bytes 884740
  24.2 1.0 %copy-start.6 = (bf16[384,384]{1,0:T(8,128)(2,1)S(1)}, bf16[384,384]{1,0:T(8,128)(2,1)}, u32[]{:S(2)}) copy-start(bf16[384,384]{1,0:T(8,128)(2,1)} %w_key.1) | copy-start | bytes 884740
  30.0 1.6 %collective-permute-start.6 = (bf16[960,128]{1,0:T(8,128)(2,1)S(1)}, bf16[960,128]{1,0:T(8,128)(2,1)S(1)}, u32[]{:S(2)}, u32[]{:S(2)}) collective-permute-start(bf16[960,128]{1,0:T(8,128)(2,1)S(1)} %collective-permute-done.5.mine), channel_id=1, source_target_pairs={{0,1},{1,0},{2,3},{3,2},{4,5},{5,4},{6,7},{7,6},{8,9},{9,8},{10,11... | collective-permute-start | bytes 737288 | tf_op jit(solution)/shard_map/ppermute | solution.py:18
  30.1 10.2 %collective-permute-start.8 = (bf16[2,160,384]{2,1,0:T(8,128)(2,1)S(1)}, bf16[2,160,384]{2,1,0:T(8,128)(2,1)S(1)}, u32[]{:S(2)}, u32[]{:S(2)}) collective-permute-start(bf16[2,160,384]{2,1,0:T(8,128)(2,1)S(1)} %fusion), channel_id=1, source_target_pairs={{0,4},{1,13},{4,8},{5,1},{8,12},{9,5},{12,0},{13,9},{2,6},{3,15},{... | collective-permute-start | bytes 737288 | tf_op jit(solution)/shard_map/ppermute | solution.py:268
  31.5 12.7 %copy-start.4 = (bf16[2,4,160,384]{3,2,1,0:T(8,128)(2,1)S(1)}, bf16[2,4,160,384]{3,2,1,0:T(8,128)(2,1)}, u32[]{:S(2)}) copy-start(bf16[2,4,160,384]{3,2,1,0:T(8,128)(2,1)} %param.10) | copy-start | bytes 2949124
  35.1 5.2 %collective-permute-start.7 = (bf16[480,384]{1,0:T(8,128)(2,1)S(1)}, bf16[480,384]{1,0:T(8,128)(2,1)S(1)}, u32[]{:S(2)}, u32[]{:S(2)}) collective-permute-start(bf16[480,384]{1,0:T(8,128)(2,1)S(1)} %get-tuple-element.25.act), channel_id=1, source_target_pairs={{0,1},{1,0},{2,3},{3,2},{4,5},{5,4},{6,7},{7,6},{8,9},{9,8},{10,11... | collective-permute-start | bytes 1105928 | tf_op jit(solution)/shard_map/ppermute | solution.py:18
  40.3 3.9 %collective-permute-start.9 = (bf16[2,160,384]{2,1,0:T(8,128)(2,1)S(1)}, bf16[2,160,384]{2,1,0:T(8,128)(2,1)S(1)}, u32[]{:S(2)}, u32[]{:S(2)}) collective-permute-start(bf16[2,160,384]{2,1,0:T(8,128)(2,1)S(1)} %collective-permute-done.8.halo), channel_id=1, source_target_pairs={{0,1},{1,0},{2,3},{3,2},{4,5},{5,4},{6,7},{7,6},{8,9},{9,8},{10,11... | collective-permute-start | bytes 737288 | tf_op jit(solution)/shard_map/ppermute | solution.py:18
  42.4 8.4 %collective-permute-start.11 = (bf16[960,128]{1,0:T(8,128)(2,1)S(1)}, bf16[960,128]{1,0:T(8,128)(2,1)S(1)}, u32[]{:S(2)}, u32[]{:S(2)}) collective-permute-start(bf16[960,128]{1,0:T(8,128)(2,1)S(1)} %shard_map.95), channel_id=1, source_target_pairs={{0,2},{2,0},{1,3},{3,1},{4,6},{6,4},{5,7},{7,5},{8,10},{10,8},{9,1... | collective-permute-start | bytes 737288 | tf_op jit(solution)/shard_map/ppermute | solution.py:18
  44.0 5.3 %collective-permute-start.10 = (bf16[320,192]{1,0:T(8,128)(2,1)S(1)}, bf16[320,192]{1,0:T(8,128)(2,1)S(1)}, u32[]{:S(2)}, u32[]{:S(2)}) collective-permute-start(bf16[320,192]{1,0:T(8,128)(2,1)S(1)} %get-tuple-element.28), channel_id=1, source_target_pairs={{0,1},{1,0},{2,3},{3,2},{4,5},{5,4},{6,7},{7,6},{8,9},{9,8},{10,11... | collective-permute-start | bytes 368648 | tf_op jit(solution)/shard_map/ppermute | solution.py:18

commit v3 on v2

--- a/solution.py
+++ b/solution.py
@@ -18,9 +18,12 @@
     return lax.ppermute(array, axis, [(i, (i + by) % count) for i in range(count)])
 
 
-def call(kernel, outs, args, scratch=(), flops=0, exps=0):
+def between_cores(array, pieces=2):
+    return jnp.concatenate([cycle(piece, "chan", 1) for piece in jnp.split(array, pieces)])
+
+
+def call(kernel, outs, args, scratch=(), flops=1000):
     vmem = pl.BlockSpec(memory_space=pltpu.VMEM)
-    moved = sum(math.prod(a.shape) * a.dtype.itemsize for a in list(args) + list(outs))
     return pl.pallas_call(
         kernel,
         out_shape=outs,
@@ -28,7 +31,7 @@
         out_specs=[vmem] * len(outs),
         scratch_shapes=list(scratch),
         compiler_params=pltpu.CompilerParams(vmem_limit_bytes=36 * 2**20),
-        cost_estimate=pl.CostEstimate(flops=flops, bytes_accessed=moved, transcendentals=exps),
+        cost_estimate=pl.CostEstimate(flops=flops, bytes_accessed=1000, transcendentals=0),
     )(*args)
 
 
@@ -44,12 +47,22 @@
     return lax.dot_general(a, b, (((1,), (1,)), ((), ())), preferred_element_type=F32)
 
 
+def pack(x, out):
+    tokens = x.shape[0]
+    out[:tokens, :] = x[:, :LANES].astype(BF)
+    rest = x[:, LANES:]
+    out[tokens:, :] = jnp.concatenate([rest[: tokens // 2], rest[tokens // 2 :]], axis=1).astype(BF)
+
+
+def unpacked(packed):
+    tokens = packed.shape[0] * 2 // 3
+    rest = packed[tokens:].astype(F32)
+    rest = jnp.concatenate([rest[:, : LANES // 2], rest[:, LANES // 2 :]], axis=0)
+    return jnp.concatenate([packed[:tokens].astype(F32), rest], axis=1)
+
+
 def pack_kernel(where, x, out):
-    tokens, width = x.shape
-    rest = width - LANES
-    out[:tokens, :] = x[:, :LANES]
-    out[tokens:, :rest] = x[: tokens // 2, LANES:]
-    out[tokens:, rest:] = x[tokens // 2 :, LANES:]
+    pack(x[...], out)
 
 
 def joined_halves(core, mine, theirs):
@@ -90,28 +103,49 @@
     return new_top, total, accum
 
 
-def first_kernel(where, gain, w_query, w_key, *refs):
+def queries(rows, w_query, w_key):
+    scale = rows.shape[1] ** (-0.5) * math.log2(math.e)
+    return (dot_t(dot(rows, w_query).astype(BF), w_key) * scale).astype(BF)
+
+
+def own_rows_kernel(where, gain, mine, theirs, w_query, w_key, *refs):
+    raw_out, keys_out, query_out, w_query_out, w_key_out = refs
     core = where[0]
-    tiles, (query_out, raw_out, top_out, total_out, accum_out), normed = refs[:6], refs[6:11], refs[11]
-    tokens = normed.shape[1]
-    edge = raw_out.shape[0] - tokens // 2
-    raws = [joined_halves(core, tiles[2 * i], tiles[2 * i + 1]) for i in range(3)]
-    for i in range(3):
-        normed[i] = rms_scaled(raws[i], gain[...]).astype(BF)
-    own, behind, ahead = raws
+    raw = joined_halves(core, mine, theirs)
+    half = raw.shape[0] // 2
+    keys = rms_scaled(raw, gain[...]).astype(BF)
+    keys_out[...] = keys
+    raw_out[...] = jnp.where(core == 0, raw[:half], raw[half:]).astype(BF)
+    rows = jnp.where(core == 0, keys[:half], keys[half:])
+    query_out[...] = queries(rows, w_query[...], w_key[...])
+    w_query_out[...] = w_query[...]
+    w_key_out[...] = w_key[...]
+
+
+def first_kernel(where, gain, raw_own, keys_own, query_own, w_query, w_key, *refs):
+    core = where[0]
+    tiles, (query_out, raw_out, top_out, total_out, accum_out, keys) = refs[:4], refs[4:]
+    tokens = keys_own.shape[0]
     half = tokens // 2
-    raw_out[...] = jnp.where(
-        core == 0,
-        jnp.concatenate([behind[tokens - edge :], own[:half]], axis=0),
-        jnp.concatenate([own[half:], ahead[:edge]], axis=0),
-    ).astype(BF)
-    rows = rms_scaled(raw_out[...].astype(F32), gain[...]).astype(BF)
-    width = rows.shape[1]
-    query = dot(rows, w_query[...]).astype(BF)
-    scale = width ** (-0.5) * math.log2(math.e)
-    query = (dot_t(query, w_key[...]) * scale).astype(BF)
+    edge = raw_out.shape[0] - half
+    behind, ahead = [joined_halves(core, tiles[2 * i], tiles[2 * i + 1]) for i in range(2)]
+    keys[:tokens] = keys_own[...]
+    keys[tokens : 2 * tokens] = rms_scaled(behind, gain[...]).astype(BF)
+    keys[2 * tokens :] = rms_scaled(ahead, gain[...]).astype(BF)
+    beyond = jnp.where(core == 0, behind[tokens - edge :], ahead[:edge])
+    rows = jnp.where(core == 0, keys[2 * tokens - edge : 2 * tokens], keys[2 * tokens : 2 * tokens + edge])
+    beyond = beyond.astype(BF)
+    further = queries(rows, w_query[...], w_key[...])
+
+    def ordered(own, other):
+        return jnp.where(
+            core == 0, jnp.concatenate([other, own], axis=0), jnp.concatenate([own, other], axis=0)
+        )
+
+    raw_out[...] = ordered(raw_own[...], beyond)
+    query = ordered(query_own[...], further)
     query_out[...] = query
-    top, total, accum = attend(query, [normed[i] for i in range(3)], None, None, None)
+    top, total, accum = attend(query, [keys[...]], None, None, None)
     top_out[...] = jnp.broadcast_to(top, top_out.shape)
     total_out[...] = jnp.broadcast_to(total, total_out.shape)
     accum_out[...] = accum
@@ -152,11 +186,11 @@
     act_out[...] = jnp.where(beyond, 0.0, act).astype(BF)
 
 
-def taps(padded, weights, back, cells):
+def taps(padded, weights, cells):
     tokens = padded.shape[0] - 2 * cells
     wide = jnp.concatenate([padded[i * cells : i * cells + tokens] for i in range(3)], axis=1)
     return [
-        dot_t(wide, jnp.concatenate([weights[back, row, cell] for row in range(3)], axis=1))
+        dot_t(wide, jnp.concatenate([weights[row, cell] for row in range(3)], axis=1))
         for cell in range(3)
     ]
 
@@ -176,57 +210,69 @@
 
 
 def send_kernel(cells, back, where, act, other, weights, out):
-    conv = gathered(taps(whole_tile(where[0], act, other), weights, back, cells), cells)
-    tokens, width = conv.shape
-    rest = width - LANES
-    out[:tokens, :] = conv[:, :LANES].astype(BF)
-    out[tokens:, :] = jnp.concatenate(
-        [conv[: tokens // 2, LANES:], conv[tokens // 2 :, LANES:]], axis=1
-    ).astype(BF)
-
-
-def rest_kernel(cells, where, act, other, cache, halo, halo_other, weights, out, sums):
-    core, place, places, moment = where[0], where[1], where[2], where[3]
-    for i, part in enumerate(taps(whole_tile(core, act, other), weights, 2, cells)):
-        sums[i] = part
-    above = jnp.where(core == 0, halo[...], halo_other[...])
-    below = jnp.where(core == 0, halo_other[...], halo[...])
-    above = jnp.where(place == 0, jnp.zeros_like(above), above)
-    below = jnp.where(place == places - 1, jnp.zeros_like(below), below)
-
-    def add(frame, back):
-        padded = jnp.concatenate([above[frame], cache[frame], below[frame]], axis=0)
-        for i, part in enumerate(taps(padded, weights, back, cells)):
-            sums[i] += part
+    conv = gathered(taps(whole_tile(where[0], act, other), weights.at[back], cells), cells)
+    pack(conv, out)
+
+
+def cache_kernel(cells, where, cache, weights, sums, up, down):
+    moment = where[3]
+    tokens = cache.shape[1]
+    ends = jnp.zeros((cells, cache.shape[2]), cache.dtype)
+
+    def products(pairs):
+        for i in range(3):
+            sums[i] = sum(
+                dot_t(
+                    jnp.concatenate([padded[r * cells : r * cells + tokens] for r in range(3)], axis=1),
+                    jnp.concatenate([weights[back, row, i] for row in range(3)], axis=1),
+                )
+                for padded, back in [
+                    (jnp.concatenate([ends, cache[frame], ends], axis=0), back) for frame, back in pairs
+                ]
+            )
+        for out, start, row in ((up, tokens - cells, 0), (down, 0, 2)):
+            edge = jnp.concatenate([cache[frame, start : start + cells] for frame, _ in pairs], axis=1)
+            parts = [
+                dot_t(edge, jnp.concatenate([weights[back, row, i] for _, back in pairs], axis=1))
+                for i in range(3)
+            ]
+            pack(gathered(parts, cells), out)
 
     @pl.when(moment == 0)
     def _():
-        add(0, 0)
-        add(1, 1)
+        products([(0, 0), (1, 1)])
 
     @pl.when(moment == 1)
     def _():
-        add(1, 0)
-
-    out[...] = gathered([sums[i] for i in range(3)], cells)
-
-
-def final_kernel(where, rest, mine, theirs, *refs):
-    core, moment = where[0], where[3]
+        products([(1, 0)])
+
+    @pl.when(moment > 1)
+    def _():
+        for out in (sums, up, down):
+            out[...] = jnp.zeros_like(out)
+
+
+def rest_kernel(cells, where, act, other, cached, weights, out):
+    parts = taps(whole_tile(where[0], act, other), weights.at[2], cells)
+    out[...] = gathered([part + cached[i] for i, part in enumerate(parts)], cells)
+
+
+def final_kernel(cells, where, rest, mine, theirs, above, below, *refs):
+    core, place, places, moment = where[0], where[1], where[2], where[3]
     received, out = refs[:-1], refs[-1]
-    tokens, width = rest.shape
-    more = width - LANES
-    total = rest[...]
-    for back, ref in enumerate(received):
-        packed = jnp.where(moment > back, ref[...].astype(F32), 0.0)
-        tail = packed[tokens:]
-        tail = jnp.concatenate([tail[:, :more], tail[:, more:]], axis=0)
-        total = total + jnp.concatenate([packed[:tokens], tail], axis=1)
-    total = total + jnp.where(
+    tokens = rest.shape[0]
+    total = rest[...] + jnp.where(
         core == 0,
         jnp.concatenate([mine[...], theirs[...]], axis=0),
         jnp.concatenate([theirs[...], mine[...]], axis=0),
     ).astype(F32)
+    first = jnp.where(place == 0, 0.0, unpacked(above[...]))
+    last = jnp.where(place == places - 1, 0.0, unpacked(below[...]))
+    total = jnp.concatenate(
+        [total[:cells] + first, total[cells : tokens - cells], total[tokens - cells :] + last], axis=0
+    )
+    for back, ref in enumerate(received):
+        total = total + jnp.where(moment > back, unpacked(ref[...]), 0.0)
     out[...] = total.astype(BF)
 
 
@@ -243,12 +289,36 @@
     weights = conv_weight.transpose(0, 1, 2, 4, 3)
 
     (packed,) = call(
-        pack_kernel, [shaped((tokens * 3 // 2, LANES), BF)], [where, frames_in.reshape(tokens, half)]
+        pack_kernel,
+        [shaped((tokens * 3 // 2, LANES), BF)],
+        [where, frames_in.reshape(tokens, half)],
+        flops=4 * 10**9,
     )
     behind, ahead = cycle(packed, "space", 1), cycle(packed, "space", -1)
-    tiles = []
-    for tile in (packed, behind, ahead):
-        tiles += [tile, cycle(tile, "chan", 1)]
+    cache = cache.reshape(2, tokens, width)
+    own_other = cycle(packed, "chan", 1)
+    raw_own, keys_own, query_own, w_query, w_key = call(
+        own_rows_kernel,
+        [
+            shaped((tokens // 2, width), BF),
+            shaped((tokens, width), BF),
+            shaped((tokens // 2, width), BF),
+            shaped((width, width), BF),
+            shaped((width, width), BF),
+        ],
+        [where, gain, packed, own_other, w_query, w_key],
+        flops=4 * 10**9,
+    )
+    raw_own, cache = lax.optimization_barrier((raw_own, cache))
+    cached, up_term, down_term = call(
+        functools.partial(cache_kernel, cells),
+        [shaped((3, tokens, half), F32)] + [shaped((cells * 3 // 2, LANES), BF)] * 2,
+        [where, cache, weights],
+    )
+    ahead, cached = lax.optimization_barrier((ahead, cached))
+    ahead_other = between_cores(ahead)
+    behind, ahead_other = lax.optimization_barrier((behind, ahead_other))
+    tiles = [behind, between_cores(behind), ahead, ahead_other]
     up, down = behind, ahead
     groups = []
     for step in range(2, places // 2 + 1):
@@ -259,28 +329,16 @@
         else:
             groups.append([down])
 
-    edge = jnp.where(core == 0, cache[:, rows - 1], cache[:, 0])
-    edge, down = lax.optimization_barrier((edge, down))
-    groups[-1][-1] = down
-    pairs = [
-        (2 * i + c, 2 * ((i + 1 - 2 * c) % places) + c) for i in range(places) for c in range(2)
-    ]
-    halo = lax.ppermute(edge, ("space", "chan"), pairs)
-    halo_other = cycle(halo, "chan", 1)
-
     state = [
         shaped((count, LANES), F32),
         shaped((count, LANES), F32),
         shaped((count, width), F32),
     ]
-    pair_flops = 4 * count * width * tokens
     query, raw, top, total, accum = call(
         first_kernel,
         [shaped((count, width), BF), shaped((count, width), BF)] + state,
-        [where, gain, w_query, w_key] + tiles,
-        [pltpu.VMEM((3, tokens, width), BF)],
-        flops=3 * pair_flops,
-        exps=3 * count * tokens,
+        [where, gain, raw_own, keys_own, query_own, w_query, w_key] + tiles,
+        [pltpu.VMEM((3 * tokens, width), BF)],
     )
     for group in groups[:-1]:
         tiles = []
@@ -290,41 +348,38 @@
             functools.partial(middle_kernel, len(group)),
             state,
             [where, gain, query, top, total, accum] + tiles,
-            flops=len(group) * pair_flops,
-            exps=len(group) * count * tokens,
-        )
+                )
     tile, accum = lax.optimization_barrier((groups[-1][0], accum))
+    tile_other = between_cores(tile)
     act, keep, give = call(
         last_kernel,
         [shaped((count, width), BF)] + [shaped((tokens // 2, half), BF)] * 2,
-        [where, gain, gain_act, w_value, w_out, query, raw, top, total, accum, tile, cycle(tile, "chan", 1)],
-        flops=pair_flops + 4 * count * width * width,
-        exps=count * tokens,
+        [where, gain, gain_act, w_value, w_out, query, raw, top, total, accum, tile, tile_other],
     )
     other = cycle(act, "chan", 1)
     theirs = cycle(give, "chan", 1)
 
-    conv_flops = 2 * tokens * 9 * width * half
     received = []
     for back in range(1, min(moments, 3)):
         (term,) = call(
             functools.partial(send_kernel, cells, 2 - back),
             [shaped((tokens * 3 // 2, LANES), BF)],
             [where, act, other, weights],
-            flops=conv_flops,
-        )
-        received.append(cycle(term, "tm", back))
+            )
+        received.append(term)
+    act, received = lax.optimization_barrier((act, received))
+    received = [cycle(term, "tm", 1 + i) for i, term in enumerate(received)]
     (rest,) = call(
         functools.partial(rest_kernel, cells),
         [shaped((tokens, half), F32)],
-        [where, act, other, cache.reshape(2, tokens, width), halo, halo_other, weights],
-        [pltpu.VMEM((3, tokens, half), F32)],
-        flops=3 * conv_flops,
-    )
+        [where, act, other, cached, weights],
+    )
+    up_term, down_term, act = lax.optimization_barrier((up_term, down_term, act))
+    above, below = cycle(up_term, "space", 1), cycle(down_term, "space", -1)
     (out,) = call(
-        final_kernel,
+        functools.partial(final_kernel, cells),
         [shaped((tokens, half), BF)],
-        [where, rest, keep, theirs] + received,
+        [where, rest, keep, theirs, above, below] + received,
     )
     return out.reshape(1, rows, cells, half)
 

time: 52.5 us -> 43.9 us (0.84)
  waiting for transfers between devices: 15 us -> 5.69 us
  starting transfers between devices: 14.9 us -> 16.8 us
  local copies, waits for them, and re-layouts: 3.6 us -> 1.82 us
  Pallas kernels: 17.5 us -> 19.1 us
  other arithmetic: 1.17 us -> 0.13 us
    ppermute x11 -> x15, waiting for transfers between devices: 12.2 us -> 5.69 us  [cycle(): lax.ppermute(array, axis, [(i, (i + by) % count) for i in range(count)])]
    ppermute x1 -> x0, waiting for transfers between devices: 2.79 us -> none  [body(): halo = lax.ppermute(edge, ('space', 'chan'), pairs)]
    ppermute x11 -> x15, starting transfers between devices: 14.2 us -> 16.8 us  [cycle(): lax.ppermute(array, axis, [(i, (i + by) % count) for i in range(count)])]
    pallas_call x6 -> x8, Pallas kernels: 17.5 us -> 19.1 us  [call(): pl.pallas_call(kernel, out_shape=outs, in_specs=[pl.BlockSpec(memory_spac...]
    unnamed x16 -> x18, local copies, waits for them, and re-layouts: 2.91 us -> 1.76 us
    select_n x1 -> x0, other arithmetic: 1.1 us -> none  [body(): edge = jnp.where(core == 0, cache[:, rows - 1], cache[:, 0])]
    ppermute x1 -> x0, starting transfers between devices: 0.69 us -> none  [body(): halo = lax.ppermute(edge, ('space', 'chan'), pairs)]
    reshape x1, local copies, waits for them, and re-layouts: 0.68 us -> 0.01 us  [body(): gain = gain_one.reshape(1, width)]
  transfers between devices with their start and end apart: 12 -> 15, of which waited for: 6 -> 9; matrix products, arithmetic and copies ran while one was open for 3% -> 0% of each run, Pallas kernels for 20% -> 26%
where the time goes in v3:
time: 43.9 us; the launch traced here: 43.7 us
  Pallas kernels  19.1 us (44%)
  starting transfers between devices  16.8 us (38%)
  waiting for transfers between devices  5.69 us (13%)
  local copies, waits for them, and re-layouts  1.82 us (4%)
    pallas_call x8, Pallas kernels, call(): pl.pallas_call(kernel, out_shape=outs, in_specs=[pl.BlockSpec(memory_spac...  19.1 us
    ppermute x15, starting transfers between devices, cycle(): lax.ppermute(array, axis, [(i, (i + by) % count) for i in range(count)])  16.8 us
    ppermute x15, waiting for transfers between devices, cycle(): lax.ppermute(array, axis, [(i, (i + by) % count) for i in range(count)])  5.69 us
    unnamed x18, local copies, waits for them, and re-layouts  1.76 us
  transfers between devices with their start and end apart: 15, of which 9 were waited for; matrix products, arithmetic and copies ran while one was open for 0% of the time, Pallas kernels for 26%

profile of v3, /device:TPU:0, one launch (start us, length us, event | category | flops | bytes accessed | tf_op | source)
XLA Modules:
  0.0 43.7 jit_solution(11693132592470362249)
XLA Ops:
  0.0 0.1 pad_add_fusion.where
  0.1 1.0 %copy-done.4 = bf16[1,4,160,192]{3,2,1,0:T(8,128)(2,1)S(1)} copy-done((bf16[1,4,160,192]{3,2,1,0:T(8,128)(2,1)S(1)}, bf16[1,4,160,192]{3,2,1,0:T(8,128)(2,1)}, u32[]{:S(2)}) %copy-start.4) | copy-done | bytes 245784
  1.1 0.6 %shard_map.91.mine = bf16[960,128]{1,0:T(8,128)(2,1)S(1)} custom-call(s32[4]{0:T(128)S(1)} %pad_add_fusion.where, bf16[640,192]{1,0:T(8,128)(2,1)S(1)} %bitcast.11), custom_call_target="tpu_custom_call" | custom-call | flops 4000000000 | bytes 1000 | tf_op jit(solution)/shard_map/pallas_call | solution.py:27
  1.7 0.5 %collective-permute-start = (bf16[960,128]{1,0:T(8,128)(2,1)S(1)}, bf16[960,128]{1,0:T(8,128)(2,1)S(1)}, u32[]{:S(2)}, u32[]{:S(2)}) collective-permute-start(bf16[960,128]{1,0:T(8,128)(2,1)S(1)} %shard_map.91.mine), channel_id=1, source_target_pairs={{0,1},{1,0},{2,3},{3,2},{4,5},{5,4},{6,7},{7,6},{8,9},{9,8},{10,11... | collective-permute-start | bytes 737288 | tf_op jit(solution)/shard_map/ppermute | solution.py:18
  2.2 4.7 %collective-permute-start.2 = (bf16[960,128]{1,0:T(8,128)(2,1)S(1)}, bf16[960,128]{1,0:T(8,128)(2,1)S(1)}, u32[]{:S(2)}, u32[]{:S(2)}) collective-permute-start(bf16[960,128]{1,0:T(8,128)(2,1)S(1)} %shard_map.91.mine), channel_id=1, source_target_pairs={{0,12},{4,0},{8,4},{12,8},{1,13},{5,1},{9,5},{13,9},{2,14},{6,2},{... | collective-permute-start | bytes 737288 | tf_op jit(solution)/shard_map/ppermute | solution.py:18
  6.9 0.0 collective-permute-start.1
  6.9 0.0 copy-start
  6.9 0.0 copy-start.1
  6.9 0.0 collective-permute-done.theirs
  6.9 0.0 copy-done.5
  6.9 0.0 copy-done.6
  6.9 1.6 %shard_map.92 = (bf16[320,384]{1,0:T(8,128)(2,1)S(1)}, bf16[640,384]{1,0:T(8,128)(2,1)S(1)}, bf16[320,384]{1,0:T(8,128)(2,1)S(1)}, bf16[384,384]{1,0:T(8,128)(2,1)S(1)}, bf16[384,384]{1,0:T(8,128)(2,1)S(1)}) custom-call(s32[4]{0:T(128)S(1)} %pad_add_fusion.where, bf16[1,384]{1,0:T(2,128)(2,1)S(1)} %reshape.15.gain, bf16[960,128]{1,0:T(8,128)(2,1)S(1)} %shard_map.91.mine, ...), custom_call_target="tpu_custom_call" | custom-call | flops 4000000000 | bytes 1000 | tf_op jit(solution)/shard_map/pallas_call | solution.py:27
  8.5 0.5 %copy-done = bf16[3,3,3,384,192]{3,4,2,1,0:T(8,128)(2,1)S(1)} copy-done((bf16[3,3,3,384,192]{3,4,2,1,0:T(8,128)(2,1)S(1)}, bf16[3,3,3,384,192]{3,4,2,1,0:T(8,128)(2,1)}, u32[]{:S(2)}) %copy-start) | copy-done | bytes 3981336
  9.0 0.3 copy-done.1
  9.3 3.8 %shard_map.93 = (f32[3,640,192]{2,1,0:T(8,128)S(1)}, bf16[240,128]{1,0:T(8,128)(2,1)S(1)}, bf16[240,128]{1,0:T(8,128)(2,1)S(1)}) custom-call(s32[4]{0:T(128)S(1)} %pad_add_fusion.where, bf16[2,640,384]{2,1,0:T(8,128)(2,1)S(1)} %bitcast.10, bf16[3,3,3,192,384]{4,3,2,1,0:T(8,128)(2,1)S(1)} %bitcast.7), custom_call_target="tpu_custom_call" | custom-call | flops 1000 | bytes 1000 | tf_op jit(solution)/shard_map/pallas_call | solution.py:27
  13.1 0.0 copy-start.2
  13.1 0.0 copy-start.3
  13.1 0.1 collective-permute-done.2.refs_2_
  13.2 0.2 collective-permute-start.3
  13.4 0.4 collective-permute-start.4
  13.8 4.3 %collective-permute-start.7 = (bf16[960,128]{1,0:T(8,128)(2,1)S(1)}, bf16[960,128]{1,0:T(8,128)(2,1)S(1)}, u32[]{:S(2)}, u32[]{:S(2)}) collective-permute-start(bf16[960,128]{1,0:T(8,128)(2,1)S(1)} %collective-permute-done.2.refs_2_), channel_id=1, source_target_pairs={{0,12},{4,0},{8,4},{12,8},{1,13},{5,1},{9,5},{13,9},{2,14},{6,2},{... | collective-permute-start | bytes 737288 | tf_op jit(solution)/shard_map/ppermute | solution.py:18
  18.1 0.0 collective-permute-done.3
  18.1 0.0 collective-permute-done.4
  18.1 0.9 %collective-permute-done.1.refs_0_ = bf16[960,128]{1,0:T(8,128)(2,1)S(1)} collective-permute-done((bf16[960,128]{1,0:T(8,128)(2,1)S(1)}, bf16[960,128]{1,0:T(8,128)(2,1)S(1)}, u32[]{:S(2)}, u32[]{:S(2)}) %collective-permute-start.1) | collective-permute-done | bytes 245792 | tf_op jit(solution)/shard_map/ppermute | solution.py:18
  19.1 0.1 collective-permute-start.5
  19.1 0.5 %collective-permute-start.6 = (bf16[480,128]{1,0:T(8,128)(2,1)S(1)}, bf16[480,128]{1,0:T(8,128)(2,1)S(1)}, u32[]{:S(2)}, u32[]{:S(2)}) collective-permute-start(bf16[480,128]{1,0:T(8,128)(2,1)S(1)} %get-tuple-element.64), channel_id=1, source_target_pairs={{0,1},{1,0},{2,3},{3,2},{4,5},{5,4},{6,7},{7,6},{8,9},{9,8},{10,11... | collective-permute-start | bytes 368648 | tf_op jit(solution)/shard_map/ppermute | solution.py:18
  19.6 0.8 %collective-permute-done.5 = bf16[480,128]{1,0:T(8,128)(2,1)S(1)} collective-permute-done((bf16[480,128]{1,0:T(8,128)(2,1)S(1)}, bf16[480,128]{1,0:T(8,128)(2,1)S(1)}, u32[]{:S(2)}, u32[]{:S(2)}) %collective-permute-start.5) | collective-permute-done | bytes 122912 | tf_op jit(solution)/shard_map/ppermute | solution.py:18
  20.5 0.2 collective-permute-done.6
  20.7 3.9 %shard_map.94 = (bf16[480,384]{1,0:T(8,128)(2,1)S(1)}, bf16[480,384]{1,0:T(8,128)(2,1)S(1)}, f32[480,128]{1,0:T(8,128)S(1)}, f32[480,128]{1,0:T(8,128)S(1)}, f32[480,384]{1,0:T(8,128)S(1)}) custom-call(s32[4]{0:T(128)S(1)} %pad_add_fusion.where, bf16[1,384]{1,0:T(2,128)(2,1)S(1)} %reshape.15.gain, bf16[320,384]{1,0:T(8,128)(2,1)S(1)} %get-tuple-element.34.raw_own, ...), custom_call_target="tpu_custom_call" | custom-call | flops 1000 | bytes 1000 | tf_op jit(solution)/shard_map/pallas_call | solution.py:27
  24.6 0.0 collective-permute-done.7.mine
  24.6 0.4 collective-permute-start.8
  25.0 0.2 collective-permute-start.9
  25.2 0.8 %collective-permute-done.8 = bf16[480,128]{1,0:T(8,128)(2,1)S(1)} collective-permute-done((bf16[480,128]{1,0:T(8,128)(2,1)S(1)}, bf16[480,128]{1,0:T(8,128)(2,1)S(1)}, u32[]{:S(2)}, u32[]{:S(2)}) %collective-permute-start.8) | collective-permute-done | bytes 122912 | tf_op jit(solution)/shard_map/ppermute | solution.py:18
  26.0 0.3 collective-permute-done.9
  26.4 3.5 %shard_map.95 = (bf16[480,384]{1,0:T(8,128)(2,1)S(1)}, bf16[320,192]{1,0:T(8,128)(2,1)S(1)}, bf16[320,192]{1,0:T(8,128)(2,1)S(1)}) custom-call(s32[4]{0:T(128)S(1)} %pad_add_fusion.where, bf16[1,384]{1,0:T(2,128)(2,1)S(1)} %reshape.15.gain, bf16[1,384]{1,0:T(2,128)(2,1)S(1)} %reshape.16.gain_two, bf16[384,384]{1,0:T(8,128)(2,1)S(1)} %copy-done.2, ...), custom_call_target="tpu_custom_call" | custom-call | flops 1000 | bytes 1000 | tf_op jit(solution)/shard_map/pallas_call | solution.py:27
  29.9 0.3 collective-permute-start.10
  30.1 1.5 %collective-permute-done.10.other = bf16[480,384]{1,0:T(8,128)(2,1)S(1)} collective-permute-done((bf16[480,384]{1,0:T(8,128)(2,1)S(1)}, bf16[480,384]{1,0:T(8,128)(2,1)S(1)}, u32[]{:S(2)}, u32[]{:S(2)}) %collective-permute-start.10) | collective-permute-done | bytes 368672 | tf_op jit(solution)/shard_map/ppermute | solution.py:18
  31.6 2.1 %shard_map.96 = bf16[960,128]{1,0:T(8,128)(2,1)S(1)} custom-call(s32[4]{0:T(128)S(1)} %pad_add_fusion.where, bf16[480,384]{1,0:T(8,128)(2,1)S(1)} %get-tuple-element.52.act, bf16[480,384]{1,0:T(8,128)(2,1)S(1)} %collective-permute-done.10.other, bf16[3,3,3,192,384]{4,3,2,1,0:T(8,128)(2,1)S(1)} %bitcast.8), custom_call_target="tpu_custom_call" | custom-call | flops 1000 | bytes 1000 | tf_op jit(solution)/shard_map/pallas_call | solution.py:27
  33.8 1.6 %collective-permute-start.14 = (bf16[960,128]{1,0:T(8,128)(2,1)S(1)}, bf16[960,128]{1,0:T(8,128)(2,1)S(1)}, u32[]{:S(2)}, u32[]{:S(2)}) collective-permute-start(bf16[960,128]{1,0:T(8,128)(2,1)S(1)} %shard_map.96), channel_id=1, source_target_pairs={{0,2},{2,0},{1,3},{3,1},{4,6},{6,4},{5,7},{7,5},{8,10},{10,8},{9,1... | collective-permute-start | bytes 737288 | tf_op jit(solution)/shard_map/ppermute | solution.py:18
  35.3 0.0 collective-permute-start.11
  35.3 1.5 %collective-permute-start.12 = (bf16[240,128]{1,0:T(8,128)(2,1)S(1)}, bf16[240,128]{1,0:T(8,128)(2,1)S(1)}, u32[]{:S(2)}, u32[]{:S(2)}) collective-permute-start(bf16[240,128]{1,0:T(8,128)(2,1)S(1)} %get-tuple-element.58), channel_id=1, source_target_pairs={{0,4},{4,8},{8,12},{12,0},{1,5},{5,9},{9,13},{13,1},{2,6},{6,10},{... | collective-permute-start | bytes 184328 | tf_op jit(solution)/shard_map/ppermute | solution.py:18
  36.8 2.4 %collective-permute-start.13 = (bf16[240,128]{1,0:T(8,128)(2,1)S(1)}, bf16[240,128]{1,0:T(8,128)(2,1)S(1)}, u32[]{:S(2)}, u32[]{:S(2)}) collective-permute-start(bf16[240,128]{1,0:T(8,128)(2,1)S(1)} %get-tuple-element.59), channel_id=1, source_target_pairs={{0,12},{4,0},{8,4},{12,8},{1,13},{5,1},{9,5},{13,9},{2,14},{6,2},{... | collective-permute-start | bytes 184328 | tf_op jit(solution)/shard_map/ppermute | solution.py:18
  39.1 2.1 %shard_map.97.rest = f32[640,192]{1,0:T(8,128)S(1)} custom-call(s32[4]{0:T(128)S(1)} %pad_add_fusion.where, bf16[480,384]{1,0:T(8,128)(2,1)S(1)} %get-tuple-element.52.act, bf16[480,384]{1,0:T(8,128)(2,1)S(1)} %collective-permute-done.10.other, f32[3,640,192]{2,1,0:T(8,128)S(1)} %get-tuple-element.53.cached, bf16[3,3,3,192,384]{4,3,2,1,0:T(8,128)(2,1)S(1)} %bitcast.9), custom_call_target="tpu_custom_call" | custom-call | flops 1000 | bytes 1000 | tf_op jit(solution)/shard_map/pallas_call | solution.py:27
  41.2 0.0 collective-permute-done.11.theirs
  41.2 0.7 %collective-permute-done.12.above = bf16[240,128]{1,0:T(8,128)(2,1)S(1)} collective-permute-done((bf16[240,128]{1,0:T(8,128)(2,1)S(1)}, bf16[240,128]{1,0:T(8,128)(2,1)S(1)}, u32[]{:S(2)}, u32[]{:S(2)}) %collective-permute-start.12) | collective-permute-done | bytes 61472 | tf_op jit(solution)/shard_map/ppermute | solution.py:18
  41.9 0.4 collective-permute-done.13.below
  42.3 0.0 collective-permute-done.14.refs_0_
  42.3 1.4 %shard_map.98 = bf16[640,192]{1,0:T(8,128)(2,1)} custom-call(s32[4]{0:T(128)S(1)} %pad_add_fusion.where, f32[640,192]{1,0:T(8,128)S(1)} %shard_map.97.rest, bf16[320,192]{1,0:T(8,128)(2,1)S(1)} %get-tuple-element.54.mine, bf16[320,192]{1,0:T(8,128)(2,1)S(1)} %collective-permute-done.11.theirs, bf16[240,128]{1,0:T(8,128)(2,1)S(1)} %collective-permute-done.12.above, ...), custom_call_target="tpu_custom_call" | custom-call | flops 1000 | bytes 1000 | tf_op jit(solution)/shard_map/pallas_call | solution.py:27
  (17 shorter events, 0.1 us)
Async XLA Ops:
  0.1 1.0 %copy-start.4 = (bf16[1,4,160,192]{3,2,1,0:T(8,128)(2,1)S(1)}, bf16[1,4,160,192]{3,2,1,0:T(8,128)(2,1)}, u32[]{:S(2)}) copy-start(bf16[1,4,160,192]{3,2,1,0:T(8,128)(2,1)} %param.9) | copy-start | bytes 737284
  1.1 5.8 %copy-start.7 = (bf16[384]{0:T(512)(128)(2,1)S(1)}, bf16[384]{0:T(512)(128)(2,1)}, u32[]{:S(2)}) copy-start(bf16[384]{0:T(512)(128)(2,1)} %param.11) | copy-start | bytes 2308
  1.1 5.9 %copy-start.5 = (bf16[384,384]{1,0:T(8,128)(2,1)S(1)}, bf16[384,384]{1,0:T(8,128)(2,1)}, u32[]{:S(2)}) copy-start(bf16[384,384]{1,0:T(8,128)(2,1)} %w_query.1) | copy-start | bytes 884740
  1.1 5.9 %copy-start.6 = (bf16[384,384]{1,0:T(8,128)(2,1)S(1)}, bf16[384,384]{1,0:T(8,128)(2,1)}, u32[]{:S(2)}) copy-start(bf16[384,384]{1,0:T(8,128)(2,1)} %w_key.1) | copy-start | bytes 884740
  1.7 5.2 %collective-permute-start = (bf16[960,128]{1,0:T(8,128)(2,1)S(1)}, bf16[960,128]{1,0:T(8,128)(2,1)S(1)}, u32[]{:S(2)}, u32[]{:S(2)}) collective-permute-start(bf16[960,128]{1,0:T(8,128)(2,1)S(1)} %shard_map.91.mine), channel_id=1, source_target_pairs={{0,1},{1,0},{2,3},{3,2},{4,5},{5,4},{6,7},{7,6},{8,9},{9,8},{10,11... | collective-permute-start | bytes 737288 | tf_op jit(solution)/shard_map/ppermute | solution.py:18
  2.2 11.0 %collective-permute-start.2 = (bf16[960,128]{1,0:T(8,128)(2,1)S(1)}, bf16[960,128]{1,0:T(8,128)(2,1)S(1)}, u32[]{:S(2)}, u32[]{:S(2)}) collective-permute-start(bf16[960,128]{1,0:T(8,128)(2,1)S(1)} %shard_map.91.mine), channel_id=1, source_target_pairs={{0,12},{4,0},{8,4},{12,8},{1,13},{5,1},{9,5},{13,9},{2,14},{6,2},{... | collective-permute-start | bytes 737288 | tf_op jit(solution)/shard_map/ppermute | solution.py:18
  6.9 12.2 %collective-permute-start.1 = (bf16[960,128]{1,0:T(8,128)(2,1)S(1)}, bf16[960,128]{1,0:T(8,128)(2,1)S(1)}, u32[]{:S(2)}, u32[]{:S(2)}) collective-permute-start(bf16[960,128]{1,0:T(8,128)(2,1)S(1)} %shard_map.91.mine), channel_id=1, source_target_pairs={{0,4},{4,8},{8,12},{12,0},{1,5},{5,9},{9,13},{13,1},{2,6},{6,10},{... | collective-permute-start | bytes 737288 | tf_op jit(solution)/shard_map/ppermute | solution.py:18
  6.9 2.1 %copy-start = (bf16[3,3,3,384,192]{3,4,2,1,0:T(8,128)(2,1)S(1)}, bf16[3,3,3,384,192]{3,4,2,1,0:T(8,128)(2,1)}, u32[]{:S(2)}) copy-start(bf16[3,3,3,384,192]{3,4,2,1,0:T(8,128)(2,1)} %param.17) | copy-start | bytes 11943940
  6.9 2.4 %copy-start.1 = (bf16[2,4,160,384]{3,2,1,0:T(8,128)(2,1)S(1)}, bf16[2,4,160,384]{3,2,1,0:T(8,128)(2,1)}, u32[]{:S(2)}) copy-start(bf16[2,4,160,384]{3,2,1,0:T(8,128)(2,1)} %param.10) | copy-start | bytes 2949124
  9.3 15.9 %copy-start.8 = (bf16[384]{0:T(512)(128)(2,1)S(1)}, bf16[384]{0:T(512)(128)(2,1)}, u32[]{:S(2)}) copy-start(bf16[384]{0:T(512)(128)(2,1)} %param.12) | copy-start | bytes 2308
  13.1 13.2 %copy-start.2 = (bf16[384,384]{1,0:T(8,128)(2,1)S(1)}, bf16[384,384]{1,0:T(8,128)(2,1)}, u32[]{:S(2)}) copy-start(bf16[384,384]{1,0:T(8,128)(2,1)} %w_value.1) | copy-start | bytes 884740
  13.1 13.2 %copy-start.3 = (bf16[384,384]{1,0:T(8,128)(2,1)S(1)}, bf16[384,384]{1,0:T(8,128)(2,1)}, u32[]{:S(2)}) copy-start(bf16[384,384]{1,0:T(8,128)(2,1)} %w_out.1) | copy-start | bytes 884740
  13.2 4.9 %collective-permute-start.3 = (bf16[480,128]{1,0:T(8,128)(2,1)S(1)}, bf16[480,128]{1,0:T(8,128)(2,1)S(1)}, u32[]{:S(2)}, u32[]{:S(2)}) collective-permute-start(bf16[480,128]{1,0:T(8,128)(2,1)S(1)} %get-tuple-element.65), channel_id=1, source_target_pairs={{0,1},{1,0},{2,3},{3,2},{4,5},{5,4},{6,7},{7,6},{8,9},{9,8},{10,11... | collective-permute-start | bytes 368648 | tf_op jit(solution)/shard_map/ppermute | solution.py:18
  13.4 4.7 %collective-permute-start.4 = (bf16[480,128]{1,0:T(8,128)(2,1)S(1)}, bf16[480,128]{1,0:T(8,128)(2,1)S(1)}, u32[]{:S(2)}, u32[]{:S(2)}) collective-permute-start(bf16[480,128]{1,0:T(8,128)(2,1)S(1)} %get-tuple-element.66), channel_id=1, source_target_pairs={{0,1},{1,0},{2,3},{3,2},{4,5},{5,4},{6,7},{7,6},{8,9},{9,8},{10,11... | collective-permute-start | bytes 368648 | tf_op jit(solution)/shard_map/ppermute | solution.py:18
  13.8 10.8 %collective-permute-start.7 = (bf16[960,128]{1,0:T(8,128)(2,1)S(1)}, bf16[960,128]{1,0:T(8,128)(2,1)S(1)}, u32[]{:S(2)}, u32[]{:S(2)}) collective-permute-start(bf16[960,128]{1,0:T(8,128)(2,1)S(1)} %collective-permute-done.2.refs_2_), channel_id=1, source_target_pairs={{0,12},{4,0},{8,4},{12,8},{1,13},{5,1},{9,5},{13,9},{2,14},{6,2},{... | collective-permute-start | bytes 737288 | tf_op jit(solution)/shard_map/ppermute | solution.py:18
  19.1 1.4 %collective-permute-start.5 = (bf16[480,128]{1,0:T(8,128)(2,1)S(1)}, bf16[480,128]{1,0:T(8,128)(2,1)S(1)}, u32[]{:S(2)}, u32[]{:S(2)}) collective-permute-start(bf16[480,128]{1,0:T(8,128)(2,1)S(1)} %get-tuple-element.63), channel_id=1, source_target_pairs={{0,1},{1,0},{2,3},{3,2},{4,5},{5,4},{6,7},{7,6},{8,9},{9,8},{10,11... | collective-permute-start | bytes 368648 | tf_op jit(solution)/shard_map/ppermute | solution.py:18
  19.1 1.5 %collective-permute-start.6 = (bf16[480,128]{1,0:T(8,128)(2,1)S(1)}, bf16[480,128]{1,0:T(8,128)(2,1)S(1)}, u32[]{:S(2)}, u32[]{:S(2)}) collective-permute-start(bf16[480,128]{1,0:T(8,128)(2,1)S(1)} %get-tuple-element.64), channel_id=1, source_target_pairs={{0,1},{1,0},{2,3},{3,2},{4,5},{5,4},{6,7},{7,6},{8,9},{9,8},{10,11... | collective-permute-start | bytes 368648 | tf_op jit(solution)/shard_map/ppermute | solution.py:18
  24.6 1.4 %collective-permute-start.8 = (bf16[480,128]{1,0:T(8,128)(2,1)S(1)}, bf16[480,128]{1,0:T(8,128)(2,1)S(1)}, u32[]{:S(2)}, u32[]{:S(2)}) collective-permute-start(bf16[480,128]{1,0:T(8,128)(2,1)S(1)} %get-tuple-element.61), channel_id=1, source_target_pairs={{0,1},{1,0},{2,3},{3,2},{4,5},{5,4},{6,7},{7,6},{8,9},{9,8},{10,11... | collective-permute-start | bytes 368648 | tf_op jit(solution)/shard_map/ppermute | solution.py:18
  25.0 1.3 %collective-permute-start.9 = (bf16[480,128]{1,0:T(8,128)(2,1)S(1)}, bf16[480,128]{1,0:T(8,128)(2,1)S(1)}, u32[]{:S(2)}, u32[]{:S(2)}) collective-permute-start(bf16[480,128]{1,0:T(8,128)(2,1)S(1)} %get-tuple-element.62), channel_id=1, source_target_pairs={{0,1},{1,0},{2,3},{3,2},{4,5},{5,4},{6,7},{7,6},{8,9},{9,8},{10,11... | collective-permute-start | bytes 368648 | tf_op jit(solution)/shard_map/ppermute | solution.py:18
  29.9 1.8 %collective-permute-start.10 = (bf16[480,384]{1,0:T(8,128)(2,1)S(1)}, bf16[480,384]{1,0:T(8,128)(2,1)S(1)}, u32[]{:S(2)}, u32[]{:S(2)}) collective-permute-start(bf16[480,384]{1,0:T(8,128)(2,1)S(1)} %get-tuple-element.52.act), channel_id=1, source_target_pairs={{0,1},{1,0},{2,3},{3,2},{4,5},{5,4},{6,7},{7,6},{8,9},{9,8},{10,11... | collective-permute-start | bytes 1105928 | tf_op jit(solution)/shard_map/ppermute | solution.py:18
  33.8 8.5 %collective-permute-start.14 = (bf16[960,128]{1,0:T(8,128)(2,1)S(1)}, bf16[960,128]{1,0:T(8,128)(2,1)S(1)}, u32[]{:S(2)}, u32[]{:S(2)}) collective-permute-start(bf16[960,128]{1,0:T(8,128)(2,1)S(1)} %shard_map.96), channel_id=1, source_target_pairs={{0,2},{2,0},{1,3},{3,1},{4,6},{6,4},{5,7},{7,5},{8,10},{10,8},{9,1... | collective-permute-start | bytes 737288 | tf_op jit(solution)/shard_map/ppermute | solution.py:18
  35.3 5.9 %collective-permute-start.11 = (bf16[320,192]{1,0:T(8,128)(2,1)S(1)}, bf16[320,192]{1,0:T(8,128)(2,1)S(1)}, u32[]{:S(2)}, u32[]{:S(2)}) collective-permute-start(bf16[320,192]{1,0:T(8,128)(2,1)S(1)} %get-tuple-element.55), channel_id=1, source_target_pairs={{0,1},{1,0},{2,3},{3,2},{4,5},{5,4},{6,7},{7,6},{8,9},{9,8},{10,11... | collective-permute-start | bytes 368648 | tf_op jit(solution)/shard_map/ppermute | solution.py:18
  35.3 6.6 %collective-permute-start.12 = (bf16[240,128]{1,0:T(8,128)(2,1)S(1)}, bf16[240,128]{1,0:T(8,128)(2,1)S(1)}, u32[]{:S(2)}, u32[]{:S(2)}) collective-permute-start(bf16[240,128]{1,0:T(8,128)(2,1)S(1)} %get-tuple-element.58), channel_id=1, source_target_pairs={{0,4},{4,8},{8,12},{12,0},{1,5},{5,9},{9,13},{13,1},{2,6},{6,10},{... | collective-permute-start | bytes 184328 | tf_op jit(solution)/shard_map/ppermute | solution.py:18
  36.8 5.5 %collective-permute-start.13 = (bf16[240,128]{1,0:T(8,128)(2,1)S(1)}, bf16[240,128]{1,0:T(8,128)(2,1)S(1)}, u32[]{:S(2)}, u32[]{:S(2)}) collective-permute-start(bf16[240,128]{1,0:T(8,128)(2,1)S(1)} %get-tuple-element.59), channel_id=1, source_target_pairs={{0,12},{4,0},{8,4},{12,8},{1,13},{5,1},{9,5},{13,9},{2,14},{6,2},{... | collective-permute-start | bytes 184328 | tf_op jit(solution)/shard_map/ppermute | solution.py:18

commit v4 on v3

--- a/solution.py
+++ b/solution.py
@@ -27,7 +27,7 @@
     return pl.pallas_call(
         kernel,
         out_shape=outs,
-        in_specs=[pl.BlockSpec(memory_space=pltpu.SMEM)] + [vmem] * (len(args) - 1),
+        in_specs=[vmem] * len(args),
         out_specs=[vmem] * len(outs),
         scratch_shapes=list(scratch),
         compiler_params=pltpu.CompilerParams(vmem_limit_bytes=36 * 2**20),
@@ -35,6 +35,10 @@
     )(*args)
 
 
+def place_of():
+    return lax.axis_index("chan"), lax.axis_index("space"), lax.axis_size("space"), lax.axis_index("tm")
+
+
 def shaped(shape, dtype):
     return jax.ShapeDtypeStruct(shape, dtype)
 
@@ -61,7 +65,7 @@
     return jnp.concatenate([packed[:tokens].astype(F32), rest], axis=1)
 
 
-def pack_kernel(where, x, out):
+def pack_kernel(x, out):
     pack(x[...], out)
 
 
@@ -108,9 +112,9 @@
     return (dot_t(dot(rows, w_query).astype(BF), w_key) * scale).astype(BF)
 
 
-def own_rows_kernel(where, gain, mine, theirs, w_query, w_key, *refs):
+def own_rows_kernel(gain, mine, theirs, w_query, w_key, *refs):
     raw_out, keys_out, query_out, w_query_out, w_key_out = refs
-    core = where[0]
+    core = place_of()[0]
     raw = joined_halves(core, mine, theirs)
     half = raw.shape[0] // 2
     keys = rms_scaled(raw, gain[...]).astype(BF)
@@ -122,8 +126,8 @@
     w_key_out[...] = w_key[...]
 
 
-def first_kernel(where, gain, raw_own, keys_own, query_own, w_query, w_key, *refs):
-    core = where[0]
+def first_kernel(gain, raw_own, keys_own, query_own, w_query, w_key, *refs):
+    core = place_of()[0]
     tiles, (query_out, raw_out, top_out, total_out, accum_out, keys) = refs[:4], refs[4:]
     tokens = keys_own.shape[0]
     half = tokens // 2
@@ -151,8 +155,8 @@
     accum_out[...] = accum
 
 
-def middle_kernel(count, where, gain, query, top, total, accum, *refs):
-    core = where[0]
+def middle_kernel(count, gain, query, top, total, accum, *refs):
+    core = place_of()[0]
     tiles, (top_out, total_out, accum_out) = refs[: 2 * count], refs[2 * count :]
     keys = [
         rms_scaled(joined_halves(core, tiles[2 * i], tiles[2 * i + 1]), gain[...]).astype(BF)
@@ -164,8 +168,8 @@
     accum_out[...] = new[2]
 
 
-def last_kernel(where, gain, gain_two, w_value, w_out, query, raw, top, total, accum, mine, theirs, act_out, keep_out, give_out):
-    core, place, places = where[0], where[1], where[2]
+def last_kernel(gain, gain_two, w_value, w_out, query, raw, top, total, accum, mine, theirs, act_out, keep_out, give_out):
+    core, place, places, _ = place_of()
     keys = [rms_scaled(joined_halves(core, mine, theirs), gain[...]).astype(BF)]
     _, total, accum = attend(query[...], keys, top[:, :1], total[:, :1], accum[...])
     mixed = (accum / total).astype(BF)
@@ -209,13 +213,13 @@
     return jnp.concatenate([jnp.where(core == 0, a, b), jnp.where(core == 0, b, a)], axis=0)
 
 
-def send_kernel(cells, back, where, act, other, weights, out):
-    conv = gathered(taps(whole_tile(where[0], act, other), weights.at[back], cells), cells)
+def send_kernel(cells, back, act, other, weights, out):
+    conv = gathered(taps(whole_tile(place_of()[0], act, other), weights.at[back], cells), cells)
     pack(conv, out)
 
 
-def cache_kernel(cells, where, cache, weights, sums, up, down):
-    moment = where[3]
+def cache_kernel(cells, cache, weights, sums, up, down):
+    moment = place_of()[3]
     tokens = cache.shape[1]
     ends = jnp.zeros((cells, cache.shape[2]), cache.dtype)
 
@@ -252,13 +256,13 @@
             out[...] = jnp.zeros_like(out)
 
 
-def rest_kernel(cells, where, act, other, cached, weights, out):
-    parts = taps(whole_tile(where[0], act, other), weights.at[2], cells)
+def rest_kernel(cells, act, other, cached, weights, out):
+    parts = taps(whole_tile(place_of()[0], act, other), weights.at[2], cells)
     out[...] = gathered([part + cached[i] for i, part in enumerate(parts)], cells)
 
 
-def final_kernel(cells, where, rest, mine, theirs, above, below, *refs):
-    core, place, places, moment = where[0], where[1], where[2], where[3]
+def final_kernel(cells, rest, mine, theirs, above, below, *refs):
+    core, place, places, moment = place_of()
     received, out = refs[:-1], refs[-1]
     tokens = rest.shape[0]
     total = rest[...] + jnp.where(
@@ -277,9 +281,7 @@
 
 
 def body(frames_in, cache, gain_one, gain_two, w_query, w_key, w_value, w_out, conv_weight):
-    core, place, moment = lax.axis_index("chan"), lax.axis_index("space"), lax.axis_index("tm")
     places, moments = lax.axis_size("space"), lax.axis_size("tm")
-    where = jnp.stack([core, place, jnp.int32(places), moment]).astype(jnp.int32)
     _, rows, cells, half = frames_in.shape
     tokens, width = rows * cells, 2 * half
     count = tokens // 2 + cells
@@ -291,7 +293,7 @@
     (packed,) = call(
         pack_kernel,
         [shaped((tokens * 3 // 2, LANES), BF)],
-        [where, frames_in.reshape(tokens, half)],
+        [frames_in.reshape(tokens, half)],
         flops=4 * 10**9,
     )
     behind, ahead = cycle(packed, "space", 1), cycle(packed, "space", -1)
@@ -306,14 +308,14 @@
             shaped((width, width), BF),
             shaped((width, width), BF),
         ],
-        [where, gain, packed, own_other, w_query, w_key],
+        [gain, packed, own_other, w_query, w_key],
         flops=4 * 10**9,
     )
     raw_own, cache = lax.optimization_barrier((raw_own, cache))
     cached, up_term, down_term = call(
         functools.partial(cache_kernel, cells),
         [shaped((3, tokens, half), F32)] + [shaped((cells * 3 // 2, LANES), BF)] * 2,
-        [where, cache, weights],
+        [cache, weights],
     )
     ahead, cached = lax.optimization_barrier((ahead, cached))
     ahead_other = between_cores(ahead)
@@ -337,7 +339,7 @@
     query, raw, top, total, accum = call(
         first_kernel,
         [shaped((count, width), BF), shaped((count, width), BF)] + state,
-        [where, gain, raw_own, keys_own, query_own, w_query, w_key] + tiles,
+        [gain, raw_own, keys_own, query_own, w_query, w_key] + tiles,
         [pltpu.VMEM((3 * tokens, width), BF)],
     )
     for group in groups[:-1]:
@@ -347,14 +349,14 @@
         top, total, accum = call(
             functools.partial(middle_kernel, len(group)),
             state,
-            [where, gain, query, top, total, accum] + tiles,
+            [gain, query, top, total, accum] + tiles,
                 )
     tile, accum = lax.optimization_barrier((groups[-1][0], accum))
     tile_other = between_cores(tile)
     act, keep, give = call(
         last_kernel,
         [shaped((count, width), BF)] + [shaped((tokens // 2, half), BF)] * 2,
-        [where, gain, gain_act, w_value, w_out, query, raw, top, total, accum, tile, tile_other],
+        [gain, gain_act, w_value, w_out, query, raw, top, total, accum, tile, tile_other],
     )
     other = cycle(act, "chan", 1)
     theirs = cycle(give, "chan", 1)
@@ -364,7 +366,7 @@
         (term,) = call(
             functools.partial(send_kernel, cells, 2 - back),
             [shaped((tokens * 3 // 2, LANES), BF)],
-            [where, act, other, weights],
+            [act, other, weights],
             )
         received.append(term)
     act, received = lax.optimization_barrier((act, received))
@@ -372,14 +374,14 @@
     (rest,) = call(
         functools.partial(rest_kernel, cells),
         [shaped((tokens, half), F32)],
-        [where, act, other, cached, weights],
+        [act, other, cached, weights],
     )
     up_term, down_term, act = lax.optimization_barrier((up_term, down_term, act))
     above, below = cycle(up_term, "space", 1), cycle(down_term, "space", -1)
     (out,) = call(
         functools.partial(final_kernel, cells),
         [shaped((tokens, half), BF)],
-        [where, rest, keep, theirs, above, below] + received,
+        [rest, keep, theirs, above, below] + received,
     )
     return out.reshape(1, rows, cells, half)
 

time: 43.9 us -> 41.1 us (0.936)
  Pallas kernels: 19.1 us -> 14.7 us
  waiting for transfers between devices: 5.69 us -> 6.66 us
  local copies, waits for them, and re-layouts: 1.82 us -> 2.36 us
    pallas_call x8, Pallas kernels: 19.1 us -> 14.7 us  [call(): pl.pallas_call(kernel, out_shape=outs, in_specs=[vmem] * len(args), out_s...]
    ppermute x15, waiting for transfers between devices: 5.69 us -> 6.66 us  [cycle(): lax.ppermute(array, axis, [(i, (i + by) % count) for i in range(count)])]
    unnamed x18, local copies, waits for them, and re-layouts: 1.76 us -> 2.3 us
  transfers between devices with their start and end apart: 15 -> 15, of which waited for: 9 -> 10; matrix products, arithmetic and copies ran while one was open for 0% -> 0% of each run, Pallas kernels for 26% -> 22%
where the time goes in v4:
time: 41.1 us; the launch traced here: 40.9 us
  starting transfers between devices  17 us (41%)
  Pallas kernels  14.7 us (36%)
  waiting for transfers between devices  6.66 us (16%)
  local copies, waits for them, and re-layouts  2.36 us (6%)
    ppermute x15, starting transfers between devices, cycle(): lax.ppermute(array, axis, [(i, (i + by) % count) for i in range(count)])  17 us
    pallas_call x8, Pallas kernels, call(): pl.pallas_call(kernel, out_shape=outs, in_specs=[vmem] * len(args), out_s...  14.7 us
    ppermute x15, waiting for transfers between devices, cycle(): lax.ppermute(array, axis, [(i, (i + by) % count) for i in range(count)])  6.66 us
    unnamed x18, local copies, waits for them, and re-layouts  2.3 us
  transfers between devices with their start and end apart: 15, of which 10 were waited for; matrix products, arithmetic and copies ran while one was open for 0% of the time, Pallas kernels for 22%

profile of v4, /device:TPU:0, one launch (start us, length us, event | category | flops | bytes accessed | tf_op | source)
XLA Modules:
  0.0 40.9 jit_solution(17857107552020154110)
XLA Ops:
  0.0 1.0 %copy-done.4 = bf16[1,4,160,192]{3,2,1,0:T(8,128)(2,1)S(1)} copy-done((bf16[1,4,160,192]{3,2,1,0:T(8,128)(2,1)S(1)}, bf16[1,4,160,192]{3,2,1,0:T(8,128)(2,1)}, u32[]{:S(2)}) %copy-start.4) | copy-done | bytes 245784
  1.0 0.1 shard_map.91.mine
  1.1 0.5 %collective-permute-start = (bf16[960,128]{1,0:T(8,128)(2,1)S(1)}, bf16[960,128]{1,0:T(8,128)(2,1)S(1)}, u32[]{:S(2)}, u32[]{:S(2)}) collective-permute-start(bf16[960,128]{1,0:T(8,128)(2,1)S(1)} %shard_map.91.mine), channel_id=1, source_target_pairs={{0,1},{1,0},{2,3},{3,2},{4,5},{5,4},{6,7},{7,6},{8,9},{9,8},{10,11... | collective-permute-start | bytes 737288 | tf_op jit(solution)/shard_map/ppermute | solution.py:18
  1.6 4.7 %collective-permute-start.2 = (bf16[960,128]{1,0:T(8,128)(2,1)S(1)}, bf16[960,128]{1,0:T(8,128)(2,1)S(1)}, u32[]{:S(2)}, u32[]{:S(2)}) collective-permute-start(bf16[960,128]{1,0:T(8,128)(2,1)S(1)} %shard_map.91.mine), channel_id=1, source_target_pairs={{0,12},{4,0},{8,4},{12,8},{1,13},{5,1},{9,5},{13,9},{2,14},{6,2},{... | collective-permute-start | bytes 737288 | tf_op jit(solution)/shard_map/ppermute | solution.py:18
  6.3 0.0 collective-permute-start.1
  6.3 0.0 copy-done.7
  6.3 0.0 copy-start
  6.3 0.0 copy-start.1
  6.3 0.0 collective-permute-done.theirs
  6.3 1.0 %shard_map.92 = (bf16[320,384]{1,0:T(8,128)(2,1)S(1)}, bf16[640,384]{1,0:T(8,128)(2,1)S(1)}, bf16[320,384]{1,0:T(8,128)(2,1)S(1)}, bf16[384,384]{1,0:T(8,128)(2,1)S(1)}, bf16[384,384]{1,0:T(8,128)(2,1)S(1)}) custom-call(bf16[1,384]{1,0:T(2,128)(2,1)S(1)} %reshape.15.gain, bf16[960,128]{1,0:T(8,128)(2,1)S(1)} %shard_map.91.mine, ...), custom_call_target="tpu_custom_call" | custom-call | flops 4000000000 | bytes 1000 | tf_op jit(solution)/shard_map/pallas_call | solution.py:27
  7.4 1.0 %copy-done = bf16[3,3,3,384,192]{3,4,2,1,0:T(8,128)(2,1)S(1)} copy-done((bf16[3,3,3,384,192]{3,4,2,1,0:T(8,128)(2,1)S(1)}, bf16[3,3,3,384,192]{3,4,2,1,0:T(8,128)(2,1)}, u32[]{:S(2)}) %copy-start) | copy-done | bytes 3981336
  8.4 0.3 copy-done.1
  8.7 3.3 %shard_map.93 = (f32[3,640,192]{2,1,0:T(8,128)S(1)}, bf16[240,128]{1,0:T(8,128)(2,1)S(1)}, bf16[240,128]{1,0:T(8,128)(2,1)S(1)}) custom-call(bf16[2,640,384]{2,1,0:T(8,128)(2,1)S(1)} %bitcast.7, bf16[3,3,3,192,384]{4,3,2,1,0:T(8,128)(2,1)S(1)} %bitcast.4), custom_call_target="tpu_custom_call" | custom-call | flops 1000 | bytes 1000 | tf_op jit(solution)/shard_map/pallas_call | solution.py:27
  11.9 0.0 copy-start.2
  12.0 0.0 copy-start.3
  12.0 0.6 %collective-permute-done.2.refs_2_ = bf16[960,128]{1,0:T(8,128)(2,1)S(1)} collective-permute-done((bf16[960,128]{1,0:T(8,128)(2,1)S(1)}, bf16[960,128]{1,0:T(8,128)(2,1)S(1)}, u32[]{:S(2)}, u32[]{:S(2)}) %collective-permute-start.2) | collective-permute-done | bytes 245792 | tf_op jit(solution)/shard_map/ppermute | solution.py:18
  12.6 0.1 collective-permute-start.3
  12.7 0.5 %collective-permute-start.4 = (bf16[480,128]{1,0:T(8,128)(2,1)S(1)}, bf16[480,128]{1,0:T(8,128)(2,1)S(1)}, u32[]{:S(2)}, u32[]{:S(2)}) collective-permute-start(bf16[480,128]{1,0:T(8,128)(2,1)S(1)} %get-tuple-element.66), channel_id=1, source_target_pairs={{0,1},{1,0},{2,3},{3,2},{4,5},{5,4},{6,7},{7,6},{8,9},{9,8},{10,11... | collective-permute-start | bytes 368648 | tf_op jit(solution)/shard_map/ppermute | solution.py:18
  13.2 4.3 %collective-permute-start.7 = (bf16[960,128]{1,0:T(8,128)(2,1)S(1)}, bf16[960,128]{1,0:T(8,128)(2,1)S(1)}, u32[]{:S(2)}, u32[]{:S(2)}) collective-permute-start(bf16[960,128]{1,0:T(8,128)(2,1)S(1)} %collective-permute-done.2.refs_2_), channel_id=1, source_target_pairs={{0,12},{4,0},{8,4},{12,8},{1,13},{5,1},{9,5},{13,9},{2,14},{6,2},{... | collective-permute-start | bytes 737288 | tf_op jit(solution)/shard_map/ppermute | solution.py:18
  17.5 0.0 collective-permute-done.3
  17.5 0.0 collective-permute-done.4
  17.5 0.9 %collective-permute-done.1.refs_0_ = bf16[960,128]{1,0:T(8,128)(2,1)S(1)} collective-permute-done((bf16[960,128]{1,0:T(8,128)(2,1)S(1)}, bf16[960,128]{1,0:T(8,128)(2,1)S(1)}, u32[]{:S(2)}, u32[]{:S(2)}) %collective-permute-start.1) | collective-permute-done | bytes 245792 | tf_op jit(solution)/shard_map/ppermute | solution.py:18
  18.4 0.1 collective-permute-start.5
  18.5 0.5 %collective-permute-start.6 = (bf16[480,128]{1,0:T(8,128)(2,1)S(1)}, bf16[480,128]{1,0:T(8,128)(2,1)S(1)}, u32[]{:S(2)}, u32[]{:S(2)}) collective-permute-start(bf16[480,128]{1,0:T(8,128)(2,1)S(1)} %get-tuple-element.64), channel_id=1, source_target_pairs={{0,1},{1,0},{2,3},{3,2},{4,5},{5,4},{6,7},{7,6},{8,9},{9,8},{10,11... | collective-permute-start | bytes 368648 | tf_op jit(solution)/shard_map/ppermute | solution.py:18
  19.0 0.8 %collective-permute-done.5 = bf16[480,128]{1,0:T(8,128)(2,1)S(1)} collective-permute-done((bf16[480,128]{1,0:T(8,128)(2,1)S(1)}, bf16[480,128]{1,0:T(8,128)(2,1)S(1)}, u32[]{:S(2)}, u32[]{:S(2)}) %collective-permute-start.5) | collective-permute-done | bytes 122912 | tf_op jit(solution)/shard_map/ppermute | solution.py:18
  19.8 0.2 collective-permute-done.6
  20.0 3.4 %shard_map.94 = (bf16[480,384]{1,0:T(8,128)(2,1)S(1)}, bf16[480,384]{1,0:T(8,128)(2,1)S(1)}, f32[480,128]{1,0:T(8,128)S(1)}, f32[480,128]{1,0:T(8,128)S(1)}, f32[480,384]{1,0:T(8,128)S(1)}) custom-call(bf16[1,384]{1,0:T(2,128)(2,1)S(1)} %reshape.15.gain, bf16[320,384]{1,0:T(8,128)(2,1)S(1)} %get-tuple-element.34.raw_own, ...), custom_call_target="tpu_custom_call" | custom-call | flops 1000 | bytes 1000 | tf_op jit(solution)/shard_map/pallas_call | solution.py:27
  23.4 0.2 collective-permute-done.7.mine
  23.6 0.3 collective-permute-start.8
  23.8 0.3 collective-permute-start.9
  24.2 0.8 %collective-permute-done.8 = bf16[480,128]{1,0:T(8,128)(2,1)S(1)} collective-permute-done((bf16[480,128]{1,0:T(8,128)(2,1)S(1)}, bf16[480,128]{1,0:T(8,128)(2,1)S(1)}, u32[]{:S(2)}, u32[]{:S(2)}) %collective-permute-start.8) | collective-permute-done | bytes 122912 | tf_op jit(solution)/shard_map/ppermute | solution.py:18
  25.0 0.2 collective-permute-done.9
  25.2 0.0 copy-done.2
  25.2 0.0 copy-done.3
  25.2 3.0 %shard_map.95 = (bf16[480,384]{1,0:T(8,128)(2,1)S(1)}, bf16[320,192]{1,0:T(8,128)(2,1)S(1)}, bf16[320,192]{1,0:T(8,128)(2,1)S(1)}) custom-call(bf16[1,384]{1,0:T(2,128)(2,1)S(1)} %reshape.15.gain, bf16[1,384]{1,0:T(2,128)(2,1)S(1)} %reshape.16.gain_two, bf16[384,384]{1,0:T(8,128)(2,1)S(1)} %copy-done.2, bf16[384,384]{1,0:T(8,128)(2,1)S(1)} %copy-done.3, ...), custom_call_target="tpu_custom_call" | custom-call | flops 1000 | bytes 1000 | tf_op jit(solution)/shard_map/pallas_call | solution.py:27
  28.2 0.4 collective-permute-start.10
  28.6 1.4 %collective-permute-done.10.other = bf16[480,384]{1,0:T(8,128)(2,1)S(1)} collective-permute-done((bf16[480,384]{1,0:T(8,128)(2,1)S(1)}, bf16[480,384]{1,0:T(8,128)(2,1)S(1)}, u32[]{:S(2)}, u32[]{:S(2)}) %collective-permute-start.10) | collective-permute-done | bytes 368672 | tf_op jit(solution)/shard_map/ppermute | solution.py:18
  29.9 1.6 %shard_map.96 = bf16[960,128]{1,0:T(8,128)(2,1)S(1)} custom-call(bf16[480,384]{1,0:T(8,128)(2,1)S(1)} %get-tuple-element.52.act, bf16[480,384]{1,0:T(8,128)(2,1)S(1)} %collective-permute-done.10.other, bf16[3,3,3,192,384]{4,3,2,1,0:T(8,128)(2,1)S(1)} %bitcast.5), custom_call_target="tpu_custom_call" | custom-call | flops 1000 | bytes 1000 | tf_op jit(solution)/shard_map/pallas_call | solution.py:27
  31.5 1.6 %collective-permute-start.14 = (bf16[960,128]{1,0:T(8,128)(2,1)S(1)}, bf16[960,128]{1,0:T(8,128)(2,1)S(1)}, u32[]{:S(2)}, u32[]{:S(2)}) collective-permute-start(bf16[960,128]{1,0:T(8,128)(2,1)S(1)} %shard_map.96), channel_id=1, source_target_pairs={{0,2},{2,0},{1,3},{3,1},{4,6},{6,4},{5,7},{7,5},{8,10},{10,8},{9,1... | collective-permute-start | bytes 737288 | tf_op jit(solution)/shard_map/ppermute | solution.py:18
  33.1 0.0 collective-permute-start.11
  33.1 1.4 %collective-permute-start.12 = (bf16[240,128]{1,0:T(8,128)(2,1)S(1)}, bf16[240,128]{1,0:T(8,128)(2,1)S(1)}, u32[]{:S(2)}, u32[]{:S(2)}) collective-permute-start(bf16[240,128]{1,0:T(8,128)(2,1)S(1)} %get-tuple-element.58), channel_id=1, source_target_pairs={{0,4},{4,8},{8,12},{12,0},{1,5},{5,9},{9,13},{13,1},{2,6},{6,10},{... | collective-permute-start | bytes 184328 | tf_op jit(solution)/shard_map/ppermute | solution.py:18
  34.5 2.4 %collective-permute-start.13 = (bf16[240,128]{1,0:T(8,128)(2,1)S(1)}, bf16[240,128]{1,0:T(8,128)(2,1)S(1)}, u32[]{:S(2)}, u32[]{:S(2)}) collective-permute-start(bf16[240,128]{1,0:T(8,128)(2,1)S(1)} %get-tuple-element.59), channel_id=1, source_target_pairs={{0,12},{4,0},{8,4},{12,8},{1,13},{5,1},{9,5},{13,9},{2,14},{6,2},{... | collective-permute-start | bytes 184328 | tf_op jit(solution)/shard_map/ppermute | solution.py:18
  36.9 1.5 %shard_map.97.rest = f32[640,192]{1,0:T(8,128)S(1)} custom-call(bf16[480,384]{1,0:T(8,128)(2,1)S(1)} %get-tuple-element.52.act, bf16[480,384]{1,0:T(8,128)(2,1)S(1)} %collective-permute-done.10.other, f32[3,640,192]{2,1,0:T(8,128)S(1)} %get-tuple-element.53.cached, bf16[3,3,3,192,384]{4,3,2,1,0:T(8,128)(2,1)S(1)} %bitcast.6), custom_call_target="tpu_custom_call" | custom-call | flops 1000 | bytes 1000 | tf_op jit(solution)/shard_map/pallas_call | solution.py:27
  38.4 0.0 collective-permute-done.11.theirs
  38.5 1.1 %collective-permute-done.12.above = bf16[240,128]{1,0:T(8,128)(2,1)S(1)} collective-permute-done((bf16[240,128]{1,0:T(8,128)(2,1)S(1)}, bf16[240,128]{1,0:T(8,128)(2,1)S(1)}, u32[]{:S(2)}, u32[]{:S(2)}) %collective-permute-start.12) | collective-permute-done | bytes 61472 | tf_op jit(solution)/shard_map/ppermute | solution.py:18
  39.5 0.5 %collective-permute-done.13.below = bf16[240,128]{1,0:T(8,128)(2,1)S(1)} collective-permute-done((bf16[240,128]{1,0:T(8,128)(2,1)S(1)}, bf16[240,128]{1,0:T(8,128)(2,1)S(1)}, u32[]{:S(2)}, u32[]{:S(2)}) %collective-permute-start.13) | collective-permute-done | bytes 61472 | tf_op jit(solution)/shard_map/ppermute | solution.py:18
  40.0 0.0 collective-permute-done.14.refs_0_
  40.0 0.9 %shard_map.98 = bf16[640,192]{1,0:T(8,128)(2,1)} custom-call(f32[640,192]{1,0:T(8,128)S(1)} %shard_map.97.rest, bf16[320,192]{1,0:T(8,128)(2,1)S(1)} %get-tuple-element.54.mine, bf16[320,192]{1,0:T(8,128)(2,1)S(1)} %collective-permute-done.11.theirs, bf16[240,128]{1,0:T(8,128)(2,1)S(1)} %collective-permute-done.12.above, ...), custom_call_target="tpu_custom_call" | custom-call | flops 1000 | bytes 1000 | tf_op jit(solution)/shard_map/pallas_call | solution.py:27
  (16 shorter events, 0.1 us)
Async XLA Ops:
  0.0 1.0 %copy-start.4 = (bf16[1,4,160,192]{3,2,1,0:T(8,128)(2,1)S(1)}, bf16[1,4,160,192]{3,2,1,0:T(8,128)(2,1)}, u32[]{:S(2)}) copy-start(bf16[1,4,160,192]{3,2,1,0:T(8,128)(2,1)} %param.9) | copy-start | bytes 737284
  1.0 5.3 %copy-start.7 = (bf16[384]{0:T(512)(128)(2,1)S(1)}, bf16[384]{0:T(512)(128)(2,1)}, u32[]{:S(2)}) copy-start(bf16[384]{0:T(512)(128)(2,1)} %param.11) | copy-start | bytes 2308
  1.0 5.3 %copy-start.5 = (bf16[384,384]{1,0:T(8,128)(2,1)S(1)}, bf16[384,384]{1,0:T(8,128)(2,1)}, u32[]{:S(2)}) copy-start(bf16[384,384]{1,0:T(8,128)(2,1)} %w_query.1) | copy-start | bytes 884740
  1.0 5.3 %copy-start.6 = (bf16[384,384]{1,0:T(8,128)(2,1)S(1)}, bf16[384,384]{1,0:T(8,128)(2,1)}, u32[]{:S(2)}) copy-start(bf16[384,384]{1,0:T(8,128)(2,1)} %w_key.1) | copy-start | bytes 884740
  1.1 5.2 %collective-permute-start = (bf16[960,128]{1,0:T(8,128)(2,1)S(1)}, bf16[960,128]{1,0:T(8,128)(2,1)S(1)}, u32[]{:S(2)}, u32[]{:S(2)}) collective-permute-start(bf16[960,128]{1,0:T(8,128)(2,1)S(1)} %shard_map.91.mine), channel_id=1, source_target_pairs={{0,1},{1,0},{2,3},{3,2},{4,5},{5,4},{6,7},{7,6},{8,9},{9,8},{10,11... | collective-permute-start | bytes 737288 | tf_op jit(solution)/shard_map/ppermute | solution.py:18
  1.6 11.0 %collective-permute-start.2 = (bf16[960,128]{1,0:T(8,128)(2,1)S(1)}, bf16[960,128]{1,0:T(8,128)(2,1)S(1)}, u32[]{:S(2)}, u32[]{:S(2)}) collective-permute-start(bf16[960,128]{1,0:T(8,128)(2,1)S(1)} %shard_map.91.mine), channel_id=1, source_target_pairs={{0,12},{4,0},{8,4},{12,8},{1,13},{5,1},{9,5},{13,9},{2,14},{6,2},{... | collective-permute-start | bytes 737288 | tf_op jit(solution)/shard_map/ppermute | solution.py:18
  6.3 12.2 %collective-permute-start.1 = (bf16[960,128]{1,0:T(8,128)(2,1)S(1)}, bf16[960,128]{1,0:T(8,128)(2,1)S(1)}, u32[]{:S(2)}, u32[]{:S(2)}) collective-permute-start(bf16[960,128]{1,0:T(8,128)(2,1)S(1)} %shard_map.91.mine), channel_id=1, source_target_pairs={{0,4},{4,8},{8,12},{12,0},{1,5},{5,9},{9,13},{13,1},{2,6},{6,10},{... | collective-permute-start | bytes 737288 | tf_op jit(solution)/shard_map/ppermute | solution.py:18
  6.3 2.1 %copy-start = (bf16[3,3,3,384,192]{3,4,2,1,0:T(8,128)(2,1)S(1)}, bf16[3,3,3,384,192]{3,4,2,1,0:T(8,128)(2,1)}, u32[]{:S(2)}) copy-start(bf16[3,3,3,384,192]{3,4,2,1,0:T(8,128)(2,1)} %param.17) | copy-start | bytes 11943940
  6.3 2.4 %copy-start.1 = (bf16[2,4,160,384]{3,2,1,0:T(8,128)(2,1)S(1)}, bf16[2,4,160,384]{3,2,1,0:T(8,128)(2,1)}, u32[]{:S(2)}) copy-start(bf16[2,4,160,384]{3,2,1,0:T(8,128)(2,1)} %param.10) | copy-start | bytes 2949124
  8.7 15.5 %copy-start.8 = (bf16[384]{0:T(512)(128)(2,1)S(1)}, bf16[384]{0:T(512)(128)(2,1)}, u32[]{:S(2)}) copy-start(bf16[384]{0:T(512)(128)(2,1)} %param.12) | copy-start | bytes 2308
  11.9 13.2 %copy-start.2 = (bf16[384,384]{1,0:T(8,128)(2,1)S(1)}, bf16[384,384]{1,0:T(8,128)(2,1)}, u32[]{:S(2)}) copy-start(bf16[384,384]{1,0:T(8,128)(2,1)} %w_value.1) | copy-start | bytes 884740
  12.0 13.2 %copy-start.3 = (bf16[384,384]{1,0:T(8,128)(2,1)S(1)}, bf16[384,384]{1,0:T(8,128)(2,1)}, u32[]{:S(2)}) copy-start(bf16[384,384]{1,0:T(8,128)(2,1)} %w_out.1) | copy-start | bytes 884740
  12.6 4.9 %collective-permute-start.3 = (bf16[480,128]{1,0:T(8,128)(2,1)S(1)}, bf16[480,128]{1,0:T(8,128)(2,1)S(1)}, u32[]{:S(2)}, u32[]{:S(2)}) collective-permute-start(bf16[480,128]{1,0:T(8,128)(2,1)S(1)} %get-tuple-element.65), channel_id=1, source_target_pairs={{0,1},{1,0},{2,3},{3,2},{4,5},{5,4},{6,7},{7,6},{8,9},{9,8},{10,11... | collective-permute-start | bytes 368648 | tf_op jit(solution)/shard_map/ppermute | solution.py:18
  12.7 4.8 %collective-permute-start.4 = (bf16[480,128]{1,0:T(8,128)(2,1)S(1)}, bf16[480,128]{1,0:T(8,128)(2,1)S(1)}, u32[]{:S(2)}, u32[]{:S(2)}) collective-permute-start(bf16[480,128]{1,0:T(8,128)(2,1)S(1)} %get-tuple-element.66), channel_id=1, source_target_pairs={{0,1},{1,0},{2,3},{3,2},{4,5},{5,4},{6,7},{7,6},{8,9},{9,8},{10,11... | collective-permute-start | bytes 368648 | tf_op jit(solution)/shard_map/ppermute | solution.py:18
  13.2 10.4 %collective-permute-start.7 = (bf16[960,128]{1,0:T(8,128)(2,1)S(1)}, bf16[960,128]{1,0:T(8,128)(2,1)S(1)}, u32[]{:S(2)}, u32[]{:S(2)}) collective-permute-start(bf16[960,128]{1,0:T(8,128)(2,1)S(1)} %collective-permute-done.2.refs_2_), channel_id=1, source_target_pairs={{0,12},{4,0},{8,4},{12,8},{1,13},{5,1},{9,5},{13,9},{2,14},{6,2},{... | collective-permute-start | bytes 737288 | tf_op jit(solution)/shard_map/ppermute | solution.py:18
  18.4 1.4 %collective-permute-start.5 = (bf16[480,128]{1,0:T(8,128)(2,1)S(1)}, bf16[480,128]{1,0:T(8,128)(2,1)S(1)}, u32[]{:S(2)}, u32[]{:S(2)}) collective-permute-start(bf16[480,128]{1,0:T(8,128)(2,1)S(1)} %get-tuple-element.63), channel_id=1, source_target_pairs={{0,1},{1,0},{2,3},{3,2},{4,5},{5,4},{6,7},{7,6},{8,9},{9,8},{10,11... | collective-permute-start | bytes 368648 | tf_op jit(solution)/shard_map/ppermute | solution.py:18
  18.5 1.5 %collective-permute-start.6 = (bf16[480,128]{1,0:T(8,128)(2,1)S(1)}, bf16[480,128]{1,0:T(8,128)(2,1)S(1)}, u32[]{:S(2)}, u32[]{:S(2)}) collective-permute-start(bf16[480,128]{1,0:T(8,128)(2,1)S(1)} %get-tuple-element.64), channel_id=1, source_target_pairs={{0,1},{1,0},{2,3},{3,2},{4,5},{5,4},{6,7},{7,6},{8,9},{9,8},{10,11... | collective-permute-start | bytes 368648 | tf_op jit(solution)/shard_map/ppermute | solution.py:18
  23.6 1.4 %collective-permute-start.8 = (bf16[480,128]{1,0:T(8,128)(2,1)S(1)}, bf16[480,128]{1,0:T(8,128)(2,1)S(1)}, u32[]{:S(2)}, u32[]{:S(2)}) collective-permute-start(bf16[480,128]{1,0:T(8,128)(2,1)S(1)} %get-tuple-element.61), channel_id=1, source_target_pairs={{0,1},{1,0},{2,3},{3,2},{4,5},{5,4},{6,7},{7,6},{8,9},{9,8},{10,11... | collective-permute-start | bytes 368648 | tf_op jit(solution)/shard_map/ppermute | solution.py:18
  23.8 1.3 %collective-permute-start.9 = (bf16[480,128]{1,0:T(8,128)(2,1)S(1)}, bf16[480,128]{1,0:T(8,128)(2,1)S(1)}, u32[]{:S(2)}, u32[]{:S(2)}) collective-permute-start(bf16[480,128]{1,0:T(8,128)(2,1)S(1)} %get-tuple-element.62), channel_id=1, source_target_pairs={{0,1},{1,0},{2,3},{3,2},{4,5},{5,4},{6,7},{7,6},{8,9},{9,8},{10,11... | collective-permute-start | bytes 368648 | tf_op jit(solution)/shard_map/ppermute | solution.py:18
  28.2 1.8 %collective-permute-start.10 = (bf16[480,384]{1,0:T(8,128)(2,1)S(1)}, bf16[480,384]{1,0:T(8,128)(2,1)S(1)}, u32[]{:S(2)}, u32[]{:S(2)}) collective-permute-start(bf16[480,384]{1,0:T(8,128)(2,1)S(1)} %get-tuple-element.52.act), channel_id=1, source_target_pairs={{0,1},{1,0},{2,3},{3,2},{4,5},{5,4},{6,7},{7,6},{8,9},{9,8},{10,11... | collective-permute-start | bytes 1105928 | tf_op jit(solution)/shard_map/ppermute | solution.py:18
  31.5 8.5 %collective-permute-start.14 = (bf16[960,128]{1,0:T(8,128)(2,1)S(1)}, bf16[960,128]{1,0:T(8,128)(2,1)S(1)}, u32[]{:S(2)}, u32[]{:S(2)}) collective-permute-start(bf16[960,128]{1,0:T(8,128)(2,1)S(1)} %shard_map.96), channel_id=1, source_target_pairs={{0,2},{2,0},{1,3},{3,1},{4,6},{6,4},{5,7},{7,5},{8,10},{10,8},{9,1... | collective-permute-start | bytes 737288 | tf_op jit(solution)/shard_map/ppermute | solution.py:18
  33.1 5.4 %collective-permute-start.11 = (bf16[320,192]{1,0:T(8,128)(2,1)S(1)}, bf16[320,192]{1,0:T(8,128)(2,1)S(1)}, u32[]{:S(2)}, u32[]{:S(2)}) collective-permute-start(bf16[320,192]{1,0:T(8,128)(2,1)S(1)} %get-tuple-element.55), channel_id=1, source_target_pairs={{0,1},{1,0},{2,3},{3,2},{4,5},{5,4},{6,7},{7,6},{8,9},{9,8},{10,11... | collective-permute-start | bytes 368648 | tf_op jit(solution)/shard_map/ppermute | solution.py:18
  33.1 6.4 %collective-permute-start.12 = (bf16[240,128]{1,0:T(8,128)(2,1)S(1)}, bf16[240,128]{1,0:T(8,128)(2,1)S(1)}, u32[]{:S(2)}, u32[]{:S(2)}) collective-permute-start(bf16[240,128]{1,0:T(8,128)(2,1)S(1)} %get-tuple-element.58), channel_id=1, source_target_pairs={{0,4},{4,8},{8,12},{12,0},{1,5},{5,9},{9,13},{13,1},{2,6},{6,10},{... | collective-permute-start | bytes 184328 | tf_op jit(solution)/shard_map/ppermute | solution.py:18
  34.5 5.5 %collective-permute-start.13 = (bf16[240,128]{1,0:T(8,128)(2,1)S(1)}, bf16[240,128]{1,0:T(8,128)(2,1)S(1)}, u32[]{:S(2)}, u32[]{:S(2)}) collective-permute-start(bf16[240,128]{1,0:T(8,128)(2,1)S(1)} %get-tuple-element.59), channel_id=1, source_target_pairs={{0,12},{4,0},{8,4},{12,8},{1,13},{5,1},{9,5},{13,9},{2,14},{6,2},{... | collective-permute-start | bytes 184328 | tf_op jit(solution)/shard_map/ppermute | solution.py:18

commit v5 on v4

--- a/solution.py
+++ b/solution.py
@@ -22,13 +22,16 @@
     return jnp.concatenate([cycle(piece, "chan", 1) for piece in jnp.split(array, pieces)])
 
 
-def call(kernel, outs, args, scratch=(), flops=1000):
+def call(kernel, outs, args, scratch=(), flops=1000, kept=False):
     vmem = pl.BlockSpec(memory_space=pltpu.VMEM)
+    anywhere = pl.BlockSpec(memory_space=pl.ANY)
+    into = kept and args[-1].shape == outs[0].shape and args[-1].dtype == outs[0].dtype
     return pl.pallas_call(
         kernel,
         out_shape=outs,
-        in_specs=[vmem] * len(args),
-        out_specs=[vmem] * len(outs),
+        in_specs=[vmem] * (len(args) - into) + [anywhere] * into,
+        out_specs=[anywhere if kept else vmem] * len(outs),
+        input_output_aliases={len(args) - 1: 0} if into else {},
         scratch_shapes=list(scratch),
         compiler_params=pltpu.CompilerParams(vmem_limit_bytes=36 * 2**20),
         cost_estimate=pl.CostEstimate(flops=flops, bytes_accessed=1000, transcendentals=0),
@@ -112,8 +115,8 @@
     return (dot_t(dot(rows, w_query).astype(BF), w_key) * scale).astype(BF)
 
 
-def own_rows_kernel(gain, mine, theirs, w_query, w_key, *refs):
-    raw_out, keys_out, query_out, w_query_out, w_key_out = refs
+def own_rows_kernel(gain, mine, theirs, w_query, w_key, w_value, w_out, *refs):
+    raw_out, keys_out, query_out, w_query_out, w_key_out, w_mixed_out = refs
     core = place_of()[0]
     raw = joined_halves(core, mine, theirs)
     half = raw.shape[0] // 2
@@ -124,6 +127,7 @@
     query_out[...] = queries(rows, w_query[...], w_key[...])
     w_query_out[...] = w_query[...]
     w_key_out[...] = w_key[...]
+    w_mixed_out[...] = dot(w_value[...], w_out[...]).astype(BF)
 
 
 def first_kernel(gain, raw_own, keys_own, query_own, w_query, w_key, *refs):
@@ -168,13 +172,12 @@
     accum_out[...] = new[2]
 
 
-def last_kernel(gain, gain_two, w_value, w_out, query, raw, top, total, accum, mine, theirs, act_out, keep_out, give_out):
+def last_kernel(gain, gain_two, w_mixed, query, raw, top, total, accum, mine, theirs, act_out, keep_out, give_out):
     core, place, places, _ = place_of()
     keys = [rms_scaled(joined_halves(core, mine, theirs), gain[...]).astype(BF)]
     _, total, accum = attend(query[...], keys, top[:, :1], total[:, :1], accum[...])
     mixed = (accum / total).astype(BF)
-    attended = dot(mixed, w_value[...]).astype(BF)
-    joined = (raw[...].astype(F32) + dot(attended, w_out[...])).astype(BF)
+    joined = (raw[...].astype(F32) + dot(mixed, w_mixed[...])).astype(BF)
     edge = joined.shape[0] // 3
     own = jnp.where(core == 0, joined[edge:], joined[: 2 * edge]).astype(F32)
     half = own.shape[1] // 2
@@ -208,14 +211,21 @@
     return middle + left + right
 
 
-def whole_tile(core, mine, theirs):
-    a, b = mine[...], theirs[...]
+def by_core(mine, theirs):
+    core, a, b = place_of()[0], mine[...], theirs[...]
     return jnp.concatenate([jnp.where(core == 0, a, b), jnp.where(core == 0, b, a)], axis=0)
 
 
 def send_kernel(cells, back, act, other, weights, out):
-    conv = gathered(taps(whole_tile(place_of()[0], act, other), weights.at[back], cells), cells)
-    pack(conv, out)
+    wanted = place_of()[3] + back < lax.axis_size("tm")
+
+    @pl.when(wanted)
+    def _():
+        pack(gathered(taps(by_core(act, other), weights.at[2 - back], cells), cells), out)
+
+    @pl.when(jnp.logical_not(wanted))
+    def _():
+        out[...] = jnp.zeros_like(out)
 
 
 def cache_kernel(cells, cache, weights, sums, up, down):
@@ -256,28 +266,43 @@
             out[...] = jnp.zeros_like(out)
 
 
-def rest_kernel(cells, act, other, cached, weights, out):
-    parts = taps(whole_tile(place_of()[0], act, other), weights.at[2], cells)
-    out[...] = gathered([part + cached[i] for i, part in enumerate(parts)], cells)
-
-
-def final_kernel(cells, rest, mine, theirs, above, below, *refs):
-    core, place, places, moment = place_of()
-    received, out = refs[:-1], refs[-1]
+def rest_kernel(cells, act, other, cached, keep, theirs, weights, out):
+    parts = taps(by_core(act, other), weights.at[2], cells)
+    terms = gathered([part + cached[i] for i, part in enumerate(parts)], cells)
+    out[...] = by_core(keep, theirs).astype(F32) + terms
+
+
+def edge_kernel(cells, rest, above, below, out):
+    _, place, places, _ = place_of()
     tokens = rest.shape[0]
-    total = rest[...] + jnp.where(
-        core == 0,
-        jnp.concatenate([mine[...], theirs[...]], axis=0),
-        jnp.concatenate([theirs[...], mine[...]], axis=0),
-    ).astype(F32)
-    first = jnp.where(place == 0, 0.0, unpacked(above[...]))
-    last = jnp.where(place == places - 1, 0.0, unpacked(below[...]))
-    total = jnp.concatenate(
-        [total[:cells] + first, total[cells : tokens - cells], total[tokens - cells :] + last], axis=0
-    )
-    for back, ref in enumerate(received):
-        total = total + jnp.where(moment > back, unpacked(ref[...]), 0.0)
-    out[...] = total.astype(BF)
+    out[:cells] = rest[:cells] + jnp.where(place == 0, 0.0, unpacked(above[...]))
+    out[cells : tokens - cells] = rest[cells : tokens - cells]
+    out[tokens - cells :] = rest[tokens - cells :] + jnp.where(place == places - 1, 0.0, unpacked(below[...]))
+
+
+def write(total, out, held, sem):
+    held[...] = total.astype(BF)
+    copy = pltpu.make_async_copy(held, out, sem)
+    copy.start()
+    copy.wait()
+
+
+def early_kernel(rest, out, held, sem):
+    @pl.when(place_of()[3] == 0)
+    def _():
+        write(rest[...], out, held, sem)
+
+
+def final_kernel(rest, *refs):
+    moment = place_of()[3]
+    received, (_, out, held, sem) = refs[:-4], refs[-4:]
+
+    @pl.when(moment > 0)
+    def _():
+        total = rest[...]
+        for back, ref in enumerate(received):
+            total = total + jnp.where(moment > back, unpacked(ref[...]), 0.0)
+        write(total, out, held, sem)
 
 
 def body(frames_in, cache, gain_one, gain_two, w_query, w_key, w_value, w_out, conv_weight):
@@ -299,7 +324,7 @@
     behind, ahead = cycle(packed, "space", 1), cycle(packed, "space", -1)
     cache = cache.reshape(2, tokens, width)
     own_other = cycle(packed, "chan", 1)
-    raw_own, keys_own, query_own, w_query, w_key = call(
+    raw_own, keys_own, query_own, w_query, w_key, w_mixed = call(
         own_rows_kernel,
         [
             shaped((tokens // 2, width), BF),
@@ -307,8 +332,9 @@
             shaped((tokens // 2, width), BF),
             shaped((width, width), BF),
             shaped((width, width), BF),
+            shaped((width, width), BF),
         ],
-        [gain, packed, own_other, w_query, w_key],
+        [gain, packed, own_other, w_query, w_key, w_value, w_out],
         flops=4 * 10**9,
     )
     raw_own, cache = lax.optimization_barrier((raw_own, cache))
@@ -352,11 +378,11 @@
             [gain, query, top, total, accum] + tiles,
                 )
     tile, accum = lax.optimization_barrier((groups[-1][0], accum))
-    tile_other = between_cores(tile)
+    tile_other = cycle(tile, "chan", 1)
     act, keep, give = call(
         last_kernel,
         [shaped((count, width), BF)] + [shaped((tokens // 2, half), BF)] * 2,
-        [gain, gain_act, w_value, w_out, query, raw, top, total, accum, tile, tile_other],
+        [gain, gain_act, w_mixed, query, raw, top, total, accum, tile, tile_other],
     )
     other = cycle(act, "chan", 1)
     theirs = cycle(give, "chan", 1)
@@ -364,7 +390,7 @@
     received = []
     for back in range(1, min(moments, 3)):
         (term,) = call(
-            functools.partial(send_kernel, cells, 2 - back),
+            functools.partial(send_kernel, cells, back),
             [shaped((tokens * 3 // 2, LANES), BF)],
             [act, other, weights],
             )
@@ -374,15 +400,16 @@
     (rest,) = call(
         functools.partial(rest_kernel, cells),
         [shaped((tokens, half), F32)],
-        [act, other, cached, weights],
+        [act, other, cached, keep, theirs, weights],
     )
     up_term, down_term, act = lax.optimization_barrier((up_term, down_term, act))
     above, below = cycle(up_term, "space", 1), cycle(down_term, "space", -1)
-    (out,) = call(
-        functools.partial(final_kernel, cells),
-        [shaped((tokens, half), BF)],
-        [rest, keep, theirs, above, below] + received,
-    )
+    (rest,) = call(
+        functools.partial(edge_kernel, cells), [shaped((tokens, half), F32)], [rest, above, below]
+    )
+    written = [pltpu.VMEM((tokens, half), BF), pltpu.SemaphoreType.DMA]
+    (out,) = call(early_kernel, [shaped((tokens, half), BF)], [rest], written, kept=True)
+    (out,) = call(final_kernel, [shaped((tokens, half), BF)], [rest] + received + [out], written, kept=True)
     return out.reshape(1, rows, cells, half)
 
 

time: 41.1 us -> 39.3 us (0.956)
  starting transfers between devices: 17 us -> 15.4 us
    ppermute x15 -> x14, starting transfers between devices: 17 us -> 15.4 us  [cycle(): lax.ppermute(array, axis, [(i, (i + by) % count) for i in range(count)])]
    ppermute x15 -> x14, waiting for transfers between devices: 6.66 us -> 6.9 us  [cycle(): lax.ppermute(array, axis, [(i, (i + by) % count) for i in range(count)])]
    pallas_call x8 -> x10, Pallas kernels: 14.7 us -> 14.5 us  [call(): pl.pallas_call(kernel, out_shape=outs, in_specs=[vmem] * (len(args) - int...]
  transfers between devices with their start and end apart: 15 -> 14, of which waited for: 10 -> 10; matrix products, arithmetic and copies ran while one was open for 0% -> 0% of each run, Pallas kernels for 22% -> 26%
where the time goes in v5:
time: 39.3 us; the launch traced here: 39.2 us
  starting transfers between devices  15.4 us (39%)
  Pallas kernels  14.5 us (37%)
  waiting for transfers between devices  6.9 us (18%)
  local copies, waits for them, and re-layouts  2.16 us (5%)
    ppermute x14, starting transfers between devices, cycle(): lax.ppermute(array, axis, [(i, (i + by) % count) for i in range(count)])  15.4 us
    pallas_call x10, Pallas kernels, call(): pl.pallas_call(kernel, out_shape=outs, in_specs=[vmem] * (len(args) - int...  14.5 us
    ppermute x14, waiting for transfers between devices, cycle(): lax.ppermute(array, axis, [(i, (i + by) % count) for i in range(count)])  6.9 us
    unnamed x18, local copies, waits for them, and re-layouts  2.12 us
  transfers between devices with their start and end apart: 14, of which 10 were waited for; matrix products, arithmetic and copies ran while one was open for 0% of the time, Pallas kernels for 26%

profile of v5, /device:TPU:0, one launch (start us, length us, event | category | flops | bytes accessed | tf_op | source)
XLA Modules:
  0.0 39.2 jit_solution(15002890337049699459)
XLA Ops:
  0.0 1.0 %copy-done.2 = bf16[1,4,160,192]{3,2,1,0:T(8,128)(2,1)S(1)} copy-done((bf16[1,4,160,192]{3,2,1,0:T(8,128)(2,1)S(1)}, bf16[1,4,160,192]{3,2,1,0:T(8,128)(2,1)}, u32[]{:S(2)}) %copy-start.2) | copy-done | bytes 245784
  1.0 0.0 copy-start.6
  1.0 0.1 shard_map.91.mine
  1.1 0.5 %collective-permute-start = (bf16[960,128]{1,0:T(8,128)(2,1)S(1)}, bf16[960,128]{1,0:T(8,128)(2,1)S(1)}, u32[]{:S(2)}, u32[]{:S(2)}) collective-permute-start(bf16[960,128]{1,0:T(8,128)(2,1)S(1)} %shard_map.91.mine), channel_id=1, source_target_pairs={{0,1},{1,0},{2,3},{3,2},{4,5},{5,4},{6,7},{7,6},{8,9},{9,8},{10,11... | collective-permute-start | bytes 737288 | tf_op jit(solution)/shard_map/ppermute | solution.py:18
  1.6 4.7 %collective-permute-start.2 = (bf16[960,128]{1,0:T(8,128)(2,1)S(1)}, bf16[960,128]{1,0:T(8,128)(2,1)S(1)}, u32[]{:S(2)}, u32[]{:S(2)}) collective-permute-start(bf16[960,128]{1,0:T(8,128)(2,1)S(1)} %shard_map.91.mine), channel_id=1, source_target_pairs={{0,12},{4,0},{8,4},{12,8},{1,13},{5,1},{9,5},{13,9},{2,14},{6,2},{... | collective-permute-start | bytes 737288 | tf_op jit(solution)/shard_map/ppermute | solution.py:18
  6.3 0.0 collective-permute-start.1
  6.3 0.0 copy-done.7
  6.3 0.0 copy-start
  6.3 0.0 copy-start.1
  6.3 0.0 collective-permute-done.theirs
  6.3 0.0 copy-done.3
  6.3 0.0 copy-done.4
  6.3 0.0 copy-done.5
  6.4 0.0 copy-done.6
  6.4 1.2 %shard_map.92 = (bf16[320,384]{1,0:T(8,128)(2,1)S(1)}, bf16[640,384]{1,0:T(8,128)(2,1)S(1)}, bf16[320,384]{1,0:T(8,128)(2,1)S(1)}, bf16[384,384]{1,0:T(8,128)(2,...) custom-call(bf16[1,384]{1,0:T(2,128)(2,1)S(1)} %reshape.15.gain, ...), custom_call_target="tpu_custom_call" | custom-call | flops 4000000000 | bytes 1000 | tf_op jit(solution)/shard_map/pallas_call | solution.py:29
  7.6 0.8 %copy-done = bf16[3,3,3,384,192]{3,4,2,1,0:T(8,128)(2,1)S(1)} copy-done((bf16[3,3,3,384,192]{3,4,2,1,0:T(8,128)(2,1)S(1)}, bf16[3,3,3,384,192]{3,4,2,1,0:T(8,128)(2,1)}, u32[]{:S(2)}) %copy-start) | copy-done | bytes 3981336
  8.4 0.3 copy-done.1
  8.7 3.3 %shard_map.93 = (f32[3,640,192]{2,1,0:T(8,128)S(1)}, bf16[240,128]{1,0:T(8,128)(2,1)S(1)}, bf16[240,128]{1,0:T(8,128)(2,1)S(1)}) custom-call(bf16[2,640,384]{2,1,0:T(8,128)(2,1)S(1)} %bitcast.7, bf16[3,3,3,192,384]{4,3,2,1,0:T(8,128)(2,1)S(1)} %bitcast.4), custom_call_target="tpu_custom_call" | custom-call | flops 1000 | bytes 1000 | tf_op jit(solution)/shard_map/pallas_call | solution.py:29
  12.0 0.6 %collective-permute-done.2.refs_2_ = bf16[960,128]{1,0:T(8,128)(2,1)S(1)} collective-permute-done((bf16[960,128]{1,0:T(8,128)(2,1)S(1)}, bf16[960,128]{1,0:T(8,128)(2,1)S(1)}, u32[]{:S(2)}, u32[]{:S(2)}) %collective-permute-start.2) | collective-permute-done | bytes 245792 | tf_op jit(solution)/shard_map/ppermute | solution.py:18
  12.6 0.1 collective-permute-start.3
  12.7 0.5 %collective-permute-start.4 = (bf16[480,128]{1,0:T(8,128)(2,1)S(1)}, bf16[480,128]{1,0:T(8,128)(2,1)S(1)}, u32[]{:S(2)}, u32[]{:S(2)}) collective-permute-start(bf16[480,128]{1,0:T(8,128)(2,1)S(1)} %get-tuple-element.66), channel_id=1, source_target_pairs={{0,1},{1,0},{2,3},{3,2},{4,5},{5,4},{6,7},{7,6},{8,9},{9,8},{10,11... | collective-permute-start | bytes 368648 | tf_op jit(solution)/shard_map/ppermute | solution.py:18
  13.2 4.3 %collective-permute-start.7 = (bf16[960,128]{1,0:T(8,128)(2,1)S(1)}, bf16[960,128]{1,0:T(8,128)(2,1)S(1)}, u32[]{:S(2)}, u32[]{:S(2)}) collective-permute-start(bf16[960,128]{1,0:T(8,128)(2,1)S(1)} %collective-permute-done.2.refs_2_), channel_id=1, source_target_pairs={{0,12},{4,0},{8,4},{12,8},{1,13},{5,1},{9,5},{13,9},{2,14},{6,2},{... | collective-permute-start | bytes 737288 | tf_op jit(solution)/shard_map/ppermute | solution.py:18
  17.5 0.0 collective-permute-done.3
  17.5 0.0 collective-permute-done.4
  17.5 0.9 %collective-permute-done.1.refs_0_ = bf16[960,128]{1,0:T(8,128)(2,1)S(1)} collective-permute-done((bf16[960,128]{1,0:T(8,128)(2,1)S(1)}, bf16[960,128]{1,0:T(8,128)(2,1)S(1)}, u32[]{:S(2)}, u32[]{:S(2)}) %collective-permute-start.1) | collective-permute-done | bytes 245792 | tf_op jit(solution)/shard_map/ppermute | solution.py:18
  18.5 0.1 collective-permute-start.5
  18.5 0.5 %collective-permute-start.6 = (bf16[480,128]{1,0:T(8,128)(2,1)S(1)}, bf16[480,128]{1,0:T(8,128)(2,1)S(1)}, u32[]{:S(2)}, u32[]{:S(2)}) collective-permute-start(bf16[480,128]{1,0:T(8,128)(2,1)S(1)} %get-tuple-element.64), channel_id=1, source_target_pairs={{0,1},{1,0},{2,3},{3,2},{4,5},{5,4},{6,7},{7,6},{8,9},{9,8},{10,11... | collective-permute-start | bytes 368648 | tf_op jit(solution)/shard_map/ppermute | solution.py:18
  19.0 0.8 %collective-permute-done.5 = bf16[480,128]{1,0:T(8,128)(2,1)S(1)} collective-permute-done((bf16[480,128]{1,0:T(8,128)(2,1)S(1)}, bf16[480,128]{1,0:T(8,128)(2,1)S(1)}, u32[]{:S(2)}, u32[]{:S(2)}) %collective-permute-start.5) | collective-permute-done | bytes 122912 | tf_op jit(solution)/shard_map/ppermute | solution.py:18
  19.9 0.2 collective-permute-done.6
  20.1 3.4 %shard_map.94 = (bf16[480,384]{1,0:T(8,128)(2,1)S(1)}, bf16[480,384]{1,0:T(8,128)(2,1)S(1)}, f32[480,128]{1,0:T(8,128)S(1)}, f32[480,128]{1,0:T(8,128)S(1)}, f32[480,384]{1,0:T(8,128)S(1)}) custom-call(bf16[1,384]{1,0:T(2,128)(2,1)S(1)} %reshape.15.gain, bf16[320,384]{1,0:T(8,128)(2,1)S(1)} %get-tuple-element.36.raw_own, ...), custom_call_target="tpu_custom_call" | custom-call | flops 1000 | bytes 1000 | tf_op jit(solution)/shard_map/pallas_call | solution.py:29
  23.4 0.2 collective-permute-done.7.mine
  23.6 0.3 collective-permute-start.8
  23.8 1.2 %collective-permute-done.8.theirs = bf16[960,128]{1,0:T(8,128)(2,1)S(1)} collective-permute-done((bf16[960,128]{1,0:T(8,128)(2,1)S(1)}, bf16[960,128]{1,0:T(8,128)(2,1)S(1)}, u32[]{:S(2)}, u32[]{:S(2)}) %collective-permute-start.8) | collective-permute-done | bytes 245792 | tf_op jit(solution)/shard_map/ppermute | solution.py:18
  25.1 2.6 %shard_map.95 = (bf16[480,384]{1,0:T(8,128)(2,1)S(1)}, bf16[320,192]{1,0:T(8,128)(2,1)S(1)}, bf16[320,192]{1,0:T(8,128)(2,1)S(1)}) custom-call(bf16[1,384]{1,0:T(2,128)(2,1)S(1)} %reshape.15.gain, bf16[1,384]{1,0:T(2,128)(2,1)S(1)} %reshape.16.gain_two, bf16[384,384]{1,0:T(8,128)(2,1)S(1)} %get-tuple-element.34.w_mixed, ...), custom_call_target="tpu_custom_call" | custom-call | flops 1000 | bytes 1000 | tf_op jit(solution)/shard_map/pallas_call | solution.py:29
  27.7 0.3 collective-permute-start.9
  28.0 1.4 %collective-permute-done.9.other = bf16[480,384]{1,0:T(8,128)(2,1)S(1)} collective-permute-done((bf16[480,384]{1,0:T(8,128)(2,1)S(1)}, bf16[480,384]{1,0:T(8,128)(2,1)S(1)}, u32[]{:S(2)}, u32[]{:S(2)}) %collective-permute-start.9) | collective-permute-done | bytes 368672 | tf_op jit(solution)/shard_map/ppermute | solution.py:18
  29.4 1.6 %shard_map.96 = bf16[960,128]{1,0:T(8,128)(2,1)S(1)} custom-call(bf16[480,384]{1,0:T(8,128)(2,1)S(1)} %get-tuple-element.54.act, bf16[480,384]{1,0:T(8,128)(2,1)S(1)} %collective-permute-done.9.other, bf16[3,3,3,192,384]{4,3,2,1,0:T(8,128)(2,1)S(1)} %bitcast.5), custom_call_target="tpu_custom_call" | custom-call | flops 1000 | bytes 1000 | tf_op jit(solution)/shard_map/pallas_call | solution.py:29
  31.0 0.1 collective-permute-start.13
  31.1 0.3 collective-permute-start.10
  31.4 1.5 %collective-permute-start.11 = (bf16[240,128]{1,0:T(8,128)(2,1)S(1)}, bf16[240,128]{1,0:T(8,128)(2,1)S(1)}, u32[]{:S(2)}, u32[]{:S(2)}) collective-permute-start(bf16[240,128]{1,0:T(8,128)(2,1)S(1)} %get-tuple-element.60), channel_id=1, source_target_pairs={{0,4},{4,8},{8,12},{12,0},{1,5},{5,9},{9,13},{13,1},{2,6},{6,10},{... | collective-permute-start | bytes 184328 | tf_op jit(solution)/shard_map/ppermute | solution.py:18
  32.8 2.4 %collective-permute-start.12 = (bf16[240,128]{1,0:T(8,128)(2,1)S(1)}, bf16[240,128]{1,0:T(8,128)(2,1)S(1)}, u32[]{:S(2)}, u32[]{:S(2)}) collective-permute-start(bf16[240,128]{1,0:T(8,128)(2,1)S(1)} %get-tuple-element.61), channel_id=1, source_target_pairs={{0,12},{4,0},{8,4},{12,8},{1,13},{5,1},{9,5},{13,9},{2,14},{6,2},{... | collective-permute-start | bytes 184328 | tf_op jit(solution)/shard_map/ppermute | solution.py:18
  35.2 0.0 collective-permute-done.10.theirs
  35.2 1.6 %shard_map.97.rest = f32[640,192]{1,0:T(8,128)S(1)} custom-call(bf16[480,384]{1,0:T(8,128)(2,1)S(1)} %get-tuple-element.54.act, bf16[480,384]{1,0:T(8,128)(2,1)S(1)} %collective-permute-done.9.other, f32[3,640,192]{2,1,0:T(8,128)S(1)} %get-tuple-element.55.cached, bf16[320,192]{1,0:T(8,128)(2,1)S(1)} %get-tuple-element.56.keep, ...), custom_call_target="tpu_custom_call" | custom-call | flops 1000 | bytes 1000 | tf_op jit(solution)/shard_map/pallas_call | solution.py:29
  36.8 0.8 %collective-permute-done.11.above = bf16[240,128]{1,0:T(8,128)(2,1)S(1)} collective-permute-done((bf16[240,128]{1,0:T(8,128)(2,1)S(1)}, bf16[240,128]{1,0:T(8,128)(2,1)S(1)}, u32[]{:S(2)}, u32[]{:S(2)}) %collective-permute-start.11) | collective-permute-done | bytes 61472 | tf_op jit(solution)/shard_map/ppermute | solution.py:18
  37.6 0.5 %collective-permute-done.12.below = bf16[240,128]{1,0:T(8,128)(2,1)S(1)} collective-permute-done((bf16[240,128]{1,0:T(8,128)(2,1)S(1)}, bf16[240,128]{1,0:T(8,128)(2,1)S(1)}, u32[]{:S(2)}, u32[]{:S(2)}) %collective-permute-start.12) | collective-permute-done | bytes 61472 | tf_op jit(solution)/shard_map/ppermute | solution.py:18
  38.1 0.1 shard_map.98.rest
  38.2 0.8 %shard_map.99.refs_1_ = bf16[640,192]{1,0:T(8,128)(2,1)} custom-call(f32[640,192]{1,0:T(8,128)S(1)} %shard_map.98.rest), custom_call_target="tpu_custom_call" | custom-call | flops 1000 | bytes 1000 | tf_op jit(solution)/shard_map/pallas_call | solution.py:29
  39.0 0.2 collective-permute-done.13.refs_0_
  (14 shorter events, 0.1 us)
Async XLA Ops:
  0.0 1.0 %copy-start.2 = (bf16[1,4,160,192]{3,2,1,0:T(8,128)(2,1)S(1)}, bf16[1,4,160,192]{3,2,1,0:T(8,128)(2,1)}, u32[]{:S(2)}) copy-start(bf16[1,4,160,192]{3,2,1,0:T(8,128)(2,1)} %param.9) | copy-start | bytes 737284
  1.0 5.3 %copy-start.7 = (bf16[384]{0:T(512)(128)(2,1)S(1)}, bf16[384]{0:T(512)(128)(2,1)}, u32[]{:S(2)}) copy-start(bf16[384]{0:T(512)(128)(2,1)} %param.11) | copy-start | bytes 2308
  1.0 5.4 %copy-start.3 = (bf16[384,384]{1,0:T(8,128)(2,1)S(1)}, bf16[384,384]{1,0:T(8,128)(2,1)}, u32[]{:S(2)}) copy-start(bf16[384,384]{1,0:T(8,128)(2,1)} %w_query.1) | copy-start | bytes 884740
  1.0 5.4 %copy-start.4 = (bf16[384,384]{1,0:T(8,128)(2,1)S(1)}, bf16[384,384]{1,0:T(8,128)(2,1)}, u32[]{:S(2)}) copy-start(bf16[384,384]{1,0:T(8,128)(2,1)} %w_key.1) | copy-start | bytes 884740
  1.0 5.4 %copy-start.5 = (bf16[384,384]{1,0:T(8,128)(2,1)S(1)}, bf16[384,384]{1,0:T(8,128)(2,1)}, u32[]{:S(2)}) copy-start(bf16[384,384]{1,0:T(8,128)(2,1)} %w_value.1) | copy-start | bytes 884740
  1.0 5.4 %copy-start.6 = (bf16[384,384]{1,0:T(8,128)(2,1)S(1)}, bf16[384,384]{1,0:T(8,128)(2,1)}, u32[]{:S(2)}) copy-start(bf16[384,384]{1,0:T(8,128)(2,1)} %w_out.1) | copy-start | bytes 884740
  1.1 5.2 %collective-permute-start = (bf16[960,128]{1,0:T(8,128)(2,1)S(1)}, bf16[960,128]{1,0:T(8,128)(2,1)S(1)}, u32[]{:S(2)}, u32[]{:S(2)}) collective-permute-start(bf16[960,128]{1,0:T(8,128)(2,1)S(1)} %shard_map.91.mine), channel_id=1, source_target_pairs={{0,1},{1,0},{2,3},{3,2},{4,5},{5,4},{6,7},{7,6},{8,9},{9,8},{10,11... | collective-permute-start | bytes 737288 | tf_op jit(solution)/shard_map/ppermute | solution.py:18
  1.6 11.0 %collective-permute-start.2 = (bf16[960,128]{1,0:T(8,128)(2,1)S(1)}, bf16[960,128]{1,0:T(8,128)(2,1)S(1)}, u32[]{:S(2)}, u32[]{:S(2)}) collective-permute-start(bf16[960,128]{1,0:T(8,128)(2,1)S(1)} %shard_map.91.mine), channel_id=1, source_target_pairs={{0,12},{4,0},{8,4},{12,8},{1,13},{5,1},{9,5},{13,9},{2,14},{6,2},{... | collective-permute-start | bytes 737288 | tf_op jit(solution)/shard_map/ppermute | solution.py:18
  6.3 12.2 %collective-permute-start.1 = (bf16[960,128]{1,0:T(8,128)(2,1)S(1)}, bf16[960,128]{1,0:T(8,128)(2,1)S(1)}, u32[]{:S(2)}, u32[]{:S(2)}) collective-permute-start(bf16[960,128]{1,0:T(8,128)(2,1)S(1)} %shard_map.91.mine), channel_id=1, source_target_pairs={{0,4},{4,8},{8,12},{12,0},{1,5},{5,9},{9,13},{13,1},{2,6},{6,10},{... | collective-permute-start | bytes 737288 | tf_op jit(solution)/shard_map/ppermute | solution.py:18
  6.3 2.1 %copy-start = (bf16[3,3,3,384,192]{3,4,2,1,0:T(8,128)(2,1)S(1)}, bf16[3,3,3,384,192]{3,4,2,1,0:T(8,128)(2,1)}, u32[]{:S(2)}) copy-start(bf16[3,3,3,384,192]{3,4,2,1,0:T(8,128)(2,1)} %param.17) | copy-start | bytes 11943940
  6.3 2.4 %copy-start.1 = (bf16[2,4,160,384]{3,2,1,0:T(8,128)(2,1)S(1)}, bf16[2,4,160,384]{3,2,1,0:T(8,128)(2,1)}, u32[]{:S(2)}) copy-start(bf16[2,4,160,384]{3,2,1,0:T(8,128)(2,1)} %param.10) | copy-start | bytes 2949124
  8.7 15.1 %copy-start.8 = (bf16[384]{0:T(512)(128)(2,1)S(1)}, bf16[384]{0:T(512)(128)(2,1)}, u32[]{:S(2)}) copy-start(bf16[384]{0:T(512)(128)(2,1)} %param.12) | copy-start | bytes 2308
  12.6 4.9 %collective-permute-start.3 = (bf16[480,128]{1,0:T(8,128)(2,1)S(1)}, bf16[480,128]{1,0:T(8,128)(2,1)S(1)}, u32[]{:S(2)}, u32[]{:S(2)}) collective-permute-start(bf16[480,128]{1,0:T(8,128)(2,1)S(1)} %get-tuple-element.65), channel_id=1, source_target_pairs={{0,1},{1,0},{2,3},{3,2},{4,5},{5,4},{6,7},{7,6},{8,9},{9,8},{10,11... | collective-permute-start | bytes 368648 | tf_op jit(solution)/shard_map/ppermute | solution.py:18
  12.7 4.8 %collective-permute-start.4 = (bf16[480,128]{1,0:T(8,128)(2,1)S(1)}, bf16[480,128]{1,0:T(8,128)(2,1)S(1)}, u32[]{:S(2)}, u32[]{:S(2)}) collective-permute-start(bf16[480,128]{1,0:T(8,128)(2,1)S(1)} %get-tuple-element.66), channel_id=1, source_target_pairs={{0,1},{1,0},{2,3},{3,2},{4,5},{5,4},{6,7},{7,6},{8,9},{9,8},{10,11... | collective-permute-start | bytes 368648 | tf_op jit(solution)/shard_map/ppermute | solution.py:18
  13.2 10.4 %collective-permute-start.7 = (bf16[960,128]{1,0:T(8,128)(2,1)S(1)}, bf16[960,128]{1,0:T(8,128)(2,1)S(1)}, u32[]{:S(2)}, u32[]{:S(2)}) collective-permute-start(bf16[960,128]{1,0:T(8,128)(2,1)S(1)} %collective-permute-done.2.refs_2_), channel_id=1, source_target_pairs={{0,12},{4,0},{8,4},{12,8},{1,13},{5,1},{9,5},{13,9},{2,14},{6,2},{... | collective-permute-start | bytes 737288 | tf_op jit(solution)/shard_map/ppermute | solution.py:18
  18.5 1.4 %collective-permute-start.5 = (bf16[480,128]{1,0:T(8,128)(2,1)S(1)}, bf16[480,128]{1,0:T(8,128)(2,1)S(1)}, u32[]{:S(2)}, u32[]{:S(2)}) collective-permute-start(bf16[480,128]{1,0:T(8,128)(2,1)S(1)} %get-tuple-element.63), channel_id=1, source_target_pairs={{0,1},{1,0},{2,3},{3,2},{4,5},{5,4},{6,7},{7,6},{8,9},{9,8},{10,11... | collective-permute-start | bytes 368648 | tf_op jit(solution)/shard_map/ppermute | solution.py:18
  18.5 1.5 %collective-permute-start.6 = (bf16[480,128]{1,0:T(8,128)(2,1)S(1)}, bf16[480,128]{1,0:T(8,128)(2,1)S(1)}, u32[]{:S(2)}, u32[]{:S(2)}) collective-permute-start(bf16[480,128]{1,0:T(8,128)(2,1)S(1)} %get-tuple-element.64), channel_id=1, source_target_pairs={{0,1},{1,0},{2,3},{3,2},{4,5},{5,4},{6,7},{7,6},{8,9},{9,8},{10,11... | collective-permute-start | bytes 368648 | tf_op jit(solution)/shard_map/ppermute | solution.py:18
  23.6 1.5 %collective-permute-start.8 = (bf16[960,128]{1,0:T(8,128)(2,1)S(1)}, bf16[960,128]{1,0:T(8,128)(2,1)S(1)}, u32[]{:S(2)}, u32[]{:S(2)}) collective-permute-start(bf16[960,128]{1,0:T(8,128)(2,1)S(1)} %collective-permute-done.7.mine), channel_id=1, source_target_pairs={{0,1},{1,0},{2,3},{3,2},{4,5},{5,4},{6,7},{7,6},{8,9},{9,8},{10,11... | collective-permute-start | bytes 737288 | tf_op jit(solution)/shard_map/ppermute | solution.py:18
  27.7 1.8 %collective-permute-start.9 = (bf16[480,384]{1,0:T(8,128)(2,1)S(1)}, bf16[480,384]{1,0:T(8,128)(2,1)S(1)}, u32[]{:S(2)}, u32[]{:S(2)}) collective-permute-start(bf16[480,384]{1,0:T(8,128)(2,1)S(1)} %get-tuple-element.54.act), channel_id=1, source_target_pairs={{0,1},{1,0},{2,3},{3,2},{4,5},{5,4},{6,7},{7,6},{8,9},{9,8},{10,11... | collective-permute-start | bytes 1105928 | tf_op jit(solution)/shard_map/ppermute | solution.py:18
  31.0 8.2 %collective-permute-start.13 = (bf16[960,128]{1,0:T(8,128)(2,1)S(1)}, bf16[960,128]{1,0:T(8,128)(2,1)S(1)}, u32[]{:S(2)}, u32[]{:S(2)}) collective-permute-start(bf16[960,128]{1,0:T(8,128)(2,1)S(1)} %shard_map.96), channel_id=1, source_target_pairs={{0,2},{2,0},{1,3},{3,1},{4,6},{6,4},{5,7},{7,5},{8,10},{10,8},{9,1... | collective-permute-start | bytes 737288 | tf_op jit(solution)/shard_map/ppermute | solution.py:18
  31.1 4.1 %collective-permute-start.10 = (bf16[320,192]{1,0:T(8,128)(2,1)S(1)}, bf16[320,192]{1,0:T(8,128)(2,1)S(1)}, u32[]{:S(2)}, u32[]{:S(2)}) collective-permute-start(bf16[320,192]{1,0:T(8,128)(2,1)S(1)} %get-tuple-element.57), channel_id=1, source_target_pairs={{0,1},{1,0},{2,3},{3,2},{4,5},{5,4},{6,7},{7,6},{8,9},{9,8},{10,11... | collective-permute-start | bytes 368648 | tf_op jit(solution)/shard_map/ppermute | solution.py:18
  31.4 6.2 %collective-permute-start.11 = (bf16[240,128]{1,0:T(8,128)(2,1)S(1)}, bf16[240,128]{1,0:T(8,128)(2,1)S(1)}, u32[]{:S(2)}, u32[]{:S(2)}) collective-permute-start(bf16[240,128]{1,0:T(8,128)(2,1)S(1)} %get-tuple-element.60), channel_id=1, source_target_pairs={{0,4},{4,8},{8,12},{12,0},{1,5},{5,9},{9,13},{13,1},{2,6},{6,10},{... | collective-permute-start | bytes 184328 | tf_op jit(solution)/shard_map/ppermute | solution.py:18
  32.8 5.3 %collective-permute-start.12 = (bf16[240,128]{1,0:T(8,128)(2,1)S(1)}, bf16[240,128]{1,0:T(8,128)(2,1)S(1)}, u32[]{:S(2)}, u32[]{:S(2)}) collective-permute-start(bf16[240,128]{1,0:T(8,128)(2,1)S(1)} %get-tuple-element.61), channel_id=1, source_target_pairs={{0,12},{4,0},{8,4},{12,8},{1,13},{5,1},{9,5},{13,9},{2,14},{6,2},{... | collective-permute-start | bytes 184328 | tf_op jit(solution)/shard_map/ppermute | solution.py:18

commit v6 on v5

--- a/solution.py
+++ b/solution.py
@@ -172,11 +172,20 @@
     accum_out[...] = new[2]
 
 
-def last_kernel(gain, gain_two, w_mixed, query, raw, top, total, accum, mine, theirs, act_out, keep_out, give_out):
+def last_kernel(gain, gain_two, w_mixed, query, raw, top, total, accum, mine, theirs, *refs):
     core, place, places, _ = place_of()
-    keys = [rms_scaled(joined_halves(core, mine, theirs), gain[...]).astype(BF)]
-    _, total, accum = attend(query[...], keys, top[:, :1], total[:, :1], accum[...])
-    mixed = (accum / total).astype(BF)
+    act_out, keep_out, give_out, total_now, accum_now = refs
+    keys = rms_scaled(joined_halves(core, mine, theirs), gain[...]).astype(BF)
+    scores = dot_t(query[...], keys) - top[:, :1]
+    weights = jnp.exp2(scores)
+    total_now[...] = total[:, :1] + jnp.sum(weights, axis=-1, keepdims=True)
+    accum_now[...] = accum[...] + dot(weights.astype(BF), keys)
+
+    @pl.when(jnp.max(scores) > 60.0)
+    def _():
+        _, total_now[...], accum_now[...] = attend(query[...], [keys], top[:, :1], total[:, :1], accum[...])
+
+    mixed = (accum_now[...] / total_now[...]).astype(BF)
     joined = (raw[...].astype(F32) + dot(mixed, w_mixed[...])).astype(BF)
     edge = joined.shape[0] // 3
     own = jnp.where(core == 0, joined[edge:], joined[: 2 * edge]).astype(F32)
@@ -228,8 +237,8 @@
         out[...] = jnp.zeros_like(out)
 
 
-def cache_kernel(cells, cache, weights, sums, up, down):
-    moment = place_of()[3]
+def cache_kernel(cells, cache, weights, sums, inner, outer):
+    _, place, _, moment = place_of()
     tokens = cache.shape[1]
     ends = jnp.zeros((cells, cache.shape[2]), cache.dtype)
 
@@ -244,13 +253,18 @@
                     (jnp.concatenate([ends, cache[frame], ends], axis=0), back) for frame, back in pairs
                 ]
             )
-        for out, start, row in ((up, tokens - cells, 0), (down, 0, 2)):
+        finished = []
+        for start, row in ((tokens - cells, 0), (0, 2)):
             edge = jnp.concatenate([cache[frame, start : start + cells] for frame, _ in pairs], axis=1)
             parts = [
                 dot_t(edge, jnp.concatenate([weights[back, row, i] for _, back in pairs], axis=1))
                 for i in range(3)
             ]
-            pack(gathered(parts, cells), out)
+            finished.append(gathered(parts, cells))
+        up, down = finished
+        even = lax.rem(place, 2) == 0
+        pack(jnp.where(even, up, down), inner)
+        pack(jnp.where(even, down, up), outer)
 
     @pl.when(moment == 0)
     def _():
@@ -262,7 +276,7 @@
 
     @pl.when(moment > 1)
     def _():
-        for out in (sums, up, down):
+        for out in (sums, inner, outer):
             out[...] = jnp.zeros_like(out)
 
 
@@ -272,12 +286,14 @@
     out[...] = by_core(keep, theirs).astype(F32) + terms
 
 
-def edge_kernel(cells, rest, above, below, out):
+def edge_kernel(cells, rest, outer, inner, out):
     _, place, places, _ = place_of()
     tokens = rest.shape[0]
-    out[:cells] = rest[:cells] + jnp.where(place == 0, 0.0, unpacked(above[...]))
+    even = lax.rem(place, 2) == 0
+    above, below = jnp.where(even, outer[...], inner[...]), jnp.where(even, inner[...], outer[...])
+    out[:cells] = rest[:cells] + jnp.where(place == 0, 0.0, unpacked(above))
     out[cells : tokens - cells] = rest[cells : tokens - cells]
-    out[tokens - cells :] = rest[tokens - cells :] + jnp.where(place == places - 1, 0.0, unpacked(below[...]))
+    out[tokens - cells :] = rest[tokens - cells :] + jnp.where(place == places - 1, 0.0, unpacked(below))
 
 
 def write(total, out, held, sem):
@@ -323,7 +339,7 @@
     )
     behind, ahead = cycle(packed, "space", 1), cycle(packed, "space", -1)
     cache = cache.reshape(2, tokens, width)
-    own_other = cycle(packed, "chan", 1)
+    own_other = between_cores(packed)
     raw_own, keys_own, query_own, w_query, w_key, w_mixed = call(
         own_rows_kernel,
         [
@@ -335,10 +351,10 @@
             shaped((width, width), BF),
         ],
         [gain, packed, own_other, w_query, w_key, w_value, w_out],
-        flops=4 * 10**9,
+        flops=1000,
     )
     raw_own, cache = lax.optimization_barrier((raw_own, cache))
-    cached, up_term, down_term = call(
+    cached, inner, outer = call(
         functools.partial(cache_kernel, cells),
         [shaped((3, tokens, half), F32)] + [shaped((cells * 3 // 2, LANES), BF)] * 2,
         [cache, weights],
@@ -383,6 +399,7 @@
         last_kernel,
         [shaped((count, width), BF)] + [shaped((tokens // 2, half), BF)] * 2,
         [gain, gain_act, w_mixed, query, raw, top, total, accum, tile, tile_other],
+        [pltpu.VMEM((count, 1), F32), pltpu.VMEM((count, width), F32)],
     )
     other = cycle(act, "chan", 1)
     theirs = cycle(give, "chan", 1)
@@ -402,10 +419,13 @@
         [shaped((tokens, half), F32)],
         [act, other, cached, keep, theirs, weights],
     )
-    up_term, down_term, act = lax.optimization_barrier((up_term, down_term, act))
-    above, below = cycle(up_term, "space", 1), cycle(down_term, "space", -1)
+    inner, outer, act = lax.optimization_barrier((inner, outer, act))
+    outer = lax.ppermute(
+        outer, "space", [(i, min(max(((i + 1) ^ 1) - 1, 0), places - 1)) for i in range(places)]
+    )
+    inner = lax.ppermute(inner, "space", [(i, i ^ 1) for i in range(places)])
     (rest,) = call(
-        functools.partial(edge_kernel, cells), [shaped((tokens, half), F32)], [rest, above, below]
+        functools.partial(edge_kernel, cells), [shaped((tokens, half), F32)], [rest, outer, inner]
     )
     written = [pltpu.VMEM((tokens, half), BF), pltpu.SemaphoreType.DMA]
     (out,) = call(early_kernel, [shaped((tokens, half), BF)], [rest], written, kept=True)

time: 39.3 us -> 38.5 us (0.980)
  local copies, waits for them, and re-layouts: 2.16 us -> 1.06 us
  starting transfers between devices: 15.4 us -> 16.2 us
  waiting for transfers between devices: 6.9 us -> 6.39 us
    ppermute x0 -> x2, starting transfers between devices: none -> 4.22 us  [the longest x1 3.57 us: body(): inner = lax.ppermute(inner, 'space', [(i, i ^ 1) for i in range(places)])]
    ppermute x14 -> x13, starting transfers between devices: 15.4 us -> 12 us  [cycle(): lax.ppermute(array, axis, [(i, (i + by) % count) for i in range(count)])]
    ppermute x14 -> x13, waiting for transfers between devices: 6.9 us -> 5.78 us  [cycle(): lax.ppermute(array, axis, [(i, (i + by) % count) for i in range(count)])]
    unnamed x18, local copies, waits for them, and re-layouts: 2.12 us -> 1.01 us
    ppermute x0 -> x2, waiting for transfers between devices: none -> 0.62 us  [the longest x1 0.61 us: body(): inner = lax.ppermute(inner, 'space', [(i, i ^ 1) for i in range(places)])]
  transfers between devices with their start and end apart: 14 -> 15, of which waited for: 10 -> 11; matrix products, arithmetic and copies ran while one was open for 0% -> 0% of each run, Pallas kernels for 26% -> 27%
where the time goes in v6:
time: 38.5 us; the launch traced here: 38.4 us
  starting transfers between devices  16.2 us (42%)
  Pallas kernels  14.3 us (37%)
  waiting for transfers between devices  6.39 us (17%)
  local copies, waits for them, and re-layouts  1.06 us (3%)
    pallas_call x10, Pallas kernels, call(): pl.pallas_call(kernel, out_shape=outs, in_specs=[vmem] * (len(args) - int...  14.3 us
    ppermute x13, starting transfers between devices, cycle(): lax.ppermute(array, axis, [(i, (i + by) % count) for i in range(count)])  12 us
    ppermute x13, waiting for transfers between devices, cycle(): lax.ppermute(array, axis, [(i, (i + by) % count) for i in range(count)])  5.78 us
    ppermute x1, starting transfers between devices, body(): inner = lax.ppermute(inner, 'space', [(i, i ^ 1) for i in range(places)])  3.57 us
    unnamed x18, local copies, waits for them, and re-layouts  1.01 us
  transfers between devices with their start and end apart: 15, of which 11 were waited for; matrix products, arithmetic and copies ran while one was open for 0% of the time, Pallas kernels for 27%

profile of v6, /device:TPU:0, one launch (start us, length us, event | category | flops | bytes accessed | tf_op | source)
XLA Modules:
  0.0 38.4 jit_solution(3875823630371561182)
XLA Ops:
  0.0 1.0 %copy-done.6 = bf16[1,4,160,192]{3,2,1,0:T(8,128)(2,1)S(1)} copy-done((bf16[1,4,160,192]{3,2,1,0:T(8,128)(2,1)S(1)}, bf16[1,4,160,192]{3,2,1,0:T(8,128)(2,1)}, u32[]{:S(2)}) %copy-start.6) | copy-done | bytes 245784
  1.0 0.0 copy-start.5
  1.0 0.0 copy-start
  1.0 0.0 copy-start.1
  1.0 0.1 shard_map.91.mine
  1.1 5.1 %collective-permute-start.3 = (bf16[960,128]{1,0:T(8,128)(2,1)S(1)}, bf16[960,128]{1,0:T(8,128)(2,1)S(1)}, u32[]{:S(2)}, u32[]{:S(2)}) collective-permute-start(bf16[960,128]{1,0:T(8,128)(2,1)S(1)} %shard_map.91.mine), channel_id=1, source_target_pairs={{0,12},{4,0},{8,4},{12,8},{1,13},{5,1},{9,5},{13,9},{2,14},{6,2},{... | collective-permute-start | bytes 737288 | tf_op jit(solution)/shard_map/ppermute | solution.py:18
  6.2 0.1 collective-permute-start
  6.3 0.5 %collective-permute-start.1 = (bf16[480,128]{1,0:T(8,128)(2,1)S(1)}, bf16[480,128]{1,0:T(8,128)(2,1)S(1)}, u32[]{:S(2)}, u32[]{:S(2)}) collective-permute-start(bf16[480,128]{1,0:T(8,128)(2,1)S(1)} %get-tuple-element.68), channel_id=1, source_target_pairs={{0,1},{1,0},{2,3},{3,2},{4,5},{5,4},{6,7},{7,6},{8,9},{9,8},{10,11... | collective-permute-start | bytes 368648 | tf_op jit(solution)/shard_map/ppermute | solution.py:18
  6.8 0.0 collective-permute-start.2
  6.8 0.0 copy-done.7
  6.8 0.8 %collective-permute-done = bf16[480,128]{1,0:T(8,128)(2,1)S(1)} collective-permute-done((bf16[480,128]{1,0:T(8,128)(2,1)S(1)}, bf16[480,128]{1,0:T(8,128)(2,1)S(1)}, u32[]{:S(2)}, u32[]{:S(2)}) %collective-permute-start) | collective-permute-done | bytes 122912 | tf_op jit(solution)/shard_map/ppermute | solution.py:18
  7.6 0.2 collective-permute-done.1
  7.8 0.0 copy-done.2
  7.8 0.0 copy-done.3
  7.9 0.0 copy-done.4
  7.9 1.2 %shard_map.92 = (bf16[320,384]{1,0:T(8,128)(2,1)S(1)}, bf16[640,384]{1,0:T(8,128)(2,1)S(1)}, bf16[320,384]{1,0:T(8,128)(2,1)S(1)}, bf16[384,384]{1,0:T(8,128)(2,...) custom-call(bf16[1,384]{1,0:T(2,128)(2,1)S(1)} %reshape.15.gain, ...), custom_call_target="tpu_custom_call" | custom-call | flops 1000 | bytes 1000 | tf_op jit(solution)/shard_map/pallas_call | solution.py:29
  9.1 0.0 copy-start.8
  9.1 3.3 %shard_map.93 = (f32[3,640,192]{2,1,0:T(8,128)S(1)}, bf16[240,128]{1,0:T(8,128)(2,1)S(1)}, bf16[240,128]{1,0:T(8,128)(2,1)S(1)}) custom-call(bf16[2,640,384]{2,1,0:T(8,128)(2,1)S(1)} %bitcast.7, bf16[3,3,3,192,384]{4,3,2,1,0:T(8,128)(2,1)S(1)} %bitcast.4), custom_call_target="tpu_custom_call" | custom-call | flops 1000 | bytes 1000 | tf_op jit(solution)/shard_map/pallas_call | solution.py:29
  12.4 0.2 collective-permute-done.3.refs_2_
  12.6 0.3 collective-permute-start.4
  12.9 0.3 collective-permute-start.5
  13.2 4.3 %collective-permute-start.8 = (bf16[960,128]{1,0:T(8,128)(2,1)S(1)}, bf16[960,128]{1,0:T(8,128)(2,1)S(1)}, u32[]{:S(2)}, u32[]{:S(2)}) collective-permute-start(bf16[960,128]{1,0:T(8,128)(2,1)S(1)} %collective-permute-done.3.refs_2_), channel_id=1, source_target_pairs={{0,12},{4,0},{8,4},{12,8},{1,13},{5,1},{9,5},{13,9},{2,14},{6,2},{... | collective-permute-start | bytes 737288 | tf_op jit(solution)/shard_map/ppermute | solution.py:18
  17.5 0.0 collective-permute-done.4
  17.5 0.0 collective-permute-done.5
  17.5 0.3 collective-permute-done.2.refs_0_
  17.8 0.1 collective-permute-start.6
  17.9 0.5 %collective-permute-start.7 = (bf16[480,128]{1,0:T(8,128)(2,1)S(1)}, bf16[480,128]{1,0:T(8,128)(2,1)S(1)}, u32[]{:S(2)}, u32[]{:S(2)}) collective-permute-start(bf16[480,128]{1,0:T(8,128)(2,1)S(1)} %get-tuple-element.64), channel_id=1, source_target_pairs={{0,1},{1,0},{2,3},{3,2},{4,5},{5,4},{6,7},{7,6},{8,9},{9,8},{10,11... | collective-permute-start | bytes 368648 | tf_op jit(solution)/shard_map/ppermute | solution.py:18
  18.4 0.8 %collective-permute-done.6 = bf16[480,128]{1,0:T(8,128)(2,1)S(1)} collective-permute-done((bf16[480,128]{1,0:T(8,128)(2,1)S(1)}, bf16[480,128]{1,0:T(8,128)(2,1)S(1)}, u32[]{:S(2)}, u32[]{:S(2)}) %collective-permute-start.6) | collective-permute-done | bytes 122912 | tf_op jit(solution)/shard_map/ppermute | solution.py:18
  19.2 0.2 collective-permute-done.7
  19.4 3.4 %shard_map.94 = (bf16[480,384]{1,0:T(8,128)(2,1)S(1)}, bf16[480,384]{1,0:T(8,128)(2,1)S(1)}, f32[480,128]{1,0:T(8,128)S(1)}, f32[480,128]{1,0:T(8,128)S(1)}, f32[480,384]{1,0:T(8,128)S(1)}) custom-call(bf16[1,384]{1,0:T(2,128)(2,1)S(1)} %reshape.15.gain, bf16[320,384]{1,0:T(8,128)(2,1)S(1)} %get-tuple-element.36.raw_own, ...), custom_call_target="tpu_custom_call" | custom-call | flops 1000 | bytes 1000 | tf_op jit(solution)/shard_map/pallas_call | solution.py:29
  22.7 0.2 collective-permute-done.8.mine
  22.9 0.2 collective-permute-start.9
  23.2 1.3 %collective-permute-done.9.theirs = bf16[960,128]{1,0:T(8,128)(2,1)S(1)} collective-permute-done((bf16[960,128]{1,0:T(8,128)(2,1)S(1)}, bf16[960,128]{1,0:T(8,128)(2,1)S(1)}, u32[]{:S(2)}, u32[]{:S(2)}) %collective-permute-start.9) | collective-permute-done | bytes 245792 | tf_op jit(solution)/shard_map/ppermute | solution.py:18
  24.4 2.3 %shard_map.95 = (bf16[480,384]{1,0:T(8,128)(2,1)S(1)}, bf16[320,192]{1,0:T(8,128)(2,1)S(1)}, bf16[320,192]{1,0:T(8,128)(2,1)S(1)}) custom-call(bf16[1,384]{1,0:T(2,128)(2,1)S(1)} %reshape.15.gain, bf16[1,384]{1,0:T(2,128)(2,1)S(1)} %reshape.16.gain_two, bf16[384,384]{1,0:T(8,128)(2,1)S(1)} %get-tuple-element.34.w_mixed, ...), custom_call_target="tpu_custom_call" | custom-call | flops 1000 | bytes 1000 | tf_op jit(solution)/shard_map/pallas_call | solution.py:29
  26.7 0.3 collective-permute-start.10
  27.0 1.5 %collective-permute-done.10.other = bf16[480,384]{1,0:T(8,128)(2,1)S(1)} collective-permute-done((bf16[480,384]{1,0:T(8,128)(2,1)S(1)}, bf16[480,384]{1,0:T(8,128)(2,1)S(1)}, u32[]{:S(2)}, u32[]{:S(2)}) %collective-permute-start.10) | collective-permute-done | bytes 368672 | tf_op jit(solution)/shard_map/ppermute | solution.py:18
  28.5 1.6 %shard_map.96 = bf16[960,128]{1,0:T(8,128)(2,1)S(1)} custom-call(bf16[480,384]{1,0:T(8,128)(2,1)S(1)} %get-tuple-element.54.act, bf16[480,384]{1,0:T(8,128)(2,1)S(1)} %collective-permute-done.10.other, bf16[3,3,3,192,384]{4,3,2,1,0:T(8,128)(2,1)S(1)} %bitcast.5), custom_call_target="tpu_custom_call" | custom-call | flops 1000 | bytes 1000 | tf_op jit(solution)/shard_map/pallas_call | solution.py:29
  30.1 0.1 collective-permute-start.14
  30.1 0.3 collective-permute-start.11
  30.4 0.7 %collective-permute-start.12 = (bf16[240,128]{1,0:T(8,128)(2,1)S(1)}, bf16[240,128]{1,0:T(8,128)(2,1)S(1)}, u32[]{:S(2)}, u32[]{:S(2)}) collective-permute-start(bf16[240,128]{1,0:T(8,128)(2,1)S(1)} %get-tuple-element.60), channel_id=1, source_target_pairs={{0,0},{4,8},{8,4},{12,12},{1,1},{5,9},{9,5},{13,13},{2,2},{6,10},{... | collective-permute-start | bytes 184328 | tf_op jit(solution)/shard_map/ppermute | solution.py:423
  31.1 3.6 %collective-permute-start.13 = (bf16[240,128]{1,0:T(8,128)(2,1)S(1)}, bf16[240,128]{1,0:T(8,128)(2,1)S(1)}, u32[]{:S(2)}, u32[]{:S(2)}) collective-permute-start(bf16[240,128]{1,0:T(8,128)(2,1)S(1)} %get-tuple-element.61), channel_id=1, source_target_pairs={{0,4},{4,0},{8,12},{12,8},{1,5},{5,1},{9,13},{13,9},{2,6},{6,2},{1... | collective-permute-start | bytes 184328 | tf_op jit(solution)/shard_map/ppermute | solution.py:426
  34.7 0.0 collective-permute-done.11.theirs
  34.7 1.6 %shard_map.97.rest = f32[640,192]{1,0:T(8,128)S(1)} custom-call(bf16[480,384]{1,0:T(8,128)(2,1)S(1)} %get-tuple-element.54.act, bf16[480,384]{1,0:T(8,128)(2,1)S(1)} %collective-permute-done.10.other, f32[3,640,192]{2,1,0:T(8,128)S(1)} %get-tuple-element.55.cached, bf16[320,192]{1,0:T(8,128)(2,1)S(1)} %get-tuple-element.56.keep, ...), custom_call_target="tpu_custom_call" | custom-call | flops 1000 | bytes 1000 | tf_op jit(solution)/shard_map/pallas_call | solution.py:29
  36.3 0.0 collective-permute-done.12.outer
  36.3 0.6 %collective-permute-done.13.inner = bf16[240,128]{1,0:T(8,128)(2,1)S(1)} collective-permute-done((bf16[240,128]{1,0:T(8,128)(2,1)S(1)}, bf16[240,128]{1,0:T(8,128)(2,1)S(1)}, u32[]{:S(2)}, u32[]{:S(2)}) %collective-permute-start.13) | collective-permute-done | bytes 61472 | tf_op jit(solution)/shard_map/ppermute | solution.py:426
  36.9 0.1 shard_map.98.rest
  37.0 0.8 %shard_map.99.refs_1_ = bf16[640,192]{1,0:T(8,128)(2,1)} custom-call(f32[640,192]{1,0:T(8,128)S(1)} %shard_map.98.rest), custom_call_target="tpu_custom_call" | custom-call | flops 1000 | bytes 1000 | tf_op jit(solution)/shard_map/pallas_call | solution.py:29
  37.8 0.4 %collective-permute-done.14.refs_0_ = bf16[960,128]{1,0:T(8,128)(2,1)S(1)} collective-permute-done((bf16[960,128]{1,0:T(8,128)(2,1)S(1)}, bf16[960,128]{1,0:T(8,128)(2,1)S(1)}, u32[]{:S(2)}, u32[]{:S(2)}) %collective-permute-start.14) | collective-permute-done | bytes 245792 | tf_op jit(solution)/shard_map/ppermute | solution.py:18
  (18 shorter events, 0.1 us)
Async XLA Ops:
  0.0 1.0 %copy-start.6 = (bf16[1,4,160,192]{3,2,1,0:T(8,128)(2,1)S(1)}, bf16[1,4,160,192]{3,2,1,0:T(8,128)(2,1)}, u32[]{:S(2)}) copy-start(bf16[1,4,160,192]{3,2,1,0:T(8,128)(2,1)} %param.9) | copy-start | bytes 737284
  1.0 5.8 %copy-start.7 = (bf16[384]{0:T(512)(128)(2,1)S(1)}, bf16[384]{0:T(512)(128)(2,1)}, u32[]{:S(2)}) copy-start(bf16[384]{0:T(512)(128)(2,1)} %param.11) | copy-start | bytes 2308
  1.0 6.9 %copy-start.2 = (bf16[384,384]{1,0:T(8,128)(2,1)S(1)}, bf16[384,384]{1,0:T(8,128)(2,1)}, u32[]{:S(2)}) copy-start(bf16[384,384]{1,0:T(8,128)(2,1)} %w_query.1) | copy-start | bytes 884740
  1.0 6.9 %copy-start.3 = (bf16[384,384]{1,0:T(8,128)(2,1)S(1)}, bf16[384,384]{1,0:T(8,128)(2,1)}, u32[]{:S(2)}) copy-start(bf16[384,384]{1,0:T(8,128)(2,1)} %w_key.1) | copy-start | bytes 884740
  1.0 6.9 %copy-start.4 = (bf16[384,384]{1,0:T(8,128)(2,1)S(1)}, bf16[384,384]{1,0:T(8,128)(2,1)}, u32[]{:S(2)}) copy-start(bf16[384,384]{1,0:T(8,128)(2,1)} %w_value.1) | copy-start | bytes 884740
  1.0 6.9 %copy-start.5 = (bf16[384,384]{1,0:T(8,128)(2,1)S(1)}, bf16[384,384]{1,0:T(8,128)(2,1)}, u32[]{:S(2)}) copy-start(bf16[384,384]{1,0:T(8,128)(2,1)} %w_out.1) | copy-start | bytes 884740
  1.0 8.1 %copy-start = (bf16[3,3,3,384,192]{3,4,2,1,0:T(8,128)(2,1)S(1)}, bf16[3,3,3,384,192]{3,4,2,1,0:T(8,128)(2,1)}, u32[]{:S(2)}) copy-start(bf16[3,3,3,384,192]{3,4,2,1,0:T(8,128)(2,1)} %param.17) | copy-start | bytes 11943940
  1.0 8.1 %copy-start.1 = (bf16[2,4,160,384]{3,2,1,0:T(8,128)(2,1)S(1)}, bf16[2,4,160,384]{3,2,1,0:T(8,128)(2,1)}, u32[]{:S(2)}) copy-start(bf16[2,4,160,384]{3,2,1,0:T(8,128)(2,1)} %param.10) | copy-start | bytes 2949124
  1.1 11.5 %collective-permute-start.3 = (bf16[960,128]{1,0:T(8,128)(2,1)S(1)}, bf16[960,128]{1,0:T(8,128)(2,1)S(1)}, u32[]{:S(2)}, u32[]{:S(2)}) collective-permute-start(bf16[960,128]{1,0:T(8,128)(2,1)S(1)} %shard_map.91.mine), channel_id=1, source_target_pairs={{0,12},{4,0},{8,4},{12,8},{1,13},{5,1},{9,5},{13,9},{2,14},{6,2},{... | collective-permute-start | bytes 737288 | tf_op jit(solution)/shard_map/ppermute | solution.py:18
  6.2 1.4 %collective-permute-start = (bf16[480,128]{1,0:T(8,128)(2,1)S(1)}, bf16[480,128]{1,0:T(8,128)(2,1)S(1)}, u32[]{:S(2)}, u32[]{:S(2)}) collective-permute-start(bf16[480,128]{1,0:T(8,128)(2,1)S(1)} %get-tuple-element.67), channel_id=1, source_target_pairs={{0,1},{1,0},{2,3},{3,2},{4,5},{5,4},{6,7},{7,6},{8,9},{9,8},{10,11... | collective-permute-start | bytes 368648 | tf_op jit(solution)/shard_map/ppermute | solution.py:18
  6.3 1.5 %collective-permute-start.1 = (bf16[480,128]{1,0:T(8,128)(2,1)S(1)}, bf16[480,128]{1,0:T(8,128)(2,1)S(1)}, u32[]{:S(2)}, u32[]{:S(2)}) collective-permute-start(bf16[480,128]{1,0:T(8,128)(2,1)S(1)} %get-tuple-element.68), channel_id=1, source_target_pairs={{0,1},{1,0},{2,3},{3,2},{4,5},{5,4},{6,7},{7,6},{8,9},{9,8},{10,11... | collective-permute-start | bytes 368648 | tf_op jit(solution)/shard_map/ppermute | solution.py:18
  6.8 10.9 %collective-permute-start.2 = (bf16[960,128]{1,0:T(8,128)(2,1)S(1)}, bf16[960,128]{1,0:T(8,128)(2,1)S(1)}, u32[]{:S(2)}, u32[]{:S(2)}) collective-permute-start(bf16[960,128]{1,0:T(8,128)(2,1)S(1)} %shard_map.91.mine), channel_id=1, source_target_pairs={{0,4},{4,8},{8,12},{12,0},{1,5},{5,9},{9,13},{13,1},{2,6},{6,10},{... | collective-permute-start | bytes 737288 | tf_op jit(solution)/shard_map/ppermute | solution.py:18
  9.1 14.0 %copy-start.8 = (bf16[384]{0:T(512)(128)(2,1)S(1)}, bf16[384]{0:T(512)(128)(2,1)}, u32[]{:S(2)}) copy-start(bf16[384]{0:T(512)(128)(2,1)} %param.12) | copy-start | bytes 2308
  12.6 4.9 %collective-permute-start.4 = (bf16[480,128]{1,0:T(8,128)(2,1)S(1)}, bf16[480,128]{1,0:T(8,128)(2,1)S(1)}, u32[]{:S(2)}, u32[]{:S(2)}) collective-permute-start(bf16[480,128]{1,0:T(8,128)(2,1)S(1)} %get-tuple-element.65), channel_id=1, source_target_pairs={{0,1},{1,0},{2,3},{3,2},{4,5},{5,4},{6,7},{7,6},{8,9},{9,8},{10,11... | collective-permute-start | bytes 368648 | tf_op jit(solution)/shard_map/ppermute | solution.py:18
  12.9 4.6 %collective-permute-start.5 = (bf16[480,128]{1,0:T(8,128)(2,1)S(1)}, bf16[480,128]{1,0:T(8,128)(2,1)S(1)}, u32[]{:S(2)}, u32[]{:S(2)}) collective-permute-start(bf16[480,128]{1,0:T(8,128)(2,1)S(1)} %get-tuple-element.66), channel_id=1, source_target_pairs={{0,1},{1,0},{2,3},{3,2},{4,5},{5,4},{6,7},{7,6},{8,9},{9,8},{10,11... | collective-permute-start | bytes 368648 | tf_op jit(solution)/shard_map/ppermute | solution.py:18
  13.2 9.7 %collective-permute-start.8 = (bf16[960,128]{1,0:T(8,128)(2,1)S(1)}, bf16[960,128]{1,0:T(8,128)(2,1)S(1)}, u32[]{:S(2)}, u32[]{:S(2)}) collective-permute-start(bf16[960,128]{1,0:T(8,128)(2,1)S(1)} %collective-permute-done.3.refs_2_), channel_id=1, source_target_pairs={{0,12},{4,0},{8,4},{12,8},{1,13},{5,1},{9,5},{13,9},{2,14},{6,2},{... | collective-permute-start | bytes 737288 | tf_op jit(solution)/shard_map/ppermute | solution.py:18
  17.8 1.4 %collective-permute-start.6 = (bf16[480,128]{1,0:T(8,128)(2,1)S(1)}, bf16[480,128]{1,0:T(8,128)(2,1)S(1)}, u32[]{:S(2)}, u32[]{:S(2)}) collective-permute-start(bf16[480,128]{1,0:T(8,128)(2,1)S(1)} %get-tuple-element.63), channel_id=1, source_target_pairs={{0,1},{1,0},{2,3},{3,2},{4,5},{5,4},{6,7},{7,6},{8,9},{9,8},{10,11... | collective-permute-start | bytes 368648 | tf_op jit(solution)/shard_map/ppermute | solution.py:18
  17.9 1.5 %collective-permute-start.7 = (bf16[480,128]{1,0:T(8,128)(2,1)S(1)}, bf16[480,128]{1,0:T(8,128)(2,1)S(1)}, u32[]{:S(2)}, u32[]{:S(2)}) collective-permute-start(bf16[480,128]{1,0:T(8,128)(2,1)S(1)} %get-tuple-element.64), channel_id=1, source_target_pairs={{0,1},{1,0},{2,3},{3,2},{4,5},{5,4},{6,7},{7,6},{8,9},{9,8},{10,11... | collective-permute-start | bytes 368648 | tf_op jit(solution)/shard_map/ppermute | solution.py:18
  22.9 1.5 %collective-permute-start.9 = (bf16[960,128]{1,0:T(8,128)(2,1)S(1)}, bf16[960,128]{1,0:T(8,128)(2,1)S(1)}, u32[]{:S(2)}, u32[]{:S(2)}) collective-permute-start(bf16[960,128]{1,0:T(8,128)(2,1)S(1)} %collective-permute-done.8.mine), channel_id=1, source_target_pairs={{0,1},{1,0},{2,3},{3,2},{4,5},{5,4},{6,7},{7,6},{8,9},{9,8},{10,11... | collective-permute-start | bytes 737288 | tf_op jit(solution)/shard_map/ppermute | solution.py:18
  26.7 1.8 %collective-permute-start.10 = (bf16[480,384]{1,0:T(8,128)(2,1)S(1)}, bf16[480,384]{1,0:T(8,128)(2,1)S(1)}, u32[]{:S(2)}, u32[]{:S(2)}) collective-permute-start(bf16[480,384]{1,0:T(8,128)(2,1)S(1)} %get-tuple-element.54.act), channel_id=1, source_target_pairs={{0,1},{1,0},{2,3},{3,2},{4,5},{5,4},{6,7},{7,6},{8,9},{9,8},{10,11... | collective-permute-start | bytes 1105928 | tf_op jit(solution)/shard_map/ppermute | solution.py:18
  30.1 8.2 %collective-permute-start.14 = (bf16[960,128]{1,0:T(8,128)(2,1)S(1)}, bf16[960,128]{1,0:T(8,128)(2,1)S(1)}, u32[]{:S(2)}, u32[]{:S(2)}) collective-permute-start(bf16[960,128]{1,0:T(8,128)(2,1)S(1)} %shard_map.96), channel_id=1, source_target_pairs={{0,2},{2,0},{1,3},{3,1},{4,6},{6,4},{5,7},{7,5},{8,10},{10,8},{9,1... | collective-permute-start | bytes 737288 | tf_op jit(solution)/shard_map/ppermute | solution.py:18
  30.1 4.5 %collective-permute-start.11 = (bf16[320,192]{1,0:T(8,128)(2,1)S(1)}, bf16[320,192]{1,0:T(8,128)(2,1)S(1)}, u32[]{:S(2)}, u32[]{:S(2)}) collective-permute-start(bf16[320,192]{1,0:T(8,128)(2,1)S(1)} %get-tuple-element.57), channel_id=1, source_target_pairs={{0,1},{1,0},{2,3},{3,2},{4,5},{5,4},{6,7},{7,6},{8,9},{9,8},{10,11... | collective-permute-start | bytes 368648 | tf_op jit(solution)/shard_map/ppermute | solution.py:18
  30.4 5.8 %collective-permute-start.12 = (bf16[240,128]{1,0:T(8,128)(2,1)S(1)}, bf16[240,128]{1,0:T(8,128)(2,1)S(1)}, u32[]{:S(2)}, u32[]{:S(2)}) collective-permute-start(bf16[240,128]{1,0:T(8,128)(2,1)S(1)} %get-tuple-element.60), channel_id=1, source_target_pairs={{0,0},{4,8},{8,4},{12,12},{1,1},{5,9},{9,5},{13,13},{2,2},{6,10},{... | collective-permute-start | bytes 184328 | tf_op jit(solution)/shard_map/ppermute | solution.py:423
  31.1 5.8 %collective-permute-start.13 = (bf16[240,128]{1,0:T(8,128)(2,1)S(1)}, bf16[240,128]{1,0:T(8,128)(2,1)S(1)}, u32[]{:S(2)}, u32[]{:S(2)}) collective-permute-start(bf16[240,128]{1,0:T(8,128)(2,1)S(1)} %get-tuple-element.61), channel_id=1, source_target_pairs={{0,4},{4,0},{8,12},{12,8},{1,5},{5,1},{9,13},{13,9},{2,6},{6,2},{1... | collective-permute-start | bytes 184328 | tf_op jit(solution)/shard_map/ppermute | solution.py:426

commit v7 on v6

--- a/solution.py
+++ b/solution.py
@@ -174,7 +174,7 @@
 
 def last_kernel(gain, gain_two, w_mixed, query, raw, top, total, accum, mine, theirs, *refs):
     core, place, places, _ = place_of()
-    act_out, keep_out, give_out, total_now, accum_now = refs
+    act_out, joined_out, total_now, accum_now = refs
     keys = rms_scaled(joined_halves(core, mine, theirs), gain[...]).astype(BF)
     scores = dot_t(query[...], keys) - top[:, :1]
     weights = jnp.exp2(scores)
@@ -187,19 +187,25 @@
 
     mixed = (accum_now[...] / total_now[...]).astype(BF)
     joined = (raw[...].astype(F32) + dot(mixed, w_mixed[...])).astype(BF)
+    joined_out[...] = joined
+    edge = joined.shape[0] // 3
+    act = rms_scaled(joined.astype(F32), gain_two[...])
+    act = act / (1.0 + jnp.exp(-act))
+    row = lax.broadcasted_iota(jnp.int32, (act.shape[0], 1), 0)
+    beyond = ((core == 0) & (place == 0) & (row < edge)) | (
+        (core == 1) & (place == places - 1) & (row >= 2 * edge)
+    )
+    act_out[...] = jnp.where(beyond, 0.0, act).astype(BF)
+
+
+def residual_kernel(joined, keep_out, give_out):
+    core = place_of()[0]
     edge = joined.shape[0] // 3
     own = jnp.where(core == 0, joined[edge:], joined[: 2 * edge]).astype(F32)
     half = own.shape[1] // 2
     low, high = own[:, :half], own[:, half:]
     keep_out[...] = jnp.where(core == 0, low, high).astype(BF)
     give_out[...] = jnp.where(core == 0, high, low).astype(BF)
-    act = rms_scaled(joined.astype(F32), gain_two[...])
-    act = act / (1.0 + jnp.exp(-act))
-    row = lax.broadcasted_iota(jnp.int32, (act.shape[0], 1), 0)
-    beyond = ((core == 0) & (place == 0) & (row < edge)) | (
-        (core == 1) & (place == places - 1) & (row >= 2 * edge)
-    )
-    act_out[...] = jnp.where(beyond, 0.0, act).astype(BF)
 
 
 def taps(padded, weights, cells):
@@ -395,15 +401,13 @@
                 )
     tile, accum = lax.optimization_barrier((groups[-1][0], accum))
     tile_other = cycle(tile, "chan", 1)
-    act, keep, give = call(
+    act, joined = call(
         last_kernel,
-        [shaped((count, width), BF)] + [shaped((tokens // 2, half), BF)] * 2,
+        [shaped((count, width), BF)] * 2,
         [gain, gain_act, w_mixed, query, raw, top, total, accum, tile, tile_other],
         [pltpu.VMEM((count, 1), F32), pltpu.VMEM((count, width), F32)],
     )
     other = cycle(act, "chan", 1)
-    theirs = cycle(give, "chan", 1)
-
     received = []
     for back in range(1, min(moments, 3)):
         (term,) = call(
@@ -412,8 +416,10 @@
             [act, other, weights],
             )
         received.append(term)
-    act, received = lax.optimization_barrier((act, received))
+    act, joined, received = lax.optimization_barrier((act, joined, received))
     received = [cycle(term, "tm", 1 + i) for i, term in enumerate(received)]
+    keep, give = call(residual_kernel, [shaped((tokens // 2, half), BF)] * 2, [joined])
+    theirs = cycle(give, "chan", 1)
     (rest,) = call(
         functools.partial(rest_kernel, cells),
         [shaped((tokens, half), F32)],

time: 38.5 us -> 38.3 us (level)
    pallas_call x10 -> x11, Pallas kernels: 14.3 us -> 14.3 us  [call(): pl.pallas_call(kernel, out_shape=outs, in_specs=[vmem] * (len(args) - int...]
  transfers between devices with their start and end apart: 15 -> 15, of which waited for: 11 -> 11; matrix products, arithmetic and copies ran while one was open for 0% -> 0% of each run, Pallas kernels for 27% -> 28%
where the time goes in v7:
time: 38.3 us; the launch traced here: 38.2 us
  starting transfers between devices  16.2 us (42%)
  Pallas kernels  14.3 us (37%)
  waiting for transfers between devices  6.15 us (16%)
  local copies, waits for them, and re-layouts  1.06 us (3%)
    pallas_call x11, Pallas kernels, call(): pl.pallas_call(kernel, out_shape=outs, in_specs=[vmem] * (len(args) - int...  14.3 us
    ppermute x13, starting transfers between devices, cycle(): lax.ppermute(array, axis, [(i, (i + by) % count) for i in range(count)])  12 us
    ppermute x13, waiting for transfers between devices, cycle(): lax.ppermute(array, axis, [(i, (i + by) % count) for i in range(count)])  5.53 us
    ppermute x1, starting transfers between devices, body(): inner = lax.ppermute(inner, 'space', [(i, i ^ 1) for i in range(places)])  3.57 us
    unnamed x18, local copies, waits for them, and re-layouts  1.01 us
  transfers between devices with their start and end apart: 15, of which 11 were waited for; matrix products, arithmetic and copies ran while one was open for 0% of the time, Pallas kernels for 28%

profile of v7, /device:TPU:0, one launch (start us, length us, event | category | flops | bytes accessed | tf_op | source)
XLA Modules:
  0.0 38.2 jit_solution(17603416639033610332)
XLA Ops:
  0.0 1.0 %copy-done.6 = bf16[1,4,160,192]{3,2,1,0:T(8,128)(2,1)S(1)} copy-done((bf16[1,4,160,192]{3,2,1,0:T(8,128)(2,1)S(1)}, bf16[1,4,160,192]{3,2,1,0:T(8,128)(2,1)}, u32[]{:S(2)}) %copy-start.6) | copy-done | bytes 245784
  1.0 0.0 copy-start.5
  1.0 0.0 copy-start
  1.0 0.0 copy-start.1
  1.0 0.1 shard_map.91.mine
  1.1 5.1 %collective-permute-start.3 = (bf16[960,128]{1,0:T(8,128)(2,1)S(1)}, bf16[960,128]{1,0:T(8,128)(2,1)S(1)}, u32[]{:S(2)}, u32[]{:S(2)}) collective-permute-start(bf16[960,128]{1,0:T(8,128)(2,1)S(1)} %shard_map.91.mine), channel_id=1, source_target_pairs={{0,12},{4,0},{8,4},{12,8},{1,13},{5,1},{9,5},{13,9},{2,14},{6,2},{... | collective-permute-start | bytes 737288 | tf_op jit(solution)/shard_map/ppermute | solution.py:18
  6.2 0.1 collective-permute-start
  6.3 0.5 %collective-permute-start.1 = (bf16[480,128]{1,0:T(8,128)(2,1)S(1)}, bf16[480,128]{1,0:T(8,128)(2,1)S(1)}, u32[]{:S(2)}, u32[]{:S(2)}) collective-permute-start(bf16[480,128]{1,0:T(8,128)(2,1)S(1)} %get-tuple-element.72), channel_id=1, source_target_pairs={{0,1},{1,0},{2,3},{3,2},{4,5},{5,4},{6,7},{7,6},{8,9},{9,8},{10,11... | collective-permute-start | bytes 368648 | tf_op jit(solution)/shard_map/ppermute | solution.py:18
  6.8 0.0 collective-permute-start.2
  6.8 0.0 copy-done.7
  6.8 0.8 %collective-permute-done = bf16[480,128]{1,0:T(8,128)(2,1)S(1)} collective-permute-done((bf16[480,128]{1,0:T(8,128)(2,1)S(1)}, bf16[480,128]{1,0:T(8,128)(2,1)S(1)}, u32[]{:S(2)}, u32[]{:S(2)}) %collective-permute-start) | collective-permute-done | bytes 122912 | tf_op jit(solution)/shard_map/ppermute | solution.py:18
  7.6 0.2 collective-permute-done.1
  7.8 0.0 copy-done.2
  7.8 0.0 copy-done.3
  7.9 1.2 %shard_map.92 = (bf16[320,384]{1,0:T(8,128)(2,1)S(1)}, bf16[640,384]{1,0:T(8,128)(2,1)S(1)}, bf16[320,384]{1,0:T(8,128)(2,1)S(1)}, bf16[384,384]{1,0:T(8,128)(2,...) custom-call(bf16[1,384]{1,0:T(2,128)(2,1)S(1)} %reshape.15.gain, ...), custom_call_target="tpu_custom_call" | custom-call | flops 1000 | bytes 1000 | tf_op jit(solution)/shard_map/pallas_call | solution.py:29
  9.1 0.0 copy-start.8
  9.1 3.3 %shard_map.93 = (f32[3,640,192]{2,1,0:T(8,128)S(1)}, bf16[240,128]{1,0:T(8,128)(2,1)S(1)}, bf16[240,128]{1,0:T(8,128)(2,1)S(1)}) custom-call(bf16[2,640,384]{2,1,0:T(8,128)(2,1)S(1)} %bitcast.7, bf16[3,3,3,192,384]{4,3,2,1,0:T(8,128)(2,1)S(1)} %bitcast.4), custom_call_target="tpu_custom_call" | custom-call | flops 1000 | bytes 1000 | tf_op jit(solution)/shard_map/pallas_call | solution.py:29
  12.4 0.2 collective-permute-done.3.refs_2_
  12.6 0.3 collective-permute-start.4
  12.9 0.3 collective-permute-start.5
  13.2 4.3 %collective-permute-start.8 = (bf16[960,128]{1,0:T(8,128)(2,1)S(1)}, bf16[960,128]{1,0:T(8,128)(2,1)S(1)}, u32[]{:S(2)}, u32[]{:S(2)}) collective-permute-start(bf16[960,128]{1,0:T(8,128)(2,1)S(1)} %collective-permute-done.3.refs_2_), channel_id=1, source_target_pairs={{0,12},{4,0},{8,4},{12,8},{1,13},{5,1},{9,5},{13,9},{2,14},{6,2},{... | collective-permute-start | bytes 737288 | tf_op jit(solution)/shard_map/ppermute | solution.py:18
  17.5 0.0 collective-permute-done.4
  17.5 0.0 collective-permute-done.5
  17.5 0.3 collective-permute-done.2.refs_0_
  17.8 0.1 collective-permute-start.6
  17.9 0.5 %collective-permute-start.7 = (bf16[480,128]{1,0:T(8,128)(2,1)S(1)}, bf16[480,128]{1,0:T(8,128)(2,1)S(1)}, u32[]{:S(2)}, u32[]{:S(2)}) collective-permute-start(bf16[480,128]{1,0:T(8,128)(2,1)S(1)} %get-tuple-element.68), channel_id=1, source_target_pairs={{0,1},{1,0},{2,3},{3,2},{4,5},{5,4},{6,7},{7,6},{8,9},{9,8},{10,11... | collective-permute-start | bytes 368648 | tf_op jit(solution)/shard_map/ppermute | solution.py:18
  18.4 0.8 %collective-permute-done.6 = bf16[480,128]{1,0:T(8,128)(2,1)S(1)} collective-permute-done((bf16[480,128]{1,0:T(8,128)(2,1)S(1)}, bf16[480,128]{1,0:T(8,128)(2,1)S(1)}, u32[]{:S(2)}, u32[]{:S(2)}) %collective-permute-start.6) | collective-permute-done | bytes 122912 | tf_op jit(solution)/shard_map/ppermute | solution.py:18
  19.2 0.2 collective-permute-done.7
  19.4 3.4 %shard_map.94 = (bf16[480,384]{1,0:T(8,128)(2,1)S(1)}, bf16[480,384]{1,0:T(8,128)(2,1)S(1)}, f32[480,128]{1,0:T(8,128)S(1)}, f32[480,128]{1,0:T(8,128)S(1)}, f32[480,384]{1,0:T(8,128)S(1)}) custom-call(bf16[1,384]{1,0:T(2,128)(2,1)S(1)} %reshape.15.gain, bf16[320,384]{1,0:T(8,128)(2,1)S(1)} %get-tuple-element.38.raw_own, ...), custom_call_target="tpu_custom_call" | custom-call | flops 1000 | bytes 1000 | tf_op jit(solution)/shard_map/pallas_call | solution.py:29
  22.7 0.2 collective-permute-done.8.mine
  22.9 0.2 collective-permute-start.9
  23.2 1.3 %collective-permute-done.9.theirs = bf16[960,128]{1,0:T(8,128)(2,1)S(1)} collective-permute-done((bf16[960,128]{1,0:T(8,128)(2,1)S(1)}, bf16[960,128]{1,0:T(8,128)(2,1)S(1)}, u32[]{:S(2)}, u32[]{:S(2)}) %collective-permute-start.9) | collective-permute-done | bytes 245792 | tf_op jit(solution)/shard_map/ppermute | solution.py:18
  24.4 2.1 %shard_map.95 = (bf16[480,384]{1,0:T(8,128)(2,1)S(1)}, bf16[480,384]{1,0:T(8,128)(2,1)S(1)}) custom-call(bf16[1,384]{1,0:T(2,128)(2,1)S(1)} %reshape.15.gain, bf16[1,384]{1,0:T(2,128)(2,1)S(1)} %reshape.16.gain_two, bf16[384,384]{1,0:T(8,128)(2,1)S(1)} %get-tuple-element.36.w_mixed, bf16[480,384]{1,0:T(8,128)(2,1)S(1)} %get-tuple-element.48.query, ...), custom_call_target="tpu_custom_call" | custom-call | flops 1000 | bytes 1000 | tf_op jit(solution)/shard_map/pallas_call | solution.py:29
  26.5 0.3 collective-permute-start.10
  26.8 1.5 %collective-permute-done.10.other = bf16[480,384]{1,0:T(8,128)(2,1)S(1)} collective-permute-done((bf16[480,384]{1,0:T(8,128)(2,1)S(1)}, bf16[480,384]{1,0:T(8,128)(2,1)S(1)}, u32[]{:S(2)}, u32[]{:S(2)}) %collective-permute-start.10) | collective-permute-done | bytes 368672 | tf_op jit(solution)/shard_map/ppermute | solution.py:18
  28.3 1.6 %shard_map.96 = bf16[960,128]{1,0:T(8,128)(2,1)S(1)} custom-call(bf16[480,384]{1,0:T(8,128)(2,1)S(1)} %get-tuple-element.57.act, bf16[480,384]{1,0:T(8,128)(2,1)S(1)} %collective-permute-done.10.other, bf16[3,3,3,192,384]{4,3,2,1,0:T(8,128)(2,1)S(1)} %bitcast.5), custom_call_target="tpu_custom_call" | custom-call | flops 1000 | bytes 1000 | tf_op jit(solution)/shard_map/pallas_call | solution.py:29
  29.8 0.1 collective-permute-start.14
  29.9 0.2 shard_map.97
  30.2 0.3 collective-permute-start.11
  30.4 0.7 %collective-permute-start.12 = (bf16[240,128]{1,0:T(8,128)(2,1)S(1)}, bf16[240,128]{1,0:T(8,128)(2,1)S(1)}, u32[]{:S(2)}, u32[]{:S(2)}) collective-permute-start(bf16[240,128]{1,0:T(8,128)(2,1)S(1)} %get-tuple-element.64), channel_id=1, source_target_pairs={{0,0},{4,8},{8,4},{12,12},{1,1},{5,9},{9,5},{13,13},{2,2},{6,10},{... | collective-permute-start | bytes 184328 | tf_op jit(solution)/shard_map/ppermute | solution.py:429
  31.1 3.6 %collective-permute-start.13 = (bf16[240,128]{1,0:T(8,128)(2,1)S(1)}, bf16[240,128]{1,0:T(8,128)(2,1)S(1)}, u32[]{:S(2)}, u32[]{:S(2)}) collective-permute-start(bf16[240,128]{1,0:T(8,128)(2,1)S(1)} %get-tuple-element.65), channel_id=1, source_target_pairs={{0,4},{4,0},{8,12},{12,8},{1,5},{5,1},{9,13},{13,9},{2,6},{6,2},{1... | collective-permute-start | bytes 184328 | tf_op jit(solution)/shard_map/ppermute | solution.py:432
  34.7 0.0 collective-permute-done.11.theirs
  34.7 1.6 %shard_map.98.rest = f32[640,192]{1,0:T(8,128)S(1)} custom-call(bf16[480,384]{1,0:T(8,128)(2,1)S(1)} %get-tuple-element.57.act, bf16[480,384]{1,0:T(8,128)(2,1)S(1)} %collective-permute-done.10.other, f32[3,640,192]{2,1,0:T(8,128)S(1)} %get-tuple-element.58.cached, bf16[320,192]{1,0:T(8,128)(2,1)S(1)} %get-tuple-element.60.keep, ...), custom_call_target="tpu_custom_call" | custom-call | flops 1000 | bytes 1000 | tf_op jit(solution)/shard_map/pallas_call | solution.py:29
  36.3 0.0 collective-permute-done.12.outer
  36.3 0.6 %collective-permute-done.13.inner = bf16[240,128]{1,0:T(8,128)(2,1)S(1)} collective-permute-done((bf16[240,128]{1,0:T(8,128)(2,1)S(1)}, bf16[240,128]{1,0:T(8,128)(2,1)S(1)}, u32[]{:S(2)}, u32[]{:S(2)}) %collective-permute-start.13) | collective-permute-done | bytes 61472 | tf_op jit(solution)/shard_map/ppermute | solution.py:432
  36.9 0.1 shard_map.99.rest
  37.0 0.8 %shard_map.100.refs_1_ = bf16[640,192]{1,0:T(8,128)(2,1)} custom-call(f32[640,192]{1,0:T(8,128)S(1)} %shard_map.99.rest), custom_call_target="tpu_custom_call" | custom-call | flops 1000 | bytes 1000 | tf_op jit(solution)/shard_map/pallas_call | solution.py:29
  37.8 0.2 collective-permute-done.14.refs_0_
  (19 shorter events, 0.1 us)
Async XLA Ops:
  0.0 1.0 %copy-start.6 = (bf16[1,4,160,192]{3,2,1,0:T(8,128)(2,1)S(1)}, bf16[1,4,160,192]{3,2,1,0:T(8,128)(2,1)}, u32[]{:S(2)}) copy-start(bf16[1,4,160,192]{3,2,1,0:T(8,128)(2,1)} %param.9) | copy-start | bytes 737284
  1.0 5.8 %copy-start.7 = (bf16[384]{0:T(512)(128)(2,1)S(1)}, bf16[384]{0:T(512)(128)(2,1)}, u32[]{:S(2)}) copy-start(bf16[384]{0:T(512)(128)(2,1)} %param.11) | copy-start | bytes 2308
  1.0 6.9 %copy-start.2 = (bf16[384,384]{1,0:T(8,128)(2,1)S(1)}, bf16[384,384]{1,0:T(8,128)(2,1)}, u32[]{:S(2)}) copy-start(bf16[384,384]{1,0:T(8,128)(2,1)} %w_query.1) | copy-start | bytes 884740
  1.0 6.9 %copy-start.3 = (bf16[384,384]{1,0:T(8,128)(2,1)S(1)}, bf16[384,384]{1,0:T(8,128)(2,1)}, u32[]{:S(2)}) copy-start(bf16[384,384]{1,0:T(8,128)(2,1)} %w_key.1) | copy-start | bytes 884740
  1.0 6.9 %copy-start.4 = (bf16[384,384]{1,0:T(8,128)(2,1)S(1)}, bf16[384,384]{1,0:T(8,128)(2,1)}, u32[]{:S(2)}) copy-start(bf16[384,384]{1,0:T(8,128)(2,1)} %w_value.1) | copy-start | bytes 884740
  1.0 6.9 %copy-start.5 = (bf16[384,384]{1,0:T(8,128)(2,1)S(1)}, bf16[384,384]{1,0:T(8,128)(2,1)}, u32[]{:S(2)}) copy-start(bf16[384,384]{1,0:T(8,128)(2,1)} %w_out.1) | copy-start | bytes 884740
  1.0 8.1 %copy-start = (bf16[3,3,3,384,192]{3,4,2,1,0:T(8,128)(2,1)S(1)}, bf16[3,3,3,384,192]{3,4,2,1,0:T(8,128)(2,1)}, u32[]{:S(2)}) copy-start(bf16[3,3,3,384,192]{3,4,2,1,0:T(8,128)(2,1)} %param.17) | copy-start | bytes 11943940
  1.0 8.1 %copy-start.1 = (bf16[2,4,160,384]{3,2,1,0:T(8,128)(2,1)S(1)}, bf16[2,4,160,384]{3,2,1,0:T(8,128)(2,1)}, u32[]{:S(2)}) copy-start(bf16[2,4,160,384]{3,2,1,0:T(8,128)(2,1)} %param.10) | copy-start | bytes 2949124
  1.1 11.5 %collective-permute-start.3 = (bf16[960,128]{1,0:T(8,128)(2,1)S(1)}, bf16[960,128]{1,0:T(8,128)(2,1)S(1)}, u32[]{:S(2)}, u32[]{:S(2)}) collective-permute-start(bf16[960,128]{1,0:T(8,128)(2,1)S(1)} %shard_map.91.mine), channel_id=1, source_target_pairs={{0,12},{4,0},{8,4},{12,8},{1,13},{5,1},{9,5},{13,9},{2,14},{6,2},{... | collective-permute-start | bytes 737288 | tf_op jit(solution)/shard_map/ppermute | solution.py:18
  6.2 1.4 %collective-permute-start = (bf16[480,128]{1,0:T(8,128)(2,1)S(1)}, bf16[480,128]{1,0:T(8,128)(2,1)S(1)}, u32[]{:S(2)}, u32[]{:S(2)}) collective-permute-start(bf16[480,128]{1,0:T(8,128)(2,1)S(1)} %get-tuple-element.71), channel_id=1, source_target_pairs={{0,1},{1,0},{2,3},{3,2},{4,5},{5,4},{6,7},{7,6},{8,9},{9,8},{10,11... | collective-permute-start | bytes 368648 | tf_op jit(solution)/shard_map/ppermute | solution.py:18
  6.3 1.5 %collective-permute-start.1 = (bf16[480,128]{1,0:T(8,128)(2,1)S(1)}, bf16[480,128]{1,0:T(8,128)(2,1)S(1)}, u32[]{:S(2)}, u32[]{:S(2)}) collective-permute-start(bf16[480,128]{1,0:T(8,128)(2,1)S(1)} %get-tuple-element.72), channel_id=1, source_target_pairs={{0,1},{1,0},{2,3},{3,2},{4,5},{5,4},{6,7},{7,6},{8,9},{9,8},{10,11... | collective-permute-start | bytes 368648 | tf_op jit(solution)/shard_map/ppermute | solution.py:18
  6.8 10.9 %collective-permute-start.2 = (bf16[960,128]{1,0:T(8,128)(2,1)S(1)}, bf16[960,128]{1,0:T(8,128)(2,1)S(1)}, u32[]{:S(2)}, u32[]{:S(2)}) collective-permute-start(bf16[960,128]{1,0:T(8,128)(2,1)S(1)} %shard_map.91.mine), channel_id=1, source_target_pairs={{0,4},{4,8},{8,12},{12,0},{1,5},{5,9},{9,13},{13,1},{2,6},{6,10},{... | collective-permute-start | bytes 737288 | tf_op jit(solution)/shard_map/ppermute | solution.py:18
  9.1 14.0 %copy-start.8 = (bf16[384]{0:T(512)(128)(2,1)S(1)}, bf16[384]{0:T(512)(128)(2,1)}, u32[]{:S(2)}) copy-start(bf16[384]{0:T(512)(128)(2,1)} %param.12) | copy-start | bytes 2308
  12.6 4.9 %collective-permute-start.4 = (bf16[480,128]{1,0:T(8,128)(2,1)S(1)}, bf16[480,128]{1,0:T(8,128)(2,1)S(1)}, u32[]{:S(2)}, u32[]{:S(2)}) collective-permute-start(bf16[480,128]{1,0:T(8,128)(2,1)S(1)} %get-tuple-element.69), channel_id=1, source_target_pairs={{0,1},{1,0},{2,3},{3,2},{4,5},{5,4},{6,7},{7,6},{8,9},{9,8},{10,11... | collective-permute-start | bytes 368648 | tf_op jit(solution)/shard_map/ppermute | solution.py:18
  12.9 4.6 %collective-permute-start.5 = (bf16[480,128]{1,0:T(8,128)(2,1)S(1)}, bf16[480,128]{1,0:T(8,128)(2,1)S(1)}, u32[]{:S(2)}, u32[]{:S(2)}) collective-permute-start(bf16[480,128]{1,0:T(8,128)(2,1)S(1)} %get-tuple-element.70), channel_id=1, source_target_pairs={{0,1},{1,0},{2,3},{3,2},{4,5},{5,4},{6,7},{7,6},{8,9},{9,8},{10,11... | collective-permute-start | bytes 368648 | tf_op jit(solution)/shard_map/ppermute | solution.py:18
  13.2 9.7 %collective-permute-start.8 = (bf16[960,128]{1,0:T(8,128)(2,1)S(1)}, bf16[960,128]{1,0:T(8,128)(2,1)S(1)}, u32[]{:S(2)}, u32[]{:S(2)}) collective-permute-start(bf16[960,128]{1,0:T(8,128)(2,1)S(1)} %collective-permute-done.3.refs_2_), channel_id=1, source_target_pairs={{0,12},{4,0},{8,4},{12,8},{1,13},{5,1},{9,5},{13,9},{2,14},{6,2},{... | collective-permute-start | bytes 737288 | tf_op jit(solution)/shard_map/ppermute | solution.py:18
  17.8 1.4 %collective-permute-start.6 = (bf16[480,128]{1,0:T(8,128)(2,1)S(1)}, bf16[480,128]{1,0:T(8,128)(2,1)S(1)}, u32[]{:S(2)}, u32[]{:S(2)}) collective-permute-start(bf16[480,128]{1,0:T(8,128)(2,1)S(1)} %get-tuple-element.67), channel_id=1, source_target_pairs={{0,1},{1,0},{2,3},{3,2},{4,5},{5,4},{6,7},{7,6},{8,9},{9,8},{10,11... | collective-permute-start | bytes 368648 | tf_op jit(solution)/shard_map/ppermute | solution.py:18
  17.9 1.5 %collective-permute-start.7 = (bf16[480,128]{1,0:T(8,128)(2,1)S(1)}, bf16[480,128]{1,0:T(8,128)(2,1)S(1)}, u32[]{:S(2)}, u32[]{:S(2)}) collective-permute-start(bf16[480,128]{1,0:T(8,128)(2,1)S(1)} %get-tuple-element.68), channel_id=1, source_target_pairs={{0,1},{1,0},{2,3},{3,2},{4,5},{5,4},{6,7},{7,6},{8,9},{9,8},{10,11... | collective-permute-start | bytes 368648 | tf_op jit(solution)/shard_map/ppermute | solution.py:18
  22.9 1.5 %collective-permute-start.9 = (bf16[960,128]{1,0:T(8,128)(2,1)S(1)}, bf16[960,128]{1,0:T(8,128)(2,1)S(1)}, u32[]{:S(2)}, u32[]{:S(2)}) collective-permute-start(bf16[960,128]{1,0:T(8,128)(2,1)S(1)} %collective-permute-done.8.mine), channel_id=1, source_target_pairs={{0,1},{1,0},{2,3},{3,2},{4,5},{5,4},{6,7},{7,6},{8,9},{9,8},{10,11... | collective-permute-start | bytes 737288 | tf_op jit(solution)/shard_map/ppermute | solution.py:18
  26.5 1.8 %collective-permute-start.10 = (bf16[480,384]{1,0:T(8,128)(2,1)S(1)}, bf16[480,384]{1,0:T(8,128)(2,1)S(1)}, u32[]{:S(2)}, u32[]{:S(2)}) collective-permute-start(bf16[480,384]{1,0:T(8,128)(2,1)S(1)} %get-tuple-element.57.act), channel_id=1, source_target_pairs={{0,1},{1,0},{2,3},{3,2},{4,5},{5,4},{6,7},{7,6},{8,9},{9,8},{10,11... | collective-permute-start | bytes 1105928 | tf_op jit(solution)/shard_map/ppermute | solution.py:18
  29.8 8.2 %collective-permute-start.14 = (bf16[960,128]{1,0:T(8,128)(2,1)S(1)}, bf16[960,128]{1,0:T(8,128)(2,1)S(1)}, u32[]{:S(2)}, u32[]{:S(2)}) collective-permute-start(bf16[960,128]{1,0:T(8,128)(2,1)S(1)} %shard_map.96), channel_id=1, source_target_pairs={{0,2},{2,0},{1,3},{3,1},{4,6},{6,4},{5,7},{7,5},{8,10},{10,8},{9,1... | collective-permute-start | bytes 737288 | tf_op jit(solution)/shard_map/ppermute | solution.py:18
  30.2 4.5 %collective-permute-start.11 = (bf16[320,192]{1,0:T(8,128)(2,1)S(1)}, bf16[320,192]{1,0:T(8,128)(2,1)S(1)}, u32[]{:S(2)}, u32[]{:S(2)}) collective-permute-start(bf16[320,192]{1,0:T(8,128)(2,1)S(1)} %get-tuple-element.61), channel_id=1, source_target_pairs={{0,1},{1,0},{2,3},{3,2},{4,5},{5,4},{6,7},{7,6},{8,9},{9,8},{10,11... | collective-permute-start | bytes 368648 | tf_op jit(solution)/shard_map/ppermute | solution.py:18
  30.4 5.8 %collective-permute-start.12 = (bf16[240,128]{1,0:T(8,128)(2,1)S(1)}, bf16[240,128]{1,0:T(8,128)(2,1)S(1)}, u32[]{:S(2)}, u32[]{:S(2)}) collective-permute-start(bf16[240,128]{1,0:T(8,128)(2,1)S(1)} %get-tuple-element.64), channel_id=1, source_target_pairs={{0,0},{4,8},{8,4},{12,12},{1,1},{5,9},{9,5},{13,13},{2,2},{6,10},{... | collective-permute-start | bytes 184328 | tf_op jit(solution)/shard_map/ppermute | solution.py:429
  31.1 5.8 %collective-permute-start.13 = (bf16[240,128]{1,0:T(8,128)(2,1)S(1)}, bf16[240,128]{1,0:T(8,128)(2,1)S(1)}, u32[]{:S(2)}, u32[]{:S(2)}) collective-permute-start(bf16[240,128]{1,0:T(8,128)(2,1)S(1)} %get-tuple-element.65), channel_id=1, source_target_pairs={{0,4},{4,0},{8,12},{12,8},{1,5},{5,1},{9,13},{13,9},{2,6},{6,2},{1... | collective-permute-start | bytes 184328 | tf_op jit(solution)/shard_map/ppermute | solution.py:432

commit v8 on v7

--- a/solution.py
+++ b/solution.py
@@ -176,21 +176,22 @@
     core, place, places, _ = place_of()
     act_out, joined_out, total_now, accum_now = refs
     keys = rms_scaled(joined_halves(core, mine, theirs), gain[...]).astype(BF)
-    scores = dot_t(query[...], keys) - top[:, :1]
-    weights = jnp.exp2(scores)
+    scores = dot_t(query[...], keys)
+    weights = jnp.exp2(scores - top[:, :1])
     total_now[...] = total[:, :1] + jnp.sum(weights, axis=-1, keepdims=True)
     accum_now[...] = accum[...] + dot(weights.astype(BF), keys)
 
-    @pl.when(jnp.max(scores) > 60.0)
+    @pl.when(jnp.max(jnp.max(scores, axis=-1, keepdims=True) - top[:, :1]) > 60.0)
     def _():
         _, total_now[...], accum_now[...] = attend(query[...], [keys], top[:, :1], total[:, :1], accum[...])
 
-    mixed = (accum_now[...] / total_now[...]).astype(BF)
+    mixed = (accum_now[...] * (1.0 / total_now[...])).astype(BF)
     joined = (raw[...].astype(F32) + dot(mixed, w_mixed[...])).astype(BF)
     joined_out[...] = joined
     edge = joined.shape[0] // 3
     act = rms_scaled(joined.astype(F32), gain_two[...])
-    act = act / (1.0 + jnp.exp(-act))
+    act = 0.5 * act
+    act = act + act * jnp.tanh(act)
     row = lax.broadcasted_iota(jnp.int32, (act.shape[0], 1), 0)
     beyond = ((core == 0) & (place == 0) & (row < edge)) | (
         (core == 1) & (place == places - 1) & (row >= 2 * edge)

time: 38.3 us -> 38.2 us (level)
  no operation moved by 1% of the time
where the time goes in v8:
time: 38.2 us; the launch traced here: 38.1 us
  starting transfers between devices  16.2 us (42%)
  Pallas kernels  14.2 us (37%)
  waiting for transfers between devices  6.14 us (16%)
  local copies, waits for them, and re-layouts  1.06 us (3%)
    pallas_call x11, Pallas kernels, call(): pl.pallas_call(kernel, out_shape=outs, in_specs=[vmem] * (len(args) - int...  14.2 us
    ppermute x13, starting transfers between devices, cycle(): lax.ppermute(array, axis, [(i, (i + by) % count) for i in range(count)])  12 us
    ppermute x13, waiting for transfers between devices, cycle(): lax.ppermute(array, axis, [(i, (i + by) % count) for i in range(count)])  5.53 us
    ppermute x1, starting transfers between devices, body(): inner = lax.ppermute(inner, 'space', [(i, i ^ 1) for i in range(places)])  3.57 us
    unnamed x18, local copies, waits for them, and re-layouts  1.01 us
  transfers between devices with their start and end apart: 15, of which 11 were waited for; matrix products, arithmetic and copies ran while one was open for 0% of the time, Pallas kernels for 28%

profile of v8, /device:TPU:0, one launch (start us, length us, event | category | flops | bytes accessed | tf_op | source)
XLA Modules:
  0.0 38.1 jit_solution(18223881735329606037)
XLA Ops:
  0.0 1.0 %copy-done.6 = bf16[1,4,160,192]{3,2,1,0:T(8,128)(2,1)S(1)} copy-done((bf16[1,4,160,192]{3,2,1,0:T(8,128)(2,1)S(1)}, bf16[1,4,160,192]{3,2,1,0:T(8,128)(2,1)}, u32[]{:S(2)}) %copy-start.6) | copy-done | bytes 245784
  1.0 0.0 copy-start.5
  1.0 0.0 copy-start
  1.0 0.0 copy-start.1
  1.0 0.1 shard_map.91.mine
  1.1 5.1 %collective-permute-start.3 = (bf16[960,128]{1,0:T(8,128)(2,1)S(1)}, bf16[960,128]{1,0:T(8,128)(2,1)S(1)}, u32[]{:S(2)}, u32[]{:S(2)}) collective-permute-start(bf16[960,128]{1,0:T(8,128)(2,1)S(1)} %shard_map.91.mine), channel_id=1, source_target_pairs={{0,12},{4,0},{8,4},{12,8},{1,13},{5,1},{9,5},{13,9},{2,14},{6,2},{... | collective-permute-start | bytes 737288 | tf_op jit(solution)/shard_map/ppermute | solution.py:18
  6.2 0.1 collective-permute-start
  6.3 0.5 %collective-permute-start.1 = (bf16[480,128]{1,0:T(8,128)(2,1)S(1)}, bf16[480,128]{1,0:T(8,128)(2,1)S(1)}, u32[]{:S(2)}, u32[]{:S(2)}) collective-permute-start(bf16[480,128]{1,0:T(8,128)(2,1)S(1)} %get-tuple-element.72), channel_id=1, source_target_pairs={{0,1},{1,0},{2,3},{3,2},{4,5},{5,4},{6,7},{7,6},{8,9},{9,8},{10,11... | collective-permute-start | bytes 368648 | tf_op jit(solution)/shard_map/ppermute | solution.py:18
  6.8 0.0 collective-permute-start.2
  6.8 0.0 copy-done.7
  6.8 0.8 %collective-permute-done = bf16[480,128]{1,0:T(8,128)(2,1)S(1)} collective-permute-done((bf16[480,128]{1,0:T(8,128)(2,1)S(1)}, bf16[480,128]{1,0:T(8,128)(2,1)S(1)}, u32[]{:S(2)}, u32[]{:S(2)}) %collective-permute-start) | collective-permute-done | bytes 122912 | tf_op jit(solution)/shard_map/ppermute | solution.py:18
  7.6 0.2 collective-permute-done.1
  7.9 1.2 %shard_map.92 = (bf16[320,384]{1,0:T(8,128)(2,1)S(1)}, bf16[640,384]{1,0:T(8,128)(2,1)S(1)}, bf16[320,384]{1,0:T(8,128)(2,1)S(1)}, bf16[384,384]{1,0:T(8,128)(2,...) custom-call(bf16[1,384]{1,0:T(2,128)(2,1)S(1)} %reshape.15.gain, ...), custom_call_target="tpu_custom_call" | custom-call | flops 1000 | bytes 1000 | tf_op jit(solution)/shard_map/pallas_call | solution.py:29
  9.1 0.0 copy-done
  9.1 0.0 copy-done.1
  9.1 0.0 copy-start.8
  9.1 3.3 %shard_map.93 = (f32[3,640,192]{2,1,0:T(8,128)S(1)}, bf16[240,128]{1,0:T(8,128)(2,1)S(1)}, bf16[240,128]{1,0:T(8,128)(2,1)S(1)}) custom-call(bf16[2,640,384]{2,1,0:T(8,128)(2,1)S(1)} %bitcast.7, bf16[3,3,3,192,384]{4,3,2,1,0:T(8,128)(2,1)S(1)} %bitcast.4), custom_call_target="tpu_custom_call" | custom-call | flops 1000 | bytes 1000 | tf_op jit(solution)/shard_map/pallas_call | solution.py:29
  12.4 0.2 collective-permute-done.3.refs_2_
  12.6 0.3 collective-permute-start.4
  12.9 0.3 collective-permute-start.5
  13.2 4.3 %collective-permute-start.8 = (bf16[960,128]{1,0:T(8,128)(2,1)S(1)}, bf16[960,128]{1,0:T(8,128)(2,1)S(1)}, u32[]{:S(2)}, u32[]{:S(2)}) collective-permute-start(bf16[960,128]{1,0:T(8,128)(2,1)S(1)} %collective-permute-done.3.refs_2_), channel_id=1, source_target_pairs={{0,12},{4,0},{8,4},{12,8},{1,13},{5,1},{9,5},{13,9},{2,14},{6,2},{... | collective-permute-start | bytes 737288 | tf_op jit(solution)/shard_map/ppermute | solution.py:18
  17.5 0.0 collective-permute-done.4
  17.5 0.0 collective-permute-done.5
  17.5 0.3 collective-permute-done.2.refs_0_
  17.8 0.1 collective-permute-start.6
  17.9 0.5 %collective-permute-start.7 = (bf16[480,128]{1,0:T(8,128)(2,1)S(1)}, bf16[480,128]{1,0:T(8,128)(2,1)S(1)}, u32[]{:S(2)}, u32[]{:S(2)}) collective-permute-start(bf16[480,128]{1,0:T(8,128)(2,1)S(1)} %get-tuple-element.68), channel_id=1, source_target_pairs={{0,1},{1,0},{2,3},{3,2},{4,5},{5,4},{6,7},{7,6},{8,9},{9,8},{10,11... | collective-permute-start | bytes 368648 | tf_op jit(solution)/shard_map/ppermute | solution.py:18
  18.4 0.8 %collective-permute-done.6 = bf16[480,128]{1,0:T(8,128)(2,1)S(1)} collective-permute-done((bf16[480,128]{1,0:T(8,128)(2,1)S(1)}, bf16[480,128]{1,0:T(8,128)(2,1)S(1)}, u32[]{:S(2)}, u32[]{:S(2)}) %collective-permute-start.6) | collective-permute-done | bytes 122912 | tf_op jit(solution)/shard_map/ppermute | solution.py:18
  19.2 0.2 collective-permute-done.7
  19.4 3.4 %shard_map.94 = (bf16[480,384]{1,0:T(8,128)(2,1)S(1)}, bf16[480,384]{1,0:T(8,128)(2,1)S(1)}, f32[480,128]{1,0:T(8,128)S(1)}, f32[480,128]{1,0:T(8,128)S(1)}, f32[480,384]{1,0:T(8,128)S(1)}) custom-call(bf16[1,384]{1,0:T(2,128)(2,1)S(1)} %reshape.15.gain, bf16[320,384]{1,0:T(8,128)(2,1)S(1)} %get-tuple-element.38.raw_own, ...), custom_call_target="tpu_custom_call" | custom-call | flops 1000 | bytes 1000 | tf_op jit(solution)/shard_map/pallas_call | solution.py:29
  22.7 0.2 collective-permute-done.8.mine
  22.9 0.2 collective-permute-start.9
  23.2 1.3 %collective-permute-done.9.theirs = bf16[960,128]{1,0:T(8,128)(2,1)S(1)} collective-permute-done((bf16[960,128]{1,0:T(8,128)(2,1)S(1)}, bf16[960,128]{1,0:T(8,128)(2,1)S(1)}, u32[]{:S(2)}, u32[]{:S(2)}) %collective-permute-start.9) | collective-permute-done | bytes 245792 | tf_op jit(solution)/shard_map/ppermute | solution.py:18
  24.4 2.0 %shard_map.95 = (bf16[480,384]{1,0:T(8,128)(2,1)S(1)}, bf16[480,384]{1,0:T(8,128)(2,1)S(1)}) custom-call(bf16[1,384]{1,0:T(2,128)(2,1)S(1)} %reshape.15.gain, bf16[1,384]{1,0:T(2,128)(2,1)S(1)} %reshape.16.gain_two, bf16[384,384]{1,0:T(8,128)(2,1)S(1)} %get-tuple-element.36.w_mixed, bf16[480,384]{1,0:T(8,128)(2,1)S(1)} %get-tuple-element.48.query, ...), custom_call_target="tpu_custom_call" | custom-call | flops 1000 | bytes 1000 | tf_op jit(solution)/shard_map/pallas_call | solution.py:29
  26.4 0.3 collective-permute-start.10
  26.7 1.5 %collective-permute-done.10.other = bf16[480,384]{1,0:T(8,128)(2,1)S(1)} collective-permute-done((bf16[480,384]{1,0:T(8,128)(2,1)S(1)}, bf16[480,384]{1,0:T(8,128)(2,1)S(1)}, u32[]{:S(2)}, u32[]{:S(2)}) %collective-permute-start.10) | collective-permute-done | bytes 368672 | tf_op jit(solution)/shard_map/ppermute | solution.py:18
  28.2 1.6 %shard_map.96 = bf16[960,128]{1,0:T(8,128)(2,1)S(1)} custom-call(bf16[480,384]{1,0:T(8,128)(2,1)S(1)} %get-tuple-element.57.act, bf16[480,384]{1,0:T(8,128)(2,1)S(1)} %collective-permute-done.10.other, bf16[3,3,3,192,384]{4,3,2,1,0:T(8,128)(2,1)S(1)} %bitcast.5), custom_call_target="tpu_custom_call" | custom-call | flops 1000 | bytes 1000 | tf_op jit(solution)/shard_map/pallas_call | solution.py:29
  29.8 0.1 collective-permute-start.14
  29.8 0.2 shard_map.97
  30.1 0.3 collective-permute-start.11
  30.4 0.7 %collective-permute-start.12 = (bf16[240,128]{1,0:T(8,128)(2,1)S(1)}, bf16[240,128]{1,0:T(8,128)(2,1)S(1)}, u32[]{:S(2)}, u32[]{:S(2)}) collective-permute-start(bf16[240,128]{1,0:T(8,128)(2,1)S(1)} %get-tuple-element.64), channel_id=1, source_target_pairs={{0,0},{4,8},{8,4},{12,12},{1,1},{5,9},{9,5},{13,13},{2,2},{6,10},{... | collective-permute-start | bytes 184328 | tf_op jit(solution)/shard_map/ppermute | solution.py:430
  31.1 3.6 %collective-permute-start.13 = (bf16[240,128]{1,0:T(8,128)(2,1)S(1)}, bf16[240,128]{1,0:T(8,128)(2,1)S(1)}, u32[]{:S(2)}, u32[]{:S(2)}) collective-permute-start(bf16[240,128]{1,0:T(8,128)(2,1)S(1)} %get-tuple-element.65), channel_id=1, source_target_pairs={{0,4},{4,0},{8,12},{12,8},{1,5},{5,1},{9,13},{13,9},{2,6},{6,2},{1... | collective-permute-start | bytes 184328 | tf_op jit(solution)/shard_map/ppermute | solution.py:433
  34.6 0.0 collective-permute-done.11.theirs
  34.6 1.6 %shard_map.98.rest = f32[640,192]{1,0:T(8,128)S(1)} custom-call(bf16[480,384]{1,0:T(8,128)(2,1)S(1)} %get-tuple-element.57.act, bf16[480,384]{1,0:T(8,128)(2,1)S(1)} %collective-permute-done.10.other, f32[3,640,192]{2,1,0:T(8,128)S(1)} %get-tuple-element.58.cached, bf16[320,192]{1,0:T(8,128)(2,1)S(1)} %get-tuple-element.60.keep, ...), custom_call_target="tpu_custom_call" | custom-call | flops 1000 | bytes 1000 | tf_op jit(solution)/shard_map/pallas_call | solution.py:29
  36.2 0.0 collective-permute-done.12.outer
  36.2 0.6 %collective-permute-done.13.inner = bf16[240,128]{1,0:T(8,128)(2,1)S(1)} collective-permute-done((bf16[240,128]{1,0:T(8,128)(2,1)S(1)}, bf16[240,128]{1,0:T(8,128)(2,1)S(1)}, u32[]{:S(2)}, u32[]{:S(2)}) %collective-permute-start.13) | collective-permute-done | bytes 61472 | tf_op jit(solution)/shard_map/ppermute | solution.py:433
  36.8 0.1 shard_map.99.rest
  36.9 0.8 %shard_map.100.refs_1_ = bf16[640,192]{1,0:T(8,128)(2,1)} custom-call(f32[640,192]{1,0:T(8,128)S(1)} %shard_map.99.rest), custom_call_target="tpu_custom_call" | custom-call | flops 1000 | bytes 1000 | tf_op jit(solution)/shard_map/pallas_call | solution.py:29
  37.7 0.2 collective-permute-done.14.refs_0_
  (19 shorter events, 0.1 us)
Async XLA Ops:
  0.0 1.0 %copy-start.6 = (bf16[1,4,160,192]{3,2,1,0:T(8,128)(2,1)S(1)}, bf16[1,4,160,192]{3,2,1,0:T(8,128)(2,1)}, u32[]{:S(2)}) copy-start(bf16[1,4,160,192]{3,2,1,0:T(8,128)(2,1)} %param.9) | copy-start | bytes 737284
  1.0 5.8 %copy-start.7 = (bf16[384]{0:T(512)(128)(2,1)S(1)}, bf16[384]{0:T(512)(128)(2,1)}, u32[]{:S(2)}) copy-start(bf16[384]{0:T(512)(128)(2,1)} %param.11) | copy-start | bytes 2308
  1.0 6.9 %copy-start.2 = (bf16[384,384]{1,0:T(8,128)(2,1)S(1)}, bf16[384,384]{1,0:T(8,128)(2,1)}, u32[]{:S(2)}) copy-start(bf16[384,384]{1,0:T(8,128)(2,1)} %w_query.1) | copy-start | bytes 884740
  1.0 6.9 %copy-start.3 = (bf16[384,384]{1,0:T(8,128)(2,1)S(1)}, bf16[384,384]{1,0:T(8,128)(2,1)}, u32[]{:S(2)}) copy-start(bf16[384,384]{1,0:T(8,128)(2,1)} %w_key.1) | copy-start | bytes 884740
  1.0 6.9 %copy-start.4 = (bf16[384,384]{1,0:T(8,128)(2,1)S(1)}, bf16[384,384]{1,0:T(8,128)(2,1)}, u32[]{:S(2)}) copy-start(bf16[384,384]{1,0:T(8,128)(2,1)} %w_value.1) | copy-start | bytes 884740
  1.0 6.9 %copy-start.5 = (bf16[384,384]{1,0:T(8,128)(2,1)S(1)}, bf16[384,384]{1,0:T(8,128)(2,1)}, u32[]{:S(2)}) copy-start(bf16[384,384]{1,0:T(8,128)(2,1)} %w_out.1) | copy-start | bytes 884740
  1.0 8.1 %copy-start = (bf16[3,3,3,384,192]{3,4,2,1,0:T(8,128)(2,1)S(1)}, bf16[3,3,3,384,192]{3,4,2,1,0:T(8,128)(2,1)}, u32[]{:S(2)}) copy-start(bf16[3,3,3,384,192]{3,4,2,1,0:T(8,128)(2,1)} %param.17) | copy-start | bytes 11943940
  1.0 8.1 %copy-start.1 = (bf16[2,4,160,384]{3,2,1,0:T(8,128)(2,1)S(1)}, bf16[2,4,160,384]{3,2,1,0:T(8,128)(2,1)}, u32[]{:S(2)}) copy-start(bf16[2,4,160,384]{3,2,1,0:T(8,128)(2,1)} %param.10) | copy-start | bytes 2949124
  1.1 11.5 %collective-permute-start.3 = (bf16[960,128]{1,0:T(8,128)(2,1)S(1)}, bf16[960,128]{1,0:T(8,128)(2,1)S(1)}, u32[]{:S(2)}, u32[]{:S(2)}) collective-permute-start(bf16[960,128]{1,0:T(8,128)(2,1)S(1)} %shard_map.91.mine), channel_id=1, source_target_pairs={{0,12},{4,0},{8,4},{12,8},{1,13},{5,1},{9,5},{13,9},{2,14},{6,2},{... | collective-permute-start | bytes 737288 | tf_op jit(solution)/shard_map/ppermute | solution.py:18
  6.2 1.4 %collective-permute-start = (bf16[480,128]{1,0:T(8,128)(2,1)S(1)}, bf16[480,128]{1,0:T(8,128)(2,1)S(1)}, u32[]{:S(2)}, u32[]{:S(2)}) collective-permute-start(bf16[480,128]{1,0:T(8,128)(2,1)S(1)} %get-tuple-element.71), channel_id=1, source_target_pairs={{0,1},{1,0},{2,3},{3,2},{4,5},{5,4},{6,7},{7,6},{8,9},{9,8},{10,11... | collective-permute-start | bytes 368648 | tf_op jit(solution)/shard_map/ppermute | solution.py:18
  6.3 1.5 %collective-permute-start.1 = (bf16[480,128]{1,0:T(8,128)(2,1)S(1)}, bf16[480,128]{1,0:T(8,128)(2,1)S(1)}, u32[]{:S(2)}, u32[]{:S(2)}) collective-permute-start(bf16[480,128]{1,0:T(8,128)(2,1)S(1)} %get-tuple-element.72), channel_id=1, source_target_pairs={{0,1},{1,0},{2,3},{3,2},{4,5},{5,4},{6,7},{7,6},{8,9},{9,8},{10,11... | collective-permute-start | bytes 368648 | tf_op jit(solution)/shard_map/ppermute | solution.py:18
  6.8 10.9 %collective-permute-start.2 = (bf16[960,128]{1,0:T(8,128)(2,1)S(1)}, bf16[960,128]{1,0:T(8,128)(2,1)S(1)}, u32[]{:S(2)}, u32[]{:S(2)}) collective-permute-start(bf16[960,128]{1,0:T(8,128)(2,1)S(1)} %shard_map.91.mine), channel_id=1, source_target_pairs={{0,4},{4,8},{8,12},{12,0},{1,5},{5,9},{9,13},{13,1},{2,6},{6,10},{... | collective-permute-start | bytes 737288 | tf_op jit(solution)/shard_map/ppermute | solution.py:18
  9.1 14.0 %copy-start.8 = (bf16[384]{0:T(512)(128)(2,1)S(1)}, bf16[384]{0:T(512)(128)(2,1)}, u32[]{:S(2)}) copy-start(bf16[384]{0:T(512)(128)(2,1)} %param.12) | copy-start | bytes 2308
  12.6 4.9 %collective-permute-start.4 = (bf16[480,128]{1,0:T(8,128)(2,1)S(1)}, bf16[480,128]{1,0:T(8,128)(2,1)S(1)}, u32[]{:S(2)}, u32[]{:S(2)}) collective-permute-start(bf16[480,128]{1,0:T(8,128)(2,1)S(1)} %get-tuple-element.69), channel_id=1, source_target_pairs={{0,1},{1,0},{2,3},{3,2},{4,5},{5,4},{6,7},{7,6},{8,9},{9,8},{10,11... | collective-permute-start | bytes 368648 | tf_op jit(solution)/shard_map/ppermute | solution.py:18
  12.9 4.6 %collective-permute-start.5 = (bf16[480,128]{1,0:T(8,128)(2,1)S(1)}, bf16[480,128]{1,0:T(8,128)(2,1)S(1)}, u32[]{:S(2)}, u32[]{:S(2)}) collective-permute-start(bf16[480,128]{1,0:T(8,128)(2,1)S(1)} %get-tuple-element.70), channel_id=1, source_target_pairs={{0,1},{1,0},{2,3},{3,2},{4,5},{5,4},{6,7},{7,6},{8,9},{9,8},{10,11... | collective-permute-start | bytes 368648 | tf_op jit(solution)/shard_map/ppermute | solution.py:18
  13.2 9.7 %collective-permute-start.8 = (bf16[960,128]{1,0:T(8,128)(2,1)S(1)}, bf16[960,128]{1,0:T(8,128)(2,1)S(1)}, u32[]{:S(2)}, u32[]{:S(2)}) collective-permute-start(bf16[960,128]{1,0:T(8,128)(2,1)S(1)} %collective-permute-done.3.refs_2_), channel_id=1, source_target_pairs={{0,12},{4,0},{8,4},{12,8},{1,13},{5,1},{9,5},{13,9},{2,14},{6,2},{... | collective-permute-start | bytes 737288 | tf_op jit(solution)/shard_map/ppermute | solution.py:18
  17.8 1.4 %collective-permute-start.6 = (bf16[480,128]{1,0:T(8,128)(2,1)S(1)}, bf16[480,128]{1,0:T(8,128)(2,1)S(1)}, u32[]{:S(2)}, u32[]{:S(2)}) collective-permute-start(bf16[480,128]{1,0:T(8,128)(2,1)S(1)} %get-tuple-element.67), channel_id=1, source_target_pairs={{0,1},{1,0},{2,3},{3,2},{4,5},{5,4},{6,7},{7,6},{8,9},{9,8},{10,11... | collective-permute-start | bytes 368648 | tf_op jit(solution)/shard_map/ppermute | solution.py:18
  17.9 1.5 %collective-permute-start.7 = (bf16[480,128]{1,0:T(8,128)(2,1)S(1)}, bf16[480,128]{1,0:T(8,128)(2,1)S(1)}, u32[]{:S(2)}, u32[]{:S(2)}) collective-permute-start(bf16[480,128]{1,0:T(8,128)(2,1)S(1)} %get-tuple-element.68), channel_id=1, source_target_pairs={{0,1},{1,0},{2,3},{3,2},{4,5},{5,4},{6,7},{7,6},{8,9},{9,8},{10,11... | collective-permute-start | bytes 368648 | tf_op jit(solution)/shard_map/ppermute | solution.py:18
  22.9 1.5 %collective-permute-start.9 = (bf16[960,128]{1,0:T(8,128)(2,1)S(1)}, bf16[960,128]{1,0:T(8,128)(2,1)S(1)}, u32[]{:S(2)}, u32[]{:S(2)}) collective-permute-start(bf16[960,128]{1,0:T(8,128)(2,1)S(1)} %collective-permute-done.8.mine), channel_id=1, source_target_pairs={{0,1},{1,0},{2,3},{3,2},{4,5},{5,4},{6,7},{7,6},{8,9},{9,8},{10,11... | collective-permute-start | bytes 737288 | tf_op jit(solution)/shard_map/ppermute | solution.py:18
  26.4 1.8 %collective-permute-start.10 = (bf16[480,384]{1,0:T(8,128)(2,1)S(1)}, bf16[480,384]{1,0:T(8,128)(2,1)S(1)}, u32[]{:S(2)}, u32[]{:S(2)}) collective-permute-start(bf16[480,384]{1,0:T(8,128)(2,1)S(1)} %get-tuple-element.57.act), channel_id=1, source_target_pairs={{0,1},{1,0},{2,3},{3,2},{4,5},{5,4},{6,7},{7,6},{8,9},{9,8},{10,11... | collective-permute-start | bytes 1105928 | tf_op jit(solution)/shard_map/ppermute | solution.py:18
  29.8 8.2 %collective-permute-start.14 = (bf16[960,128]{1,0:T(8,128)(2,1)S(1)}, bf16[960,128]{1,0:T(8,128)(2,1)S(1)}, u32[]{:S(2)}, u32[]{:S(2)}) collective-permute-start(bf16[960,128]{1,0:T(8,128)(2,1)S(1)} %shard_map.96), channel_id=1, source_target_pairs={{0,2},{2,0},{1,3},{3,1},{4,6},{6,4},{5,7},{7,5},{8,10},{10,8},{9,1... | collective-permute-start | bytes 737288 | tf_op jit(solution)/shard_map/ppermute | solution.py:18
  30.1 4.5 %collective-permute-start.11 = (bf16[320,192]{1,0:T(8,128)(2,1)S(1)}, bf16[320,192]{1,0:T(8,128)(2,1)S(1)}, u32[]{:S(2)}, u32[]{:S(2)}) collective-permute-start(bf16[320,192]{1,0:T(8,128)(2,1)S(1)} %get-tuple-element.61), channel_id=1, source_target_pairs={{0,1},{1,0},{2,3},{3,2},{4,5},{5,4},{6,7},{7,6},{8,9},{9,8},{10,11... | collective-permute-start | bytes 368648 | tf_op jit(solution)/shard_map/ppermute | solution.py:18
  30.4 5.8 %collective-permute-start.12 = (bf16[240,128]{1,0:T(8,128)(2,1)S(1)}, bf16[240,128]{1,0:T(8,128)(2,1)S(1)}, u32[]{:S(2)}, u32[]{:S(2)}) collective-permute-start(bf16[240,128]{1,0:T(8,128)(2,1)S(1)} %get-tuple-element.64), channel_id=1, source_target_pairs={{0,0},{4,8},{8,4},{12,12},{1,1},{5,9},{9,5},{13,13},{2,2},{6,10},{... | collective-permute-start | bytes 184328 | tf_op jit(solution)/shard_map/ppermute | solution.py:430
  31.1 5.8 %collective-permute-start.13 = (bf16[240,128]{1,0:T(8,128)(2,1)S(1)}, bf16[240,128]{1,0:T(8,128)(2,1)S(1)}, u32[]{:S(2)}, u32[]{:S(2)}) collective-permute-start(bf16[240,128]{1,0:T(8,128)(2,1)S(1)} %get-tuple-element.65), channel_id=1, source_target_pairs={{0,4},{4,0},{8,12},{12,8},{1,5},{5,1},{9,13},{13,9},{2,6},{6,2},{1... | collective-permute-start | bytes 184328 | tf_op jit(solution)/shard_map/ppermute | solution.py:433

commit v9 on v8

--- a/solution.py
+++ b/solution.py
@@ -232,12 +232,33 @@
     return jnp.concatenate([jnp.where(core == 0, a, b), jnp.where(core == 0, b, a)], axis=0)
 
 
-def send_kernel(cells, back, act, other, weights, out):
+def near_kernel(cells, back, act, weights, out):
+    @pl.when(place_of()[3] + back < lax.axis_size("tm"))
+    def _():
+        out[...] = gathered(taps(act, weights.at[2 - back], cells), cells)
+
+
+def send_kernel(cells, back, near, act, other, weights, out):
     wanted = place_of()[3] + back < lax.axis_size("tm")
 
     @pl.when(wanted)
     def _():
-        pack(gathered(taps(by_core(act, other), weights.at[2 - back], cells), cells), out)
+        core, mine, theirs = place_of()[0], act[...], other[...]
+        own = mine.shape[0] - cells
+        padded = jnp.where(
+            core == 0,
+            jnp.concatenate([mine[cells:], theirs], axis=0),
+            jnp.concatenate([theirs, mine[:own]], axis=0),
+        )
+        rows = gathered(taps(padded, weights.at[2 - back], cells), cells)
+        pack(
+            jnp.where(
+                core == 0,
+                jnp.concatenate([near[...], rows], axis=0),
+                jnp.concatenate([rows, near[...]], axis=0),
+            ),
+            out,
+        )
 
     @pl.when(jnp.logical_not(wanted))
     def _():
@@ -411,10 +432,13 @@
     other = cycle(act, "chan", 1)
     received = []
     for back in range(1, min(moments, 3)):
+        (near,) = call(
+            functools.partial(near_kernel, cells, back), [shaped((cells, half), F32)], [act, weights]
+        )
         (term,) = call(
             functools.partial(send_kernel, cells, back),
             [shaped((tokens * 3 // 2, LANES), BF)],
-            [act, other, weights],
+            [near, act, other, weights],
             )
         received.append(term)
     act, joined, received = lax.optimization_barrier((act, joined, received))

time: 38.2 us -> 37.9 us (level)
  waiting for transfers between devices: 6.14 us -> 5.49 us
  Pallas kernels: 14.2 us -> 14.6 us
    ppermute x13, waiting for transfers between devices: 5.53 us -> 4.76 us  [cycle(): lax.ppermute(array, axis, [(i, (i + by) % count) for i in range(count)])]
    pallas_call x11 -> x12, Pallas kernels: 14.2 us -> 14.6 us  [call(): pl.pallas_call(kernel, out_shape=outs, in_specs=[vmem] * (len(args) - int...]
  transfers between devices with their start and end apart: 15 -> 15, of which waited for: 11 -> 11; matrix products, arithmetic and copies ran while one was open for 0% -> 0% of each run, Pallas kernels for 28% -> 30%
where the time goes in v9:
time: 37.9 us; the launch traced here: 37.8 us
  starting transfers between devices  16.2 us (43%)
  Pallas kernels  14.6 us (39%)
  waiting for transfers between devices  5.49 us (14%)
  local copies, waits for them, and re-layouts  1.06 us (3%)
  between operations  0.39 us (1%)
    pallas_call x12, Pallas kernels, call(): pl.pallas_call(kernel, out_shape=outs, in_specs=[vmem] * (len(args) - int...  14.6 us
    ppermute x13, starting transfers between devices, cycle(): lax.ppermute(array, axis, [(i, (i + by) % count) for i in range(count)])  12 us
    ppermute x13, waiting for transfers between devices, cycle(): lax.ppermute(array, axis, [(i, (i + by) % count) for i in range(count)])  4.76 us
    ppermute x1, starting transfers between devices, body(): inner = lax.ppermute(inner, 'space', [(i, i ^ 1) for i in range(places)])  3.5 us
    unnamed x18, local copies, waits for them, and re-layouts  1.01 us
  transfers between devices with their start and end apart: 15, of which 11 were waited for; matrix products, arithmetic and copies ran while one was open for 0% of the time, Pallas kernels for 30%

profile of v9, /device:TPU:0, one launch (start us, length us, event | category | flops | bytes accessed | tf_op | source)
XLA Modules:
  0.0 37.8 jit_solution(3177643994439555420)
XLA Ops:
  0.0 1.0 %copy-done.6 = bf16[1,4,160,192]{3,2,1,0:T(8,128)(2,1)S(1)} copy-done((bf16[1,4,160,192]{3,2,1,0:T(8,128)(2,1)S(1)}, bf16[1,4,160,192]{3,2,1,0:T(8,128)(2,1)}, u32[]{:S(2)}) %copy-start.6) | copy-done | bytes 245784
  1.0 0.0 copy-start.5
  1.0 0.0 copy-start
  1.0 0.0 copy-start.1
  1.0 0.1 shard_map.91.mine
  1.1 5.1 %collective-permute-start.3 = (bf16[960,128]{1,0:T(8,128)(2,1)S(1)}, bf16[960,128]{1,0:T(8,128)(2,1)S(1)}, u32[]{:S(2)}, u32[]{:S(2)}) collective-permute-start(bf16[960,128]{1,0:T(8,128)(2,1)S(1)} %shard_map.91.mine), channel_id=1, source_target_pairs={{0,12},{4,0},{8,4},{12,8},{1,13},{5,1},{9,5},{13,9},{2,14},{6,2},{... | collective-permute-start | bytes 737288 | tf_op jit(solution)/shard_map/ppermute | solution.py:18
  6.2 0.1 collective-permute-start
  6.3 0.5 %collective-permute-start.1 = (bf16[480,128]{1,0:T(8,128)(2,1)S(1)}, bf16[480,128]{1,0:T(8,128)(2,1)S(1)}, u32[]{:S(2)}, u32[]{:S(2)}) collective-permute-start(bf16[480,128]{1,0:T(8,128)(2,1)S(1)} %get-tuple-element.72), channel_id=1, source_target_pairs={{0,1},{1,0},{2,3},{3,2},{4,5},{5,4},{6,7},{7,6},{8,9},{9,8},{10,11... | collective-permute-start | bytes 368648 | tf_op jit(solution)/shard_map/ppermute | solution.py:18
  6.8 0.0 collective-permute-start.2
  6.8 0.0 copy-done.7
  6.8 0.8 %collective-permute-done = bf16[480,128]{1,0:T(8,128)(2,1)S(1)} collective-permute-done((bf16[480,128]{1,0:T(8,128)(2,1)S(1)}, bf16[480,128]{1,0:T(8,128)(2,1)S(1)}, u32[]{:S(2)}, u32[]{:S(2)}) %collective-permute-start) | collective-permute-done | bytes 122912 | tf_op jit(solution)/shard_map/ppermute | solution.py:18
  7.6 0.2 collective-permute-done.1
  7.8 0.0 copy-done.2
  7.9 1.2 %shard_map.92 = (bf16[320,384]{1,0:T(8,128)(2,1)S(1)}, bf16[640,384]{1,0:T(8,128)(2,1)S(1)}, bf16[320,384]{1,0:T(8,128)(2,1)S(1)}, bf16[384,384]{1,0:T(8,128)(2,...) custom-call(bf16[1,384]{1,0:T(2,128)(2,1)S(1)} %reshape.15.gain, ...), custom_call_target="tpu_custom_call" | custom-call | flops 1000 | bytes 1000 | tf_op jit(solution)/shard_map/pallas_call | solution.py:29
  9.1 0.0 copy-start.8
  9.1 3.3 %shard_map.93 = (f32[3,640,192]{2,1,0:T(8,128)S(1)}, bf16[240,128]{1,0:T(8,128)(2,1)S(1)}, bf16[240,128]{1,0:T(8,128)(2,1)S(1)}) custom-call(bf16[2,640,384]{2,1,0:T(8,128)(2,1)S(1)} %bitcast.8, bf16[3,3,3,192,384]{4,3,2,1,0:T(8,128)(2,1)S(1)} %bitcast.4), custom_call_target="tpu_custom_call" | custom-call | flops 1000 | bytes 1000 | tf_op jit(solution)/shard_map/pallas_call | solution.py:29
  12.4 0.2 collective-permute-done.3.refs_2_
  12.6 0.3 collective-permute-start.4
  12.9 0.3 collective-permute-start.5
  13.2 4.3 %collective-permute-start.8 = (bf16[960,128]{1,0:T(8,128)(2,1)S(1)}, bf16[960,128]{1,0:T(8,128)(2,1)S(1)}, u32[]{:S(2)}, u32[]{:S(2)}) collective-permute-start(bf16[960,128]{1,0:T(8,128)(2,1)S(1)} %collective-permute-done.3.refs_2_), channel_id=1, source_target_pairs={{0,12},{4,0},{8,4},{12,8},{1,13},{5,1},{9,5},{13,9},{2,14},{6,2},{... | collective-permute-start | bytes 737288 | tf_op jit(solution)/shard_map/ppermute | solution.py:18
  17.5 0.0 collective-permute-done.4
  17.5 0.0 collective-permute-done.5
  17.5 0.3 collective-permute-done.2.refs_0_
  17.8 0.1 collective-permute-start.6
  17.9 0.5 %collective-permute-start.7 = (bf16[480,128]{1,0:T(8,128)(2,1)S(1)}, bf16[480,128]{1,0:T(8,128)(2,1)S(1)}, u32[]{:S(2)}, u32[]{:S(2)}) collective-permute-start(bf16[480,128]{1,0:T(8,128)(2,1)S(1)} %get-tuple-element.68), channel_id=1, source_target_pairs={{0,1},{1,0},{2,3},{3,2},{4,5},{5,4},{6,7},{7,6},{8,9},{9,8},{10,11... | collective-permute-start | bytes 368648 | tf_op jit(solution)/shard_map/ppermute | solution.py:18
  18.4 0.8 %collective-permute-done.6 = bf16[480,128]{1,0:T(8,128)(2,1)S(1)} collective-permute-done((bf16[480,128]{1,0:T(8,128)(2,1)S(1)}, bf16[480,128]{1,0:T(8,128)(2,1)S(1)}, u32[]{:S(2)}, u32[]{:S(2)}) %collective-permute-start.6) | collective-permute-done | bytes 122912 | tf_op jit(solution)/shard_map/ppermute | solution.py:18
  19.2 0.2 collective-permute-done.7
  19.4 3.4 %shard_map.94 = (bf16[480,384]{1,0:T(8,128)(2,1)S(1)}, bf16[480,384]{1,0:T(8,128)(2,1)S(1)}, f32[480,128]{1,0:T(8,128)S(1)}, f32[480,128]{1,0:T(8,128)S(1)}, f32[480,384]{1,0:T(8,128)S(1)}) custom-call(bf16[1,384]{1,0:T(2,128)(2,1)S(1)} %reshape.15.gain, bf16[320,384]{1,0:T(8,128)(2,1)S(1)} %get-tuple-element.38.raw_own, ...), custom_call_target="tpu_custom_call" | custom-call | flops 1000 | bytes 1000 | tf_op jit(solution)/shard_map/pallas_call | solution.py:29
  22.7 0.2 collective-permute-done.8.mine
  22.9 0.2 collective-permute-start.9
  23.2 1.3 %collective-permute-done.9.theirs = bf16[960,128]{1,0:T(8,128)(2,1)S(1)} collective-permute-done((bf16[960,128]{1,0:T(8,128)(2,1)S(1)}, bf16[960,128]{1,0:T(8,128)(2,1)S(1)}, u32[]{:S(2)}, u32[]{:S(2)}) %collective-permute-start.9) | collective-permute-done | bytes 245792 | tf_op jit(solution)/shard_map/ppermute | solution.py:18
  24.4 2.0 %shard_map.95 = (bf16[480,384]{1,0:T(8,128)(2,1)S(1)}, bf16[480,384]{1,0:T(8,128)(2,1)S(1)}) custom-call(bf16[1,384]{1,0:T(2,128)(2,1)S(1)} %reshape.15.gain, bf16[1,384]{1,0:T(2,128)(2,1)S(1)} %reshape.16.gain_two, bf16[384,384]{1,0:T(8,128)(2,1)S(1)} %get-tuple-element.36.w_mixed, bf16[480,384]{1,0:T(8,128)(2,1)S(1)} %get-tuple-element.48.query, ...), custom_call_target="tpu_custom_call" | custom-call | flops 1000 | bytes 1000 | tf_op jit(solution)/shard_map/pallas_call | solution.py:29
  26.4 0.3 collective-permute-start.10
  26.7 0.6 %shard_map.96.near = f32[160,192]{1,0:T(8,128)S(1)} custom-call(bf16[480,384]{1,0:T(8,128)(2,1)S(1)} %get-tuple-element.57.act, bf16[3,3,3,192,384]{4,3,2,1,0:T(8,128)(2,1)S(1)} %bitcast.5), custom_call_target="tpu_custom_call" | custom-call | flops 1000 | bytes 1000 | tf_op jit(solution)/shard_map/pallas_call | solution.py:29
  27.4 0.8 %collective-permute-done.10.other = bf16[480,384]{1,0:T(8,128)(2,1)S(1)} collective-permute-done((bf16[480,384]{1,0:T(8,128)(2,1)S(1)}, bf16[480,384]{1,0:T(8,128)(2,1)S(1)}, u32[]{:S(2)}, u32[]{:S(2)}) %collective-permute-start.10) | collective-permute-done | bytes 368672 | tf_op jit(solution)/shard_map/ppermute | solution.py:18
  28.2 1.2 %shard_map.97 = bf16[960,128]{1,0:T(8,128)(2,1)S(1)} custom-call(f32[160,192]{1,0:T(8,128)S(1)} %shard_map.96.near, bf16[480,384]{1,0:T(8,128)(2,1)S(1)} %get-tuple-element.57.act, bf16[480,384]{1,0:T(8,128)(2,1)S(1)} %collective-permute-done.10.other, bf16[3,3,3,192,384]{4,3,2,1,0:T(8,128)(2,1)S(1)} %bitcast.6), custom_call_target="tpu_custom_call" | custom-call | flops 1000 | bytes 1000 | tf_op jit(solution)/shard_map/pallas_call | solution.py:29
  29.4 0.4 collective-permute-start.14
  29.8 0.2 shard_map.98
  30.0 0.1 collective-permute-start.11
  30.1 0.7 %collective-permute-start.12 = (bf16[240,128]{1,0:T(8,128)(2,1)S(1)}, bf16[240,128]{1,0:T(8,128)(2,1)S(1)}, u32[]{:S(2)}, u32[]{:S(2)}) collective-permute-start(bf16[240,128]{1,0:T(8,128)(2,1)S(1)} %get-tuple-element.64), channel_id=1, source_target_pairs={{0,0},{4,8},{8,4},{12,12},{1,1},{5,9},{9,5},{13,13},{2,2},{6,10},{... | collective-permute-start | bytes 184328 | tf_op jit(solution)/shard_map/ppermute | solution.py:454
  30.8 3.5 %collective-permute-start.13 = (bf16[240,128]{1,0:T(8,128)(2,1)S(1)}, bf16[240,128]{1,0:T(8,128)(2,1)S(1)}, u32[]{:S(2)}, u32[]{:S(2)}) collective-permute-start(bf16[240,128]{1,0:T(8,128)(2,1)S(1)} %get-tuple-element.65), channel_id=1, source_target_pairs={{0,4},{4,0},{8,12},{12,8},{1,5},{5,1},{9,13},{13,9},{2,6},{6,2},{1... | collective-permute-start | bytes 184328 | tf_op jit(solution)/shard_map/ppermute | solution.py:457
  34.3 0.0 collective-permute-done.11.theirs
  34.3 1.6 %shard_map.99.rest = f32[640,192]{1,0:T(8,128)S(1)} custom-call(bf16[480,384]{1,0:T(8,128)(2,1)S(1)} %get-tuple-element.57.act, bf16[480,384]{1,0:T(8,128)(2,1)S(1)} %collective-permute-done.10.other, f32[3,640,192]{2,1,0:T(8,128)S(1)} %get-tuple-element.58.cached, bf16[320,192]{1,0:T(8,128)(2,1)S(1)} %get-tuple-element.60.keep, ...), custom_call_target="tpu_custom_call" | custom-call | flops 1000 | bytes 1000 | tf_op jit(solution)/shard_map/pallas_call | solution.py:29
  35.9 0.0 collective-permute-done.12.outer
  35.9 0.7 %collective-permute-done.13.inner = bf16[240,128]{1,0:T(8,128)(2,1)S(1)} collective-permute-done((bf16[240,128]{1,0:T(8,128)(2,1)S(1)}, bf16[240,128]{1,0:T(8,128)(2,1)S(1)}, u32[]{:S(2)}, u32[]{:S(2)}) %collective-permute-start.13) | collective-permute-done | bytes 61472 | tf_op jit(solution)/shard_map/ppermute | solution.py:457
  36.6 0.1 shard_map.100.rest
  36.8 0.8 %shard_map.101.refs_1_ = bf16[640,192]{1,0:T(8,128)(2,1)} custom-call(f32[640,192]{1,0:T(8,128)S(1)} %shard_map.100.rest), custom_call_target="tpu_custom_call" | custom-call | flops 1000 | bytes 1000 | tf_op jit(solution)/shard_map/pallas_call | solution.py:29
  37.5 0.1 collective-permute-done.14.refs_0_
  (20 shorter events, 0.1 us)
Async XLA Ops:
  0.0 1.0 %copy-start.6 = (bf16[1,4,160,192]{3,2,1,0:T(8,128)(2,1)S(1)}, bf16[1,4,160,192]{3,2,1,0:T(8,128)(2,1)}, u32[]{:S(2)}) copy-start(bf16[1,4,160,192]{3,2,1,0:T(8,128)(2,1)} %param.9) | copy-start | bytes 737284
  1.0 5.8 %copy-start.7 = (bf16[384]{0:T(512)(128)(2,1)S(1)}, bf16[384]{0:T(512)(128)(2,1)}, u32[]{:S(2)}) copy-start(bf16[384]{0:T(512)(128)(2,1)} %param.11) | copy-start | bytes 2308
  1.0 6.9 %copy-start.2 = (bf16[384,384]{1,0:T(8,128)(2,1)S(1)}, bf16[384,384]{1,0:T(8,128)(2,1)}, u32[]{:S(2)}) copy-start(bf16[384,384]{1,0:T(8,128)(2,1)} %w_query.1) | copy-start | bytes 884740
  1.0 6.9 %copy-start.3 = (bf16[384,384]{1,0:T(8,128)(2,1)S(1)}, bf16[384,384]{1,0:T(8,128)(2,1)}, u32[]{:S(2)}) copy-start(bf16[384,384]{1,0:T(8,128)(2,1)} %w_key.1) | copy-start | bytes 884740
  1.0 6.9 %copy-start.4 = (bf16[384,384]{1,0:T(8,128)(2,1)S(1)}, bf16[384,384]{1,0:T(8,128)(2,1)}, u32[]{:S(2)}) copy-start(bf16[384,384]{1,0:T(8,128)(2,1)} %w_value.1) | copy-start | bytes 884740
  1.0 6.9 %copy-start.5 = (bf16[384,384]{1,0:T(8,128)(2,1)S(1)}, bf16[384,384]{1,0:T(8,128)(2,1)}, u32[]{:S(2)}) copy-start(bf16[384,384]{1,0:T(8,128)(2,1)} %w_out.1) | copy-start | bytes 884740
  1.0 8.1 %copy-start = (bf16[3,3,3,384,192]{3,4,2,1,0:T(8,128)(2,1)S(1)}, bf16[3,3,3,384,192]{3,4,2,1,0:T(8,128)(2,1)}, u32[]{:S(2)}) copy-start(bf16[3,3,3,384,192]{3,4,2,1,0:T(8,128)(2,1)} %param.17) | copy-start | bytes 11943940
  1.0 8.1 %copy-start.1 = (bf16[2,4,160,384]{3,2,1,0:T(8,128)(2,1)S(1)}, bf16[2,4,160,384]{3,2,1,0:T(8,128)(2,1)}, u32[]{:S(2)}) copy-start(bf16[2,4,160,384]{3,2,1,0:T(8,128)(2,1)} %param.10) | copy-start | bytes 2949124
  1.1 11.5 %collective-permute-start.3 = (bf16[960,128]{1,0:T(8,128)(2,1)S(1)}, bf16[960,128]{1,0:T(8,128)(2,1)S(1)}, u32[]{:S(2)}, u32[]{:S(2)}) collective-permute-start(bf16[960,128]{1,0:T(8,128)(2,1)S(1)} %shard_map.91.mine), channel_id=1, source_target_pairs={{0,12},{4,0},{8,4},{12,8},{1,13},{5,1},{9,5},{13,9},{2,14},{6,2},{... | collective-permute-start | bytes 737288 | tf_op jit(solution)/shard_map/ppermute | solution.py:18
  6.2 1.4 %collective-permute-start = (bf16[480,128]{1,0:T(8,128)(2,1)S(1)}, bf16[480,128]{1,0:T(8,128)(2,1)S(1)}, u32[]{:S(2)}, u32[]{:S(2)}) collective-permute-start(bf16[480,128]{1,0:T(8,128)(2,1)S(1)} %get-tuple-element.71), channel_id=1, source_target_pairs={{0,1},{1,0},{2,3},{3,2},{4,5},{5,4},{6,7},{7,6},{8,9},{9,8},{10,11... | collective-permute-start | bytes 368648 | tf_op jit(solution)/shard_map/ppermute | solution.py:18
  6.3 1.5 %collective-permute-start.1 = (bf16[480,128]{1,0:T(8,128)(2,1)S(1)}, bf16[480,128]{1,0:T(8,128)(2,1)S(1)}, u32[]{:S(2)}, u32[]{:S(2)}) collective-permute-start(bf16[480,128]{1,0:T(8,128)(2,1)S(1)} %get-tuple-element.72), channel_id=1, source_target_pairs={{0,1},{1,0},{2,3},{3,2},{4,5},{5,4},{6,7},{7,6},{8,9},{9,8},{10,11... | collective-permute-start | bytes 368648 | tf_op jit(solution)/shard_map/ppermute | solution.py:18
  6.8 10.9 %collective-permute-start.2 = (bf16[960,128]{1,0:T(8,128)(2,1)S(1)}, bf16[960,128]{1,0:T(8,128)(2,1)S(1)}, u32[]{:S(2)}, u32[]{:S(2)}) collective-permute-start(bf16[960,128]{1,0:T(8,128)(2,1)S(1)} %shard_map.91.mine), channel_id=1, source_target_pairs={{0,4},{4,8},{8,12},{12,0},{1,5},{5,9},{9,13},{13,1},{2,6},{6,10},{... | collective-permute-start | bytes 737288 | tf_op jit(solution)/shard_map/ppermute | solution.py:18
  9.1 14.0 %copy-start.8 = (bf16[384]{0:T(512)(128)(2,1)S(1)}, bf16[384]{0:T(512)(128)(2,1)}, u32[]{:S(2)}) copy-start(bf16[384]{0:T(512)(128)(2,1)} %param.12) | copy-start | bytes 2308
  12.6 4.9 %collective-permute-start.4 = (bf16[480,128]{1,0:T(8,128)(2,1)S(1)}, bf16[480,128]{1,0:T(8,128)(2,1)S(1)}, u32[]{:S(2)}, u32[]{:S(2)}) collective-permute-start(bf16[480,128]{1,0:T(8,128)(2,1)S(1)} %get-tuple-element.69), channel_id=1, source_target_pairs={{0,1},{1,0},{2,3},{3,2},{4,5},{5,4},{6,7},{7,6},{8,9},{9,8},{10,11... | collective-permute-start | bytes 368648 | tf_op jit(solution)/shard_map/ppermute | solution.py:18
  12.9 4.6 %collective-permute-start.5 = (bf16[480,128]{1,0:T(8,128)(2,1)S(1)}, bf16[480,128]{1,0:T(8,128)(2,1)S(1)}, u32[]{:S(2)}, u32[]{:S(2)}) collective-permute-start(bf16[480,128]{1,0:T(8,128)(2,1)S(1)} %get-tuple-element.70), channel_id=1, source_target_pairs={{0,1},{1,0},{2,3},{3,2},{4,5},{5,4},{6,7},{7,6},{8,9},{9,8},{10,11... | collective-permute-start | bytes 368648 | tf_op jit(solution)/shard_map/ppermute | solution.py:18
  13.2 9.7 %collective-permute-start.8 = (bf16[960,128]{1,0:T(8,128)(2,1)S(1)}, bf16[960,128]{1,0:T(8,128)(2,1)S(1)}, u32[]{:S(2)}, u32[]{:S(2)}) collective-permute-start(bf16[960,128]{1,0:T(8,128)(2,1)S(1)} %collective-permute-done.3.refs_2_), channel_id=1, source_target_pairs={{0,12},{4,0},{8,4},{12,8},{1,13},{5,1},{9,5},{13,9},{2,14},{6,2},{... | collective-permute-start | bytes 737288 | tf_op jit(solution)/shard_map/ppermute | solution.py:18
  17.8 1.4 %collective-permute-start.6 = (bf16[480,128]{1,0:T(8,128)(2,1)S(1)}, bf16[480,128]{1,0:T(8,128)(2,1)S(1)}, u32[]{:S(2)}, u32[]{:S(2)}) collective-permute-start(bf16[480,128]{1,0:T(8,128)(2,1)S(1)} %get-tuple-element.67), channel_id=1, source_target_pairs={{0,1},{1,0},{2,3},{3,2},{4,5},{5,4},{6,7},{7,6},{8,9},{9,8},{10,11... | collective-permute-start | bytes 368648 | tf_op jit(solution)/shard_map/ppermute | solution.py:18
  17.9 1.5 %collective-permute-start.7 = (bf16[480,128]{1,0:T(8,128)(2,1)S(1)}, bf16[480,128]{1,0:T(8,128)(2,1)S(1)}, u32[]{:S(2)}, u32[]{:S(2)}) collective-permute-start(bf16[480,128]{1,0:T(8,128)(2,1)S(1)} %get-tuple-element.68), channel_id=1, source_target_pairs={{0,1},{1,0},{2,3},{3,2},{4,5},{5,4},{6,7},{7,6},{8,9},{9,8},{10,11... | collective-permute-start | bytes 368648 | tf_op jit(solution)/shard_map/ppermute | solution.py:18
  22.9 1.5 %collective-permute-start.9 = (bf16[960,128]{1,0:T(8,128)(2,1)S(1)}, bf16[960,128]{1,0:T(8,128)(2,1)S(1)}, u32[]{:S(2)}, u32[]{:S(2)}) collective-permute-start(bf16[960,128]{1,0:T(8,128)(2,1)S(1)} %collective-permute-done.8.mine), channel_id=1, source_target_pairs={{0,1},{1,0},{2,3},{3,2},{4,5},{5,4},{6,7},{7,6},{8,9},{9,8},{10,11... | collective-permute-start | bytes 737288 | tf_op jit(solution)/shard_map/ppermute | solution.py:18
  26.4 1.8 %collective-permute-start.10 = (bf16[480,384]{1,0:T(8,128)(2,1)S(1)}, bf16[480,384]{1,0:T(8,128)(2,1)S(1)}, u32[]{:S(2)}, u32[]{:S(2)}) collective-permute-start(bf16[480,384]{1,0:T(8,128)(2,1)S(1)} %get-tuple-element.57.act), channel_id=1, source_target_pairs={{0,1},{1,0},{2,3},{3,2},{4,5},{5,4},{6,7},{7,6},{8,9},{9,8},{10,11... | collective-permute-start | bytes 1105928 | tf_op jit(solution)/shard_map/ppermute | solution.py:18
  29.4 8.2 %collective-permute-start.14 = (bf16[960,128]{1,0:T(8,128)(2,1)S(1)}, bf16[960,128]{1,0:T(8,128)(2,1)S(1)}, u32[]{:S(2)}, u32[]{:S(2)}) collective-permute-start(bf16[960,128]{1,0:T(8,128)(2,1)S(1)} %shard_map.97), channel_id=1, source_target_pairs={{0,2},{2,0},{1,3},{3,1},{4,6},{6,4},{5,7},{7,5},{8,10},{10,8},{9,1... | collective-permute-start | bytes 737288 | tf_op jit(solution)/shard_map/ppermute | solution.py:18
  30.0 4.3 %collective-permute-start.11 = (bf16[320,192]{1,0:T(8,128)(2,1)S(1)}, bf16[320,192]{1,0:T(8,128)(2,1)S(1)}, u32[]{:S(2)}, u32[]{:S(2)}) collective-permute-start(bf16[320,192]{1,0:T(8,128)(2,1)S(1)} %get-tuple-element.61), channel_id=1, source_target_pairs={{0,1},{1,0},{2,3},{3,2},{4,5},{5,4},{6,7},{7,6},{8,9},{9,8},{10,11... | collective-permute-start | bytes 368648 | tf_op jit(solution)/shard_map/ppermute | solution.py:18
  30.1 5.8 %collective-permute-start.12 = (bf16[240,128]{1,0:T(8,128)(2,1)S(1)}, bf16[240,128]{1,0:T(8,128)(2,1)S(1)}, u32[]{:S(2)}, u32[]{:S(2)}) collective-permute-start(bf16[240,128]{1,0:T(8,128)(2,1)S(1)} %get-tuple-element.64), channel_id=1, source_target_pairs={{0,0},{4,8},{8,4},{12,12},{1,1},{5,9},{9,5},{13,13},{2,2},{6,10},{... | collective-permute-start | bytes 184328 | tf_op jit(solution)/shard_map/ppermute | solution.py:454
  30.8 5.8 %collective-permute-start.13 = (bf16[240,128]{1,0:T(8,128)(2,1)S(1)}, bf16[240,128]{1,0:T(8,128)(2,1)S(1)}, u32[]{:S(2)}, u32[]{:S(2)}) collective-permute-start(bf16[240,128]{1,0:T(8,128)(2,1)S(1)} %get-tuple-element.65), channel_id=1, source_target_pairs={{0,4},{4,0},{8,12},{12,8},{1,5},{5,1},{9,13},{13,9},{2,6},{6,2},{1... | collective-permute-start | bytes 184328 | tf_op jit(solution)/shard_map/ppermute | solution.py:457

commit v10 on v9

--- a/solution.py
+++ b/solution.py
@@ -430,6 +430,8 @@
         [pltpu.VMEM((count, 1), F32), pltpu.VMEM((count, width), F32)],
     )
     other = cycle(act, "chan", 1)
+    keep, give = call(residual_kernel, [shaped((tokens // 2, half), BF)] * 2, [joined])
+    other, give = lax.optimization_barrier((other, give))
     received = []
     for back in range(1, min(moments, 3)):
         (near,) = call(
@@ -441,9 +443,8 @@
             [near, act, other, weights],
             )
         received.append(term)
-    act, joined, received = lax.optimization_barrier((act, joined, received))
+    act, give, received = lax.optimization_barrier((act, give, received))
     received = [cycle(term, "tm", 1 + i) for i, term in enumerate(received)]
-    keep, give = call(residual_kernel, [shaped((tokens // 2, half), BF)] * 2, [joined])
     theirs = cycle(give, "chan", 1)
     (rest,) = call(
         functools.partial(rest_kernel, cells),

time: 37.9 us -> 37.8 us (level)
  no operation moved by 1% of the time
where the time goes in v10:
time: 37.8 us; the launch traced here: 37.6 us
  starting transfers between devices  16.3 us (43%)
  Pallas kernels  14.5 us (38%)
  waiting for transfers between devices  5.48 us (14%)
  local copies, waits for them, and re-layouts  1.06 us (3%)
    pallas_call x12, Pallas kernels, call(): pl.pallas_call(kernel, out_shape=outs, in_specs=[vmem] * (len(args) - int...  14.5 us
    ppermute x13, starting transfers between devices, cycle(): lax.ppermute(array, axis, [(i, (i + by) % count) for i in range(count)])  12 us
    ppermute x13, waiting for transfers between devices, cycle(): lax.ppermute(array, axis, [(i, (i + by) % count) for i in range(count)])  4.83 us
    ppermute x1, starting transfers between devices, body(): inner = lax.ppermute(inner, 'space', [(i, i ^ 1) for i in range(places)])  3.58 us
    unnamed x18, local copies, waits for them, and re-layouts  1.01 us
  transfers between devices with their start and end apart: 15, of which 11 were waited for; matrix products, arithmetic and copies ran while one was open for 0% of the time, Pallas kernels for 30%

profile of v10, /device:TPU:0, one launch (start us, length us, event | category | flops | bytes accessed | tf_op | source)
XLA Modules:
  0.0 37.6 jit_solution(6263041033007868347)
XLA Ops:
  0.0 1.0 %copy-done.6 = bf16[1,4,160,192]{3,2,1,0:T(8,128)(2,1)S(1)} copy-done((bf16[1,4,160,192]{3,2,1,0:T(8,128)(2,1)S(1)}, bf16[1,4,160,192]{3,2,1,0:T(8,128)(2,1)}, u32[]{:S(2)}) %copy-start.6) | copy-done | bytes 245784
  1.0 0.1 shard_map.91.mine
  1.1 5.1 %collective-permute-start.3 = (bf16[960,128]{1,0:T(8,128)(2,1)S(1)}, bf16[960,128]{1,0:T(8,128)(2,1)S(1)}, u32[]{:S(2)}, u32[]{:S(2)}) collective-permute-start(bf16[960,128]{1,0:T(8,128)(2,1)S(1)} %shard_map.91.mine), channel_id=1, source_target_pairs={{0,12},{4,0},{8,4},{12,8},{1,13},{5,1},{9,5},{13,9},{2,14},{6,2},{... | collective-permute-start | bytes 737288 | tf_op jit(solution)/shard_map/ppermute | solution.py:18
  6.2 0.1 collective-permute-start
  6.3 0.5 %collective-permute-start.1 = (bf16[480,128]{1,0:T(8,128)(2,1)S(1)}, bf16[480,128]{1,0:T(8,128)(2,1)S(1)}, u32[]{:S(2)}, u32[]{:S(2)}) collective-permute-start(bf16[480,128]{1,0:T(8,128)(2,1)S(1)} %get-tuple-element.76), channel_id=1, source_target_pairs={{0,1},{1,0},{2,3},{3,2},{4,5},{5,4},{6,7},{7,6},{8,9},{9,8},{10,11... | collective-permute-start | bytes 368648 | tf_op jit(solution)/shard_map/ppermute | solution.py:18
  6.8 0.0 collective-permute-start.2
  6.8 0.8 %collective-permute-done = bf16[480,128]{1,0:T(8,128)(2,1)S(1)} collective-permute-done((bf16[480,128]{1,0:T(8,128)(2,1)S(1)}, bf16[480,128]{1,0:T(8,128)(2,1)S(1)}, u32[]{:S(2)}, u32[]{:S(2)}) %collective-permute-start) | collective-permute-done | bytes 122912 | tf_op jit(solution)/shard_map/ppermute | solution.py:18
  7.6 0.2 collective-permute-done.1
  7.8 0.0 copy-done.2
  7.8 0.0 copy-done.3
  7.9 0.0 copy-done.4
  7.9 0.0 copy-done.5
  7.9 1.2 %shard_map.92 = (bf16[320,384]{1,0:T(8,128)(2,1)S(1)}, bf16[640,384]{1,0:T(8,128)(2,1)S(1)}, bf16[320,384]{1,0:T(8,128)(2,1)S(1)}, bf16[384,384]{1,0:T(8,128)(2,...) custom-call(bf16[1,384]{1,0:T(2,128)(2,1)S(1)} %reshape.15.gain, ...), custom_call_target="tpu_custom_call" | custom-call | flops 1000 | bytes 1000 | tf_op jit(solution)/shard_map/pallas_call | solution.py:29
  9.1 0.0 copy-done
  9.1 0.0 copy-start.8
  9.1 3.3 %shard_map.93 = (f32[3,640,192]{2,1,0:T(8,128)S(1)}, bf16[240,128]{1,0:T(8,128)(2,1)S(1)}, bf16[240,128]{1,0:T(8,128)(2,1)S(1)}) custom-call(bf16[2,640,384]{2,1,0:T(8,128)(2,1)S(1)} %bitcast.8, bf16[3,3,3,192,384]{4,3,2,1,0:T(8,128)(2,1)S(1)} %bitcast.4), custom_call_target="tpu_custom_call" | custom-call | flops 1000 | bytes 1000 | tf_op jit(solution)/shard_map/pallas_call | solution.py:29
  12.4 0.2 collective-permute-done.3.refs_2_
  12.6 0.2 collective-permute-start.4
  12.9 0.3 collective-permute-start.5
  13.2 4.3 %collective-permute-start.8 = (bf16[960,128]{1,0:T(8,128)(2,1)S(1)}, bf16[960,128]{1,0:T(8,128)(2,1)S(1)}, u32[]{:S(2)}, u32[]{:S(2)}) collective-permute-start(bf16[960,128]{1,0:T(8,128)(2,1)S(1)} %collective-permute-done.3.refs_2_), channel_id=1, source_target_pairs={{0,12},{4,0},{8,4},{12,8},{1,13},{5,1},{9,5},{13,9},{2,14},{6,2},{... | collective-permute-start | bytes 737288 | tf_op jit(solution)/shard_map/ppermute | solution.py:18
  17.5 0.0 collective-permute-done.4
  17.5 0.0 collective-permute-done.5
  17.5 0.3 collective-permute-done.2.refs_0_
  17.8 0.1 collective-permute-start.6
  17.9 0.5 %collective-permute-start.7 = (bf16[480,128]{1,0:T(8,128)(2,1)S(1)}, bf16[480,128]{1,0:T(8,128)(2,1)S(1)}, u32[]{:S(2)}, u32[]{:S(2)}) collective-permute-start(bf16[480,128]{1,0:T(8,128)(2,1)S(1)} %get-tuple-element.72), channel_id=1, source_target_pairs={{0,1},{1,0},{2,3},{3,2},{4,5},{5,4},{6,7},{7,6},{8,9},{9,8},{10,11... | collective-permute-start | bytes 368648 | tf_op jit(solution)/shard_map/ppermute | solution.py:18
  18.4 0.8 %collective-permute-done.6 = bf16[480,128]{1,0:T(8,128)(2,1)S(1)} collective-permute-done((bf16[480,128]{1,0:T(8,128)(2,1)S(1)}, bf16[480,128]{1,0:T(8,128)(2,1)S(1)}, u32[]{:S(2)}, u32[]{:S(2)}) %collective-permute-start.6) | collective-permute-done | bytes 122912 | tf_op jit(solution)/shard_map/ppermute | solution.py:18
  19.2 0.2 collective-permute-done.7
  19.4 3.4 %shard_map.94 = (bf16[480,384]{1,0:T(8,128)(2,1)S(1)}, bf16[480,384]{1,0:T(8,128)(2,1)S(1)}, f32[480,128]{1,0:T(8,128)S(1)}, f32[480,128]{1,0:T(8,128)S(1)}, f32[480,384]{1,0:T(8,128)S(1)}) custom-call(bf16[1,384]{1,0:T(2,128)(2,1)S(1)} %reshape.15.gain, bf16[320,384]{1,0:T(8,128)(2,1)S(1)} %get-tuple-element.40.raw_own, ...), custom_call_target="tpu_custom_call" | custom-call | flops 1000 | bytes 1000 | tf_op jit(solution)/shard_map/pallas_call | solution.py:29
  22.7 0.2 collective-permute-done.8.mine
  22.9 0.2 collective-permute-start.9
  23.2 1.3 %collective-permute-done.9.theirs = bf16[960,128]{1,0:T(8,128)(2,1)S(1)} collective-permute-done((bf16[960,128]{1,0:T(8,128)(2,1)S(1)}, bf16[960,128]{1,0:T(8,128)(2,1)S(1)}, u32[]{:S(2)}, u32[]{:S(2)}) %collective-permute-start.9) | collective-permute-done | bytes 245792 | tf_op jit(solution)/shard_map/ppermute | solution.py:18
  24.4 2.0 %shard_map.95 = (bf16[480,384]{1,0:T(8,128)(2,1)S(1)}, bf16[480,384]{1,0:T(8,128)(2,1)S(1)}) custom-call(bf16[1,384]{1,0:T(2,128)(2,1)S(1)} %reshape.15.gain, bf16[1,384]{1,0:T(2,128)(2,1)S(1)} %reshape.16.gain_two, bf16[384,384]{1,0:T(8,128)(2,1)S(1)} %get-tuple-element.38.w_mixed, bf16[480,384]{1,0:T(8,128)(2,1)S(1)} %get-tuple-element.50.query, ...), custom_call_target="tpu_custom_call" | custom-call | flops 1000 | bytes 1000 | tf_op jit(solution)/shard_map/pallas_call | solution.py:29
  26.4 0.3 collective-permute-start.10
  26.8 0.6 %shard_map.97.near = f32[160,192]{1,0:T(8,128)S(1)} custom-call(bf16[480,384]{1,0:T(8,128)(2,1)S(1)} %get-tuple-element.62.act, bf16[3,3,3,192,384]{4,3,2,1,0:T(8,128)(2,1)S(1)} %bitcast.5), custom_call_target="tpu_custom_call" | custom-call | flops 1000 | bytes 1000 | tf_op jit(solution)/shard_map/pallas_call | solution.py:29
  27.4 0.2 shard_map.96
  27.6 0.6 %collective-permute-done.10.other = bf16[480,384]{1,0:T(8,128)(2,1)S(1)} collective-permute-done((bf16[480,384]{1,0:T(8,128)(2,1)S(1)}, bf16[480,384]{1,0:T(8,128)(2,1)S(1)}, u32[]{:S(2)}, u32[]{:S(2)}) %collective-permute-start.10) | collective-permute-done | bytes 368672 | tf_op jit(solution)/shard_map/ppermute | solution.py:18
  28.2 1.2 %shard_map.98 = bf16[960,128]{1,0:T(8,128)(2,1)S(1)} custom-call(f32[160,192]{1,0:T(8,128)S(1)} %shard_map.97.near, bf16[480,384]{1,0:T(8,128)(2,1)S(1)} %get-tuple-element.62.act, bf16[480,384]{1,0:T(8,128)(2,1)S(1)} %collective-permute-done.10.other, bf16[3,3,3,192,384]{4,3,2,1,0:T(8,128)(2,1)S(1)} %bitcast.6), custom_call_target="tpu_custom_call" | custom-call | flops 1000 | bytes 1000 | tf_op jit(solution)/shard_map/pallas_call | solution.py:29
  29.4 0.4 collective-permute-start.14
  29.8 0.0 collective-permute-start.11
  29.8 0.7 %collective-permute-start.12 = (bf16[240,128]{1,0:T(8,128)(2,1)S(1)}, bf16[240,128]{1,0:T(8,128)(2,1)S(1)}, u32[]{:S(2)}, u32[]{:S(2)}) collective-permute-start(bf16[240,128]{1,0:T(8,128)(2,1)S(1)} %get-tuple-element.68), channel_id=1, source_target_pairs={{0,0},{4,8},{8,4},{12,12},{1,1},{5,9},{9,5},{13,13},{2,2},{6,10},{... | collective-permute-start | bytes 184328 | tf_op jit(solution)/shard_map/ppermute | solution.py:455
  30.5 3.6 %collective-permute-start.13 = (bf16[240,128]{1,0:T(8,128)(2,1)S(1)}, bf16[240,128]{1,0:T(8,128)(2,1)S(1)}, u32[]{:S(2)}, u32[]{:S(2)}) collective-permute-start(bf16[240,128]{1,0:T(8,128)(2,1)S(1)} %get-tuple-element.69), channel_id=1, source_target_pairs={{0,4},{4,0},{8,12},{12,8},{1,5},{5,1},{9,13},{13,9},{2,6},{6,2},{1... | collective-permute-start | bytes 184328 | tf_op jit(solution)/shard_map/ppermute | solution.py:458
  34.1 0.0 collective-permute-done.11.theirs
  34.1 1.6 %shard_map.99.rest = f32[640,192]{1,0:T(8,128)S(1)} custom-call(bf16[480,384]{1,0:T(8,128)(2,1)S(1)} %get-tuple-element.62.act, bf16[480,384]{1,0:T(8,128)(2,1)S(1)} %collective-permute-done.10.other, f32[3,640,192]{2,1,0:T(8,128)S(1)} %get-tuple-element.63.cached, bf16[320,192]{1,0:T(8,128)(2,1)S(1)} %get-tuple-element.64.keep, ...), custom_call_target="tpu_custom_call" | custom-call | flops 1000 | bytes 1000 | tf_op jit(solution)/shard_map/pallas_call | solution.py:29
  35.7 0.0 collective-permute-done.12.outer
  35.7 0.6 %collective-permute-done.13.inner = bf16[240,128]{1,0:T(8,128)(2,1)S(1)} collective-permute-done((bf16[240,128]{1,0:T(8,128)(2,1)S(1)}, bf16[240,128]{1,0:T(8,128)(2,1)S(1)}, u32[]{:S(2)}, u32[]{:S(2)}) %collective-permute-start.13) | collective-permute-done | bytes 61472 | tf_op jit(solution)/shard_map/ppermute | solution.py:458
  36.3 0.1 shard_map.100.rest
  36.4 0.8 %shard_map.101.refs_1_ = bf16[640,192]{1,0:T(8,128)(2,1)} custom-call(f32[640,192]{1,0:T(8,128)S(1)} %shard_map.100.rest), custom_call_target="tpu_custom_call" | custom-call | flops 1000 | bytes 1000 | tf_op jit(solution)/shard_map/pallas_call | solution.py:29
  37.2 0.4 %collective-permute-done.14.refs_0_ = bf16[960,128]{1,0:T(8,128)(2,1)S(1)} collective-permute-done((bf16[960,128]{1,0:T(8,128)(2,1)S(1)}, bf16[960,128]{1,0:T(8,128)(2,1)S(1)}, u32[]{:S(2)}, u32[]{:S(2)}) %collective-permute-start.14) | collective-permute-done | bytes 245792 | tf_op jit(solution)/shard_map/ppermute | solution.py:18
  (20 shorter events, 0.1 us)
Async XLA Ops:
  0.0 1.0 %copy-start.6 = (bf16[1,4,160,192]{3,2,1,0:T(8,128)(2,1)S(1)}, bf16[1,4,160,192]{3,2,1,0:T(8,128)(2,1)}, u32[]{:S(2)}) copy-start(bf16[1,4,160,192]{3,2,1,0:T(8,128)(2,1)} %param.9) | copy-start | bytes 737284
  1.0 5.8 %copy-start.7 = (bf16[384]{0:T(512)(128)(2,1)S(1)}, bf16[384]{0:T(512)(128)(2,1)}, u32[]{:S(2)}) copy-start(bf16[384]{0:T(512)(128)(2,1)} %param.11) | copy-start | bytes 2308
  1.0 6.9 %copy-start.2 = (bf16[384,384]{1,0:T(8,128)(2,1)S(1)}, bf16[384,384]{1,0:T(8,128)(2,1)}, u32[]{:S(2)}) copy-start(bf16[384,384]{1,0:T(8,128)(2,1)} %w_query.1) | copy-start | bytes 884740
  1.0 6.9 %copy-start.3 = (bf16[384,384]{1,0:T(8,128)(2,1)S(1)}, bf16[384,384]{1,0:T(8,128)(2,1)}, u32[]{:S(2)}) copy-start(bf16[384,384]{1,0:T(8,128)(2,1)} %w_key.1) | copy-start | bytes 884740
  1.0 6.9 %copy-start.4 = (bf16[384,384]{1,0:T(8,128)(2,1)S(1)}, bf16[384,384]{1,0:T(8,128)(2,1)}, u32[]{:S(2)}) copy-start(bf16[384,384]{1,0:T(8,128)(2,1)} %w_value.1) | copy-start | bytes 884740
  1.0 6.9 %copy-start.5 = (bf16[384,384]{1,0:T(8,128)(2,1)S(1)}, bf16[384,384]{1,0:T(8,128)(2,1)}, u32[]{:S(2)}) copy-start(bf16[384,384]{1,0:T(8,128)(2,1)} %w_out.1) | copy-start | bytes 884740
  1.0 8.1 %copy-start = (bf16[3,3,3,384,192]{3,4,2,1,0:T(8,128)(2,1)S(1)}, bf16[3,3,3,384,192]{3,4,2,1,0:T(8,128)(2,1)}, u32[]{:S(2)}) copy-start(bf16[3,3,3,384,192]{3,4,2,1,0:T(8,128)(2,1)} %param.17) | copy-start | bytes 11943940
  1.0 8.1 %copy-start.1 = (bf16[2,4,160,384]{3,2,1,0:T(8,128)(2,1)S(1)}, bf16[2,4,160,384]{3,2,1,0:T(8,128)(2,1)}, u32[]{:S(2)}) copy-start(bf16[2,4,160,384]{3,2,1,0:T(8,128)(2,1)} %param.10) | copy-start | bytes 2949124
  1.1 11.5 %collective-permute-start.3 = (bf16[960,128]{1,0:T(8,128)(2,1)S(1)}, bf16[960,128]{1,0:T(8,128)(2,1)S(1)}, u32[]{:S(2)}, u32[]{:S(2)}) collective-permute-start(bf16[960,128]{1,0:T(8,128)(2,1)S(1)} %shard_map.91.mine), channel_id=1, source_target_pairs={{0,12},{4,0},{8,4},{12,8},{1,13},{5,1},{9,5},{13,9},{2,14},{6,2},{... | collective-permute-start | bytes 737288 | tf_op jit(solution)/shard_map/ppermute | solution.py:18
  6.2 1.4 %collective-permute-start = (bf16[480,128]{1,0:T(8,128)(2,1)S(1)}, bf16[480,128]{1,0:T(8,128)(2,1)S(1)}, u32[]{:S(2)}, u32[]{:S(2)}) collective-permute-start(bf16[480,128]{1,0:T(8,128)(2,1)S(1)} %get-tuple-element.75), channel_id=1, source_target_pairs={{0,1},{1,0},{2,3},{3,2},{4,5},{5,4},{6,7},{7,6},{8,9},{9,8},{10,11... | collective-permute-start | bytes 368648 | tf_op jit(solution)/shard_map/ppermute | solution.py:18
  6.3 1.5 %collective-permute-start.1 = (bf16[480,128]{1,0:T(8,128)(2,1)S(1)}, bf16[480,128]{1,0:T(8,128)(2,1)S(1)}, u32[]{:S(2)}, u32[]{:S(2)}) collective-permute-start(bf16[480,128]{1,0:T(8,128)(2,1)S(1)} %get-tuple-element.76), channel_id=1, source_target_pairs={{0,1},{1,0},{2,3},{3,2},{4,5},{5,4},{6,7},{7,6},{8,9},{9,8},{10,11... | collective-permute-start | bytes 368648 | tf_op jit(solution)/shard_map/ppermute | solution.py:18
  6.8 10.9 %collective-permute-start.2 = (bf16[960,128]{1,0:T(8,128)(2,1)S(1)}, bf16[960,128]{1,0:T(8,128)(2,1)S(1)}, u32[]{:S(2)}, u32[]{:S(2)}) collective-permute-start(bf16[960,128]{1,0:T(8,128)(2,1)S(1)} %shard_map.91.mine), channel_id=1, source_target_pairs={{0,4},{4,8},{8,12},{12,0},{1,5},{5,9},{9,13},{13,1},{2,6},{6,10},{... | collective-permute-start | bytes 737288 | tf_op jit(solution)/shard_map/ppermute | solution.py:18
  9.1 14.1 %copy-start.8 = (bf16[384]{0:T(512)(128)(2,1)S(1)}, bf16[384]{0:T(512)(128)(2,1)}, u32[]{:S(2)}) copy-start(bf16[384]{0:T(512)(128)(2,1)} %param.12) | copy-start | bytes 2308
  12.6 4.9 %collective-permute-start.4 = (bf16[480,128]{1,0:T(8,128)(2,1)S(1)}, bf16[480,128]{1,0:T(8,128)(2,1)S(1)}, u32[]{:S(2)}, u32[]{:S(2)}) collective-permute-start(bf16[480,128]{1,0:T(8,128)(2,1)S(1)} %get-tuple-element.73), channel_id=1, source_target_pairs={{0,1},{1,0},{2,3},{3,2},{4,5},{5,4},{6,7},{7,6},{8,9},{9,8},{10,11... | collective-permute-start | bytes 368648 | tf_op jit(solution)/shard_map/ppermute | solution.py:18
  12.9 4.6 %collective-permute-start.5 = (bf16[480,128]{1,0:T(8,128)(2,1)S(1)}, bf16[480,128]{1,0:T(8,128)(2,1)S(1)}, u32[]{:S(2)}, u32[]{:S(2)}) collective-permute-start(bf16[480,128]{1,0:T(8,128)(2,1)S(1)} %get-tuple-element.74), channel_id=1, source_target_pairs={{0,1},{1,0},{2,3},{3,2},{4,5},{5,4},{6,7},{7,6},{8,9},{9,8},{10,11... | collective-permute-start | bytes 368648 | tf_op jit(solution)/shard_map/ppermute | solution.py:18
  13.2 9.7 %collective-permute-start.8 = (bf16[960,128]{1,0:T(8,128)(2,1)S(1)}, bf16[960,128]{1,0:T(8,128)(2,1)S(1)}, u32[]{:S(2)}, u32[]{:S(2)}) collective-permute-start(bf16[960,128]{1,0:T(8,128)(2,1)S(1)} %collective-permute-done.3.refs_2_), channel_id=1, source_target_pairs={{0,12},{4,0},{8,4},{12,8},{1,13},{5,1},{9,5},{13,9},{2,14},{6,2},{... | collective-permute-start | bytes 737288 | tf_op jit(solution)/shard_map/ppermute | solution.py:18
  17.8 1.4 %collective-permute-start.6 = (bf16[480,128]{1,0:T(8,128)(2,1)S(1)}, bf16[480,128]{1,0:T(8,128)(2,1)S(1)}, u32[]{:S(2)}, u32[]{:S(2)}) collective-permute-start(bf16[480,128]{1,0:T(8,128)(2,1)S(1)} %get-tuple-element.71), channel_id=1, source_target_pairs={{0,1},{1,0},{2,3},{3,2},{4,5},{5,4},{6,7},{7,6},{8,9},{9,8},{10,11... | collective-permute-start | bytes 368648 | tf_op jit(solution)/shard_map/ppermute | solution.py:18
  17.9 1.5 %collective-permute-start.7 = (bf16[480,128]{1,0:T(8,128)(2,1)S(1)}, bf16[480,128]{1,0:T(8,128)(2,1)S(1)}, u32[]{:S(2)}, u32[]{:S(2)}) collective-permute-start(bf16[480,128]{1,0:T(8,128)(2,1)S(1)} %get-tuple-element.72), channel_id=1, source_target_pairs={{0,1},{1,0},{2,3},{3,2},{4,5},{5,4},{6,7},{7,6},{8,9},{9,8},{10,11... | collective-permute-start | bytes 368648 | tf_op jit(solution)/shard_map/ppermute | solution.py:18
  22.9 1.5 %collective-permute-start.9 = (bf16[960,128]{1,0:T(8,128)(2,1)S(1)}, bf16[960,128]{1,0:T(8,128)(2,1)S(1)}, u32[]{:S(2)}, u32[]{:S(2)}) collective-permute-start(bf16[960,128]{1,0:T(8,128)(2,1)S(1)} %collective-permute-done.8.mine), channel_id=1, source_target_pairs={{0,1},{1,0},{2,3},{3,2},{4,5},{5,4},{6,7},{7,6},{8,9},{9,8},{10,11... | collective-permute-start | bytes 737288 | tf_op jit(solution)/shard_map/ppermute | solution.py:18
  26.4 1.8 %collective-permute-start.10 = (bf16[480,384]{1,0:T(8,128)(2,1)S(1)}, bf16[480,384]{1,0:T(8,128)(2,1)S(1)}, u32[]{:S(2)}, u32[]{:S(2)}) collective-permute-start(bf16[480,384]{1,0:T(8,128)(2,1)S(1)} %get-tuple-element.62.act), channel_id=1, source_target_pairs={{0,1},{1,0},{2,3},{3,2},{4,5},{5,4},{6,7},{7,6},{8,9},{9,8},{10,11... | collective-permute-start | bytes 1105928 | tf_op jit(solution)/shard_map/ppermute | solution.py:18
  29.4 8.2 %collective-permute-start.14 = (bf16[960,128]{1,0:T(8,128)(2,1)S(1)}, bf16[960,128]{1,0:T(8,128)(2,1)S(1)}, u32[]{:S(2)}, u32[]{:S(2)}) collective-permute-start(bf16[960,128]{1,0:T(8,128)(2,1)S(1)} %shard_map.98), channel_id=1, source_target_pairs={{0,2},{2,0},{1,3},{3,1},{4,6},{6,4},{5,7},{7,5},{8,10},{10,8},{9,1... | collective-permute-start | bytes 737288 | tf_op jit(solution)/shard_map/ppermute | solution.py:18
  29.8 4.3 %collective-permute-start.11 = (bf16[320,192]{1,0:T(8,128)(2,1)S(1)}, bf16[320,192]{1,0:T(8,128)(2,1)S(1)}, u32[]{:S(2)}, u32[]{:S(2)}) collective-permute-start(bf16[320,192]{1,0:T(8,128)(2,1)S(1)} %get-tuple-element.65), channel_id=1, source_target_pairs={{0,1},{1,0},{2,3},{3,2},{4,5},{5,4},{6,7},{7,6},{8,9},{9,8},{10,11... | collective-permute-start | bytes 368648 | tf_op jit(solution)/shard_map/ppermute | solution.py:18
  29.8 5.8 %collective-permute-start.12 = (bf16[240,128]{1,0:T(8,128)(2,1)S(1)}, bf16[240,128]{1,0:T(8,128)(2,1)S(1)}, u32[]{:S(2)}, u32[]{:S(2)}) collective-permute-start(bf16[240,128]{1,0:T(8,128)(2,1)S(1)} %get-tuple-element.68), channel_id=1, source_target_pairs={{0,0},{4,8},{8,4},{12,12},{1,1},{5,9},{9,5},{13,13},{2,2},{6,10},{... | collective-permute-start | bytes 184328 | tf_op jit(solution)/shard_map/ppermute | solution.py:455
  30.5 5.8 %collective-permute-start.13 = (bf16[240,128]{1,0:T(8,128)(2,1)S(1)}, bf16[240,128]{1,0:T(8,128)(2,1)S(1)}, u32[]{:S(2)}, u32[]{:S(2)}) collective-permute-start(bf16[240,128]{1,0:T(8,128)(2,1)S(1)} %get-tuple-element.69), channel_id=1, source_target_pairs={{0,4},{4,0},{8,12},{12,8},{1,5},{5,1},{9,13},{13,9},{2,6},{6,2},{1... | collective-permute-start | bytes 184328 | tf_op jit(solution)/shard_map/ppermute | solution.py:458

commit v11 on v10

--- a/solution.py
+++ b/solution.py
@@ -251,14 +251,7 @@
             jnp.concatenate([theirs, mine[:own]], axis=0),
         )
         rows = gathered(taps(padded, weights.at[2 - back], cells), cells)
-        pack(
-            jnp.where(
-                core == 0,
-                jnp.concatenate([near[...], rows], axis=0),
-                jnp.concatenate([rows, near[...]], axis=0),
-            ),
-            out,
-        )
+        pack(jnp.concatenate([rows, near[...]], axis=0), out)
 
     @pl.when(jnp.logical_not(wanted))
     def _():
@@ -337,7 +330,7 @@
         write(rest[...], out, held, sem)
 
 
-def final_kernel(rest, *refs):
+def final_kernel(cells, rest, *refs):
     moment = place_of()[3]
     received, (_, out, held, sem) = refs[:-4], refs[-4:]
 
@@ -345,7 +338,11 @@
     def _():
         total = rest[...]
         for back, ref in enumerate(received):
-            total = total + jnp.where(moment > back, unpacked(ref[...]), 0.0)
+            term = unpacked(ref[...])
+            own = term.shape[0] - cells
+            ordered = jnp.concatenate([term[own:], term[:own]], axis=0)
+            term = jnp.where(place_of()[0] == 0, ordered, term)
+            total = total + jnp.where(moment > back, term, 0.0)
         write(total, out, held, sem)
 
 
@@ -461,7 +458,9 @@
     )
     written = [pltpu.VMEM((tokens, half), BF), pltpu.SemaphoreType.DMA]
     (out,) = call(early_kernel, [shaped((tokens, half), BF)], [rest], written, kept=True)
-    (out,) = call(final_kernel, [shaped((tokens, half), BF)], [rest] + received + [out], written, kept=True)
+    (out,) = call(
+        functools.partial(final_kernel, cells), [shaped((tokens, half), BF)], [rest] + received + [out], written, kept=True
+    )
     return out.reshape(1, rows, cells, half)
 
 

time: 37.8 us -> 37.9 us (level)
  no operation moved by 1% of the time
where the time goes in v11:
time: 37.9 us; the launch traced here: 37.8 us
  starting transfers between devices  16.2 us (43%)
  Pallas kernels  14.6 us (39%)
  waiting for transfers between devices  5.46 us (14%)
  local copies, waits for them, and re-layouts  1.06 us (3%)
  between operations  0.39 us (1%)
    pallas_call x12, Pallas kernels, call(): pl.pallas_call(kernel, out_shape=outs, in_specs=[vmem] * (len(args) - int...  14.6 us
    ppermute x13, starting transfers between devices, cycle(): lax.ppermute(array, axis, [(i, (i + by) % count) for i in range(count)])  12 us
    ppermute x13, waiting for transfers between devices, cycle(): lax.ppermute(array, axis, [(i, (i + by) % count) for i in range(count)])  4.81 us
    ppermute x1, starting transfers between devices, body(): inner = lax.ppermute(inner, 'space', [(i, i ^ 1) for i in range(places)])  3.6 us
    unnamed x18, local copies, waits for them, and re-layouts  1.01 us
  transfers between devices with their start and end apart: 15, of which 11 were waited for; matrix products, arithmetic and copies ran while one was open for 0% of the time, Pallas kernels for 30%

profile of v11, /device:TPU:0, one launch (start us, length us, event | category | flops | bytes accessed | tf_op | source)
XLA Modules:
  0.0 37.8 jit_solution(5574781134605957612)
XLA Ops:
  0.0 1.0 %copy-done.6 = bf16[1,4,160,192]{3,2,1,0:T(8,128)(2,1)S(1)} copy-done((bf16[1,4,160,192]{3,2,1,0:T(8,128)(2,1)S(1)}, bf16[1,4,160,192]{3,2,1,0:T(8,128)(2,1)}, u32[]{:S(2)}) %copy-start.6) | copy-done | bytes 245784
  1.0 0.0 copy-start.5
  1.0 0.0 copy-start
  1.0 0.0 copy-start.1
  1.0 0.1 shard_map.91.mine
  1.1 5.1 %collective-permute-start.3 = (bf16[960,128]{1,0:T(8,128)(2,1)S(1)}, bf16[960,128]{1,0:T(8,128)(2,1)S(1)}, u32[]{:S(2)}, u32[]{:S(2)}) collective-permute-start(bf16[960,128]{1,0:T(8,128)(2,1)S(1)} %shard_map.91.mine), channel_id=1, source_target_pairs={{0,12},{4,0},{8,4},{12,8},{1,13},{5,1},{9,5},{13,9},{2,14},{6,2},{... | collective-permute-start | bytes 737288 | tf_op jit(solution)/shard_map/ppermute | solution.py:18
  6.2 0.1 collective-permute-start
  6.3 0.5 %collective-permute-start.1 = (bf16[480,128]{1,0:T(8,128)(2,1)S(1)}, bf16[480,128]{1,0:T(8,128)(2,1)S(1)}, u32[]{:S(2)}, u32[]{:S(2)}) collective-permute-start(bf16[480,128]{1,0:T(8,128)(2,1)S(1)} %get-tuple-element.76), channel_id=1, source_target_pairs={{0,1},{1,0},{2,3},{3,2},{4,5},{5,4},{6,7},{7,6},{8,9},{9,8},{10,11... | collective-permute-start | bytes 368648 | tf_op jit(solution)/shard_map/ppermute | solution.py:18
  6.8 0.0 collective-permute-start.2
  6.8 0.0 copy-done.7
  6.8 0.8 %collective-permute-done = bf16[480,128]{1,0:T(8,128)(2,1)S(1)} collective-permute-done((bf16[480,128]{1,0:T(8,128)(2,1)S(1)}, bf16[480,128]{1,0:T(8,128)(2,1)S(1)}, u32[]{:S(2)}, u32[]{:S(2)}) %collective-permute-start) | collective-permute-done | bytes 122912 | tf_op jit(solution)/shard_map/ppermute | solution.py:18
  7.6 0.2 collective-permute-done.1
  7.8 0.0 copy-done.2
  7.9 1.2 %shard_map.92 = (bf16[320,384]{1,0:T(8,128)(2,1)S(1)}, bf16[640,384]{1,0:T(8,128)(2,1)S(1)}, bf16[320,384]{1,0:T(8,128)(2,1)S(1)}, bf16[384,384]{1,0:T(8,128)(2,...) custom-call(bf16[1,384]{1,0:T(2,128)(2,1)S(1)} %reshape.15.gain, ...), custom_call_target="tpu_custom_call" | custom-call | flops 1000 | bytes 1000 | tf_op jit(solution)/shard_map/pallas_call | solution.py:29
  9.1 0.0 copy-start.8
  9.1 3.3 %shard_map.93 = (f32[3,640,192]{2,1,0:T(8,128)S(1)}, bf16[240,128]{1,0:T(8,128)(2,1)S(1)}, bf16[240,128]{1,0:T(8,128)(2,1)S(1)}) custom-call(bf16[2,640,384]{2,1,0:T(8,128)(2,1)S(1)} %bitcast.8, bf16[3,3,3,192,384]{4,3,2,1,0:T(8,128)(2,1)S(1)} %bitcast.4), custom_call_target="tpu_custom_call" | custom-call | flops 1000 | bytes 1000 | tf_op jit(solution)/shard_map/pallas_call | solution.py:29
  12.4 0.2 collective-permute-done.3.refs_2_
  12.6 0.3 collective-permute-start.4
  12.9 0.3 collective-permute-start.5
  13.2 4.3 %collective-permute-start.8 = (bf16[960,128]{1,0:T(8,128)(2,1)S(1)}, bf16[960,128]{1,0:T(8,128)(2,1)S(1)}, u32[]{:S(2)}, u32[]{:S(2)}) collective-permute-start(bf16[960,128]{1,0:T(8,128)(2,1)S(1)} %collective-permute-done.3.refs_2_), channel_id=1, source_target_pairs={{0,12},{4,0},{8,4},{12,8},{1,13},{5,1},{9,5},{13,9},{2,14},{6,2},{... | collective-permute-start | bytes 737288 | tf_op jit(solution)/shard_map/ppermute | solution.py:18
  17.5 0.0 collective-permute-done.4
  17.5 0.0 collective-permute-done.5
  17.5 0.3 collective-permute-done.2.refs_0_
  17.8 0.1 collective-permute-start.6
  17.9 0.5 %collective-permute-start.7 = (bf16[480,128]{1,0:T(8,128)(2,1)S(1)}, bf16[480,128]{1,0:T(8,128)(2,1)S(1)}, u32[]{:S(2)}, u32[]{:S(2)}) collective-permute-start(bf16[480,128]{1,0:T(8,128)(2,1)S(1)} %get-tuple-element.72), channel_id=1, source_target_pairs={{0,1},{1,0},{2,3},{3,2},{4,5},{5,4},{6,7},{7,6},{8,9},{9,8},{10,11... | collective-permute-start | bytes 368648 | tf_op jit(solution)/shard_map/ppermute | solution.py:18
  18.4 0.8 %collective-permute-done.6 = bf16[480,128]{1,0:T(8,128)(2,1)S(1)} collective-permute-done((bf16[480,128]{1,0:T(8,128)(2,1)S(1)}, bf16[480,128]{1,0:T(8,128)(2,1)S(1)}, u32[]{:S(2)}, u32[]{:S(2)}) %collective-permute-start.6) | collective-permute-done | bytes 122912 | tf_op jit(solution)/shard_map/ppermute | solution.py:18
  19.2 0.2 collective-permute-done.7
  19.4 3.4 %shard_map.94 = (bf16[480,384]{1,0:T(8,128)(2,1)S(1)}, bf16[480,384]{1,0:T(8,128)(2,1)S(1)}, f32[480,128]{1,0:T(8,128)S(1)}, f32[480,128]{1,0:T(8,128)S(1)}, f32[480,384]{1,0:T(8,128)S(1)}) custom-call(bf16[1,384]{1,0:T(2,128)(2,1)S(1)} %reshape.15.gain, bf16[320,384]{1,0:T(8,128)(2,1)S(1)} %get-tuple-element.40.raw_own, ...), custom_call_target="tpu_custom_call" | custom-call | flops 1000 | bytes 1000 | tf_op jit(solution)/shard_map/pallas_call | solution.py:29
  22.7 0.2 collective-permute-done.8.mine
  22.9 0.2 collective-permute-start.9
  23.2 1.3 %collective-permute-done.9.theirs = bf16[960,128]{1,0:T(8,128)(2,1)S(1)} collective-permute-done((bf16[960,128]{1,0:T(8,128)(2,1)S(1)}, bf16[960,128]{1,0:T(8,128)(2,1)S(1)}, u32[]{:S(2)}, u32[]{:S(2)}) %collective-permute-start.9) | collective-permute-done | bytes 245792 | tf_op jit(solution)/shard_map/ppermute | solution.py:18
  24.4 2.0 %shard_map.95 = (bf16[480,384]{1,0:T(8,128)(2,1)S(1)}, bf16[480,384]{1,0:T(8,128)(2,1)S(1)}) custom-call(bf16[1,384]{1,0:T(2,128)(2,1)S(1)} %reshape.15.gain, bf16[1,384]{1,0:T(2,128)(2,1)S(1)} %reshape.16.gain_two, bf16[384,384]{1,0:T(8,128)(2,1)S(1)} %get-tuple-element.38.w_mixed, bf16[480,384]{1,0:T(8,128)(2,1)S(1)} %get-tuple-element.50.query, ...), custom_call_target="tpu_custom_call" | custom-call | flops 1000 | bytes 1000 | tf_op jit(solution)/shard_map/pallas_call | solution.py:29
  26.4 0.3 collective-permute-start.10
  26.7 0.6 %shard_map.97.near = f32[160,192]{1,0:T(8,128)S(1)} custom-call(bf16[480,384]{1,0:T(8,128)(2,1)S(1)} %get-tuple-element.62.act, bf16[3,3,3,192,384]{4,3,2,1,0:T(8,128)(2,1)S(1)} %bitcast.5), custom_call_target="tpu_custom_call" | custom-call | flops 1000 | bytes 1000 | tf_op jit(solution)/shard_map/pallas_call | solution.py:29
  27.4 0.2 shard_map.96
  27.6 0.6 %collective-permute-done.10.other = bf16[480,384]{1,0:T(8,128)(2,1)S(1)} collective-permute-done((bf16[480,384]{1,0:T(8,128)(2,1)S(1)}, bf16[480,384]{1,0:T(8,128)(2,1)S(1)}, u32[]{:S(2)}, u32[]{:S(2)}) %collective-permute-start.10) | collective-permute-done | bytes 368672 | tf_op jit(solution)/shard_map/ppermute | solution.py:18
  28.2 1.2 %shard_map.98 = bf16[960,128]{1,0:T(8,128)(2,1)S(1)} custom-call(f32[160,192]{1,0:T(8,128)S(1)} %shard_map.97.near, bf16[480,384]{1,0:T(8,128)(2,1)S(1)} %get-tuple-element.62.act, bf16[480,384]{1,0:T(8,128)(2,1)S(1)} %collective-permute-done.10.other, bf16[3,3,3,192,384]{4,3,2,1,0:T(8,128)(2,1)S(1)} %bitcast.6), custom_call_target="tpu_custom_call" | custom-call | flops 1000 | bytes 1000 | tf_op jit(solution)/shard_map/pallas_call | solution.py:29
  29.4 0.4 collective-permute-start.14
  29.8 0.0 collective-permute-start.11
  29.8 0.7 %collective-permute-start.12 = (bf16[240,128]{1,0:T(8,128)(2,1)S(1)}, bf16[240,128]{1,0:T(8,128)(2,1)S(1)}, u32[]{:S(2)}, u32[]{:S(2)}) collective-permute-start(bf16[240,128]{1,0:T(8,128)(2,1)S(1)} %get-tuple-element.68), channel_id=1, source_target_pairs={{0,0},{4,8},{8,4},{12,12},{1,1},{5,9},{9,5},{13,13},{2,2},{6,10},{... | collective-permute-start | bytes 184328 | tf_op jit(solution)/shard_map/ppermute | solution.py:452
  30.5 3.6 %collective-permute-start.13 = (bf16[240,128]{1,0:T(8,128)(2,1)S(1)}, bf16[240,128]{1,0:T(8,128)(2,1)S(1)}, u32[]{:S(2)}, u32[]{:S(2)}) collective-permute-start(bf16[240,128]{1,0:T(8,128)(2,1)S(1)} %get-tuple-element.69), channel_id=1, source_target_pairs={{0,4},{4,0},{8,12},{12,8},{1,5},{5,1},{9,13},{13,9},{2,6},{6,2},{1... | collective-permute-start | bytes 184328 | tf_op jit(solution)/shard_map/ppermute | solution.py:455
  34.1 0.0 collective-permute-done.11.theirs
  34.1 1.6 %shard_map.99.rest = f32[640,192]{1,0:T(8,128)S(1)} custom-call(bf16[480,384]{1,0:T(8,128)(2,1)S(1)} %get-tuple-element.62.act, bf16[480,384]{1,0:T(8,128)(2,1)S(1)} %collective-permute-done.10.other, f32[3,640,192]{2,1,0:T(8,128)S(1)} %get-tuple-element.63.cached, bf16[320,192]{1,0:T(8,128)(2,1)S(1)} %get-tuple-element.64.keep, ...), custom_call_target="tpu_custom_call" | custom-call | flops 1000 | bytes 1000 | tf_op jit(solution)/shard_map/pallas_call | solution.py:29
  35.7 0.0 collective-permute-done.12.outer
  35.7 0.6 %collective-permute-done.13.inner = bf16[240,128]{1,0:T(8,128)(2,1)S(1)} collective-permute-done((bf16[240,128]{1,0:T(8,128)(2,1)S(1)}, bf16[240,128]{1,0:T(8,128)(2,1)S(1)}, u32[]{:S(2)}, u32[]{:S(2)}) %collective-permute-start.13) | collective-permute-done | bytes 61472 | tf_op jit(solution)/shard_map/ppermute | solution.py:455
  36.3 0.1 shard_map.100.rest
  36.4 0.8 %shard_map.101.refs_1_ = bf16[640,192]{1,0:T(8,128)(2,1)} custom-call(f32[640,192]{1,0:T(8,128)S(1)} %shard_map.100.rest), custom_call_target="tpu_custom_call" | custom-call | flops 1000 | bytes 1000 | tf_op jit(solution)/shard_map/pallas_call | solution.py:29
  37.2 0.4 collective-permute-done.14.refs_0_
  (20 shorter events, 0.1 us)
Async XLA Ops:
  0.0 1.0 %copy-start.6 = (bf16[1,4,160,192]{3,2,1,0:T(8,128)(2,1)S(1)}, bf16[1,4,160,192]{3,2,1,0:T(8,128)(2,1)}, u32[]{:S(2)}) copy-start(bf16[1,4,160,192]{3,2,1,0:T(8,128)(2,1)} %param.9) | copy-start | bytes 737284
  1.0 5.8 %copy-start.7 = (bf16[384]{0:T(512)(128)(2,1)S(1)}, bf16[384]{0:T(512)(128)(2,1)}, u32[]{:S(2)}) copy-start(bf16[384]{0:T(512)(128)(2,1)} %param.11) | copy-start | bytes 2308
  1.0 6.9 %copy-start.2 = (bf16[384,384]{1,0:T(8,128)(2,1)S(1)}, bf16[384,384]{1,0:T(8,128)(2,1)}, u32[]{:S(2)}) copy-start(bf16[384,384]{1,0:T(8,128)(2,1)} %w_query.1) | copy-start | bytes 884740
  1.0 6.9 %copy-start.3 = (bf16[384,384]{1,0:T(8,128)(2,1)S(1)}, bf16[384,384]{1,0:T(8,128)(2,1)}, u32[]{:S(2)}) copy-start(bf16[384,384]{1,0:T(8,128)(2,1)} %w_key.1) | copy-start | bytes 884740
  1.0 6.9 %copy-start.4 = (bf16[384,384]{1,0:T(8,128)(2,1)S(1)}, bf16[384,384]{1,0:T(8,128)(2,1)}, u32[]{:S(2)}) copy-start(bf16[384,384]{1,0:T(8,128)(2,1)} %w_value.1) | copy-start | bytes 884740
  1.0 6.9 %copy-start.5 = (bf16[384,384]{1,0:T(8,128)(2,1)S(1)}, bf16[384,384]{1,0:T(8,128)(2,1)}, u32[]{:S(2)}) copy-start(bf16[384,384]{1,0:T(8,128)(2,1)} %w_out.1) | copy-start | bytes 884740
  1.0 8.1 %copy-start = (bf16[3,3,3,384,192]{3,4,2,1,0:T(8,128)(2,1)S(1)}, bf16[3,3,3,384,192]{3,4,2,1,0:T(8,128)(2,1)}, u32[]{:S(2)}) copy-start(bf16[3,3,3,384,192]{3,4,2,1,0:T(8,128)(2,1)} %param.17) | copy-start | bytes 11943940
  1.0 8.1 %copy-start.1 = (bf16[2,4,160,384]{3,2,1,0:T(8,128)(2,1)S(1)}, bf16[2,4,160,384]{3,2,1,0:T(8,128)(2,1)}, u32[]{:S(2)}) copy-start(bf16[2,4,160,384]{3,2,1,0:T(8,128)(2,1)} %param.10) | copy-start | bytes 2949124
  1.1 11.5 %collective-permute-start.3 = (bf16[960,128]{1,0:T(8,128)(2,1)S(1)}, bf16[960,128]{1,0:T(8,128)(2,1)S(1)}, u32[]{:S(2)}, u32[]{:S(2)}) collective-permute-start(bf16[960,128]{1,0:T(8,128)(2,1)S(1)} %shard_map.91.mine), channel_id=1, source_target_pairs={{0,12},{4,0},{8,4},{12,8},{1,13},{5,1},{9,5},{13,9},{2,14},{6,2},{... | collective-permute-start | bytes 737288 | tf_op jit(solution)/shard_map/ppermute | solution.py:18
  6.2 1.4 %collective-permute-start = (bf16[480,128]{1,0:T(8,128)(2,1)S(1)}, bf16[480,128]{1,0:T(8,128)(2,1)S(1)}, u32[]{:S(2)}, u32[]{:S(2)}) collective-permute-start(bf16[480,128]{1,0:T(8,128)(2,1)S(1)} %get-tuple-element.75), channel_id=1, source_target_pairs={{0,1},{1,0},{2,3},{3,2},{4,5},{5,4},{6,7},{7,6},{8,9},{9,8},{10,11... | collective-permute-start | bytes 368648 | tf_op jit(solution)/shard_map/ppermute | solution.py:18
  6.3 1.5 %collective-permute-start.1 = (bf16[480,128]{1,0:T(8,128)(2,1)S(1)}, bf16[480,128]{1,0:T(8,128)(2,1)S(1)}, u32[]{:S(2)}, u32[]{:S(2)}) collective-permute-start(bf16[480,128]{1,0:T(8,128)(2,1)S(1)} %get-tuple-element.76), channel_id=1, source_target_pairs={{0,1},{1,0},{2,3},{3,2},{4,5},{5,4},{6,7},{7,6},{8,9},{9,8},{10,11... | collective-permute-start | bytes 368648 | tf_op jit(solution)/shard_map/ppermute | solution.py:18
  6.8 10.9 %collective-permute-start.2 = (bf16[960,128]{1,0:T(8,128)(2,1)S(1)}, bf16[960,128]{1,0:T(8,128)(2,1)S(1)}, u32[]{:S(2)}, u32[]{:S(2)}) collective-permute-start(bf16[960,128]{1,0:T(8,128)(2,1)S(1)} %shard_map.91.mine), channel_id=1, source_target_pairs={{0,4},{4,8},{8,12},{12,0},{1,5},{5,9},{9,13},{13,1},{2,6},{6,10},{... | collective-permute-start | bytes 737288 | tf_op jit(solution)/shard_map/ppermute | solution.py:18
  9.1 14.0 %copy-start.8 = (bf16[384]{0:T(512)(128)(2,1)S(1)}, bf16[384]{0:T(512)(128)(2,1)}, u32[]{:S(2)}) copy-start(bf16[384]{0:T(512)(128)(2,1)} %param.12) | copy-start | bytes 2308
  12.6 4.9 %collective-permute-start.4 = (bf16[480,128]{1,0:T(8,128)(2,1)S(1)}, bf16[480,128]{1,0:T(8,128)(2,1)S(1)}, u32[]{:S(2)}, u32[]{:S(2)}) collective-permute-start(bf16[480,128]{1,0:T(8,128)(2,1)S(1)} %get-tuple-element.73), channel_id=1, source_target_pairs={{0,1},{1,0},{2,3},{3,2},{4,5},{5,4},{6,7},{7,6},{8,9},{9,8},{10,11... | collective-permute-start | bytes 368648 | tf_op jit(solution)/shard_map/ppermute | solution.py:18
  12.9 4.6 %collective-permute-start.5 = (bf16[480,128]{1,0:T(8,128)(2,1)S(1)}, bf16[480,128]{1,0:T(8,128)(2,1)S(1)}, u32[]{:S(2)}, u32[]{:S(2)}) collective-permute-start(bf16[480,128]{1,0:T(8,128)(2,1)S(1)} %get-tuple-element.74), channel_id=1, source_target_pairs={{0,1},{1,0},{2,3},{3,2},{4,5},{5,4},{6,7},{7,6},{8,9},{9,8},{10,11... | collective-permute-start | bytes 368648 | tf_op jit(solution)/shard_map/ppermute | solution.py:18
  13.2 9.7 %collective-permute-start.8 = (bf16[960,128]{1,0:T(8,128)(2,1)S(1)}, bf16[960,128]{1,0:T(8,128)(2,1)S(1)}, u32[]{:S(2)}, u32[]{:S(2)}) collective-permute-start(bf16[960,128]{1,0:T(8,128)(2,1)S(1)} %collective-permute-done.3.refs_2_), channel_id=1, source_target_pairs={{0,12},{4,0},{8,4},{12,8},{1,13},{5,1},{9,5},{13,9},{2,14},{6,2},{... | collective-permute-start | bytes 737288 | tf_op jit(solution)/shard_map/ppermute | solution.py:18
  17.8 1.4 %collective-permute-start.6 = (bf16[480,128]{1,0:T(8,128)(2,1)S(1)}, bf16[480,128]{1,0:T(8,128)(2,1)S(1)}, u32[]{:S(2)}, u32[]{:S(2)}) collective-permute-start(bf16[480,128]{1,0:T(8,128)(2,1)S(1)} %get-tuple-element.71), channel_id=1, source_target_pairs={{0,1},{1,0},{2,3},{3,2},{4,5},{5,4},{6,7},{7,6},{8,9},{9,8},{10,11... | collective-permute-start | bytes 368648 | tf_op jit(solution)/shard_map/ppermute | solution.py:18
  17.9 1.5 %collective-permute-start.7 = (bf16[480,128]{1,0:T(8,128)(2,1)S(1)}, bf16[480,128]{1,0:T(8,128)(2,1)S(1)}, u32[]{:S(2)}, u32[]{:S(2)}) collective-permute-start(bf16[480,128]{1,0:T(8,128)(2,1)S(1)} %get-tuple-element.72), channel_id=1, source_target_pairs={{0,1},{1,0},{2,3},{3,2},{4,5},{5,4},{6,7},{7,6},{8,9},{9,8},{10,11... | collective-permute-start | bytes 368648 | tf_op jit(solution)/shard_map/ppermute | solution.py:18
  22.9 1.5 %collective-permute-start.9 = (bf16[960,128]{1,0:T(8,128)(2,1)S(1)}, bf16[960,128]{1,0:T(8,128)(2,1)S(1)}, u32[]{:S(2)}, u32[]{:S(2)}) collective-permute-start(bf16[960,128]{1,0:T(8,128)(2,1)S(1)} %collective-permute-done.8.mine), channel_id=1, source_target_pairs={{0,1},{1,0},{2,3},{3,2},{4,5},{5,4},{6,7},{7,6},{8,9},{9,8},{10,11... | collective-permute-start | bytes 737288 | tf_op jit(solution)/shard_map/ppermute | solution.py:18
  26.4 1.8 %collective-permute-start.10 = (bf16[480,384]{1,0:T(8,128)(2,1)S(1)}, bf16[480,384]{1,0:T(8,128)(2,1)S(1)}, u32[]{:S(2)}, u32[]{:S(2)}) collective-permute-start(bf16[480,384]{1,0:T(8,128)(2,1)S(1)} %get-tuple-element.62.act), channel_id=1, source_target_pairs={{0,1},{1,0},{2,3},{3,2},{4,5},{5,4},{6,7},{7,6},{8,9},{9,8},{10,11... | collective-permute-start | bytes 1105928 | tf_op jit(solution)/shard_map/ppermute | solution.py:18
  29.4 8.2 %collective-permute-start.14 = (bf16[960,128]{1,0:T(8,128)(2,1)S(1)}, bf16[960,128]{1,0:T(8,128)(2,1)S(1)}, u32[]{:S(2)}, u32[]{:S(2)}) collective-permute-start(bf16[960,128]{1,0:T(8,128)(2,1)S(1)} %shard_map.98), channel_id=1, source_target_pairs={{0,2},{2,0},{1,3},{3,1},{4,6},{6,4},{5,7},{7,5},{8,10},{10,8},{9,1... | collective-permute-start | bytes 737288 | tf_op jit(solution)/shard_map/ppermute | solution.py:18
  29.8 4.3 %collective-permute-start.11 = (bf16[320,192]{1,0:T(8,128)(2,1)S(1)}, bf16[320,192]{1,0:T(8,128)(2,1)S(1)}, u32[]{:S(2)}, u32[]{:S(2)}) collective-permute-start(bf16[320,192]{1,0:T(8,128)(2,1)S(1)} %get-tuple-element.65), channel_id=1, source_target_pairs={{0,1},{1,0},{2,3},{3,2},{4,5},{5,4},{6,7},{7,6},{8,9},{9,8},{10,11... | collective-permute-start | bytes 368648 | tf_op jit(solution)/shard_map/ppermute | solution.py:18
  29.8 5.9 %collective-permute-start.12 = (bf16[240,128]{1,0:T(8,128)(2,1)S(1)}, bf16[240,128]{1,0:T(8,128)(2,1)S(1)}, u32[]{:S(2)}, u32[]{:S(2)}) collective-permute-start(bf16[240,128]{1,0:T(8,128)(2,1)S(1)} %get-tuple-element.68), channel_id=1, source_target_pairs={{0,0},{4,8},{8,4},{12,12},{1,1},{5,9},{9,5},{13,13},{2,2},{6,10},{... | collective-permute-start | bytes 184328 | tf_op jit(solution)/shard_map/ppermute | solution.py:452
  30.5 5.9 %collective-permute-start.13 = (bf16[240,128]{1,0:T(8,128)(2,1)S(1)}, bf16[240,128]{1,0:T(8,128)(2,1)S(1)}, u32[]{:S(2)}, u32[]{:S(2)}) collective-permute-start(bf16[240,128]{1,0:T(8,128)(2,1)S(1)} %get-tuple-element.69), channel_id=1, source_target_pairs={{0,4},{4,0},{8,12},{12,8},{1,5},{5,1},{9,13},{13,9},{2,6},{6,2},{1... | collective-permute-start | bytes 184328 | tf_op jit(solution)/shard_map/ppermute | solution.py:455
